TPU v7x, 32 devices: a whole 2x2x4 slice. The times are simulated.
32 devices in a mesh: section: 2 (over core), dp: 4 (over y, x), tensor: 4 (over z).
Axes of the slice: x: 2, y: 2, z: 4, core: 2. Of those that a mesh axis runs over, the one named last changes fastest.
Arguments:
- inputs: bfloat16 [8, 1024, 1536], P('dp', 'tensor'), may hold values from -6 to 6
- lengths: int32 [8], P('dp'), may hold values from 256 to 1024, as said below
- adapter_ids: int32 [8], P('dp'), may hold values from 0 to 7, as said below
- cotangent: bfloat16 [8, 1024, 1536], P('dp', 'tensor'), may hold values from -6 to 6
- norm_gain: bfloat16 [2, 2, 1536], P('section'), may hold values from 0.25 to 1.75
- query_weight: bfloat16 [2, 1536, 1536], P('section', 'dp', 'tensor'), may hold values from -0.15625 to 0.15625
- query_bias: bfloat16 [2, 1536], P('section', 'tensor'), may hold values from -3 to 3
- keyvalue_weight: bfloat16 [2, 2, 1536, 256], P('section', None, 'dp'), may hold values from -0.15625 to 0.15625
- keyvalue_bias: bfloat16 [2, 2, 256], P('section'), may hold values from -3 to 3
- output_weight: bfloat16 [2, 1536, 1536], P('section', 'tensor', 'dp'), may hold values from -1.25 to 1.25
- expand_weight: bfloat16 [2, 2, 1536, 8960], P('section', None, 'dp', 'tensor'), may hold values from -0.15625 to 0.15625
- shrink_weight: bfloat16 [2, 8960, 1536], P('section', 'tensor', 'dp'), may hold values from -0.0625 to 0.0625
- adapter_input: bfloat16 [2, 8, 1536, 80], P('section'), may hold values from -0.15625 to 0.15625
- adapter_query: bfloat16 [2, 8, 16, 1536], P('section', None, None, 'tensor'), may hold values from -0.75 to 0.75
- adapter_keyvalue: bfloat16 [2, 8, 2, 16, 256], P('section'), may hold values from -0.75 to 0.75
- adapter_expand: bfloat16 [2, 8, 2, 16, 8960], P('section', None, None, None, 'tensor'), may hold values from -0.75 to 0.75
- adapter_attend: bfloat16 [2, 8, 1536, 16], P('section', None, 'tensor'), may hold values from -1.25 to 1.25
- adapter_shrink: bfloat16 [2, 8, 8960, 16], P('section', None, 'tensor'), may hold values from -0.0625 to 0.0625
- adapter_residual: bfloat16 [2, 8, 2, 16, 1536], P('section'), may hold values from -0.75 to 0.75
Outputs:
- layer_output: bfloat16 [2, 8, 1024, 1536], P('section', 'dp', 'tensor')
- input_grad: float32 [2, 8, 1024, 1536], P('section', 'dp', 'tensor')
- grad_adapter_input: float32 [2, 8, 1536, 80], P('section')
- grad_adapter_query: float32 [2, 8, 16, 1536], P('section', None, None, 'tensor')
- grad_adapter_keyvalue: float32 [2, 8, 2, 16, 256], P('section')
- grad_adapter_expand: float32 [2, 8, 2, 16, 8960], P('section', None, None, None, 'tensor')
- grad_adapter_attend: float32 [2, 8, 1536, 16], P('section', None, 'tensor')
- grad_adapter_shrink: float32 [2, 8, 8960, 16], P('section', None, 'tensor')
- grad_adapter_residual: float32 [2, 8, 2, 16, 1536], P('section')
Inputs may be any that keep to these rules, and one draw needn't show every extreme that they name: `lengths`: slots 0 to len - 1 of a sequence are valid; some sequence is full, some holds 256. `adapter_ids`: the first and the last adapter are named by some sequence.
All inputs are finite; a program needn't handle non-finite values.
Results may differ from a plain program's by a relative error of at most 0.03.
Values may be sent and summed in bfloat16 or wider, within the bound.
A program may use at most 248 MiB of HBM per device.

v0:
```python
from functools import partial
import math

import jax
import jax.numpy as jnp
from jax import lax
from jax.sharding import PartitionSpec as P

KV_HEADS = 2
HEAD_DIM = 128
RANK = 16


HIGHEST = lax.Precision.HIGHEST
EPSILON = 1e-06
ROPE_BASE = 1000000.0
MASKED_SCORE = -1e30


def from_behind(block, axis, distance):
    devices = range(lax.axis_size(axis))
    route = [(i - distance, i) for i in devices if i - distance in devices]
    return lax.ppermute(block, axis, route)


def for_sending(x):

    def short(part):
        return part.astype(jnp.bfloat16) if part.dtype == jnp.float32 else part

    return jax.tree.map(short, x)


def exact_dot(left_side, right_side):
    return jnp.dot(left_side, right_side, precision=HIGHEST)


def contract_rows(left_side, right_side):
    return lax.dot_general(left_side, right_side, (((0,), (0,)), ((), ())), precision=HIGHEST)


def times_transpose(left_side, right_side):
    return lax.dot_general(left_side, right_side, (((1,), (1,)), ((), ())), precision=HIGHEST)


def mixed_dot(left_side, right_side):
    return jnp.dot(left_side, right_side, preferred_element_type=jnp.float32)


def mixed_transpose(left_side, right_side):
    return lax.dot_general(
        left_side, right_side, (((1,), (1,)), ((), ())), preferred_element_type=jnp.float32
    )


def rotary_tables(seq_len, head_width):
    half_width = head_width // 2
    frequency = jnp.exp(
        -math.log(ROPE_BASE) * (2.0 * jnp.arange(half_width, dtype=jnp.float32) / head_width)
    )
    angles = jnp.arange(seq_len, dtype=jnp.float32)[:, None] * frequency[None, :]
    return (jnp.cos(angles), jnp.sin(angles))


def rotate(tensor, cosine_table, sine_table):
    half_width = tensor.shape[-1] // 2
    front_half = tensor[..., :half_width]
    back_half = tensor[..., half_width:]
    cos_part = cosine_table[:, None, :]
    sin_part = sine_table[:, None, :]
    return jnp.concatenate(
        [
            front_half * cos_part - back_half * sin_part,
            back_half * cos_part + front_half * sin_part,
        ],
        axis=-1,
    )


def rotate_back(tensor, cosine_table, sine_table):
    half_width = tensor.shape[-1] // 2
    front_half = tensor[..., :half_width]
    back_half = tensor[..., half_width:]
    cos_part = cosine_table[:, None, :]
    sin_part = sine_table[:, None, :]
    return jnp.concatenate(
        [
            front_half * cos_part + back_half * sin_part,
            back_half * cos_part - front_half * sin_part,
        ],
        axis=-1,
    )


def norm_back(values, inverse, gain_row, grad_out):
    weighted = gain_row * grad_out
    return inverse * weighted - inverse * inverse * inverse * values * jnp.mean(
        weighted * values, axis=-1, keepdims=True
    )


def spread_rows(rows_low):
    return lax.all_gather(rows_low, "tensor", axis=0, tiled=True)


def fold_rows(partial_rows):
    return lax.psum_scatter(
        partial_rows.astype(jnp.bfloat16), "tensor", scatter_dimension=0, tiled=True
    ).astype(jnp.float32)


def spread_grads(rows_low):
    return lax.all_gather(rows_low, "tensor", axis=0, tiled=True)


def fold_grads(partial_rows):
    return lax.psum_scatter(
        partial_rows.astype(jnp.bfloat16), "tensor", scatter_dimension=0, tiled=True
    ).astype(jnp.float32)


def masked_scores(query_block, key_rot, offset, length, score_scale):
    key_ids = jnp.arange(key_rot.shape[0])
    row_ids = offset + jnp.arange(query_block.shape[0])
    allowed = (key_ids[None, :] <= row_ids[:, None]) & (key_ids[None, :] < length)
    scores = (
        jnp.einsum("qhd,kd->hqk", query_block, key_rot, preferred_element_type=jnp.float32)
        * score_scale
    )
    return jnp.where(allowed[None], scores, MASKED_SCORE)


def attend(query_rot, key_rot, value_rot, length):
    seq_len, heads_here, head_width = query_rot.shape
    block_rows = min(512, seq_len)
    score_scale = head_width ** (-0.5)
    pieces = []
    log_parts = []
    for offset in range(0, seq_len, block_rows):
        scores = masked_scores(
            query_rot[offset : offset + block_rows], key_rot, offset, length, score_scale
        )
        peak = jnp.max(scores, axis=-1, keepdims=True)
        log_total = peak + jnp.log(jnp.sum(jnp.exp(scores - peak), axis=-1, keepdims=True))
        soft_rounded = jnp.exp(scores - log_total).astype(jnp.bfloat16)
        pieces.append(
            jnp.einsum("hqk,kd->qhd", soft_rounded, value_rot, preferred_element_type=jnp.float32)
        )
        log_parts.append(log_total)
    attended = (
        jnp.concatenate(pieces, axis=0)
        .reshape(seq_len, heads_here * head_width)
        .astype(jnp.bfloat16)
    )
    return (attended, jnp.concatenate(log_parts, axis=1))


def attend_back(query_rot, key_rot, value_rot, log_total, attended_grad, length):
    seq_len, heads_here, head_width = query_rot.shape
    block_rows = min(512, seq_len)
    score_scale = head_width ** (-0.5)
    grad_heads = attended_grad.reshape(seq_len, heads_here, head_width)
    query_parts = []
    key_grad = jnp.zeros((seq_len, head_width), jnp.float32)
    value_grad = jnp.zeros((seq_len, head_width), jnp.float32)
    for offset in range(0, seq_len, block_rows):
        query_block = query_rot[offset : offset + block_rows]
        grad_block = grad_heads[offset : offset + block_rows]
        scores = masked_scores(query_block, key_rot, offset, length, score_scale)
        soft_values = jnp.exp(scores - log_total[:, offset : offset + block_rows])
        soft_grad = jnp.einsum(
            "qhd,kd->hqk", grad_block, value_rot, preferred_element_type=jnp.float32
        )
        score_grad = (
            soft_values * (soft_grad - jnp.sum(soft_grad * soft_values, axis=-1, keepdims=True))
        ).astype(jnp.bfloat16)
        query_parts.append(
            jnp.einsum("hqk,kd->qhd", score_grad, key_rot, preferred_element_type=jnp.float32)
            * score_scale
        )
        key_grad = (
            key_grad
            + jnp.einsum("hqk,qhd->kd", score_grad, query_block, preferred_element_type=jnp.float32)
            * score_scale
        )
        value_grad = value_grad + jnp.einsum(
            "hqk,qhd->kd",
            soft_values.astype(jnp.bfloat16),
            grad_block,
            preferred_element_type=jnp.float32,
        )
    return (jnp.concatenate(query_parts, axis=0), key_grad, value_grad)


def select_adapter(adapter, adapter_index, pair_head):
    chosen = tuple(
        (lax.dynamic_index_in_dim(stack, adapter_index, 0, keepdims=False) for stack in adapter)
    )
    pair_adapter = lax.dynamic_slice_in_dim(chosen[2], pair_head * HEAD_DIM, HEAD_DIM, 2).astype(
        jnp.float32
    )
    return (chosen, pair_adapter)


def forward(rows_in, frozen, adapter, adapter_index, length, pair_head):
    (
        norm_gains,
        query_weight,
        query_bias,
        keyvalue_weight,
        keyvalue_bias,
        output_weight,
        expand_weight,
        shrink_weight,
    ) = frozen
    chosen, pair_adapter = select_adapter(adapter, adapter_index, pair_head)
    (
        adapter_input,
        adapter_query,
        adapter_keyvalue,
        adapter_expand,
        adapter_attend,
        adapter_shrink,
        adapter_residual,
    ) = chosen
    low_width = RANK
    pair_weight = lax.dynamic_slice_in_dim(keyvalue_weight, pair_head * HEAD_DIM, HEAD_DIM, 2)
    pair_bias = lax.dynamic_slice_in_dim(keyvalue_bias, pair_head * HEAD_DIM, HEAD_DIM, 1)
    inputs_f = rows_in.astype(jnp.float32)
    inverse_one = lax.rsqrt(jnp.mean(inputs_f * inputs_f, axis=-1, keepdims=True) + EPSILON)
    normed = spread_rows((inputs_f * inverse_one * norm_gains[0]).astype(jnp.bfloat16))
    seq_len = normed.shape[0]
    low_rank = mixed_dot(normed, adapter_input[:, : 3 * low_width])
    queries = (
        mixed_dot(normed, query_weight)
        + query_bias
        + exact_dot(low_rank[:, :low_width], adapter_query.astype(jnp.float32))
    )
    key_proj = (
        mixed_dot(normed, pair_weight[0])
        + pair_bias[0]
        + exact_dot(low_rank[:, low_width : 2 * low_width], pair_adapter[0])
    )
    value_proj = (
        mixed_dot(normed, pair_weight[1])
        + pair_bias[1]
        + exact_dot(low_rank[:, 2 * low_width :], pair_adapter[1])
    )
    cosine_table, sine_table = rotary_tables(seq_len, HEAD_DIM)
    heads_here = queries.shape[1] // HEAD_DIM
    query_rot = rotate(
        queries.reshape(seq_len, heads_here, HEAD_DIM), cosine_table, sine_table
    ).astype(jnp.bfloat16)
    key_rot = rotate(key_proj[:, None, :], cosine_table, sine_table)[:, 0].astype(jnp.bfloat16)
    value_rot = value_proj.astype(jnp.bfloat16)
    attended, log_total = attend(query_rot, key_rot, value_rot, length)
    attend_rank = mixed_dot(attended, adapter_attend)
    branch = fold_rows(
        mixed_dot(attended, output_weight)
        + exact_dot(attend_rank, adapter_residual[0].astype(jnp.float32))
    )
    middle = inputs_f + branch
    inverse_two = lax.rsqrt(jnp.mean(middle * middle, axis=-1, keepdims=True) + EPSILON)
    normed_two = spread_rows((middle * inverse_two * norm_gains[1]).astype(jnp.bfloat16))
    expand_rank = mixed_dot(normed_two, adapter_input[:, 3 * low_width :])
    gate_value = mixed_dot(normed_two, expand_weight[0]) + exact_dot(
        expand_rank[:, :low_width], adapter_expand[0].astype(jnp.float32)
    )
    upward = mixed_dot(normed_two, expand_weight[1]) + exact_dot(
        expand_rank[:, low_width:], adapter_expand[1].astype(jnp.float32)
    )
    activated = (jax.nn.silu(gate_value) * upward).astype(jnp.bfloat16)
    shrink_rank = mixed_dot(activated, adapter_shrink)
    shrunk = fold_rows(
        mixed_dot(activated, shrink_weight)
        + exact_dot(shrink_rank, adapter_residual[1].astype(jnp.float32))
    )
    kept_values = (
        inputs_f,
        inverse_one,
        normed,
        low_rank,
        query_rot,
        key_rot,
        value_rot,
        log_total,
        attended,
        attend_rank,
        middle,
        inverse_two,
        normed_two,
        expand_rank,
        gate_value,
        upward,
        activated,
        shrink_rank,
        adapter_index,
        length,
    )
    return (middle + shrunk, kept_values)


def backward(grad_rows, frozen, adapter, kept_values, pair_head):
    (
        norm_gains,
        query_weight,
        query_bias,
        keyvalue_weight,
        keyvalue_bias,
        output_weight,
        expand_weight,
        shrink_weight,
    ) = frozen
    (
        inputs_f,
        inverse_one,
        normed,
        low_rank,
        query_rot,
        key_rot,
        value_rot,
        log_total,
        attended,
        attend_rank,
        middle,
        inverse_two,
        normed_two,
        expand_rank,
        gate_value,
        upward,
        activated,
        shrink_rank,
        adapter_index,
        length,
    ) = kept_values
    chosen, pair_adapter = select_adapter(adapter, adapter_index, pair_head)
    (
        adapter_input,
        adapter_query,
        adapter_keyvalue,
        adapter_expand,
        adapter_attend,
        adapter_shrink,
        adapter_residual,
    ) = chosen
    low_width = RANK
    pair_weight = lax.dynamic_slice_in_dim(keyvalue_weight, pair_head * HEAD_DIM, HEAD_DIM, 2)
    residual_f = adapter_residual.astype(jnp.float32)
    expand_f = adapter_expand.astype(jnp.float32)
    input_f = adapter_input.astype(jnp.float32)
    seq_len = normed.shape[0]
    shrunk_grad = spread_grads(grad_rows.astype(jnp.bfloat16))
    shrunk_f = shrunk_grad.astype(jnp.float32)
    shrink_rank_grad = times_transpose(shrunk_f, residual_f[1])
    activated_grad = mixed_transpose(shrunk_grad, shrink_weight) + times_transpose(
        shrink_rank_grad, adapter_shrink.astype(jnp.float32)
    )
    grad_shrink = contract_rows(activated.astype(jnp.float32), shrink_rank_grad)
    grad_residual_two = contract_rows(shrink_rank, shrunk_f)
    sigmoid_gate = jax.nn.sigmoid(gate_value)
    gate_grad = (
        activated_grad * upward * sigmoid_gate * (1.0 + gate_value * (1.0 - sigmoid_gate))
    ).astype(jnp.bfloat16)
    upward_grad = (activated_grad * gate_value * sigmoid_gate).astype(jnp.bfloat16)
    gate_f = gate_grad.astype(jnp.float32)
    upward_f = upward_grad.astype(jnp.float32)
    expand_rank_grad = jnp.concatenate(
        [times_transpose(gate_f, expand_f[0]), times_transpose(upward_f, expand_f[1])], axis=1
    )
    grad_expand = jnp.stack(
        [
            contract_rows(expand_rank[:, :low_width], gate_f),
            contract_rows(expand_rank[:, low_width:], upward_f),
        ]
    )
    normed_two_grad = fold_grads(
        mixed_transpose(gate_grad, expand_weight[0])
        + mixed_transpose(upward_grad, expand_weight[1])
        + times_transpose(expand_rank_grad, input_f[:, 3 * low_width :])
    )
    grad_input_high = contract_rows(normed_two.astype(jnp.float32), expand_rank_grad)
    middle_grad = grad_rows + norm_back(middle, inverse_two, norm_gains[1], normed_two_grad)
    branch_grad = spread_grads(middle_grad.astype(jnp.bfloat16))
    branch_f = branch_grad.astype(jnp.float32)
    attend_rank_grad = times_transpose(branch_f, residual_f[0])
    attended_grad = (
        mixed_transpose(branch_grad, output_weight)
        + times_transpose(attend_rank_grad, adapter_attend.astype(jnp.float32))
    ).astype(jnp.bfloat16)
    grad_attend = contract_rows(attended.astype(jnp.float32), attend_rank_grad)
    grad_residual_one = contract_rows(attend_rank, branch_f)
    query_grad, key_grad, value_grad = attend_back(
        query_rot, key_rot, value_rot, log_total, attended_grad, length
    )
    cosine_table, sine_table = rotary_tables(seq_len, HEAD_DIM)
    query_grad = (
        rotate_back(query_grad, cosine_table, sine_table).reshape(seq_len, -1).astype(jnp.bfloat16)
    )
    key_grad = rotate_back(key_grad[:, None, :], cosine_table, sine_table)[:, 0].astype(
        jnp.bfloat16
    )
    value_grad = value_grad.astype(jnp.bfloat16)
    query_f = query_grad.astype(jnp.float32)
    key_f = key_grad.astype(jnp.float32)
    value_f = value_grad.astype(jnp.float32)
    low_rank_grad = jnp.concatenate(
        [
            times_transpose(query_f, adapter_query.astype(jnp.float32)),
            times_transpose(key_f, pair_adapter[0]),
            times_transpose(value_f, pair_adapter[1]),
        ],
        axis=1,
    )
    grad_query = contract_rows(low_rank[:, :low_width], query_f)
    pair_grad = jnp.stack(
        [
            contract_rows(low_rank[:, low_width : 2 * low_width], key_f),
            contract_rows(low_rank[:, 2 * low_width :], value_f),
        ]
    )
    grad_keyvalue = lax.dynamic_update_slice_in_dim(
        jnp.zeros(adapter_keyvalue.shape, jnp.float32), pair_grad, pair_head * HEAD_DIM, 2
    )
    normed_grad = fold_grads(
        mixed_transpose(query_grad, query_weight)
        + mixed_transpose(key_grad, pair_weight[0])
        + mixed_transpose(value_grad, pair_weight[1])
        + times_transpose(low_rank_grad, input_f[:, : 3 * low_width])
    )
    grad_input_low = contract_rows(normed.astype(jnp.float32), low_rank_grad)
    inputs_grad = middle_grad + norm_back(inputs_f, inverse_one, norm_gains[0], normed_grad)
    grads = (
        jnp.concatenate([grad_input_low, grad_input_high], axis=1),
        grad_query,
        grad_keyvalue,
        grad_expand,
        grad_attend,
        grad_shrink,
        jnp.stack([grad_residual_one, grad_residual_two]),
    )
    return (inputs_grad, grads, adapter_index)


def add_at(running, adapter_index, grad_term):
    current = lax.dynamic_index_in_dim(running, adapter_index, 0, keepdims=False)
    return lax.dynamic_update_index_in_dim(running, current + grad_term, adapter_index, 0)


def local(
    inputs,
    lengths,
    adapter_ids,
    cotangent,
    norm_gain,
    query_weight,
    query_bias,
    keyvalue_weight,
    keyvalue_bias,
    output_weight,
    expand_weight,
    shrink_weight,
    adapter_input,
    adapter_query,
    adapter_keyvalue,
    adapter_expand,
    adapter_attend,
    adapter_shrink,
    adapter_residual,
):
    front_section = lax.axis_index("section") == 0
    micro_count = inputs.shape[0]
    local_rows = inputs.shape[1]
    tensor_count = lax.axis_size("tensor")
    pair_head = lax.axis_index("tensor") // (tensor_count // KV_HEADS)
    grad_scale = 1.0 / math.sqrt(micro_count * local_rows * tensor_count * lax.axis_size("dp"))
    sharded = (query_weight, keyvalue_weight, output_weight, expand_weight, shrink_weight)
    norm_gains = norm_gain[0].astype(jnp.float32)
    bias_query = query_bias[0].astype(jnp.float32)
    bias_pair = keyvalue_bias[0].astype(jnp.float32)
    adapter = tuple(
        (
            stack[0]
            for stack in (
                adapter_input,
                adapter_query,
                adapter_keyvalue,
                adapter_expand,
                adapter_attend,
                adapter_shrink,
                adapter_residual,
            )
        )
    )

    def frozen_set():
        fetched = (
            lax.all_gather(sharded[0], "dp", axis=1, tiled=True),
            lax.all_gather(sharded[1], "dp", axis=2, tiled=True),
            lax.all_gather(sharded[2], "dp", axis=2, tiled=True),
            lax.all_gather(sharded[3], "dp", axis=2, tiled=True),
            lax.all_gather(sharded[4], "dp", axis=2, tiled=True),
        )
        return (
            norm_gains,
            fetched[0][0],
            bias_query,
            fetched[1][0],
            bias_pair,
            fetched[2][0],
            fetched[3][0],
            fetched[4][0],
        )

    slot_ids = lax.axis_index("tensor") * local_rows + jnp.arange(local_rows, dtype=jnp.int32)
    arriving = jnp.zeros(inputs.shape[1:], jnp.bfloat16)
    outputs_tick = []
    kept_tick = []
    for moment in range(micro_count + 1):
        micro_batch = jnp.where(front_section, min(moment, micro_count - 1), max(moment - 1, 0))
        rows_in = jnp.where(front_section, inputs[min(moment, micro_count - 1)], arriving)
        adapter_index = lax.dynamic_index_in_dim(adapter_ids, micro_batch, 0, keepdims=False)
        length = lax.dynamic_index_in_dim(lengths, micro_batch, 0, keepdims=False)
        result, kept_values = forward(
            rows_in, frozen_set(), adapter, adapter_index, length, pair_head
        )
        result = result.astype(jnp.bfloat16)
        outputs_tick.append(result)
        kept_tick.append(kept_values)
        if moment < micro_count:
            arriving = from_behind(result, "section", 1)
    returning = jnp.zeros(inputs.shape[1:], jnp.float32)
    running = tuple((jnp.zeros(stack.shape, jnp.float32) for stack in adapter))
    grads_tick = []
    for moment in range(micro_count + 1):
        back_micro = min(moment, micro_count - 1)
        front_micro = max(moment - 1, 0)
        kept_values = jax.tree.map(
            partial(jnp.where, front_section), kept_tick[front_micro], kept_tick[back_micro + 1]
        )
        valid_rows = (slot_ids < lengths[back_micro]).astype(jnp.float32)[:, None]
        incoming = jnp.where(
            front_section, returning, cotangent[back_micro].astype(jnp.float32) * valid_rows
        )
        inputs_grad, grads, adapter_index = backward(
            incoming, frozen_set(), adapter, kept_values, pair_head
        )
        weight_flag = (
            jnp.where(front_section, float(moment >= 1), float(moment < micro_count)) * grad_scale
        )
        running = tuple(
            (
                add_at(total_now, adapter_index, grad_term * weight_flag)
                for total_now, grad_term in zip(running, grads)
            )
        )
        grads_tick.append(inputs_grad)
        if moment < micro_count:
            returning = from_behind(for_sending(inputs_grad), "section", -1).astype(
                inputs_grad.dtype
            )
    layer_rows = jnp.stack(
        [
            jnp.where(front_section, outputs_tick[slot_index], outputs_tick[slot_index + 1])
            for slot_index in range(micro_count)
        ]
    )
    grad_rows_all = jnp.stack(
        [
            jnp.where(front_section, grads_tick[slot_index + 1], grads_tick[slot_index])
            for slot_index in range(micro_count)
        ]
    )
    summed_data = (
        lax.psum(running[1].astype(jnp.bfloat16), "dp").astype(jnp.float32),
        lax.psum(running[3].astype(jnp.bfloat16), "dp").astype(jnp.float32),
        lax.psum(running[4].astype(jnp.bfloat16), "dp").astype(jnp.float32),
        lax.psum(running[5].astype(jnp.bfloat16), "dp").astype(jnp.float32),
    )
    summed_whole = lax.psum((running[0], running[2], running[6]), ("dp", "tensor"))
    return (
        layer_rows[None],
        grad_rows_all[None],
        summed_whole[0][None],
        summed_data[0][None],
        summed_whole[1][None],
        summed_data[1][None],
        summed_data[2][None],
        summed_data[3][None],
        summed_whole[2][None],
    )


def solution(mesh):
    placed = (
        P("dp", "tensor", None),
        P("dp"),
        P("dp"),
        P("dp", "tensor", None),
        P("section", None, None),
        P("section", "dp", "tensor"),
        P("section", "tensor"),
        P("section", None, "dp", None),
        P("section", None, None),
        P("section", "tensor", "dp"),
        P("section", None, "dp", "tensor"),
        P("section", "tensor", "dp"),
        P("section", None, None, None),
        P("section", None, None, "tensor"),
        P("section", None, None, None, None),
        P("section", None, None, None, "tensor"),
        P("section", None, "tensor", None),
        P("section", None, "tensor", None),
        P("section", None, None, None, None),
    )
    return jax.shard_map(
        local,
        mesh=mesh,
        in_specs=placed,
        out_specs=(
            P("section", "dp", "tensor", None),
            P("section", "dp", "tensor", None),
            P("section", None, None, None),
            P("section", None, None, "tensor"),
            P("section", None, None, None, None),
            P("section", None, None, None, "tensor"),
            P("section", None, "tensor", None),
            P("section", None, "tensor", None),
            P("section", None, None, None, None),
        ),
        check_vma=False,
    )
```

profile of v0, /device:TPU:0, one launch (start us, length us, event | category | flops | bytes accessed | tf_op | source)
XLA Modules:
  0.0 2508.1 jit_solution(8872372554311025809)
XLA Ops:
  41.0 37.7 %all-gather.18.cloned.1.call-done = bf16[1024,1536]{1,0:T(8,128)(2,1)} async-done(((bf16[256,1536]{1,0:T(8,128)(2,1)}), bf16[1024,1536]{1,0:T(8,128)(2,1)}) %all-gather.18.cloned.1.call-update) | async-done | bytes 3145744 | tf_op jit(solution)/shard_map/all_gather | solution.py:103
  184.4 60.4 %reduce-scatter.13.cloned.1.call-done = bf16[256,1536]{1,0:T(8,128)(2,1)} async-done(((bf16[1024,1536]{1,0:T(8,128)(2,1)}), bf16[256,1536]{1,0:T(8,128)(2,1)}) %reduce-scatter.13.cloned.1.call-update) | async-done | bytes 786448 | tf_op jit(solution)/shard_map/reduce_scatter | solution.py:107
  250.2 62.1 %all-gather.26.cloned.1.call-done = bf16[1024,1536]{1,0:T(8,128)(2,1)} async-done(((bf16[256,1536]{1,0:T(8,128)(2,1)}), bf16[1024,1536]{1,0:T(8,128)(2,1)}) %all-gather.26.cloned.1.call-update) | async-done | bytes 3145744 | tf_op jit(solution)/shard_map/all_gather | solution.py:103
  315.2 129.8 %all-gather.28.cloned.1.call-done = bf16[1,2,1536,2240]{2,3,1,0:T(8,128)(2,1)} async-done(((bf16[1,2,384,2240]{2,3,1,0:T(8,128)(2,1)}), bf16[1,2,1536,2240]{2,3,1,0:T(8,128)(2,1)}) %all-gather.28.cloned.1.call-update) | async-done | bytes 13762576 | tf_op jit(solution)/shard_map/all_gather | solution.py:500
  496.5 25.3 %all-gather.30.cloned.1.call-done = bf16[1,2240,1536]{2,1,0:T(8,128)(2,1)} async-done(((bf16[1,2240,384]{2,1,0:T(8,128)(2,1)}), bf16[1,2240,1536]{2,1,0:T(8,128)(2,1)}) %all-gather.30.cloned.1.call-update) | async-done | bytes 6881296 | tf_op jit(solution)/shard_map/all_gather | solution.py:501
  539.1 60.4 %reduce-scatter.15.cloned.1.call-done = bf16[256,1536]{1,0:T(8,128)(2,1)} async-done(((bf16[1024,1536]{1,0:T(8,128)(2,1)}), bf16[256,1536]{1,0:T(8,128)(2,1)}) %reduce-scatter.15.cloned.1.call-update) | async-done | bytes 786448 | tf_op jit(solution)/shard_map/reduce_scatter | solution.py:107
  606.4 63.9 %all-gather.32.cloned.1.call-done = bf16[1024,1536]{1,0:T(8,128)(2,1)} async-done(((bf16[256,1536]{1,0:T(8,128)(2,1)}), bf16[1024,1536]{1,0:T(8,128)(2,1)}) %all-gather.32.cloned.1.call-update) | async-done | bytes 3145744 | tf_op jit(solution)/shard_map/all_gather | solution.py:103
  726.2 56.0 %reduce-scatter.17.cloned.1.call-done = bf16[256,1536]{1,0:T(8,128)(2,1)} async-done(((bf16[1024,1536]{1,0:T(8,128)(2,1)}), bf16[256,1536]{1,0:T(8,128)(2,1)}) %reduce-scatter.17.cloned.1.call-update) | async-done | bytes 786448 | tf_op jit(solution)/shard_map/reduce_scatter | solution.py:107
  786.6 61.1 %all-gather.40.cloned.1.call-done = bf16[1024,1536]{1,0:T(8,128)(2,1)} async-done(((bf16[256,1536]{1,0:T(8,128)(2,1)}), bf16[1024,1536]{1,0:T(8,128)(2,1)}) %all-gather.40.cloned.1.call-update) | async-done | bytes 3145744 | tf_op jit(solution)/shard_map/all_gather | solution.py:113
  862.5 49.6 %all-gather.34.cloned.1.call-done = bf16[1024,1536]{1,0:T(8,128)(2,1)} async-done(((bf16[256,1536]{1,0:T(8,128)(2,1)}), bf16[1024,1536]{1,0:T(8,128)(2,1)}) %all-gather.34.cloned.1.call-update) | async-done | bytes 3145744 | tf_op jit(solution)/shard_map/all_gather | solution.py:103
  1015.7 27.0 %reduce-scatter.19.cloned.1.call-done = bf16[256,1536]{1,0:T(8,128)(2,1)} async-done(((bf16[1024,1536]{1,0:T(8,128)(2,1)}), bf16[256,1536]{1,0:T(8,128)(2,1)}) %reduce-scatter.19.cloned.1.call-update) | async-done | bytes 786448 | tf_op jit(solution)/shard_map/reduce_scatter | solution.py:107
  1060.1 45.6 %reduce-scatter.25.cloned.1.call-done = bf16[256,1536]{1,0:T(8,128)(2,1)} async-done(((bf16[1024,1536]{1,0:T(8,128)(2,1)}), bf16[256,1536]{1,0:T(8,128)(2,1)}) %reduce-scatter.25.cloned.1.call-update) | async-done | bytes 786448 | tf_op jit(solution)/shard_map/reduce_scatter | solution.py:117
  1114.6 63.0 %all-gather.36.cloned.1.call-done = bf16[1024,1536]{1,0:T(8,128)(2,1)} async-done(((bf16[256,1536]{1,0:T(8,128)(2,1)}), bf16[1024,1536]{1,0:T(8,128)(2,1)}) %all-gather.36.cloned.1.call-update) | async-done | bytes 3145744 | tf_op jit(solution)/shard_map/all_gather | solution.py:103
  1327.0 58.7 %reduce-scatter.27.cloned.1.call-done = bf16[256,1536]{1,0:T(8,128)(2,1)} async-done(((bf16[1024,1536]{1,0:T(8,128)(2,1)}), bf16[256,1536]{1,0:T(8,128)(2,1)}) %reduce-scatter.27.cloned.1.call-update) | async-done | bytes 786448 | tf_op jit(solution)/shard_map/reduce_scatter | solution.py:117
  1397.5 53.8 %all-gather.38.cloned.1.call-done = bf16[1024,1536]{1,0:T(8,128)(2,1)} async-done(((bf16[256,1536]{1,0:T(8,128)(2,1)}), bf16[1024,1536]{1,0:T(8,128)(2,1)}) %all-gather.38.cloned.1.call-update) | async-done | bytes 3145744 | tf_op jit(solution)/shard_map/all_gather | solution.py:103
  1485.4 30.2 %all-gather.44.cloned.1.call-done = bf16[1024,1536]{1,0:T(8,128)(2,1)} async-done(((bf16[256,1536]{1,0:T(8,128)(2,1)}), bf16[1024,1536]{1,0:T(8,128)(2,1)}) %all-gather.44.cloned.1.call-update) | async-done | bytes 3145744 | tf_op jit(solution)/shard_map/all_gather | solution.py:113
  1526.1 27.1 %multiply_convert_fusion.2 = (bf16[1024,2240]{0,1:T(8,128)(2,1)}, bf16[1024,2240]{0,1:T(8,128)(2,1)}, bf16[1024,2240]{0,1:T(8,128)(2,1)}) fusion(f32[1024,2240]{0,1:T(8,128)} %copy-done.35, f32[1024,2240]{0,1:T(8,128)} %convolution_add_fusion.2, pred[]{:T(512)S(6)} %eq.3, f32[1024,2240]{0,1:T(8,128)} %get-tuple-element.159, ...), kind=kOutput, calls=%fused_computation.3 | convolution fusion | flops 7096893440 | bytes 69664768 | tf_op jit(solution)/shard_map/dot_general | solution.py:51
  1584.6 59.0 %reduce-scatter.29.cloned.1.call-done = bf16[256,1536]{1,0:T(8,128)(2,1)} async-done(((bf16[1024,1536]{1,0:T(8,128)(2,1)}), bf16[256,1536]{1,0:T(8,128)(2,1)}) %reduce-scatter.29.cloned.1.call-update) | async-done | bytes 786448 | tf_op jit(solution)/shard_map/reduce_scatter | solution.py:117
  1661.0 52.6 %all-gather.46.cloned.1.call-done = bf16[1024,1536]{1,0:T(8,128)(2,1)} async-done(((bf16[256,1536]{1,0:T(8,128)(2,1)}), bf16[1024,1536]{1,0:T(8,128)(2,1)}) %all-gather.46.cloned.1.call-update) | async-done | bytes 3145744 | tf_op jit(solution)/shard_map/all_gather | solution.py:113
  1760.9 59.0 %reduce-scatter.31.cloned.1.call-done = bf16[256,1536]{1,0:T(8,128)(2,1)} async-done(((bf16[1024,1536]{1,0:T(8,128)(2,1)}), bf16[256,1536]{1,0:T(8,128)(2,1)}) %reduce-scatter.31.cloned.1.call-update) | async-done | bytes 786448 | tf_op jit(solution)/shard_map/reduce_scatter | solution.py:117
  1832.8 63.6 %all-gather.48.cloned.1.call-done = bf16[1024,1536]{1,0:T(8,128)(2,1)} async-done(((bf16[256,1536]{1,0:T(8,128)(2,1)}), bf16[1024,1536]{1,0:T(8,128)(2,1)}) %all-gather.48.cloned.1.call-update) | async-done | bytes 3145744 | tf_op jit(solution)/shard_map/all_gather | solution.py:113
  2195.5 29.2 %all-reduce.7.cloned.1.call-done = (bf16[1,8,16,384]{3,2,1,0:T(8,128)(2,1)}, bf16[1,8,2,16,2240]{4,3,2,1,0:T(8,128)(2,1)}, bf16[1,8,384,16]{2,3,1,0:T(8,128)(2,1)}, bf16[1,8,2240,16]{2,3,1,0:T(8,128)(2,1)}) async-done(((bf16[1,8,16,384]{3,2,1,0:T(8,128)(2,1)}, bf16[1,8,2,16,2240]{4,3,2,1,0:T(8,128)(2,1)}, bf16[1,8,384,16]{2,3,1,0:T(8,128)(2,1)}, bf16[1,8,2240,16]{2,3,1,0:T(8,128)(2,1)}), ...) | async-done | bytes 1916944 | tf_op jit(solution)/shard_map/psum | solution.py:574
  2230.2 57.0 %reduce-scatter.35.cloned.1.call-done = bf16[256,1536]{1,0:T(8,128)(2,1)} async-done(((bf16[1024,1536]{1,0:T(8,128)(2,1)}), bf16[256,1536]{1,0:T(8,128)(2,1)}) %reduce-scatter.35.cloned.1.call-update) | async-done | bytes 786448 | tf_op jit(solution)/shard_map/reduce_scatter | solution.py:117
  2293.1 201.7 %all-reduce.5.cloned.1.call-done = (f32[1,8,1536,80]{2,3,1,0:T(8,128)}, f32[1,8,2,16,256]{4,3,2,1,0:T(8,128)}, f32[1,8,2,16,1536]{4,3,2,1,0:T(8,128)}) async-done(((f32[1,8,1536,80]{2,3,1,0:T(8,128)}, f32[1,8,2,16,256]{4,3,2,1,0:T(8,128)}, f32[1,8,2,16,1536]{4,3,2,1,0:T(8,128)}), (f32[1,8,1536,80]{2,3,1,0:T(8,128)}, f32[1,8,2,16,256]{4,3,2,1,0:T(8,128)}, ...) | async-done | bytes 5767184 | tf_op jit(solution)/shard_map/psum | solution.py:579
  (1195 shorter events, 1041.0 us)
Async XLA Ops:
  13.8 162.3 %all-gather.24.cloned.1.call-start = ((), (), s32[]{:S(2)}) async-start(), calls=%async_computation.15 | async-start | bytes 1474560 | tf_op jit(solution)/shard_map/all_gather | solution.py:499
  14.4 230.3 %reduce-scatter.13.cloned.1.call-start = ((), (), s32[]{:S(2)}) async-start(), calls=%async_computation.16 | async-start | bytes 3932160 | tf_op jit(solution)/shard_map/reduce_scatter | solution.py:107
  184.3 128.0 %all-gather.26.cloned.1.call-start = ((), (), s32[]{:S(2)}) async-start(), calls=%async_computation.17 | async-start | bytes 3932160 | tf_op jit(solution)/shard_map/all_gather | solution.py:103
  248.7 196.4 %all-gather.28.cloned.1.call-start = ((), (), s32[]{:S(2)}) async-start(), calls=%async_computation.18 | async-start | bytes 17203200 | tf_op jit(solution)/shard_map/all_gather | solution.py:500
  249.4 272.4 %all-gather.30.cloned.1.call-start = ((), (), s32[]{:S(2)}) async-start(), calls=%async_computation.19 | async-start | bytes 8601600 | tf_op jit(solution)/shard_map/all_gather | solution.py:501
  250.2 349.3 %reduce-scatter.15.cloned.1.call-start = ((), (), s32[]{:S(2)}) async-start(), calls=%async_computation.20 | async-start | bytes 3932160 | tf_op jit(solution)/shard_map/reduce_scatter | solution.py:107
  539.1 131.2 %all-gather.32.cloned.1.call-start = ((), (), s32[]{:S(2)}) async-start(), calls=%async_computation.21 | async-start | bytes 3932160 | tf_op jit(solution)/shard_map/all_gather | solution.py:103
  606.3 175.9 %reduce-scatter.17.cloned.1.call-start = ((), (), s32[]{:S(2)}) async-start(), calls=%async_computation.22 | async-start | bytes 3932160 | tf_op jit(solution)/shard_map/reduce_scatter | solution.py:107
  726.2 185.9 %all-gather.34.cloned.1.call-start = ((), (), s32[]{:S(2)}) async-start(), calls=%async_computation.23 | async-start | bytes 3932160 | tf_op jit(solution)/shard_map/all_gather | solution.py:103
  786.6 256.1 %reduce-scatter.19.cloned.1.call-start = ((), (), s32[]{:S(2)}) async-start(), calls=%async_computation.24 | async-start | bytes 3932160 | tf_op jit(solution)/shard_map/reduce_scatter | solution.py:107
  1015.7 162.0 %all-gather.36.cloned.1.call-start = ((), (), s32[]{:S(2)}) async-start(), calls=%async_computation.25 | async-start | bytes 3932160 | tf_op jit(solution)/shard_map/all_gather | solution.py:103
  1114.5 208.0 %reduce-scatter.21.cloned.1.call-start = ((), (), s32[]{:S(2)}) async-start(), calls=%async_computation.26 | async-start | bytes 3932160 | tf_op jit(solution)/shard_map/reduce_scatter | solution.py:107
  1308.3 143.0 %all-gather.38.cloned.1.call-start = ((), (), s32[]{:S(2)}) async-start(), calls=%async_computation.27 | async-start | bytes 3932160 | tf_op jit(solution)/shard_map/all_gather | solution.py:103
  1327.0 188.7 %all-gather.44.cloned.1.call-start = ((), (), s32[]{:S(2)}) async-start(), calls=%async_computation.33 | async-start | bytes 3932160 | tf_op jit(solution)/shard_map/all_gather | solution.py:113
  1397.4 246.2 %reduce-scatter.29.cloned.1.call-start = ((), (), s32[]{:S(2)}) async-start(), calls=%async_computation.34 | async-start | bytes 3932160 | tf_op jit(solution)/shard_map/reduce_scatter | solution.py:117
  1584.6 129.1 %all-gather.46.cloned.1.call-start = ((), (), s32[]{:S(2)}) async-start(), calls=%async_computation.35 | async-start | bytes 3932160 | tf_op jit(solution)/shard_map/all_gather | solution.py:113
  1650.0 169.9 %reduce-scatter.31.cloned.1.call-start = ((), (), s32[]{:S(2)}) async-start(), calls=%async_computation.36 | async-start | bytes 3932160 | tf_op jit(solution)/shard_map/reduce_scatter | solution.py:117
  1760.9 135.5 %all-gather.48.cloned.1.call-start = ((), (), s32[]{:S(2)}) async-start(), calls=%async_computation.37 | async-start | bytes 3932160 | tf_op jit(solution)/shard_map/all_gather | solution.py:113
  1832.7 184.4 %reduce-scatter.33.cloned.1.call-start = ((), (), s32[]{:S(2)}) async-start(), calls=%async_computation.38 | async-start | bytes 3932160 | tf_op jit(solution)/shard_map/reduce_scatter | solution.py:117
  1958.1 134.9 %all-gather.50.cloned.1.call-start = ((), (), s32[]{:S(2)}) async-start(), calls=%async_computation.39 | async-start | bytes 3932160 | tf_op jit(solution)/shard_map/all_gather | solution.py:113
  2022.2 170.2 %reduce-scatter.23.cloned.1.call-start = ((), (), s32[]{:S(2)}) async-start(), calls=%async_computation.28 | async-start | bytes 3932160 | tf_op jit(solution)/shard_map/reduce_scatter | solution.py:107
  2065.2 159.5 %all-reduce.7.cloned.1.call-start = ((), (), s32[]{:S(2)}) async-start(), calls=%async_computation.42 | async-start | bytes 3932160 | tf_op jit(solution)/shard_map/psum | solution.py:574
  2152.2 134.9 %reduce-scatter.35.cloned.1.call-start = ((), (), s32[]{:S(2)}) async-start(), calls=%async_computation.40 | async-start | bytes 3932160 | tf_op jit(solution)/shard_map/reduce_scatter | solution.py:117
  2162.9 331.9 %all-reduce.5.cloned.1.call-start = ((), (), s32[]{:S(2)}) async-start(), calls=%async_computation.41 | async-start | bytes 11534336 | tf_op jit(solution)/shard_map/psum | solution.py:579
  (383 other events, 7040.6 us)
Sparse Core Ops, SparseCore 0:
  12.5 66.1 all-gather.17
  184.4 60.2 reduce-scatter.12
  248.8 63.5 all-gather.25
  314.1 130.8 all-gather.27
  446.8 74.9 all-gather.29
  539.2 60.2 reduce-scatter.14
  606.4 63.7 all-gather.31
  784.2 63.5 all-gather.39
  849.9 62.1 all-gather.33
  983.7 58.8 reduce-scatter.18
  1045.4 60.2 reduce-scatter.24
  1114.1 63.5 all-gather.35
  1179.6 62.1 all-gather.41
  1263.6 58.8 reduce-scatter.20
  1325.4 60.2 reduce-scatter.26
  1387.7 63.5 all-gather.37
  1453.4 62.1 all-gather.43
  1584.7 58.8 reduce-scatter.28
  1650.1 63.5 all-gather.45
  1832.9 63.5 all-gather.47
  2022.3 63.5 all-gather.49
  2152.3 72.3 all-reduce.6
  2226.8 60.2 reduce-scatter.34
  2294.1 200.6 all-reduce.4
  (7 shorter events, 320.0 us)
where the time goes:
time: 2520 us; the launch traced here: 2510 us
  waiting for transfers between devices  1500 us (60%)
  matrix products  709 us (28%)
  other arithmetic  153 us (6%)
  local copies, waits for them, and re-layouts  87 us (3%)
  between operations  33.3 us (1%)
    all_gather x6, waiting for transfers between devices, spread_rows(): return lax.all_gather(rows_low, 'tensor', axis=0, tiled=True)  330 us
    reduce_scatter x6, waiting for transfers between devices, fold_grads(): lax.psum_scatter(partial_rows.astype(jnp.bfloat16), 'tensor', scatter_dim...  293 us
    all_gather x6, waiting for transfers between devices, spread_grads(): return lax.all_gather(rows_low, 'tensor', axis=0, tiled=True)  220 us
    reduce_scatter x6, waiting for transfers between devices, fold_rows(): lax.psum_scatter(partial_rows.astype(jnp.bfloat16), 'tensor', scatter_dim...  218 us
    psum x1, waiting for transfers between devices, local(): lax.psum((running[0], running[2], running[6]), ('dp', 'tensor'))  202 us
    dot_general x33, matrix products, mixed_dot(): return jnp.dot(left_side, right_side, preferred_element_type=jnp.float32)  152 us
    dot_general x21, matrix products, mixed_transpose(): lax.dot_general(left_side, right_side, (((1,), (1,)), ((), ())), preferre...  149 us
    all_gather x1, waiting for transfers between devices, frozen_set(): lax.all_gather(sharded[3], 'dp', axis=2, tiled=True)  130 us
  transfers between devices with their start and end apart: 35, of which 31 were waited for; matrix products, arithmetic and copies ran while one was open for 22% of the time, Pallas kernels for 0%

commit v1 on v0

v1 whole, which is shorter than its diff:
```python
from functools import partial
import math

import jax
import jax.numpy as jnp
from jax import lax
from jax.experimental import pallas as pl
from jax.experimental.pallas import tpu as pltpu
from jax.sharding import PartitionSpec as P

KV_HEADS = 2
HEAD_DIM = 128
RANK = 16
EPSILON = 1e-06
ROPE_BASE = 1000000.0
MASKED_SCORE = -1e30
CHUNKS = 2
BF = jnp.bfloat16
F32 = jnp.float32


def dot(a, b):
    return jnp.dot(a, b, preferred_element_type=F32)


def dot_t(a, b):
    return lax.dot_general(a, b, (((1,), (1,)), ((), ())), preferred_element_type=F32)


def t_dot(a, b):
    return lax.dot_general(a, b, (((0,), (0,)), ((), ())), preferred_element_type=F32)


def rotary_tables(first_slot, rows):
    half = HEAD_DIM // 2
    frequency = jnp.exp(-math.log(ROPE_BASE) * (2.0 * jnp.arange(half, dtype=F32) / HEAD_DIM))
    slots = (first_slot + jnp.arange(rows, dtype=jnp.int32)).astype(F32)
    angles = slots[:, None] * frequency[None, :]
    return jnp.cos(angles)[:, None, :], jnp.sin(angles)[:, None, :]


def rotate(flat, tables, sign):
    cos, sin = tables
    x = flat.reshape(flat.shape[0], -1, HEAD_DIM)
    u, w = x[..., : HEAD_DIM // 2], x[..., HEAD_DIM // 2 :]
    sin = sin * sign
    return jnp.concatenate([u * cos - w * sin, w * cos + u * sin], axis=-1).reshape(flat.shape)


def norm_back(values, inverse, gain_row, grad_out):
    weighted = gain_row * grad_out
    return inverse * weighted - inverse * inverse * inverse * values * jnp.mean(
        weighted * values, axis=-1, keepdims=True
    )


def attend_kernel(scale, info_ref, q_ref, k_ref, v_ref, out_ref, log_ref):
    keys, rows = k_ref.shape[0], q_ref.shape[0]
    scores = dot_t(k_ref[...], q_ref[...]) * scale
    row = info_ref[0] + lax.broadcasted_iota(jnp.int32, (1, rows), 1)
    last = jnp.minimum(row, info_ref[1] - 1)
    key = lax.broadcasted_iota(jnp.int32, (keys, rows), 0)
    scores = jnp.where(key <= last, scores, MASKED_SCORE)
    peak = jnp.max(scores, axis=0, keepdims=True)
    soft = jnp.exp(scores - peak)
    total = jnp.sum(soft, axis=0, keepdims=True)
    soft = (soft * (1.0 / total)).astype(BF)
    out_ref[...] = t_dot(v_ref[...], soft).T.astype(BF)
    log_ref[0] = peak + jnp.log(total)


def attend(queries, keyvalue, info):
    rows, width = queries.shape
    keys = keyvalue.shape[0]
    heads = width // HEAD_DIM
    group = heads // KV_HEADS
    return pl.pallas_call(
        partial(attend_kernel, HEAD_DIM**-0.5),
        grid=(heads,),
        in_specs=[
            pl.BlockSpec(memory_space=pltpu.SMEM),
            pl.BlockSpec((rows, HEAD_DIM), lambda h: (0, h)),
            pl.BlockSpec((keys, HEAD_DIM), lambda h: (0, h // group)),
            pl.BlockSpec((keys, HEAD_DIM), lambda h: (0, KV_HEADS + h // group)),
        ],
        out_specs=[
            pl.BlockSpec((rows, HEAD_DIM), lambda h: (0, h)),
            pl.BlockSpec((1, 1, rows), lambda h: (h, 0, 0)),
        ],
        out_shape=[
            jax.ShapeDtypeStruct((rows, width), BF),
            jax.ShapeDtypeStruct((heads, 1, rows), F32),
        ],
        compiler_params=pltpu.CompilerParams(vmem_limit_bytes=32 * 2**20),
    )(info, queries, keyvalue, keyvalue)


def attend_back_kernel(scale, group, info_ref, q_ref, k_ref, v_ref, do_ref, log_ref, dq_ref, dk_ref, dv_ref):
    keys, rows = k_ref.shape[0], q_ref.shape[0]
    first = pl.program_id(0) % group == 0
    q, k, v, do = q_ref[...], k_ref[...], v_ref[...], do_ref[...]
    scores = dot_t(k, q) * scale - log_ref[0]
    row = info_ref[0] + lax.broadcasted_iota(jnp.int32, (1, rows), 1)
    last = jnp.minimum(row, info_ref[1] - 1)
    key = lax.broadcasted_iota(jnp.int32, (keys, rows), 0)
    soft = jnp.exp(jnp.where(key <= last, scores, MASKED_SCORE))
    soft_grad = dot_t(v, do)
    delta = jnp.sum(soft_grad * soft, axis=0, keepdims=True)
    score_grad = (soft * (soft_grad - delta)).astype(BF)
    dq_ref[...] = t_dot(k, score_grad).T * scale
    dk = dot(score_grad, q) * scale
    dv = dot(soft.astype(BF), do)

    @pl.when(first)
    def _():
        dk_ref[...] = dk
        dv_ref[...] = dv

    @pl.when(jnp.logical_not(first))
    def _():
        dk_ref[...] += dk
        dv_ref[...] += dv


def attend_back(queries, keyvalue, grad_out, logs, info):
    rows, width = queries.shape
    keys = keyvalue.shape[0]
    heads = width // HEAD_DIM
    group = heads // KV_HEADS
    return pl.pallas_call(
        partial(attend_back_kernel, HEAD_DIM**-0.5, group),
        grid=(heads,),
        in_specs=[
            pl.BlockSpec(memory_space=pltpu.SMEM),
            pl.BlockSpec((rows, HEAD_DIM), lambda h: (0, h)),
            pl.BlockSpec((keys, HEAD_DIM), lambda h: (0, h // group)),
            pl.BlockSpec((keys, HEAD_DIM), lambda h: (0, KV_HEADS + h // group)),
            pl.BlockSpec((rows, HEAD_DIM), lambda h: (0, h)),
            pl.BlockSpec((1, 1, rows), lambda h: (h, 0, 0)),
        ],
        out_specs=[
            pl.BlockSpec((rows, HEAD_DIM), lambda h: (0, h)),
            pl.BlockSpec((keys, HEAD_DIM), lambda h: (0, h // group)),
            pl.BlockSpec((keys, HEAD_DIM), lambda h: (0, h // group)),
        ],
        out_shape=[
            jax.ShapeDtypeStruct((rows, width), F32),
            jax.ShapeDtypeStruct((keys, KV_HEADS * HEAD_DIM), F32),
            jax.ShapeDtypeStruct((keys, KV_HEADS * HEAD_DIM), F32),
        ],
        compiler_params=pltpu.CompilerParams(vmem_limit_bytes=40 * 2**20),
    )(info, queries, keyvalue, keyvalue, grad_out, logs)


def spread(rows):
    return lax.all_gather(rows, "tensor", axis=0, tiled=True)


def fold(partial_rows):
    return lax.psum_scatter(
        partial_rows.astype(BF), "tensor", scatter_dimension=0, tiled=True
    ).astype(F32)


def row_chunks(x):
    step = x.shape[0] // CHUNKS
    return [x[i * step : (i + 1) * step] for i in range(CHUNKS)]


def forward(x, w, ad, info, tables):
    inverse_one = lax.rsqrt(jnp.mean(x * x, axis=-1, keepdims=True) + EPSILON)
    normed = (x * inverse_one * w["gain"][0]).astype(BF)
    low = dot(normed, ad["input"][:, : 3 * RANK]).astype(BF)
    kv_width = KV_HEADS * HEAD_DIM
    kv = dot(normed, w["kv"]) + w["kv_bias"]
    kv = kv + jnp.concatenate(
        [
            dot(low[:, RANK : 2 * RANK], ad["kv"][0]),
            dot(low[:, 2 * RANK :], ad["kv"][1]),
        ],
        axis=1,
    )
    kv = jnp.concatenate(
        [rotate(kv[:, :kv_width], tables, 1.0), kv[:, kv_width:]], axis=1
    ).astype(BF)
    kv_all = spread(kv)
    q = dot(normed, w["q"]) + w["q_bias"] + dot(low[:, :RANK], ad["q"])
    q = rotate(q, tables, 1.0).astype(BF)
    attended, logs = attend(q, kv_all, info)
    attend_rank = dot(attended, ad["attend"]).astype(BF)
    middle = x + dot_t(attended, w["out_t"]) + dot(attend_rank, ad["residual"][0])
    inverse_two = lax.rsqrt(jnp.mean(middle * middle, axis=-1, keepdims=True) + EPSILON)
    normed_two = (middle * inverse_two * w["gain"][1]).astype(BF)
    shrunk, saved = [], []
    for part in row_chunks(normed_two):
        n2 = spread(part)
        expand_rank = dot(n2, ad["input"][:, 3 * RANK :]).astype(BF)
        gate = dot(n2, w["gate"]) + dot(expand_rank[:, :RANK], ad["expand"][0])
        up = dot(n2, w["up"]) + dot(expand_rank[:, RANK:], ad["expand"][1])
        act = (jax.nn.silu(gate) * up).astype(BF)
        shrink_rank = dot(act, ad["shrink"]).astype(BF)
        shrunk.append(fold(dot_t(act, w["shrink_t"]) + dot(shrink_rank, ad["residual"][1])))
        saved.append((n2, expand_rank, gate.astype(BF), up.astype(BF), act, shrink_rank))
    y = middle + jnp.concatenate(shrunk, axis=0)
    kept = (x, inverse_one, normed, low, q, kv_all, attended, logs, attend_rank, middle, inverse_two, saved)
    return y, kept


def backward(dy, w, ad, kept, info, tables):
    (x, inverse_one, normed, low, q, kv_all, attended, logs, attend_rank, middle, inverse_two, saved) = kept
    width = x.shape[1]
    high = ad["input"][:, 3 * RANK :]
    folded, g_high, g_expand, g_shrink, g_res_two = [], 0, 0, 0, 0
    for part, (n2, expand_rank, gate, up, act, shrink_rank) in zip(row_chunks(dy.astype(BF)), saved):
        ds = spread(part)
        shrink_rank_grad = dot_t(ds, ad["residual"][1]).astype(BF)
        act_grad = dot(ds, w["shrink_t"]) + dot_t(shrink_rank_grad, ad["shrink"])
        gate, up = gate.astype(F32), up.astype(F32)
        sig = jax.nn.sigmoid(gate)
        gate_grad = (act_grad * up * sig * (1.0 + gate * (1.0 - sig))).astype(BF)
        up_grad = (act_grad * gate * sig).astype(BF)
        rank_grad = jnp.concatenate(
            [dot_t(gate_grad, ad["expand"][0]), dot_t(up_grad, ad["expand"][1])], axis=1
        ).astype(BF)
        folded.append(
            fold(dot_t(gate_grad, w["gate"]) + dot_t(up_grad, w["up"]) + dot_t(rank_grad, high))
        )
        g_high = g_high + t_dot(rank_grad, n2)
        g_expand = g_expand + jnp.concatenate(
            [t_dot(expand_rank[:, :RANK], gate_grad), t_dot(expand_rank[:, RANK:], up_grad)], axis=0
        )
        g_shrink = g_shrink + t_dot(shrink_rank_grad, act)
        g_res_two = g_res_two + t_dot(shrink_rank, ds)
    middle_grad = dy + norm_back(middle, inverse_two, w["gain"][1], jnp.concatenate(folded, axis=0))
    branch_grad = middle_grad.astype(BF)
    attend_rank_grad = dot_t(branch_grad, ad["residual"][0]).astype(BF)
    attended_grad = (dot(branch_grad, w["out_t"]) + dot_t(attend_rank_grad, ad["attend"])).astype(BF)
    g_attend = t_dot(attend_rank_grad, attended)
    g_res_one = t_dot(attend_rank, branch_grad)
    dq, dk, dv = attend_back(q, kv_all, attended_grad, logs, info)
    kv_width = KV_HEADS * HEAD_DIM
    dkv = fold(jnp.concatenate([dk, dv], axis=1))
    dq = rotate(dq, tables, -1.0).astype(BF)
    dkv = jnp.concatenate([rotate(dkv[:, :kv_width], tables, -1.0), dkv[:, kv_width:]], axis=1).astype(BF)
    low_grad = jnp.concatenate(
        [
            dot_t(dq, ad["q"]),
            dot_t(dkv[:, :kv_width], ad["kv"][0]),
            dot_t(dkv[:, kv_width:], ad["kv"][1]),
        ],
        axis=1,
    ).astype(BF)
    normed_grad = dot_t(dq, w["q"]) + dot_t(dkv, w["kv"]) + dot_t(low_grad, ad["input"][:, : 3 * RANK])
    dx = middle_grad + norm_back(x, inverse_one, w["gain"][0], normed_grad)
    g_q = t_dot(low[:, :RANK], dq)
    g_kv = jnp.concatenate(
        [
            t_dot(low[:, RANK : 2 * RANK], dkv[:, :kv_width]),
            t_dot(low[:, 2 * RANK :], dkv[:, kv_width:]),
        ],
        axis=1,
    )
    g_low = t_dot(low_grad, normed)
    pad = jnp.zeros((RANK, width - 2 * kv_width), F32)
    whole = jnp.concatenate(
        [g_low, g_high, g_res_one, g_res_two, g_q, g_attend, jnp.concatenate([g_kv, pad], axis=1)], axis=0
    ).astype(BF)
    parts = jnp.concatenate([g_expand, g_shrink], axis=0).astype(BF)
    return dx, whole, parts


def swap(pair):
    return lax.all_to_all(pair, "section", split_axis=0, concat_axis=0, tiled=True)


def local(
    inputs,
    lengths,
    adapter_ids,
    cotangent,
    norm_gain,
    query_weight,
    query_bias,
    keyvalue_weight,
    keyvalue_bias,
    output_weight,
    expand_weight,
    shrink_weight,
    adapter_input,
    adapter_query,
    adapter_keyvalue,
    adapter_expand,
    adapter_attend,
    adapter_shrink,
    adapter_residual,
):
    layers = lax.axis_size("section")
    tensor = lax.axis_size("tensor")
    core = lax.axis_index("section")
    place = lax.axis_index("tensor")
    rows, width = inputs.shape[1:]
    tokens = layers * rows * tensor * lax.axis_size("dp")

    kv = jnp.concatenate([keyvalue_weight[0, 0], keyvalue_weight[0, 1]], axis=1)
    kv_cols = kv.shape[1] // tensor
    kv = lax.dynamic_slice_in_dim(kv, place * kv_cols, kv_cols, 1)
    attn = jnp.concatenate([query_weight[0], output_weight[0].T, kv], axis=1)
    q_cols = query_weight.shape[2]
    halves = [
        swap(m.reshape(layers, m.shape[0] // layers, m.shape[1]))
        for m in (attn, expand_weight[0, 0], expand_weight[0, 1], shrink_weight[0].T)
    ]
    every = ("dp", "section")
    small = jnp.concatenate(
        [norm_gain[0, 0], norm_gain[0, 1], keyvalue_bias[0].reshape(-1)], axis=0
    )
    small = lax.all_gather(small, "section", axis=0)
    q_bias = lax.all_gather(query_bias[0], ("section", "tensor"), axis=0, tiled=True).reshape(layers, -1)

    def weights(layer):
        g = lax.all_gather(halves[0][layer], every + ("tensor",), axis=0)
        g = g.reshape(-1, tensor, g.shape[1], g.shape[2])
        g = jnp.swapaxes(g, 1, 2)

        def cut(start, size):
            return g[..., start : start + size].reshape(width, tensor * size)

        gain = small[layer, : 2 * width].reshape(2, width).astype(F32)
        return dict(
            gain=gain,
            q=cut(0, q_cols),
            out_t=cut(q_cols, q_cols),
            kv=cut(2 * q_cols, kv_cols),
            gate=lax.all_gather(halves[1][layer], every, axis=0, tiled=True),
            up=lax.all_gather(halves[2][layer], every, axis=0, tiled=True),
            shrink_t=lax.all_gather(halves[3][layer], every, axis=0, tiled=True),
            q_bias=q_bias[layer].astype(F32),
            kv_bias=small[layer, 2 * width :].astype(F32),
        )

    def pick(stack):
        chosen = jnp.stack(
            [lax.dynamic_index_in_dim(stack[0], adapter_ids[i], 0, keepdims=False) for i in range(layers)]
        )
        return swap(chosen)

    picked = [
        pick(stack)
        for stack in (
            adapter_input,
            adapter_query,
            adapter_keyvalue,
            adapter_expand,
            adapter_attend,
            adapter_shrink,
            adapter_residual,
        )
    ]
    query_all = lax.all_gather(picked[1], "tensor", axis=2, tiled=True)
    attend_all = lax.all_gather(picked[4], "tensor", axis=1, tiled=True)

    def adapters(layer):
        return dict(
            input=picked[0][layer],
            q=query_all[layer],
            kv=picked[2][layer],
            expand=picked[3][layer],
            attend=attend_all[layer],
            shrink=picked[5][layer],
            residual=picked[6][layer],
        )

    x = lax.dynamic_index_in_dim(inputs, core, 0, keepdims=False).astype(F32)
    cot = lax.dynamic_index_in_dim(cotangent, core, 0, keepdims=False).astype(F32)
    length = lax.dynamic_index_in_dim(lengths, core, 0, keepdims=False)
    first_slot = place * rows
    info = jnp.stack([first_slot, length]).astype(jnp.int32)
    tables = rotary_tables(first_slot, rows)
    slot_ids = first_slot + jnp.arange(rows, dtype=jnp.int32)

    w = [weights(layer) for layer in range(layers)]
    ad = [adapters(layer) for layer in range(layers)]
    outs, kept = [], []
    for layer in range(layers):
        y, saved = forward(x, w[layer], ad[layer], info, tables)
        outs.append(y.astype(BF))
        kept.append(saved)
        x = outs[-1].astype(F32)
    grad = cot * (slot_ids < length).astype(F32)[:, None]
    grads, wholes, parts = [None] * layers, [None] * layers, [None] * layers
    for layer in reversed(range(layers)):
        grad, wholes[layer], parts[layer] = backward(grad, w[layer], ad[layer], kept[layer], info, tables)
        grads[layer] = grad
    layer_output = swap(jnp.stack(outs))
    input_grad = swap(jnp.stack(grads))

    whole = lax.psum(swap(jnp.stack(wholes)), "tensor")
    part = swap(jnp.stack(parts))
    own = 7 * RANK
    q_rows = lax.dynamic_slice_in_dim(whole[:, own : own + 2 * RANK], place * q_cols, q_cols, 2)
    rest = jnp.concatenate([whole[:, :own], whole[:, own + 2 * RANK :]], axis=1)
    rest, q_rows, part, ids = (
        lax.all_gather(a, "dp", axis=0, tiled=True) for a in (rest, q_rows, part, adapter_ids)
    )
    count = adapter_input.shape[1]
    pick_matrix = (jnp.arange(count, dtype=jnp.int32)[:, None] == ids[None, :]).astype(BF)
    scale = 1.0 / math.sqrt(tokens)

    def by_adapter(a):
        return jnp.einsum("as,srw->arw", pick_matrix, a, preferred_element_type=F32) * scale

    rest, q_rows, part = by_adapter(rest), by_adapter(q_rows), by_adapter(part)
    r = RANK
    kv_width = KV_HEADS * HEAD_DIM
    return (
        layer_output[None],
        input_grad[None],
        jnp.swapaxes(rest[:, : 5 * r], 1, 2)[None],
        q_rows[:, :r][None],
        jnp.stack([rest[:, 7 * r :, :kv_width], rest[:, 7 * r :, kv_width : 2 * kv_width]], axis=1)[None],
        jnp.stack([part[:, :r], part[:, r : 2 * r]], axis=1)[None],
        jnp.swapaxes(q_rows[:, r:], 1, 2)[None],
        jnp.swapaxes(part[:, 2 * r :], 1, 2)[None],
        jnp.stack([rest[:, 5 * r : 6 * r], rest[:, 6 * r : 7 * r]], axis=1)[None],
    )


def solution(mesh):
    placed = (
        P("dp", "tensor", None),
        P("dp"),
        P("dp"),
        P("dp", "tensor", None),
        P("section", None, None),
        P("section", "dp", "tensor"),
        P("section", "tensor"),
        P("section", None, "dp", None),
        P("section", None, None),
        P("section", "tensor", "dp"),
        P("section", None, "dp", "tensor"),
        P("section", "tensor", "dp"),
        P("section", None, None, None),
        P("section", None, None, "tensor"),
        P("section", None, None, None, None),
        P("section", None, None, None, "tensor"),
        P("section", None, "tensor", None),
        P("section", None, "tensor", None),
        P("section", None, None, None, None),
    )
    return jax.shard_map(
        local,
        mesh=mesh,
        in_specs=placed,
        out_specs=(
            P("section", "dp", "tensor", None),
            P("section", "dp", "tensor", None),
            P("section", None, None, None),
            P("section", None, None, "tensor"),
            P("section", None, None, None, None),
            P("section", None, None, None, "tensor"),
            P("section", None, "tensor", None),
            P("section", None, "tensor", None),
            P("section", None, None, None, None),
        ),
        check_vma=False,
    )
```

time: 2520 us -> 1490 us (0.59)
  waiting for transfers between devices: 1500 us -> 740 us
  matrix products: 709 us -> 338 us
  blocking collectives: 0 us -> 115 us
  other arithmetic: 153 us -> 46.4 us
  Pallas kernels: 0 us -> 61.1 us
  local copies, waits for them, and re-layouts: 87 us -> 128 us
    dot_general x183 -> x135, matrix products: 709 us -> 338 us  [the longest x50 157 us: dot(): return jnp.dot(a, b, preferred_element_type=F32)]
    reduce_scatter x12 -> x10, waiting for transfers between devices: 511 us -> 211 us  [fold(): lax.psum_scatter(partial_rows.astype(BF), 'tensor', scatter_dimension=0,...]
    all_gather x17 -> x20, waiting for transfers between devices: 752 us -> 495 us  [the longest x10 140 us: spread(): return lax.all_gather(rows, 'tensor', axis=0, tiled=True)]
    psum x2 -> x1, waiting for transfers between devices: 231 us -> 30.4 us  [local(): whole = lax.psum(swap(jnp.stack(wholes)), 'tensor')]
    all_gather x0 -> x5, blocking collectives: none -> 61.6 us  [the longest x1 23.1 us: local(): lax.all_gather(query_bias[0], ('section', 'tensor'), axis=0, tiled=True)]
    pallas_call x0 -> x4, Pallas kernels: none -> 61.1 us  [the longest x2 34.2 us: attend_back(): pl.pallas_call(partial(attend_back_kernel, HEAD_DIM ** (-0.5), group), gr...]
    slice x7 -> x31, local copies, waits for them, and re-layouts: 4.67 us -> 56.2 us  [the longest x10 40.1 us: cut(): return g[..., start:start + size].reshape(width, tensor * size)]
    convert_element_type x27 -> x9, other arithmetic: 54.8 us -> 3.37 us  [the longest x1 1.58 us: backward(): dy.astype(BF)]
  transfers between devices with their start and end apart: 35 -> 38, of which waited for: 31 -> 26; matrix products, arithmetic and copies ran while one was open for 22% -> 29% of each run, Pallas kernels for 0% -> 2%
where the time goes in v1:
time: 1490 us; the launch traced here: 1480 us
  waiting for transfers between devices  740 us (50%)
  matrix products  338 us (23%)
  local copies, waits for them, and re-layouts  128 us (9%)
  blocking collectives  115 us (8%)
  Pallas kernels  61.1 us (4%)
  other arithmetic  46.4 us (3%)
  starting transfers between devices  26.8 us (2%)
  between operations  22.5 us (2%)
    reduce_scatter x10, waiting for transfers between devices, fold(): lax.psum_scatter(partial_rows.astype(BF), 'tensor', scatter_dimension=0,...  211 us
    dot_general x50, matrix products, dot(): return jnp.dot(a, b, preferred_element_type=F32)  157 us
    all_gather x10, waiting for transfers between devices, spread(): return lax.all_gather(rows, 'tensor', axis=0, tiled=True)  140 us
    dot_general x50, matrix products, dot_t(): lax.dot_general(a, b, (((1,), (1,)), ((), ())), preferred_element_type=F32)  134 us
    all_gather x2, waiting for transfers between devices, weights(): lax.all_gather(halves[3][layer], every, axis=0, tiled=True)  86 us
    all_gather x2, waiting for transfers between devices, weights(): lax.all_gather(halves[2][layer], every, axis=0, tiled=True)  81.1 us
    all_gather x2, waiting for transfers between devices, weights(): lax.all_gather(halves[1][layer], every, axis=0, tiled=True)  78.7 us
    all_gather x2, waiting for transfers between devices, weights(): g = lax.all_gather(halves[0][layer], every + ('tensor',), axis=0)  67.3 us
  transfers between devices with their start and end apart: 38, of which 26 were waited for; matrix products, arithmetic and copies ran while one was open for 29% of the time, Pallas kernels for 2%

profile of v1, /device:TPU:0, one launch (start us, length us, event | category | flops | bytes accessed | tf_op | source)
XLA Modules:
  0.0 1478.5 jit_solution(15614374754003956191)
XLA Ops:
  28.8 23.1 %all-gather.1 = bf16[1,3072]{1,0:T(2,128)(2,1)S(1)} all-gather(bf16[1,384]{1,0:T(2,128)(2,1)S(1)} %copy-done.205), channel_id=3, replica_groups=mesh['section'=2,'dp'=4,'tensor'=4] {'section','tensor'}, dimensions={1}, use_global_device_ids=true | all-gather | bytes 6912 | tf_op jit(solution)/shard_map/all_gather | solution.py:318
  75.5 14.0 all_gather.87
  215.4 36.9 %all-gather.58.cloned.1.call-done = bf16[1,1536,2240]{2,1,0:T(8,128)(2,1)} async-done(((bf16[1,192,2240]{2,1,0:T(8,128)(2,1)}), bf16[1,1536,2240]{2,1,0:T(8,128)(2,1)}) %all-gather.58.cloned.1.call-update) | async-done | bytes 6881296 | tf_op jit(solution)/shard_map/all_gather | solution.py:334
  270.4 33.1 %all-gather.60.cloned.1.call-done = bf16[1,1536,2240]{2,1,0:T(8,128)(2,1)} async-done(((bf16[1,192,2240]{2,1,0:T(8,128)(2,1)}), bf16[1,1536,2240]{2,1,0:T(8,128)(2,1)}) %all-gather.60.cloned.1.call-update) | async-done | bytes 6881296 | tf_op jit(solution)/shard_map/all_gather | solution.py:335
  315.8 38.4 %all-gather.62.cloned.1.call-done = bf16[1,1536,2240]{2,1,0:T(8,128)(2,1)} async-done(((bf16[1,192,2240]{2,1,0:T(8,128)(2,1)}), bf16[1,1536,2240]{2,1,0:T(8,128)(2,1)}) %all-gather.62.cloned.1.call-update) | async-done | bytes 6881296 | tf_op jit(solution)/shard_map/all_gather | solution.py:336
  363.0 29.8 %all-gather.34.cloned.1.call-done = bf16[512,1536]{1,0:T(8,128)(2,1)} async-done(((bf16[128,1536]{1,0:T(8,128)(2,1)}), bf16[512,1536]{1,0:T(8,128)(2,1)}) %all-gather.34.cloned.1.call-update) | async-done | bytes 1572880 | tf_op jit(solution)/shard_map/all_gather | solution.py:156
  419.1 64.4 %all-gather.38.cloned.1.call-done = bf16[32,192,896]{2,1,0:T(8,128)(2,1)} async-done(((bf16[1,192,896]{2,1,0:T(8,128)(2,1)}), bf16[32,192,896]{2,1,0:T(8,128)(2,1)}) %all-gather.38.cloned.1.call-update) | async-done | bytes 11010064 | tf_op jit(solution)/shard_map/all_gather | solution.py:321
  487.4 32.7 %reduce-scatter.13.cloned.1.call-done = bf16[128,1536]{1,0:T(8,128)(2,1)} async-done(((bf16[512,1536]{1,0:T(8,128)(2,1)}), bf16[128,1536]{1,0:T(8,128)(2,1)}) %reduce-scatter.13.cloned.1.call-update) | async-done | bytes 393232 | tf_op jit(solution)/shard_map/reduce_scatter | solution.py:160
  520.1 37.0 %reduce-scatter.11.cloned.1.call-done = bf16[128,1536]{1,0:T(8,128)(2,1)} async-done(((bf16[512,1536]{1,0:T(8,128)(2,1)}), bf16[128,1536]{1,0:T(8,128)(2,1)}) %reduce-scatter.11.cloned.1.call-update) | async-done | bytes 393232 | tf_op jit(solution)/shard_map/reduce_scatter | solution.py:160
  633.7 36.0 %all-gather.46.cloned.1.call-done = bf16[512,1536]{1,0:T(8,128)(2,1)} async-done(((bf16[128,1536]{1,0:T(8,128)(2,1)}), bf16[512,1536]{1,0:T(8,128)(2,1)}) %all-gather.46.cloned.1.call-update) | async-done | bytes 1572880 | tf_op jit(solution)/shard_map/all_gather | solution.py:156
  671.6 47.6 %all-gather.68.cloned.1.call-done = bf16[1,1536,2240]{2,1,0:T(8,128)(2,1)} async-done(((bf16[1,192,2240]{2,1,0:T(8,128)(2,1)}), bf16[1,1536,2240]{2,1,0:T(8,128)(2,1)}) %all-gather.68.cloned.1.call-update) | async-done | bytes 6881296 | tf_op jit(solution)/shard_map/all_gather | solution.py:336
  736.2 22.1 %all-gather.44.cloned.1.call-done = bf16[512,1536]{1,0:T(8,128)(2,1)} async-done(((bf16[128,1536]{1,0:T(8,128)(2,1)}), bf16[512,1536]{1,0:T(8,128)(2,1)}) %all-gather.44.cloned.1.call-update) | async-done | bytes 1572880 | tf_op jit(solution)/shard_map/all_gather | solution.py:156
  760.3 48.1 %all-gather.66.cloned.1.call-done = bf16[1,1536,2240]{2,1,0:T(8,128)(2,1)} async-done(((bf16[1,192,2240]{2,1,0:T(8,128)(2,1)}), bf16[1,1536,2240]{2,1,0:T(8,128)(2,1)}) %all-gather.66.cloned.1.call-update) | async-done | bytes 6881296 | tf_op jit(solution)/shard_map/all_gather | solution.py:335
  817.7 41.8 %all-gather.64.cloned.1.call-done = bf16[1,1536,2240]{2,1,0:T(8,128)(2,1)} async-done(((bf16[1,192,2240]{2,1,0:T(8,128)(2,1)}), bf16[1,1536,2240]{2,1,0:T(8,128)(2,1)}) %all-gather.64.cloned.1.call-update) | async-done | bytes 6881296 | tf_op jit(solution)/shard_map/all_gather | solution.py:334
  973.6 35.2 %reduce-scatter.17.cloned.1.call-done = bf16[128,1536]{1,0:T(8,128)(2,1)} async-done(((bf16[512,1536]{1,0:T(8,128)(2,1)}), bf16[128,1536]{1,0:T(8,128)(2,1)}) %reduce-scatter.17.cloned.1.call-update) | async-done | bytes 393232 | tf_op jit(solution)/shard_map/reduce_scatter | solution.py:160
  1008.7 36.6 %reduce-scatter.15.cloned.1.call-done = bf16[128,1536]{1,0:T(8,128)(2,1)} async-done(((bf16[512,1536]{1,0:T(8,128)(2,1)}), bf16[128,1536]{1,0:T(8,128)(2,1)}) %reduce-scatter.15.cloned.1.call-update) | async-done | bytes 393232 | tf_op jit(solution)/shard_map/reduce_scatter | solution.py:160
  1054.3 17.1 %shard_map.252 = (f32[256,1536]{1,0:T(8,128)S(1)}, f32[1024,256]{1,0:T(8,128)S(1)}, f32[1024,256]{1,0:T(8,128)S(1)}) custom-call(s32[2]{0:T(128)S(1)} %copy-done.9, bf16[256,1536]{1,0:T(8,128)(2,1)S(1)} %copy.105.q_ref, bf16[1024,512]{1,0:T(8,128)(2,1)S(1)} %copy-done.3, bf16[1024,512]{1,0:T(8,128)(2,1)S(1)} %copy-done.3, ...), custom_call_target="tpu_custom_call" | custom-call | tf_op jit(solution)/shard_map/pallas_call | solution.py:130
  1082.2 16.8 %reduce-scatter.23.cloned.1.call-done = bf16[256,512]{1,0:T(8,128)(2,1)} async-done(((bf16[1024,512]{1,0:T(8,128)(2,1)}), bf16[256,512]{1,0:T(8,128)(2,1)}) %reduce-scatter.23.cloned.1.call-update) | async-done | bytes 262160 | tf_op jit(solution)/shard_map/reduce_scatter | solution.py:160
  1118.3 26.4 %all-gather.52.cloned.1.call-done = bf16[512,1536]{1,0:T(8,128)(2,1)} async-done(((bf16[128,1536]{1,0:T(8,128)(2,1)}), bf16[512,1536]{1,0:T(8,128)(2,1)}) %all-gather.52.cloned.1.call-update) | async-done | bytes 1572880 | tf_op jit(solution)/shard_map/all_gather | solution.py:156
  1227.8 28.8 %reduce-scatter.25.cloned.1.call-done = bf16[128,1536]{1,0:T(8,128)(2,1)} async-done(((bf16[512,1536]{1,0:T(8,128)(2,1)}), bf16[128,1536]{1,0:T(8,128)(2,1)}) %reduce-scatter.25.cloned.1.call-update) | async-done | bytes 393232 | tf_op jit(solution)/shard_map/reduce_scatter | solution.py:160
  1264.8 17.1 %shard_map.253 = (f32[256,1536]{1,0:T(8,128)S(1)}, f32[1024,256]{1,0:T(8,128)S(1)}, f32[1024,256]{1,0:T(8,128)S(1)}) custom-call(s32[2]{0:T(128)S(1)} %copy-done.9, bf16[256,1536]{1,0:T(8,128)(2,1)S(1)} %copy.92.q_ref, bf16[1024,512]{1,0:T(8,128)(2,1)S(1)} %copy-done.1, bf16[1024,512]{1,0:T(8,128)(2,1)S(1)} %copy-done.1, ...), custom_call_target="tpu_custom_call" | custom-call | tf_op jit(solution)/shard_map/pallas_call | solution.py:130
  1346.1 30.4 %all-reduce.3.cloned.1.call-done = bf16[2,160,1536]{2,1,0:T(8,128)(2,1)} async-done(((bf16[2,160,1536]{2,1,0:T(8,128)(2,1)}), bf16[2,160,1536]{2,1,0:T(8,128)(2,1)}) %all-reduce.3.cloned.1.call-update) | async-done | bytes 983056 | tf_op jit(solution)/shard_map/psum | solution.py:397
  1386.6 23.6 %all-gather.56.cloned.1.call-done = bf16[8,48,2240]{2,1,0:T(8,128)(2,1)} async-done(((bf16[2,48,2240]{2,1,0:T(8,128)(2,1)}), bf16[8,48,2240]{2,1,0:T(8,128)(2,1)}) %all-gather.56.cloned.1.call-update) | async-done | bytes 1720336 | tf_op jit(solution)/shard_map/all_gather | solution.py:403
  1438.9 17.9 %all-gather.54.cloned.1.call-done = bf16[8,128,1536]{2,1,0:T(8,128)(2,1)} async-done(((bf16[2,128,1536]{2,1,0:T(8,128)(2,1)}), bf16[8,128,1536]{2,1,0:T(8,128)(2,1)}) %all-gather.54.cloned.1.call-update) | async-done | bytes 3145744 | tf_op jit(solution)/shard_map/all_gather | solution.py:403
  (882 shorter events, 701.1 us)
Async XLA Ops:
  7.2 101.7 %all-gather.30.cloned.1.call-start = ((), (), s32[]{:S(2)}) async-start(), calls=%async_computation.25 | async-start | bytes 11354112 | tf_op jit(solution)/shard_map/all_gather | solution.py:321
  114.7 98.8 %all-gather.36.cloned.1.call-start = ((), (), s32[]{:S(2)}) async-start(), calls=%async_computation.29 | async-start | bytes 1966080 | tf_op jit(solution)/shard_map/all_gather | solution.py:156
  166.3 86.0 %all-gather.58.cloned.1.call-start = ((), (), s32[]{:S(2)}) async-start(), calls=%async_computation.50 | async-start | bytes 7962624 | tf_op jit(solution)/shard_map/all_gather | solution.py:334
  181.9 121.6 %all-gather.60.cloned.1.call-start = ((), (), s32[]{:S(2)}) async-start(), calls=%async_computation.51 | async-start | bytes 7962624 | tf_op jit(solution)/shard_map/all_gather | solution.py:335
  193.5 160.7 %all-gather.62.cloned.1.call-start = ((), (), s32[]{:S(2)}) async-start(), calls=%async_computation.52 | async-start | bytes 7962624 | tf_op jit(solution)/shard_map/all_gather | solution.py:336
  205.1 187.8 %all-gather.34.cloned.1.call-start = ((), (), s32[]{:S(2)}) async-start(), calls=%async_computation.27 | async-start | bytes 1966080 | tf_op jit(solution)/shard_map/all_gather | solution.py:156
  205.8 277.6 %all-gather.38.cloned.1.call-start = ((), (), s32[]{:S(2)}) async-start(), calls=%async_computation.31 | async-start | bytes 11354112 | tf_op jit(solution)/shard_map/all_gather | solution.py:321
  265.1 254.9 %reduce-scatter.13.cloned.1.call-start = ((), (), s32[]{:S(2)}) async-start(), calls=%async_computation.30 | async-start | bytes 1966080 | tf_op jit(solution)/shard_map/reduce_scatter | solution.py:160
  362.8 194.3 %reduce-scatter.11.cloned.1.call-start = ((), (), s32[]{:S(2)}) async-start(), calls=%async_computation.28 | async-start | bytes 1966080 | tf_op jit(solution)/shard_map/reduce_scatter | solution.py:160
  418.9 178.9 %all-gather.40.cloned.1.call-start = ((), (), s32[]{:S(2)}) async-start(), calls=%async_computation.32 | async-start | bytes 1310720 | tf_op jit(solution)/shard_map/all_gather | solution.py:156
  567.6 102.1 %all-gather.46.cloned.1.call-start = ((), (), s32[]{:S(2)}) async-start(), calls=%async_computation.37 | async-start | bytes 1966080 | tf_op jit(solution)/shard_map/all_gather | solution.py:156
  568.3 150.8 %all-gather.68.cloned.1.call-start = ((), (), s32[]{:S(2)}) async-start(), calls=%async_computation.55 | async-start | bytes 7962624 | tf_op jit(solution)/shard_map/all_gather | solution.py:336
  568.9 189.3 %all-gather.44.cloned.1.call-start = ((), (), s32[]{:S(2)}) async-start(), calls=%async_computation.35 | async-start | bytes 1966080 | tf_op jit(solution)/shard_map/all_gather | solution.py:156
  620.4 188.0 %all-gather.66.cloned.1.call-start = ((), (), s32[]{:S(2)}) async-start(), calls=%async_computation.54 | async-start | bytes 7962624 | tf_op jit(solution)/shard_map/all_gather | solution.py:335
  621.0 238.6 %all-gather.64.cloned.1.call-start = ((), (), s32[]{:S(2)}) async-start(), calls=%async_computation.53 | async-start | bytes 7962624 | tf_op jit(solution)/shard_map/all_gather | solution.py:334
  621.5 276.5 %all-gather.42.cloned.1.call-start = ((), (), s32[]{:S(2)}) async-start(), calls=%async_computation.33 | async-start | bytes 1966080 | tf_op jit(solution)/shard_map/all_gather | solution.py:156
  735.9 223.3 %reduce-scatter.21.cloned.1.call-start = ((), (), s32[]{:S(2)}) async-start(), calls=%async_computation.40 | async-start | bytes 1966080 | tf_op jit(solution)/shard_map/reduce_scatter | solution.py:160
  888.2 84.0 %reduce-scatter.19.cloned.1.call-start = ((), (), s32[]{:S(2)}) async-start(), calls=%async_computation.38 | async-start | bytes 1966080 | tf_op jit(solution)/shard_map/reduce_scatter | solution.py:160
  947.4 97.9 %reduce-scatter.15.cloned.1.call-start = ((), (), s32[]{:S(2)}) async-start(), calls=%async_computation.34 | async-start | bytes 1966080 | tf_op jit(solution)/shard_map/reduce_scatter | solution.py:160
  959.1 139.8 %reduce-scatter.23.cloned.1.call-start = ((), (), s32[]{:S(2)}) async-start(), calls=%async_computation.41 | async-start | bytes 1310720 | tf_op jit(solution)/shard_map/reduce_scatter | solution.py:160
  1118.3 109.5 %reduce-scatter.27.cloned.1.call-start = ((), (), s32[]{:S(2)}) async-start(), calls=%async_computation.45 | async-start | bytes 1966080 | tf_op jit(solution)/shard_map/reduce_scatter | solution.py:160
  1214.4 95.1 %reduce-scatter.29.cloned.1.call-start = ((), (), s32[]{:S(2)}) async-start(), calls=%async_computation.46 | async-start | bytes 1310720 | tf_op jit(solution)/shard_map/reduce_scatter | solution.py:160
  1283.2 93.3 %all-reduce.3.cloned.1.call-start = ((), (), s32[]{:S(2)}) async-start(), calls=%async_computation.47 | async-start | bytes 1966080 | tf_op jit(solution)/shard_map/psum | solution.py:397
  1337.0 119.8 %all-gather.54.cloned.1.call-start = ((), (), s32[]{:S(2)}) async-start(), calls=%async_computation.48 | async-start | bytes 3932160 | tf_op jit(solution)/shard_map/all_gather | solution.py:403
  (251 other events, 6096.3 us)
Sparse Core Ops, SparseCore 0:
  15.9 92.9 all-gather.29
  166.4 35.7 all-gather.35
  204.5 47.7 all-gather.57
  254.6 48.8 all-gather.59
  305.2 48.8 all-gather.61
  355.7 37.0 all-gather.33
  395.6 87.7 all-gather.37
  522.8 34.2 reduce-scatter.10
  595.1 36.6 all-gather.47
  633.3 36.2 all-gather.45
  671.4 47.6 all-gather.67
  721.1 37.0 all-gather.43
  760.6 47.7 all-gather.65
  810.7 48.8 all-gather.63
  861.0 37.0 all-gather.41
  937.9 34.2 reduce-scatter.18
  974.5 34.2 reduce-scatter.16
  1011.0 34.2 reduce-scatter.14
  1109.0 35.7 all-gather.51
  1147.0 35.9 all-gather.49
  1185.2 34.1 reduce-scatter.26
  1222.2 34.2 reduce-scatter.24
  1328.1 48.4 all-reduce.2
  1412.9 43.9 all-gather.53
  (7 shorter events, 205.0 us)

commit v2 on v1

--- a/solution.py
+++ b/solution.py
@@ -14,7 +14,10 @@
 EPSILON = 1e-06
 ROPE_BASE = 1000000.0
 MASKED_SCORE = -1e30
-CHUNKS = 2
+CHUNKS = 4
+LANES = 128
+VMEM_LIMIT = 60 * 2**20
+MESH = pl.DeviceIdType.MESH
 BF = jnp.bfloat16
 F32 = jnp.float32
 
@@ -152,6 +155,441 @@
     )(info, queries, keyvalue, keyvalue, grad_out, logs)
 
 
+def vspec():
+    return pl.BlockSpec(memory_space=pltpu.VMEM)
+
+
+def hspec():
+    return pl.BlockSpec(memory_space=pl.ANY)
+
+
+def line_barrier(me, line):
+    barrier = pltpu.get_barrier_semaphore()
+
+    @pl.when(me > 0)
+    def _():
+        pl.semaphore_signal(barrier, inc=1, device_id={"tensor": me - 1}, device_id_type=MESH)
+
+    @pl.when(me < line - 1)
+    def _():
+        pl.semaphore_signal(barrier, inc=1, device_id={"tensor": me + 1}, device_id_type=MESH)
+
+    pl.semaphore_wait(barrier, jnp.where(me > 0, 1, 0) + jnp.where(me < line - 1, 1, 0))
+
+
+def within(c, chunks):
+    return jnp.logical_and(c >= 0, c < chunks)
+
+
+def line_exchange(line, chunks, gathered, partial_ref, from_left, from_right, own_out, sems, begin, work):
+    ag_recv, ag_right, ag_left, r_recv, r_send, l_recv, l_send = sems
+    me = lax.axis_index("tensor")
+
+    def copy(ref, src, c, o, send, recv, side):
+        return pltpu.make_async_remote_copy(
+            src_ref=src.at[c, o],
+            dst_ref=ref.at[c, o],
+            send_sem=send.at[c, o],
+            recv_sem=recv.at[c, o],
+            device_id={"tensor": me + side},
+            device_id_type=MESH,
+        )
+
+    def ag(c, o, side):
+        return copy(gathered, gathered, c, o, ag_right if side > 0 else ag_left, ag_recv, side)
+
+    def rs(c, o, side):
+        if side > 0:
+            return copy(from_left, partial_ref, c, o, r_send, r_recv, 1)
+        return copy(from_right, partial_ref, c, o, l_send, l_recv, -1)
+
+    has_left, has_right = me > 0, me < line - 1
+
+    def step(s, carry):
+        first = s + line - 1
+
+        @pl.when(jnp.logical_and(within(first, chunks), has_right))
+        def _():
+            ag(first, me, 1).start()
+
+        @pl.when(jnp.logical_and(within(first, chunks), has_left))
+        def _():
+            ag(first, me, -1).start()
+
+        for d in range(1, line):
+            c = s + line - 1 - d
+
+            @pl.when(jnp.logical_and(within(c, chunks), me - d >= 0))
+            def _():
+                ag(c, me - d, 1).wait_recv()
+
+                @pl.when(has_right)
+                def _():
+                    ag(c, me - d, 1).start()
+
+            @pl.when(jnp.logical_and(within(c, chunks), me + d < line))
+            def _():
+                ag(c, me + d, -1).wait_recv()
+
+                @pl.when(has_left)
+                def _():
+                    ag(c, me + d, -1).start()
+
+        @pl.when(within(s, chunks))
+        def _():
+            work(s)
+
+        for h in range(line):
+            c = s - h
+
+            @pl.when(jnp.logical_and(within(c, chunks), me == h))
+            def _():
+                for j in range(h + 1, line):
+                    if h > 0:
+                        rs(c, j, 1).wait_recv()
+                        partial_ref[c, j] = (
+                            partial_ref[c, j].astype(F32) + from_left[c, j].astype(F32)
+                        ).astype(BF)
+                    if h < line - 1:
+                        rs(c, j, 1).start()
+
+            @pl.when(jnp.logical_and(within(c, chunks), me == line - 1 - h))
+            def _():
+                for j in range(line - 1 - h):
+                    if h > 0:
+                        rs(c, j, -1).wait_recv()
+                        partial_ref[c, j] = (
+                            partial_ref[c, j].astype(F32) + from_right[c, j].astype(F32)
+                        ).astype(BF)
+                    if h < line - 1:
+                        rs(c, j, -1).start()
+
+        last = s - (line - 1)
+
+        @pl.when(within(last, chunks))
+        def _():
+            own_out[last] = partial_ref[last, me].astype(F32)
+
+            @pl.when(has_left)
+            def _():
+                rs(last, me, 1).wait_recv()
+                own_out[last] += from_left[last, me].astype(F32)
+
+            @pl.when(has_right)
+            def _():
+                rs(last, me, -1).wait_recv()
+                own_out[last] += from_right[last, me].astype(F32)
+
+        return carry
+
+    line_barrier(me, line)
+    begin()
+    lax.fori_loop(-(line - 1), chunks + line - 1, step, 0)
+
+    def drain(c, carry):
+        for o in range(line):
+
+            @pl.when(jnp.logical_and(has_right, me >= o))
+            def _():
+                ag(c, o, 1).wait_send()
+
+            @pl.when(jnp.logical_and(has_left, me <= o))
+            def _():
+                ag(c, o, -1).wait_send()
+
+            @pl.when(me < o)
+            def _():
+                rs(c, o, 1).wait_send()
+
+            @pl.when(me > o)
+            def _():
+                rs(c, o, -1).wait_send()
+
+        return carry
+
+    lax.fori_loop(0, chunks, drain, 0)
+
+
+def exchange_scratch(line, chunks, rows, width):
+    slots = (chunks, line, rows, width)
+    return [pltpu.VMEM(slots, BF)] * 4 + [pltpu.SemaphoreType.DMA((chunks, line))] * 7
+
+
+def mlp_kernel(
+    line, chunks, tile,
+    n2_ref, gate_hbm, up_hbm, shrink_hbm, high_ref, expand_ref, ash_ref, res_ref,
+    out_ref, n2_out, gate_out, up_out,
+    gathered, partial_ref, from_left, from_right, s0, s1, s2, s3, s4, s5, s6,
+    wg, wu, ws, gate_st, up_st, acc, wsem, osem, nsem,
+):
+    rows, width = n2_ref.shape[1:]
+    every = line * rows
+    tiles = wg.shape[1] // tile
+    me = lax.axis_index("tensor")
+    loads = [
+        pltpu.make_async_copy(a, b, wsem.at[i])
+        for i, (a, b) in enumerate(((gate_hbm, wg), (up_hbm, wu), (shrink_hbm, ws)))
+    ]
+
+    def begin():
+        for load in loads:
+            load.start()
+        for c in range(chunks):
+            gathered[c, me] = n2_ref[c]
+
+    def saves(c, slot):
+        return (
+            pltpu.make_async_copy(gate_st.at[slot], gate_out.at[c], osem.at[0, slot]),
+            pltpu.make_async_copy(up_st.at[slot], up_out.at[c], osem.at[1, slot]),
+        )
+
+    def keep(c):
+        return pltpu.make_async_copy(gathered.at[c], n2_out.at[c], nsem.at[c])
+
+    def work(c):
+        slot = c % 2
+
+        @pl.when(c == 0)
+        def _():
+            for load in loads:
+                load.wait()
+
+        @pl.when(c >= 2)
+        def _():
+            for save in saves(c - 2, slot):
+                save.wait()
+
+        keep(c).start()
+        x = gathered[c].reshape(every, width)
+        er = dot(x, high_ref[...]).astype(BF)
+
+        def one(f, rank):
+            cols = pl.ds(pl.multiple_of(f * tile, tile), tile)
+            gate = dot(x, wg[:, cols]) + dot(er, expand_ref[0, :, cols])
+            up = dot(x, wu[:, cols]) + dot(er, expand_ref[1, :, cols])
+            gate_st[slot, :, cols] = gate.astype(BF)
+            up_st[slot, :, cols] = up.astype(BF)
+            act = (gate * (1.0 / (1.0 + jnp.exp(-gate))) * up).astype(BF)
+            now = dot_t(act, ws[:, cols])
+
+            @pl.when(f == 0)
+            def _():
+                acc[...] = now
+
+            @pl.when(f > 0)
+            def _():
+                acc[...] += now
+
+            return rank + dot_t(act, ash_ref[:, cols])
+
+        rank = lax.fori_loop(0, tiles, one, jnp.zeros((every, ash_ref.shape[0]), F32))
+        total = acc[...] + dot(rank.astype(BF), res_ref[...])
+        partial_ref[c] = total.astype(BF).reshape(line, rows, width)
+        for save in saves(c, slot):
+            save.start()
+
+    line_exchange(
+        line, chunks, gathered, partial_ref, from_left, from_right, out_ref,
+        (s0, s1, s2, s3, s4, s5, s6), begin, work,
+    )
+    for c in range(chunks):
+        keep(c).wait()
+    for c in range(max(chunks - 2, 0), chunks):
+        for save in saves(c, c % 2):
+            save.wait()
+
+
+def ff_tile(hidden):
+    return hidden // 3 if hidden % (3 * LANES) == 0 else LANES
+
+
+def mlp_forward(n2, w, ad):
+    line = lax.axis_size("tensor")
+    rows, width = n2.shape
+    hidden = w["gate"].shape[1]
+    part = rows // CHUNKS
+    every = line * part
+    out, n2_all, gate, up = pl.pallas_call(
+        partial(mlp_kernel, line, CHUNKS, ff_tile(hidden)),
+        in_specs=[vspec()] + [hspec()] * 3 + [vspec()] * 4,
+        out_specs=[vspec()] + [hspec()] * 3,
+        out_shape=[
+            jax.ShapeDtypeStruct((CHUNKS, part, width), F32),
+            jax.ShapeDtypeStruct((CHUNKS, line, part, width), BF),
+            jax.ShapeDtypeStruct((CHUNKS, every, hidden), BF),
+            jax.ShapeDtypeStruct((CHUNKS, every, hidden), BF),
+        ],
+        scratch_shapes=exchange_scratch(line, CHUNKS, part, width)
+        + [pltpu.VMEM((width, hidden), BF)] * 3
+        + [pltpu.VMEM((2, every, hidden), BF)] * 2
+        + [
+            pltpu.VMEM((every, width), F32),
+            pltpu.SemaphoreType.DMA((3,)),
+            pltpu.SemaphoreType.DMA((2, 2)),
+            pltpu.SemaphoreType.DMA((CHUNKS,)),
+        ],
+        compiler_params=pltpu.CompilerParams(
+            collective_id=0, has_side_effects=True, vmem_limit_bytes=VMEM_LIMIT
+        ),
+        cost_estimate=pl.CostEstimate(
+            flops=6 * line * rows * width * hidden,
+            bytes_accessed=6 * width * hidden + 4 * line * rows * hidden,
+            transcendentals=line * rows * hidden,
+        ),
+    )(
+        n2.reshape(CHUNKS, part, width), w["gate"], w["up"], w["shrink_t"],
+        ad["high"], ad["expand"], ad["shrink"], ad["residual"][1],
+    )
+    return out.reshape(rows, width), (n2_all.reshape(CHUNKS, every, width), gate, up)
+
+
+def mlp_back_kernel(
+    line, chunks, tile,
+    ds_ref, gate_hbm, up_hbm, shrink_hbm, n2_hbm, gate_in, up_in, high_ref, expand_ref, ash_ref, res_ref,
+    out_ref, ghigh_ref, gexp_ref, gsh_ref, gres_ref,
+    gathered, partial_ref, from_left, from_right, s0, s1, s2, s3, s4, s5, s6,
+    wg, wu, ws, gate_st, up_st, n2_st, acc, wsem, isem,
+):
+    rows, width = ds_ref.shape[1:]
+    every = line * rows
+    tiles = wg.shape[1] // tile
+    me = lax.axis_index("tensor")
+    loads = [
+        pltpu.make_async_copy(a, b, wsem.at[i])
+        for i, (a, b) in enumerate(((shrink_hbm, ws), (gate_hbm, wg), (up_hbm, wu)))
+    ]
+
+    def fetch(c):
+        slot = c % 2
+        return (
+            pltpu.make_async_copy(gate_in.at[c], gate_st.at[slot], isem.at[0, slot]),
+            pltpu.make_async_copy(up_in.at[c], up_st.at[slot], isem.at[1, slot]),
+            pltpu.make_async_copy(n2_hbm.at[c], n2_st.at[slot], isem.at[2, slot]),
+        )
+
+    def begin():
+        for load in loads:
+            load.start()
+        for one in fetch(0):
+            one.start()
+        for c in range(chunks):
+            gathered[c, me] = ds_ref[c]
+        for ref in (ghigh_ref, gexp_ref, gsh_ref, gres_ref):
+            ref[...] = jnp.zeros_like(ref)
+
+    def work(c):
+        slot = c % 2
+
+        @pl.when(c == 0)
+        def _():
+            for load in loads:
+                load.wait()
+
+        for one in fetch(c):
+            one.wait()
+
+        @pl.when(c + 1 < chunks)
+        def _():
+            for one in fetch(c + 1):
+                one.start()
+
+        ds = gathered[c].reshape(every, width)
+        n2 = n2_st[slot]
+        er = dot(n2, high_ref[...]).astype(BF)
+        rank_in = dot_t(ds, res_ref[...]).astype(BF)
+
+        def one(f, carry):
+            rank_out, srank = carry
+            cols = pl.ds(pl.multiple_of(f * tile, tile), tile)
+            act_grad = dot(ds, ws[:, cols]) + dot(rank_in, ash_ref[:, cols])
+            gate = gate_st[slot, :, cols].astype(F32)
+            up = up_st[slot, :, cols].astype(F32)
+            sig = 1.0 / (1.0 + jnp.exp(-gate))
+            silu = gate * sig
+            act = (silu * up).astype(BF)
+            gate_grad = (act_grad * up * (sig + silu * (1.0 - sig))).astype(BF)
+            up_grad = (act_grad * silu).astype(BF)
+            now = dot_t(gate_grad, wg[:, cols]) + dot_t(up_grad, wu[:, cols])
+
+            @pl.when(f == 0)
+            def _():
+                acc[...] = now
+
+            @pl.when(f > 0)
+            def _():
+                acc[...] += now
+
+            gexp_ref[0, :, cols] += t_dot(er, gate_grad)
+            gexp_ref[1, :, cols] += t_dot(er, up_grad)
+            gsh_ref[:, cols] += t_dot(rank_in, act)
+            rank_out = rank_out + dot_t(gate_grad, expand_ref[0, :, cols])
+            rank_out = rank_out + dot_t(up_grad, expand_ref[1, :, cols])
+            return rank_out, srank + dot_t(act, ash_ref[:, cols])
+
+        rank_out, srank = lax.fori_loop(
+            0,
+            tiles,
+            one,
+            (
+                jnp.zeros((every, expand_ref.shape[1]), F32),
+                jnp.zeros((every, ash_ref.shape[0]), F32),
+            ),
+        )
+        rank_out = rank_out.astype(BF)
+        total = acc[...] + dot_t(rank_out, high_ref[...])
+        partial_ref[c] = total.astype(BF).reshape(line, rows, width)
+        ghigh_ref[...] += t_dot(rank_out, n2)
+        gres_ref[...] += t_dot(srank.astype(BF), ds)
+
+    line_exchange(
+        line, chunks, gathered, partial_ref, from_left, from_right, out_ref,
+        (s0, s1, s2, s3, s4, s5, s6), begin, work,
+    )
+
+
+def mlp_backward(ds, w, ad, saved):
+    n2_all, gate, up = saved
+    line = lax.axis_size("tensor")
+    rows, width = ds.shape
+    hidden = w["gate"].shape[1]
+    part = rows // CHUNKS
+    every = line * part
+    out, g_high, g_expand, g_shrink, g_res = pl.pallas_call(
+        partial(mlp_back_kernel, line, CHUNKS, ff_tile(hidden)),
+        in_specs=[vspec()] + [hspec()] * 6 + [vspec()] * 4,
+        out_specs=[vspec()] * 5,
+        out_shape=[
+            jax.ShapeDtypeStruct((CHUNKS, part, width), F32),
+            jax.ShapeDtypeStruct((2 * RANK, width), F32),
+            jax.ShapeDtypeStruct((2, 2 * RANK, hidden), F32),
+            jax.ShapeDtypeStruct((RANK, hidden), F32),
+            jax.ShapeDtypeStruct((RANK, width), F32),
+        ],
+        scratch_shapes=exchange_scratch(line, CHUNKS, part, width)
+        + [pltpu.VMEM((width, hidden), BF)] * 3
+        + [pltpu.VMEM((2, every, hidden), BF)] * 2
+        + [
+            pltpu.VMEM((2, every, width), BF),
+            pltpu.VMEM((every, width), F32),
+            pltpu.SemaphoreType.DMA((3,)),
+            pltpu.SemaphoreType.DMA((3, 2)),
+        ],
+        compiler_params=pltpu.CompilerParams(
+            collective_id=1, has_side_effects=True, vmem_limit_bytes=VMEM_LIMIT
+        ),
+        cost_estimate=pl.CostEstimate(
+            flops=6 * line * rows * width * hidden,
+            bytes_accessed=6 * width * hidden + 4 * line * rows * hidden,
+            transcendentals=line * rows * hidden,
+        ),
+    )(
+        ds.reshape(CHUNKS, part, width), w["gate"], w["up"], w["shrink_t"], n2_all, gate, up,
+        ad["high"], ad["expand"], ad["shrink"], ad["residual"][1],
+    )
+    g_expand = jnp.concatenate([g_expand[0, :RANK], g_expand[1, RANK:]], axis=0)
+    return out.reshape(rows, width), g_high, g_expand, g_shrink, g_res
+
+
 def spread(rows):
     return lax.all_gather(rows, "tensor", axis=0, tiled=True)
 
@@ -160,11 +598,6 @@
     return lax.psum_scatter(
         partial_rows.astype(BF), "tensor", scatter_dimension=0, tiled=True
     ).astype(F32)
-
-
-def row_chunks(x):
-    step = x.shape[0] // CHUNKS
-    return [x[i * step : (i + 1) * step] for i in range(CHUNKS)]
 
 
 def forward(x, w, ad, info, tables):
@@ -191,17 +624,8 @@
     middle = x + dot_t(attended, w["out_t"]) + dot(attend_rank, ad["residual"][0])
     inverse_two = lax.rsqrt(jnp.mean(middle * middle, axis=-1, keepdims=True) + EPSILON)
     normed_two = (middle * inverse_two * w["gain"][1]).astype(BF)
-    shrunk, saved = [], []
-    for part in row_chunks(normed_two):
-        n2 = spread(part)
-        expand_rank = dot(n2, ad["input"][:, 3 * RANK :]).astype(BF)
-        gate = dot(n2, w["gate"]) + dot(expand_rank[:, :RANK], ad["expand"][0])
-        up = dot(n2, w["up"]) + dot(expand_rank[:, RANK:], ad["expand"][1])
-        act = (jax.nn.silu(gate) * up).astype(BF)
-        shrink_rank = dot(act, ad["shrink"]).astype(BF)
-        shrunk.append(fold(dot_t(act, w["shrink_t"]) + dot(shrink_rank, ad["residual"][1])))
-        saved.append((n2, expand_rank, gate.astype(BF), up.astype(BF), act, shrink_rank))
-    y = middle + jnp.concatenate(shrunk, axis=0)
+    shrunk, saved = mlp_forward(normed_two, w, ad)
+    y = middle + shrunk
     kept = (x, inverse_one, normed, low, q, kv_all, attended, logs, attend_rank, middle, inverse_two, saved)
     return y, kept
 
@@ -209,29 +633,8 @@
 def backward(dy, w, ad, kept, info, tables):
     (x, inverse_one, normed, low, q, kv_all, attended, logs, attend_rank, middle, inverse_two, saved) = kept
     width = x.shape[1]
-    high = ad["input"][:, 3 * RANK :]
-    folded, g_high, g_expand, g_shrink, g_res_two = [], 0, 0, 0, 0
-    for part, (n2, expand_rank, gate, up, act, shrink_rank) in zip(row_chunks(dy.astype(BF)), saved):
-        ds = spread(part)
-        shrink_rank_grad = dot_t(ds, ad["residual"][1]).astype(BF)
-        act_grad = dot(ds, w["shrink_t"]) + dot_t(shrink_rank_grad, ad["shrink"])
-        gate, up = gate.astype(F32), up.astype(F32)
-        sig = jax.nn.sigmoid(gate)
-        gate_grad = (act_grad * up * sig * (1.0 + gate * (1.0 - sig))).astype(BF)
-        up_grad = (act_grad * gate * sig).astype(BF)
-        rank_grad = jnp.concatenate(
-            [dot_t(gate_grad, ad["expand"][0]), dot_t(up_grad, ad["expand"][1])], axis=1
-        ).astype(BF)
-        folded.append(
-            fold(dot_t(gate_grad, w["gate"]) + dot_t(up_grad, w["up"]) + dot_t(rank_grad, high))
-        )
-        g_high = g_high + t_dot(rank_grad, n2)
-        g_expand = g_expand + jnp.concatenate(
-            [t_dot(expand_rank[:, :RANK], gate_grad), t_dot(expand_rank[:, RANK:], up_grad)], axis=0
-        )
-        g_shrink = g_shrink + t_dot(shrink_rank_grad, act)
-        g_res_two = g_res_two + t_dot(shrink_rank, ds)
-    middle_grad = dy + norm_back(middle, inverse_two, w["gain"][1], jnp.concatenate(folded, axis=0))
+    normed_two_grad, g_high, g_expand, g_shrink, g_res_two = mlp_backward(dy.astype(BF), w, ad, saved)
+    middle_grad = dy + norm_back(middle, inverse_two, w["gain"][1], normed_two_grad)
     branch_grad = middle_grad.astype(BF)
     attend_rank_grad = dot_t(branch_grad, ad["residual"][0]).astype(BF)
     attended_grad = (dot(branch_grad, w["out_t"]) + dot_t(attend_rank_grad, ad["attend"])).astype(BF)
@@ -306,9 +709,15 @@
     kv = lax.dynamic_slice_in_dim(kv, place * kv_cols, kv_cols, 1)
     attn = jnp.concatenate([query_weight[0], output_weight[0].T, kv], axis=1)
     q_cols = query_weight.shape[2]
+    hidden = expand_weight.shape[3]
+    padding = -hidden % (2 * LANES)
+
+    def padded(m):
+        return jnp.pad(m, [(0, 0)] * (m.ndim - 1) + [(0, padding)])
+
     halves = [
         swap(m.reshape(layers, m.shape[0] // layers, m.shape[1]))
-        for m in (attn, expand_weight[0, 0], expand_weight[0, 1], shrink_weight[0].T)
+        for m in (attn, *(padded(m) for m in (expand_weight[0, 0], expand_weight[0, 1], shrink_weight[0].T)))
     ]
     every = ("dp", "section")
     small = jnp.concatenate(
@@ -364,9 +773,15 @@
             input=picked[0][layer],
             q=query_all[layer],
             kv=picked[2][layer],
-            expand=picked[3][layer],
+            high=picked[0][layer][:, 3 * RANK :],
+            expand=jnp.pad(
+                jnp.stack(
+                    [jnp.pad(picked[3][layer][i], [(i * RANK, (1 - i) * RANK), (0, 0)]) for i in range(2)]
+                ),
+                [(0, 0), (0, 0), (0, padding)],
+            ),
             attend=attend_all[layer],
-            shrink=picked[5][layer],
+            shrink=padded(picked[5][layer].T),
             residual=picked[6][layer],
         )
 
@@ -395,7 +810,7 @@
     input_grad = swap(jnp.stack(grads))
 
     whole = lax.psum(swap(jnp.stack(wholes)), "tensor")
-    part = swap(jnp.stack(parts))
+    part = swap(jnp.stack(parts)[..., :hidden])
     own = 7 * RANK
     q_rows = lax.dynamic_slice_in_dim(whole[:, own : own + 2 * RANK], place * q_cols, q_cols, 2)
     rest = jnp.concatenate([whole[:, :own], whole[:, own + 2 * RANK :]], axis=1)

time: 1490 us -> 1280 us (0.86)
  Pallas kernels: 61.1 us -> 475 us
  waiting for transfers between devices: 740 us -> 408 us
  matrix products: 338 us -> 58.5 us
    pallas_call x0 -> x4, Pallas kernels: none -> 414 us  [the longest x2 210 us: mlp_forward(): pl.pallas_call(partial(mlp_kernel, line, CHUNKS, ff_tile(hidden)), in_spe...]
    reduce_scatter x10 -> x2, waiting for transfers between devices: 211 us -> 38.2 us  [fold(): lax.psum_scatter(partial_rows.astype(BF), 'tensor', scatter_dimension=0,...]
    all_gather x10 -> x2, waiting for transfers between devices: 140 us -> 0.02 us  [spread(): return lax.all_gather(rows, 'tensor', axis=0, tiled=True)]
    dot_general x50 -> x18, matrix products: 157 us -> 20.6 us  [dot(): return jnp.dot(a, b, preferred_element_type=F32)]
    dot_general x50 -> x18, matrix products: 134 us -> 23.7 us  [dot_t(): lax.dot_general(a, b, (((1,), (1,)), ((), ())), preferred_element_type=F32)]
    all_gather x2, waiting for transfers between devices: 78.7 us -> 21.1 us  [weights(): lax.all_gather(halves[1][layer], every, axis=0, tiled=True)]
    dot_general x32 -> x12, matrix products: 40.7 us -> 7.55 us  [t_dot(): lax.dot_general(a, b, (((0,), (0,)), ((), ())), preferred_element_type=F32)]
    all_gather x2, waiting for transfers between devices: 81.1 us -> 103 us  [weights(): lax.all_gather(halves[2][layer], every, axis=0, tiled=True)]
  transfers between devices with their start and end apart: 38 -> 22, of which waited for: 26 -> 13; matrix products, arithmetic and copies ran while one was open for 29% -> 12% of each run, Pallas kernels for 2% -> 2%
where the time goes in v2:
time: 1280 us; the launch traced here: 1270 us
  Pallas kernels  475 us (37%)
  waiting for transfers between devices  408 us (32%)
  local copies, waits for them, and re-layouts  125 us (10%)
  blocking collectives  112 us (9%)
  matrix products  58.5 us (5%)
  other arithmetic  49 us (4%)
  starting transfers between devices  25.4 us (2%)
  between operations  20.8 us (2%)
    pallas_call x2, Pallas kernels, mlp_forward(): pl.pallas_call(partial(mlp_kernel, line, CHUNKS, ff_tile(hidden)), in_spe...  210 us
    pallas_call x2, Pallas kernels, mlp_backward(): pl.pallas_call(partial(mlp_back_kernel, line, CHUNKS, ff_tile(hidden)), i...  203 us
    all_gather x2, waiting for transfers between devices, weights(): lax.all_gather(halves[2][layer], every, axis=0, tiled=True)  103 us
    all_gather x2, waiting for transfers between devices, weights(): lax.all_gather(halves[3][layer], every, axis=0, tiled=True)  101 us
    all_gather x2, waiting for transfers between devices, weights(): g = lax.all_gather(halves[0][layer], every + ('tensor',), axis=0)  68.2 us
    unnamed x287, local copies, waits for them, and re-layouts  47.1 us
    all_to_all x8, blocking collectives, swap(): lax.all_to_all(pair, 'section', split_axis=0, concat_axis=0, tiled=True)  42.2 us
    slice x10, local copies, waits for them, and re-layouts, cut(): return g[..., start:start + size].reshape(width, tensor * size)  39.9 us
  transfers between devices with their start and end apart: 22, of which 13 were waited for; matrix products, arithmetic and copies ran while one was open for 12% of the time, Pallas kernels for 2%

profile of v2, /device:TPU:0, one launch (start us, length us, event | category | flops | bytes accessed | tf_op | source)
XLA Modules:
  0.0 1272.8 jit_solution(253449661375710086)
XLA Ops:
  38.4 68.2 %all-gather.22.cloned.1.call-done = bf16[32,192,896]{2,1,0:T(8,128)(2,1)} async-done(((bf16[1,192,896]{2,1,0:T(8,128)(2,1)}), bf16[32,192,896]{2,1,0:T(8,128)(2,1)}) %all-gather.22.cloned.1.call-update) | async-done | bytes 11010064 | tf_op jit(solution)/shard_map/all_gather | solution.py:730
  155.0 22.1 %all-gather.1 = bf16[1,3072]{1,0:T(2,128)(2,1)S(1)} all-gather(bf16[1,384]{1,0:T(2,128)(2,1)S(1)} %copy-done.125), channel_id=3, replica_groups=mesh['section'=2,'dp'=4,'tensor'=4] {'section','tensor'}, dimensions={1}, use_global_device_ids=true | all-gather | bytes 6912 | tf_op jit(solution)/shard_map/all_gather | solution.py:727
  181.7 13.9 %all_gather.61 = bf16[2,16,1536]{2,1,0:T(8,128)(2,1)S(1)} all-gather(bf16[2,16,384]{2,1,0:T(8,128)(2,1)S(1)} %all-to-all-done.2), channel_id=1, replica_groups=mesh['section'=2,'dp'=4,'tensor'=4] {'tensor'}, dimensions={2}, use_global_device_ids=true | all-gather | bytes 122880 | tf_op jit(solution)/shard_map/all_gather | solution.py:768
  201.0 14.6 %all_gather.63 = bf16[2,1536,16]{1,2,0:T(8,128)(2,1)} all-gather(bf16[2,384,16]{1,2,0:T(8,128)(2,1)S(1)} %all-to-all-done.4), channel_id=1, replica_groups=mesh['section'=2,'dp'=4,'tensor'=4] {'tensor'}, dimensions={1}, use_global_device_ids=true | all-gather | bytes 122880 | tf_op jit(solution)/shard_map/all_gather | solution.py:769
  256.1 13.4 %shard_map.250 = (bf16[256,1536]{1,0:T(8,128)(2,1)S(1)}, f32[12,1,256]{2,1,0:T(1,128)S(1)}) custom-call(s32[2]{0:T(128)S(1)} %pad_add_fusion.info_ref, bf16[256,1536]{1,0:T(8,128)(2,1)S(1)} %copy.94.q_ref, bf16[1024,512]{1,0:T(8,128)(2,1)S(1)} %copy-done, bf16[1024,512]{1,0:T(8,128)(2,1)S(1)} %copy-done), custom_call_target="tpu_custom_call" | custom-call | tf_op jit(solution)/shard_map/pallas_call | solution.py:80
  278.5 51.2 %all-gather.36.cloned.1.call-done = bf16[1,1536,2304]{2,1,0:T(8,128)(2,1)} async-done(((bf16[1,192,2304]{2,1,0:T(8,128)(2,1)}), bf16[1,1536,2304]{2,1,0:T(8,128)(2,1)}) %all-gather.36.cloned.1.call-update) | async-done | bytes 7077904 | tf_op jit(solution)/shard_map/all_gather | solution.py:744
  329.7 50.6 %all-gather.38.cloned.1.call-done = bf16[1,1536,2304]{2,1,0:T(8,128)(2,1)} async-done(((bf16[1,192,2304]{2,1,0:T(8,128)(2,1)}), bf16[1,1536,2304]{2,1,0:T(8,128)(2,1)}) %all-gather.38.cloned.1.call-update) | async-done | bytes 7077904 | tf_op jit(solution)/shard_map/all_gather | solution.py:745
  380.3 105.2 %shard_map.251 = (f32[4,64,1536]{2,1,0:T(8,128)}, bf16[4,4,64,1536]{3,2,1,0:T(8,128)(2,1)}, bf16[4,256,2304]{2,1,0:T(8,128)(2,1)}, bf16[4,256,2304]{2,1,0:T(8,128)(2,1)}) custom-call(bf16[4,64,1536]{2,1,0:T(8,128)(2,1)} %bitcast.455, bf16[1536,2304]{1,0:T(8,128)(2,1)} %bitcast.470, bf16[1536,2304]{1,0:T(8,128)(2,1)} %bitcast.472, ...), custom_call_target="tpu_custom_call" | custom-call | flops 21743271936 | bytes 30670848 | tf_op jit(solution)/shard_map/pallas_call | solution.py:412
  531.4 13.4 %shard_map.252 = (bf16[256,1536]{1,0:T(8,128)(2,1)S(1)}, f32[12,1,256]{2,1,0:T(1,128)S(1)}) custom-call(s32[2]{0:T(128)S(1)} %pad_add_fusion.info_ref, bf16[256,1536]{1,0:T(8,128)(2,1)S(1)} %copy.105.q_ref, bf16[1024,512]{1,0:T(8,128)(2,1)S(1)} %copy-done.2, bf16[1024,512]{1,0:T(8,128)(2,1)S(1)} %copy-done.2), custom_call_target="tpu_custom_call" | custom-call | tf_op jit(solution)/shard_map/pallas_call | solution.py:80
  552.5 18.6 %all-gather.40.cloned.1.call-done = bf16[1,1536,2304]{2,1,0:T(8,128)(2,1)} async-done(((bf16[1,192,2304]{2,1,0:T(8,128)(2,1)}), bf16[1,1536,2304]{2,1,0:T(8,128)(2,1)}) %all-gather.40.cloned.1.call-update) | async-done | bytes 7077904 | tf_op jit(solution)/shard_map/all_gather | solution.py:743
  571.1 51.4 %all-gather.42.cloned.1.call-done = bf16[1,1536,2304]{2,1,0:T(8,128)(2,1)} async-done(((bf16[1,192,2304]{2,1,0:T(8,128)(2,1)}), bf16[1,1536,2304]{2,1,0:T(8,128)(2,1)}) %all-gather.42.cloned.1.call-update) | async-done | bytes 7077904 | tf_op jit(solution)/shard_map/all_gather | solution.py:744
  622.5 50.6 %all-gather.44.cloned.1.call-done = bf16[1,1536,2304]{2,1,0:T(8,128)(2,1)} async-done(((bf16[1,192,2304]{2,1,0:T(8,128)(2,1)}), bf16[1,1536,2304]{2,1,0:T(8,128)(2,1)}) %all-gather.44.cloned.1.call-update) | async-done | bytes 7077904 | tf_op jit(solution)/shard_map/all_gather | solution.py:745
  673.1 105.2 %shard_map.253 = (f32[4,64,1536]{2,1,0:T(8,128)}, bf16[4,4,64,1536]{3,2,1,0:T(8,128)(2,1)}, bf16[4,256,2304]{2,1,0:T(8,128)(2,1)}, bf16[4,256,2304]{2,1,0:T(8,128)(2,1)}) custom-call(bf16[4,64,1536]{2,1,0:T(8,128)(2,1)} %bitcast.454, bf16[1536,2304]{1,0:T(8,128)(2,1)} %bitcast.476, bf16[1536,2304]{1,0:T(8,128)(2,1)} %bitcast.478, ...), custom_call_target="tpu_custom_call" | custom-call | flops 21743271936 | bytes 30670848 | tf_op jit(solution)/shard_map/pallas_call | solution.py:412
  778.3 99.9 %shard_map.254 = (f32[4,64,1536]{2,1,0:T(8,128)}, f32[32,1536]{1,0:T(8,128)}, f32[2,32,2304]{2,1,0:T(8,128)}, f32[16,2304]{1,0:T(8,128)}, f32[16,1536]{1,0:T(8,128)}) custom-call(bf16[4,64,1536]{2,1,0:T(8,128)(2,1)} %multiply_convert_fusion.ds_ref, bf16[1536,2304]{1,0:T(8,128)(2,1)} %bitcast.477, bf16[1536,2304]{1,0:T(8,128)(2,1)} %bitcast.479, ...), custom_call_target="tpu_custom_call" | custom-call | flops 21743271936 | bytes 30670848 | tf_op jit(solution)/shard_map/pallas_call | solution.py:557
  891.0 17.1 %shard_map.255 = (f32[256,1536]{1,0:T(8,128)S(1)}, f32[1024,256]{1,0:T(8,128)S(1)}, f32[1024,256]{1,0:T(8,128)S(1)}) custom-call(s32[2]{0:T(128)S(1)} %pad_add_fusion.info_ref, bf16[256,1536]{1,0:T(8,128)(2,1)S(1)} %copy.105.q_ref, bf16[1024,512]{1,0:T(8,128)(2,1)S(1)} %copy-done.3, bf16[1024,512]{1,0:T(8,128)(2,1)S(1)} %copy-done.3, ...), custom_call_target="tpu_custom_call" | custom-call | tf_op jit(solution)/shard_map/pallas_call | solution.py:133
  923.2 15.6 %reduce-scatter.3.cloned.1.call-done = bf16[256,512]{1,0:T(8,128)(2,1)} async-done(((bf16[1024,512]{1,0:T(8,128)(2,1)}), bf16[256,512]{1,0:T(8,128)(2,1)}) %reduce-scatter.3.cloned.1.call-update) | async-done | bytes 262160 | tf_op jit(solution)/shard_map/reduce_scatter | solution.py:598
  949.5 103.2 %shard_map.256 = (f32[4,64,1536]{2,1,0:T(8,128)}, f32[32,1536]{1,0:T(8,128)}, f32[2,32,2304]{2,1,0:T(8,128)}, f32[16,2304]{1,0:T(8,128)}, f32[16,1536]{1,0:T(8,128)}) custom-call(bf16[4,64,1536]{2,1,0:T(8,128)(2,1)} %bitcast.453, bf16[1536,2304]{1,0:T(8,128)(2,1)} %bitcast.471, bf16[1536,2304]{1,0:T(8,128)(2,1)} %bitcast.473, bf16[1536,2304]{1,0:T(8,128)(2,1)} %bitcast.475, ...), custom_call_target="tpu_custom_call" | custom-call | flops 21743271936 | bytes 30670848 | tf_op jit(solution)/shard_map/pallas_call | solution.py:557
  1062.2 17.1 %shard_map.257 = (f32[256,1536]{1,0:T(8,128)S(1)}, f32[1024,256]{1,0:T(8,128)S(1)}, f32[1024,256]{1,0:T(8,128)S(1)}) custom-call(s32[2]{0:T(128)S(1)} %pad_add_fusion.info_ref, bf16[256,1536]{1,0:T(8,128)(2,1)S(1)} %copy.94.q_ref, bf16[1024,512]{1,0:T(8,128)(2,1)S(1)} %copy-done.1, bf16[1024,512]{1,0:T(8,128)(2,1)S(1)} %copy-done.1, ...), custom_call_target="tpu_custom_call" | custom-call | tf_op jit(solution)/shard_map/pallas_call | solution.py:133
  1088.2 22.7 %reduce-scatter.5.cloned.1.call-done = bf16[256,512]{1,0:T(8,128)(2,1)} async-done(((bf16[1024,512]{1,0:T(8,128)(2,1)}), bf16[256,512]{1,0:T(8,128)(2,1)}) %reduce-scatter.5.cloned.1.call-update) | async-done | bytes 262160 | tf_op jit(solution)/shard_map/reduce_scatter | solution.py:598
  1130.2 7.3 all-reduce.11
  1137.5 33.4 %all-reduce.14.cloned.1.call-done = bf16[2,160,1536]{2,1,0:T(8,128)(2,1)} async-done(((bf16[2,160,1536]{2,1,0:T(8,128)(2,1)}), bf16[2,160,1536]{2,1,0:T(8,128)(2,1)}) %all-reduce.14.cloned.1.call-update) | async-done | bytes 983056 | tf_op jit(solution)/shard_map/psum | solution.py:812
  1194.1 10.5 all-gather.32.cloned.1.call-done
  1210.9 9.9 all_gather.74
  1222.5 29.1 %all-gather.30.cloned.1.call-done = bf16[8,128,1536]{2,1,0:T(8,128)(2,1)} async-done(((bf16[2,128,1536]{2,1,0:T(8,128)(2,1)}), bf16[8,128,1536]{2,1,0:T(8,128)(2,1)}) %all-gather.30.cloned.1.call-update) | async-done | bytes 3145744 | tf_op jit(solution)/shard_map/all_gather | solution.py:818
  (553 shorter events, 307.7 us)
Async XLA Ops:
  7.2 99.4 %all-gather.22.cloned.1.call-start = ((), (), s32[]{:S(2)}) async-start(), calls=%async_computation.17 | async-start | bytes 11354112 | tf_op jit(solution)/shard_map/all_gather | solution.py:730
  14.9 235.9 %all-gather.26.cloned.1.call-start = ((), (), s32[]{:S(2)}) async-start(), calls=%async_computation.19 | async-start | bytes 11354112 | tf_op jit(solution)/shard_map/all_gather | solution.py:730
  22.0 5.3 all-to-all-start.1
  27.3 10.6 all-to-all-start.3
  30.6 224.0 %all-gather.24.cloned.1.call-start = ((), (), s32[]{:S(2)}) async-start(), calls=%async_computation.18 | async-start | bytes 1310720 | tf_op jit(solution)/shard_map/all_gather | solution.py:594
  112.4 166.0 %all-gather.34.cloned.1.call-start = ((), (), s32[]{:S(2)}) async-start(), calls=%async_computation.26 | async-start | bytes 7962624 | tf_op jit(solution)/shard_map/all_gather | solution.py:743
  125.3 204.4 %all-gather.36.cloned.1.call-start = ((), (), s32[]{:S(2)}) async-start(), calls=%async_computation.27 | async-start | bytes 7962624 | tf_op jit(solution)/shard_map/all_gather | solution.py:744
  133.1 247.2 %all-gather.38.cloned.1.call-start = ((), (), s32[]{:S(2)}) async-start(), calls=%async_computation.28 | async-start | bytes 7962624 | tf_op jit(solution)/shard_map/all_gather | solution.py:745
  143.2 6.3 all-to-all-start.10
  149.5 28.9 %all-to-all-start.2 = ((bf16[2,16,384]{2,1,0:T(8,128)(2,1)}), bf16[2,16,384]{2,1,0:T(8,128)(2,1)S(1)}, u32[]{:S(2)}, u32[]{:S(2)}) async-start(bf16[2,16,384]{2,1,0:T(8,128)(2,1)} %pad_maximum_fusion.24), calls=%async_computation.2 | async-start | bytes 49152 | tf_op jit(solution)/shard_map/all_to_all | solution.py:676
  178.5 19.0 %all-to-all-start.4 = ((bf16[2,384,16]{1,2,0:T(8,128)(2,1)}), bf16[2,384,16]{1,2,0:T(8,128)(2,1)S(1)}, u32[]{:S(2)}, u32[]{:S(2)}) async-start(bf16[2,384,16]{1,2,0:T(8,128)(2,1)} %pad_maximum_fusion.25), calls=%async_computation.4 | async-start | bytes 49152 | tf_op jit(solution)/shard_map/all_to_all | solution.py:676
  197.5 21.6 %all-to-all-start.9 = ((bf16[2,2,16,2240]{3,2,1,0:T(8,128)(2,1)}), bf16[2,2,16,2240]{3,2,1,0:T(8,128)(2,1)S(1)}, u32[]{:S(2)}, u32[]{:S(2)}) async-start(bf16[2,2,16,2240]{3,2,1,0:T(8,128)(2,1)} %pad_maximum_fusion.14), calls=%async_computation.9 | async-start | bytes 589824 | tf_op jit(solution)/shard_map/all_to_all | solution.py:676
  219.1 5.5 all-to-all-start.5
  222.5 307.6 %all-gather.28.cloned.1.call-start = ((), (), s32[]{:S(2)}) async-start(), calls=%async_computation.20 | async-start | bytes 1310720 | tf_op jit(solution)/shard_map/all_gather | solution.py:594
  487.2 460.3 %copy-start.18 = (bf16[256,1536]{1,0:T(8,128)(2,1)}, bf16[256,1536]{1,0:T(8,128)(2,1)S(1)}, u32[]{:S(2)}) copy-start(bf16[256,1536]{1,0:T(8,128)(2,1)S(1)} %get-tuple-element.103) | copy-start | bytes 2359300
  491.6 79.5 %all-gather.40.cloned.1.call-start = ((), (), s32[]{:S(2)}) async-start(), calls=%async_computation.29 | async-start | bytes 7962624 | tf_op jit(solution)/shard_map/all_gather | solution.py:743
  492.3 130.1 %all-gather.42.cloned.1.call-start = ((), (), s32[]{:S(2)}) async-start(), calls=%async_computation.30 | async-start | bytes 7962624 | tf_op jit(solution)/shard_map/all_gather | solution.py:744
  493.1 180.0 %all-gather.44.cloned.1.call-start = ((), (), s32[]{:S(2)}) async-start(), calls=%async_computation.31 | async-start | bytes 7962624 | tf_op jit(solution)/shard_map/all_gather | solution.py:745
  493.7 445.2 %reduce-scatter.3.cloned.1.call-start = ((), (), s32[]{:S(2)}) async-start(), calls=%async_computation.21 | async-start | bytes 1310720 | tf_op jit(solution)/shard_map/reduce_scatter | solution.py:598
  495.6 445.1 %copy-start.48 = (f32[256,64]{1,0:T(8,128)}, f32[256,64]{1,0:T(8,128)S(1)}, u32[]{:S(2)}) copy-start(f32[256,64]{1,0:T(8,128)S(1)} %copy.109) | copy-start | bytes 196612
  910.3 200.6 %reduce-scatter.5.cloned.1.call-start = ((), (), s32[]{:S(2)}) async-start(), calls=%async_computation.22 | async-start | bytes 1310720 | tf_op jit(solution)/shard_map/reduce_scatter | solution.py:598
  1081.6 89.3 %all-reduce.14.cloned.1.call-start = ((), (), s32[]{:S(2)}) async-start(), calls=%async_computation.23 | async-start | bytes 1966080 | tf_op jit(solution)/shard_map/psum | solution.py:812
  1122.3 82.4 %all-gather.32.cloned.1.call-start = ((), (), s32[]{:S(2)}) async-start(), calls=%async_computation.25 | async-start | bytes 2211840 | tf_op jit(solution)/shard_map/all_gather | solution.py:818
  1128.2 123.4 %all-gather.30.cloned.1.call-start = ((), (), s32[]{:S(2)}) async-start(), calls=%async_computation.24 | async-start | bytes 3932160 | tf_op jit(solution)/shard_map/all_gather | solution.py:818
  (130 other events, 1442.3 us)
Sparse Core Ops, SparseCore 0:
  15.0 91.5 all-gather.21
  110.0 88.6 all-gather.25
  200.8 26.8 all-gather.23
  230.1 48.3 all-gather.33
  280.8 48.8 all-gather.35
  331.4 48.8 all-gather.37
  491.7 28.5 all-gather.27
  522.7 48.3 all-gather.39
  573.6 48.8 all-gather.41
  624.2 48.8 all-gather.43
  910.4 28.3 reduce-scatter.2
  1081.7 29.1 reduce-scatter.4
  1122.4 48.4 all-reduce.13
  1172.7 31.8 all-gather.31
  1207.1 44.5 all-gather.29

commit v3 on v2

v3 whole, which is shorter than its diff:
```python
from functools import partial
import math

import jax
import jax.numpy as jnp
from jax import lax
from jax.experimental import pallas as pl
from jax.experimental.pallas import tpu as pltpu
from jax.sharding import PartitionSpec as P

KV_HEADS = 2
HEAD_DIM = 128
RANK = 16
EPSILON = 1e-06
ROPE_BASE = 1000000.0
MASKED_SCORE = -1e30
CHUNKS = 4
LANES = 128
VMEM_LIMIT = 60 * 2**20
MESH = pl.DeviceIdType.MESH
BF = jnp.bfloat16
F32 = jnp.float32


def dot(a, b):
    return jnp.dot(a, b, preferred_element_type=F32)


def dot_t(a, b):
    return lax.dot_general(a, b, (((1,), (1,)), ((), ())), preferred_element_type=F32)


def t_dot(a, b):
    return lax.dot_general(a, b, (((0,), (0,)), ((), ())), preferred_element_type=F32)


def rotary_tables(first_slot, rows):
    half = HEAD_DIM // 2
    frequency = jnp.exp(-math.log(ROPE_BASE) * (2.0 * jnp.arange(half, dtype=F32) / HEAD_DIM))
    slots = (first_slot + jnp.arange(rows, dtype=jnp.int32)).astype(F32)
    angles = slots[:, None] * frequency[None, :]
    cos, sin = jnp.cos(angles), jnp.sin(angles)
    return jnp.concatenate([cos, cos], axis=1), jnp.concatenate([-sin, sin], axis=1)


def vspec():
    return pl.BlockSpec(memory_space=pltpu.VMEM)


def hspec():
    return pl.BlockSpec(memory_space=pl.ANY)


def line_barrier(me, line):
    barrier = pltpu.get_barrier_semaphore()

    @pl.when(me > 0)
    def _():
        pl.semaphore_signal(barrier, inc=1, device_id={"tensor": me - 1}, device_id_type=MESH)

    @pl.when(me < line - 1)
    def _():
        pl.semaphore_signal(barrier, inc=1, device_id={"tensor": me + 1}, device_id_type=MESH)

    pl.semaphore_wait(barrier, jnp.where(me > 0, 1, 0) + jnp.where(me < line - 1, 1, 0))


def within(c, chunks):
    return jnp.logical_and(c >= 0, c < chunks)


def line_exchange(line, chunks, gathered, partial_ref, from_left, from_right, own_out, sems, begin, work):
    ag_recv, ag_right, ag_left, r_recv, r_send, l_recv, l_send = sems
    me = lax.axis_index("tensor")

    def copy(ref, src, c, o, send, recv, side):
        return pltpu.make_async_remote_copy(
            src_ref=src.at[c, o],
            dst_ref=ref.at[c, o],
            send_sem=send.at[c, o],
            recv_sem=recv.at[c, o],
            device_id={"tensor": me + side},
            device_id_type=MESH,
        )

    def ag(c, o, side):
        return copy(gathered, gathered, c, o, ag_right if side > 0 else ag_left, ag_recv, side)

    def rs(c, o, side):
        if side > 0:
            return copy(from_left, partial_ref, c, o, r_send, r_recv, 1)
        return copy(from_right, partial_ref, c, o, l_send, l_recv, -1)

    has_left, has_right = me > 0, me < line - 1

    def step(s, carry):
        first = s + line - 1

        @pl.when(jnp.logical_and(within(first, chunks), has_right))
        def _():
            ag(first, me, 1).start()

        @pl.when(jnp.logical_and(within(first, chunks), has_left))
        def _():
            ag(first, me, -1).start()

        for d in range(1, line):
            c = s + line - 1 - d

            @pl.when(jnp.logical_and(within(c, chunks), me - d >= 0))
            def _():
                ag(c, me - d, 1).wait_recv()

                @pl.when(has_right)
                def _():
                    ag(c, me - d, 1).start()

            @pl.when(jnp.logical_and(within(c, chunks), me + d < line))
            def _():
                ag(c, me + d, -1).wait_recv()

                @pl.when(has_left)
                def _():
                    ag(c, me + d, -1).start()

        @pl.when(within(s, chunks))
        def _():
            work(s)

        for h in range(line):
            c = s - h

            @pl.when(jnp.logical_and(within(c, chunks), me == h))
            def _():
                for j in range(h + 1, line):
                    if h > 0:
                        rs(c, j, 1).wait_recv()
                        partial_ref[c, j] = (
                            partial_ref[c, j].astype(F32) + from_left[c, j].astype(F32)
                        ).astype(BF)
                    if h < line - 1:
                        rs(c, j, 1).start()

            @pl.when(jnp.logical_and(within(c, chunks), me == line - 1 - h))
            def _():
                for j in range(line - 1 - h):
                    if h > 0:
                        rs(c, j, -1).wait_recv()
                        partial_ref[c, j] = (
                            partial_ref[c, j].astype(F32) + from_right[c, j].astype(F32)
                        ).astype(BF)
                    if h < line - 1:
                        rs(c, j, -1).start()

        last = s - (line - 1)

        @pl.when(within(last, chunks))
        def _():
            own_out[last] = partial_ref[last, me].astype(F32)

            @pl.when(has_left)
            def _():
                rs(last, me, 1).wait_recv()
                own_out[last] += from_left[last, me].astype(F32)

            @pl.when(has_right)
            def _():
                rs(last, me, -1).wait_recv()
                own_out[last] += from_right[last, me].astype(F32)

        return carry

    line_barrier(me, line)
    begin()
    lax.fori_loop(-(line - 1), chunks + line - 1, step, 0)

    def drain(c, carry):
        for o in range(line):

            @pl.when(jnp.logical_and(has_right, me >= o))
            def _():
                ag(c, o, 1).wait_send()

            @pl.when(jnp.logical_and(has_left, me <= o))
            def _():
                ag(c, o, -1).wait_send()

            @pl.when(me < o)
            def _():
                rs(c, o, 1).wait_send()

            @pl.when(me > o)
            def _():
                rs(c, o, -1).wait_send()

        return carry

    lax.fori_loop(0, chunks, drain, 0)


def exchange_scratch(line, chunks, rows, width):
    slots = (chunks, line, rows, width)
    return [pltpu.VMEM(slots, BF)] * 4 + [pltpu.SemaphoreType.DMA((chunks, line))] * 7


def mlp_kernel(
    line, chunks, tile,
    n2_ref, packed, high_ref, expand_ref, ash_ref, res_ref,
    out_ref, n2_out, gate_out, up_out,
    gathered, partial_ref, from_left, from_right, s0, s1, s2, s3, s4, s5, s6,
    wg, wu, ws, gate_st, up_st, acc, wsem, osem, nsem,
):
    rows, width = n2_ref.shape[1:]
    every = line * rows
    tiles = wg.shape[2] // tile
    me = lax.axis_index("tensor")
    loads = [pltpu.make_async_copy(packed.at[:, i], ref, wsem.at[i]) for i, ref in enumerate((wg, wu, ws))]

    def begin():
        for load in loads:
            load.start()
        for c in range(chunks):
            gathered[c, me] = n2_ref[c]

    def saves(c, slot):
        return (
            pltpu.make_async_copy(gate_st.at[slot], gate_out.at[c], osem.at[0, slot]),
            pltpu.make_async_copy(up_st.at[slot], up_out.at[c], osem.at[1, slot]),
        )

    def keep(c):
        return pltpu.make_async_copy(gathered.at[c], n2_out.at[c], nsem.at[c])

    def work(c):
        slot = c % 2

        @pl.when(c == 0)
        def _():
            for load in loads:
                load.wait()

        @pl.when(c >= 2)
        def _():
            for save in saves(c - 2, slot):
                save.wait()

        keep(c).start()
        x = gathered[c].reshape(every, width)
        er = dot(x, high_ref[...]).astype(BF)

        def one(f, rank):
            cols = pl.ds(pl.multiple_of(f * tile, tile), tile)
            gate = dot(x, wg[:, :, cols].reshape(width, tile)) + dot(er, expand_ref[0, :, cols])
            up = dot(x, wu[:, :, cols].reshape(width, tile)) + dot(er, expand_ref[1, :, cols])
            gate_st[slot, :, cols] = gate.astype(BF)
            up_st[slot, :, cols] = up.astype(BF)
            act = (gate * (1.0 / (1.0 + jnp.exp(-gate))) * up).astype(BF)
            now = dot_t(act, ws[:, :, cols].reshape(width, tile))

            @pl.when(f == 0)
            def _():
                acc[...] = now

            @pl.when(f > 0)
            def _():
                acc[...] += now

            return rank + dot_t(act, ash_ref[:, cols])

        rank = lax.fori_loop(0, tiles, one, jnp.zeros((every, ash_ref.shape[0]), F32))
        total = acc[...] + dot(rank.astype(BF), res_ref[...])
        partial_ref[c] = total.astype(BF).reshape(line, rows, width)
        for save in saves(c, slot):
            save.start()

    line_exchange(
        line, chunks, gathered, partial_ref, from_left, from_right, out_ref,
        (s0, s1, s2, s3, s4, s5, s6), begin, work,
    )
    for c in range(chunks):
        keep(c).wait()
    for c in range(max(chunks - 2, 0), chunks):
        for save in saves(c, c % 2):
            save.wait()


def ff_tile(hidden):
    return hidden // 3 if hidden % (3 * LANES) == 0 else LANES


def mlp_forward(n2, w, ad):
    line = lax.axis_size("tensor")
    rows, width = n2.shape
    groups, _, _, hidden = w["mlp"].shape
    part = rows // CHUNKS
    every = line * part
    out, n2_all, gate, up = pl.pallas_call(
        partial(mlp_kernel, line, CHUNKS, ff_tile(hidden)),
        in_specs=[vspec(), hspec()] + [vspec()] * 4,
        out_specs=[vspec()] + [hspec()] * 3,
        out_shape=[
            jax.ShapeDtypeStruct((CHUNKS, part, width), F32),
            jax.ShapeDtypeStruct((CHUNKS, line, part, width), BF),
            jax.ShapeDtypeStruct((CHUNKS, every, hidden), BF),
            jax.ShapeDtypeStruct((CHUNKS, every, hidden), BF),
        ],
        scratch_shapes=exchange_scratch(line, CHUNKS, part, width)
        + [pltpu.VMEM((groups, width // groups, hidden), BF)] * 3
        + [pltpu.VMEM((2, every, hidden), BF)] * 2
        + [
            pltpu.VMEM((every, width), F32),
            pltpu.SemaphoreType.DMA((3,)),
            pltpu.SemaphoreType.DMA((2, 2)),
            pltpu.SemaphoreType.DMA((CHUNKS,)),
        ],
        compiler_params=pltpu.CompilerParams(
            collective_id=0, has_side_effects=True, vmem_limit_bytes=VMEM_LIMIT
        ),
        cost_estimate=pl.CostEstimate(
            flops=6 * line * rows * width * hidden,
            bytes_accessed=6 * width * hidden + 4 * line * rows * hidden,
            transcendentals=line * rows * hidden,
        ),
    )(
        n2.reshape(CHUNKS, part, width), w["mlp"],
        ad["high"], ad["expand"], ad["shrink"], ad["res_two"],
    )
    return out.reshape(rows, width), (n2_all.reshape(CHUNKS, every, width), gate, up)


def mlp_back_kernel(
    line, chunks, tile,
    ds_ref, packed, n2_hbm, gate_in, up_in, high_ref, expand_ref, ash_ref, res_ref,
    out_ref, ghigh_ref, gexp_ref, gsh_ref, gres_ref,
    gathered, partial_ref, from_left, from_right, s0, s1, s2, s3, s4, s5, s6,
    wg, wu, ws, gate_st, up_st, n2_st, acc, wsem, isem,
):
    rows, width = ds_ref.shape[1:]
    every = line * rows
    tiles = wg.shape[2] // tile
    me = lax.axis_index("tensor")
    loads = [pltpu.make_async_copy(packed.at[:, i], ref, wsem.at[i]) for i, ref in enumerate((wg, wu, ws))]

    def fetch(c):
        slot = c % 2
        return (
            pltpu.make_async_copy(gate_in.at[c], gate_st.at[slot], isem.at[0, slot]),
            pltpu.make_async_copy(up_in.at[c], up_st.at[slot], isem.at[1, slot]),
            pltpu.make_async_copy(n2_hbm.at[c], n2_st.at[slot], isem.at[2, slot]),
        )

    def begin():
        for load in loads:
            load.start()
        for one in fetch(0):
            one.start()
        for c in range(chunks):
            gathered[c, me] = ds_ref[c]
        for ref in (ghigh_ref, gexp_ref, gsh_ref, gres_ref):
            ref[...] = jnp.zeros_like(ref)

    def work(c):
        slot = c % 2

        @pl.when(c == 0)
        def _():
            for load in loads:
                load.wait()

        for one in fetch(c):
            one.wait()

        @pl.when(c + 1 < chunks)
        def _():
            for one in fetch(c + 1):
                one.start()

        ds = gathered[c].reshape(every, width)
        n2 = n2_st[slot]
        er = dot(n2, high_ref[...]).astype(BF)
        rank_in = dot_t(ds, res_ref[...]).astype(BF)

        def one(f, carry):
            rank_out, srank = carry
            cols = pl.ds(pl.multiple_of(f * tile, tile), tile)
            act_grad = dot(ds, ws[:, :, cols].reshape(width, tile)) + dot(rank_in, ash_ref[:, cols])
            gate = gate_st[slot, :, cols].astype(F32)
            up = up_st[slot, :, cols].astype(F32)
            sig = 1.0 / (1.0 + jnp.exp(-gate))
            silu = gate * sig
            act = (silu * up).astype(BF)
            gate_grad = (act_grad * up * (sig + silu * (1.0 - sig))).astype(BF)
            up_grad = (act_grad * silu).astype(BF)
            now = dot_t(gate_grad, wg[:, :, cols].reshape(width, tile)) + dot_t(up_grad, wu[:, :, cols].reshape(width, tile))

            @pl.when(f == 0)
            def _():
                acc[...] = now

            @pl.when(f > 0)
            def _():
                acc[...] += now

            gexp_ref[0, :, cols] += t_dot(er, gate_grad)
            gexp_ref[1, :, cols] += t_dot(er, up_grad)
            gsh_ref[:, cols] += t_dot(rank_in, act)
            rank_out = rank_out + dot_t(gate_grad, expand_ref[0, :, cols])
            rank_out = rank_out + dot_t(up_grad, expand_ref[1, :, cols])
            return rank_out, srank + dot_t(act, ash_ref[:, cols])

        rank_out, srank = lax.fori_loop(
            0,
            tiles,
            one,
            (
                jnp.zeros((every, expand_ref.shape[1]), F32),
                jnp.zeros((every, ash_ref.shape[0]), F32),
            ),
        )
        rank_out = rank_out.astype(BF)
        total = acc[...] + dot_t(rank_out, high_ref[...])
        partial_ref[c] = total.astype(BF).reshape(line, rows, width)
        ghigh_ref[...] += t_dot(rank_out, n2)
        gres_ref[...] += t_dot(srank.astype(BF), ds)

    line_exchange(
        line, chunks, gathered, partial_ref, from_left, from_right, out_ref,
        (s0, s1, s2, s3, s4, s5, s6), begin, work,
    )


def mlp_backward(ds, w, ad, saved):
    n2_all, gate, up = saved
    line = lax.axis_size("tensor")
    rows, width = ds.shape
    groups, _, _, hidden = w["mlp"].shape
    part = rows // CHUNKS
    every = line * part
    out, g_high, g_expand, g_shrink, g_res = pl.pallas_call(
        partial(mlp_back_kernel, line, CHUNKS, ff_tile(hidden)),
        in_specs=[vspec()] + [hspec()] * 4 + [vspec()] * 4,
        out_specs=[vspec()] * 5,
        out_shape=[
            jax.ShapeDtypeStruct((CHUNKS, part, width), F32),
            jax.ShapeDtypeStruct((2 * RANK, width), F32),
            jax.ShapeDtypeStruct((2, 2 * RANK, hidden), F32),
            jax.ShapeDtypeStruct((RANK, hidden), F32),
            jax.ShapeDtypeStruct((RANK, width), F32),
        ],
        scratch_shapes=exchange_scratch(line, CHUNKS, part, width)
        + [pltpu.VMEM((groups, width // groups, hidden), BF)] * 3
        + [pltpu.VMEM((2, every, hidden), BF)] * 2
        + [
            pltpu.VMEM((2, every, width), BF),
            pltpu.VMEM((every, width), F32),
            pltpu.SemaphoreType.DMA((3,)),
            pltpu.SemaphoreType.DMA((3, 2)),
        ],
        compiler_params=pltpu.CompilerParams(
            collective_id=1, has_side_effects=True, vmem_limit_bytes=VMEM_LIMIT
        ),
        cost_estimate=pl.CostEstimate(
            flops=6 * line * rows * width * hidden,
            bytes_accessed=6 * width * hidden + 4 * line * rows * hidden,
            transcendentals=line * rows * hidden,
        ),
    )(
        ds.reshape(CHUNKS, part, width), w["mlp"], n2_all, gate, up,
        ad["high"], ad["expand"], ad["shrink"], ad["res_two"],
    )
    g_expand = jnp.concatenate([g_expand[0, :RANK], g_expand[1, RANK:]], axis=0)
    return out.reshape(rows, width), g_high, g_expand, g_shrink, g_res


def gather_kernel(
    line, peers,
    attn, extra,
    first_out, second_out, extra_out,
    own_sem, z_recv, z_right, z_left, dp_recv, dp_send, core_recv, core_send,
):
    me, spot, core = lax.axis_index("tensor"), lax.axis_index("dp"), lax.axis_index("section")
    other = 1 - core
    has_left, has_right = me > 0, me < line - 1
    barrier = pltpu.get_barrier_semaphore()

    def greet(**where):
        pl.semaphore_signal(barrier, inc=1, device_id=where, device_id_type=MESH)

    @pl.when(has_left)
    def _():
        greet(tensor=me - 1)

    @pl.when(has_right)
    def _():
        greet(tensor=me + 1)

    greet(section=other)
    for k in range(1, peers):
        greet(dp=lax.rem(spot + k, peers))
    pl.semaphore_wait(barrier, jnp.where(has_left, 1, 0) + jnp.where(has_right, 1, 0) + peers)

    mine = spot * 2 + core

    def places(o):
        return first_out.at[mine, o], second_out.at[o], extra_out.at[o]

    sources = (attn.at[0], attn.at[1], extra)
    keeps = [
        pltpu.make_async_copy(src, dst, own_sem.at[i]) for i, (src, dst) in enumerate(zip(sources, places(me)))
    ]

    def remote(src, dst, send, recv, **where):
        return pltpu.make_async_remote_copy(
            src_ref=src, dst_ref=dst, send_sem=send, recv_sem=recv, device_id=where, device_id_type=MESH
        )

    def along(i, o, side, own):
        dst = places(o)[i]
        return remote(
            sources[i] if own else dst,
            dst,
            (z_right if side > 0 else z_left).at[i, o],
            z_recv.at[i, o],
            tensor=me + side,
        )

    def to_peer(k, o, own):
        dst = first_out.at[mine, o]
        return remote(
            attn.at[0] if own else dst, dst, dp_send.at[k, o], dp_recv.at[spot, o], dp=lax.rem(spot + k, peers)
        )

    def to_core(p, o, own):
        dst = first_out.at[p * 2 + core, o]
        return remote(attn.at[0] if own else dst, dst, core_send.at[p, o], core_recv.at[p, o], section=other)

    def spread_first(o, own):
        for k in range(1, peers):
            to_peer(k, o, own).start()
        to_core(spot, o, own).start()

    for i in range(3):

        @pl.when(has_right)
        def _():
            along(i, me, 1, True).start()

        @pl.when(has_left)
        def _():
            along(i, me, -1, True).start()

        if i == 0:
            spread_first(me, True)
    for keep in keeps:
        keep.start()
    for d in range(1, line):
        for i in range(3):

            @pl.when(me >= d)
            def _():
                along(i, me - d, 1, False).wait_recv()

                @pl.when(has_right)
                def _():
                    along(i, me - d, 1, False).start()

                if i == 0:
                    spread_first(me - d, False)

            @pl.when(me + d < line)
            def _():
                along(i, me + d, -1, False).wait_recv()

                @pl.when(has_left)
                def _():
                    along(i, me + d, -1, False).start()

                if i == 0:
                    spread_first(me + d, False)

    def pass_on(o, carry):
        for k in range(1, peers):
            p = lax.rem(spot + peers - k, peers)
            remote(
                first_out.at[p * 2 + core, o], first_out.at[p * 2 + core, o], dp_send.at[k, o], dp_recv.at[p, o], dp=p
            ).wait_recv()
            to_core(p, o, False).start()
        return carry

    lax.fori_loop(0, line, pass_on, 0)

    def finish(o, carry):
        for k in range(1, peers):
            to_peer(k, o, False).wait_send()
        for p in range(peers):
            to_core(p, o, False).wait_send()
            remote(
                first_out.at[p * 2 + other, o],
                first_out.at[p * 2 + other, o],
                core_send.at[p, o],
                core_recv.at[p, o],
                section=other,
            ).wait_recv()
        for i in range(3):

            @pl.when(jnp.logical_and(has_right, me >= o))
            def _():
                along(i, o, 1, False).wait_send()

            @pl.when(jnp.logical_and(has_left, me <= o))
            def _():
                along(i, o, -1, False).wait_send()

        return carry

    lax.fori_loop(0, line, finish, 0)
    for keep in keeps:
        keep.wait()


def gather_first(attn, extra):
    line, peers = lax.axis_size("tensor"), lax.axis_size("dp")
    cores, part, cols = attn.shape
    dma = pltpu.SemaphoreType.DMA
    return pl.pallas_call(
        partial(gather_kernel, line, peers),
        in_specs=[hspec()] * 2,
        out_specs=[hspec()] * 3,
        out_shape=[
            jax.ShapeDtypeStruct((peers * cores, line, part, cols), BF),
            jax.ShapeDtypeStruct((line, part, cols), BF),
            jax.ShapeDtypeStruct((line,) + extra.shape, BF),
        ],
        scratch_shapes=[dma((3,)), dma((3, line)), dma((3, line)), dma((3, line))]
        + [dma((peers, line))] * 4,
        compiler_params=pltpu.CompilerParams(
            collective_id=4, has_side_effects=True, vmem_limit_bytes=VMEM_LIMIT
        ),
    )(attn, extra)


def rotated(x, cos, sin):
    return x * cos + pltpu.roll(x, HEAD_DIM // 2, 1) * sin


def head_cols(h):
    return pl.ds(pl.multiple_of(h * HEAD_DIM, HEAD_DIM), HEAD_DIM)


def weight_loads(packed, wq, wo, wkv, wsem):
    cols, kv_cols = wq.shape[-1], wkv.shape[-1]
    loads = []
    for i, (ref, start, size) in enumerate(((wkv, 2 * cols, kv_cols), (wq, 0, cols), (wo, cols, cols))):
        loads.append(
            [
                pltpu.make_async_copy(packed.at[:, t, :, pl.ds(start, size)], ref.at[t], wsem.at[i, t])
                for t in range(ref.shape[0])
            ]
        )
    return loads


def flat(ref, t):
    groups, rows, cols = ref.shape[1:]
    return ref[t].reshape(groups * rows, cols)


def allowed_keys(info_ref, block, keys, rows):
    row = info_ref[0] + lax.broadcasted_iota(jnp.int32, (1, rows), 1)
    last = jnp.minimum(row, info_ref[1] - 1)
    return block * keys + lax.broadcasted_iota(jnp.int32, (keys, rows), 0) <= last


def one_way_barrier(me, line, side):
    barrier = pltpu.get_barrier_semaphore()
    first, last = (0, line - 1) if side > 0 else (line - 1, 0)

    @pl.when(me != first)
    def _():
        pl.semaphore_signal(barrier, inc=1, device_id={"tensor": me - side}, device_id_type=MESH)

    @pl.when(me != last)
    def _():
        pl.semaphore_wait(barrier, 1)


def kv_exchange(me, line, kvbuf, recv, send):
    def move(o):
        return pltpu.make_async_remote_copy(
            src_ref=kvbuf.at[o],
            dst_ref=kvbuf.at[o],
            send_sem=send.at[o],
            recv_sem=recv.at[o],
            device_id={"tensor": me + 1},
            device_id_type=MESH,
        )

    return move


def attend_kernel(
    line, group,
    info_ref, x_ref, gain_ref, qb_ref, kvb_ref, low_ref, bq_ref, bkv_ref, att_ref, res_ref, cos_ref, sin_ref, packed,
    mid_ref, n2_ref, normed_ref, rank_ref, q_ref, kv_out, attended_ref, log_ref,
    wq, wo, wkv, kvbuf, acc, peak, total, wsem, recv, send, ksem,
):
    rows, width = x_ref.shape
    heads = width // HEAD_DIM
    cols = wq.shape[-1]
    kv_cols = wkv.shape[-1]
    scale = HEAD_DIM**-0.5
    me = lax.axis_index("tensor")
    one_way_barrier(me, line, 1)
    kv_loads, q_loads, o_loads = weight_loads(packed, wq, wo, wkv, wsem)
    for load in kv_loads + q_loads + o_loads:
        load.start()
    move = kv_exchange(me, line, kvbuf, recv, send)
    x = x_ref[...]
    inverse = lax.rsqrt(jnp.mean(x * x, axis=-1, keepdims=True) + EPSILON)
    normed_ref[...] = (x * inverse * gain_ref[0:1, :]).astype(BF)
    low = dot(normed_ref[...], low_ref[...]).astype(BF)
    cos, sin = cos_ref[...], sin_ref[...]
    for load in kv_loads:
        load.wait()
    for t in range(line):
        span = slice(t * kv_cols, (t + 1) * kv_cols)
        kv = dot(normed_ref[...], flat(wkv, t)) + kvb_ref[:, span] + dot(low, bkv_ref[:, span])
        for h in range(kv_cols // HEAD_DIM):
            at = t * kv_cols + h * HEAD_DIM
            one = kv[:, h * HEAD_DIM : (h + 1) * HEAD_DIM]
            if at < KV_HEADS * HEAD_DIM:
                one = rotated(one, cos, sin)
            kvbuf[me, :, at : at + HEAD_DIM] = one.astype(BF)

    @pl.when(me < line - 1)
    def _():
        move(me).start()

    for load in q_loads:
        load.wait()
    for t in range(line):
        span = slice(t * cols, (t + 1) * cols)
        q = dot(normed_ref[...], flat(wq, t)) + qb_ref[:, span] + dot(low, bq_ref[:, span])
        for h in range(cols // HEAD_DIM):
            at = t * cols + h * HEAD_DIM
            q_ref[:, at : at + HEAD_DIM] = rotated(
                q[:, h * HEAD_DIM : (h + 1) * HEAD_DIM], cos, sin
            ).astype(BF)
    acc[...] = jnp.zeros_like(acc)
    total[...] = jnp.zeros_like(total)
    peak[...] = jnp.full_like(peak, MASKED_SCORE)

    def block(o):
        allowed = allowed_keys(info_ref, o, rows, rows)

        def one(h, carry):
            kv_head = h // group
            k = kvbuf[o, :, head_cols(kv_head)]
            v = kvbuf[o, :, head_cols(KV_HEADS + kv_head)]
            scores = jnp.where(allowed, dot_t(k, q_ref[:, head_cols(h)]) * scale, MASKED_SCORE)
            top = jnp.maximum(peak[h], jnp.max(scores, axis=0, keepdims=True))
            soft = jnp.exp(scores - top)
            shift = jnp.exp(peak[h] - top)
            total[h] = total[h] * shift + jnp.sum(soft, axis=0, keepdims=True)
            acc[h] = acc[h] * shift + t_dot(v, soft.astype(BF))
            peak[h] = top
            return carry

        lax.fori_loop(0, heads, one, 0)

    for d in range(line):

        @pl.when(me >= d)
        def _():
            if d > 0:
                move(me - d).wait_recv()

                @pl.when(me < line - 1)
                def _():
                    move(me - d).start()

            block(me - d)

    keep = pltpu.make_async_copy(kvbuf, kv_out, ksem)
    keep.start()
    for h in range(heads):
        attended_ref[:, h * HEAD_DIM : (h + 1) * HEAD_DIM] = (acc[h] * (1.0 / total[h])).T.astype(BF)
        log_ref[h] = peak[h] + jnp.log(total[h])
    rank = dot_t(attended_ref[...], att_ref[...]).astype(BF)
    rank_ref[0] = low
    rank_ref[1] = rank
    middle = x_ref[...] + dot(rank, res_ref[...])
    for load in o_loads:
        load.wait()
    for t in range(line):
        middle = middle + dot_t(attended_ref[:, t * cols : (t + 1) * cols], flat(wo, t))
    mid_ref[...] = middle
    inverse = lax.rsqrt(jnp.mean(middle * middle, axis=-1, keepdims=True) + EPSILON)
    n2_ref[...] = (middle * inverse * gain_ref[1:2, :]).astype(BF)
    keep.wait()
    for o in range(line):

        @pl.when(jnp.logical_and(me < line - 1, me >= o))
        def _():
            move(o).wait_send()


def attend_forward(x, w, ad, info, tables):
    line = lax.axis_size("tensor")
    rows, width = x.shape
    heads = width // HEAD_DIM
    kv_width = 2 * KV_HEADS * HEAD_DIM
    groups, low_rows = w["packed"].shape[0], w["packed"].shape[2]
    outs = pl.pallas_call(
        partial(attend_kernel, line, heads // KV_HEADS),
        in_specs=[pl.BlockSpec(memory_space=pltpu.SMEM)] + [vspec()] * 11 + [hspec()],
        out_specs=[vspec()] * 5 + [hspec()] + [vspec()] * 2,
        out_shape=[
            jax.ShapeDtypeStruct((rows, width), F32),
            jax.ShapeDtypeStruct((rows, width), BF),
            jax.ShapeDtypeStruct((rows, width), BF),
            jax.ShapeDtypeStruct((2, rows, 3 * RANK), BF),
            jax.ShapeDtypeStruct((rows, width), BF),
            jax.ShapeDtypeStruct((line, rows, kv_width), BF),
            jax.ShapeDtypeStruct((rows, width), BF),
            jax.ShapeDtypeStruct((heads, 1, rows), F32),
        ],
        scratch_shapes=[
            pltpu.VMEM((line, groups, low_rows, width // line), BF),
            pltpu.VMEM((line, groups, low_rows, width // line), BF),
            pltpu.VMEM((line, groups, low_rows, kv_width // line), BF),
            pltpu.VMEM((line, rows, kv_width), BF),
            pltpu.VMEM((heads, HEAD_DIM, rows), F32),
            pltpu.VMEM((heads, 1, rows), F32),
            pltpu.VMEM((heads, 1, rows), F32),
            pltpu.SemaphoreType.DMA((3, line)),
            pltpu.SemaphoreType.DMA((line,)),
            pltpu.SemaphoreType.DMA((line,)),
            pltpu.SemaphoreType.DMA,
        ],
        compiler_params=pltpu.CompilerParams(
            collective_id=2, has_side_effects=True, vmem_limit_bytes=VMEM_LIMIT
        ),
        cost_estimate=pl.CostEstimate(
            flops=4 * rows * width * width * 2, bytes_accessed=5 * width * width, transcendentals=0
        ),
    )(
        info, x, w["gain"], ad["q_bias"], w["kv_bias"], ad["low"], ad["q"], ad["kv"], ad["attend"],
        ad["res_one"], tables[0], tables[1], w["packed"],
    )
    return outs[0], outs[1], outs[2:]


def attend_back_kernel(
    line, group,
    info_ref, x_ref, mid_ref, dy_ref, dn2_ref, gain_ref, low_ref, bq_ref, bkv_ref, att_ref, res_ref, cos_ref, sin_ref,
    normed_ref, rank_ref, q_ref, kv_ref, attended_ref, log_ref, packed,
    dx_ref, glow_ref, gres_ref, gq_ref, gatt_ref, gkv_ref,
    wq, wo, wkv, do_ref, dq_acc, dq_ref, dkv_acc, partial_ref, from_right, delta, wsem, recv, send,
):
    rows, width = x_ref.shape
    heads = width // HEAD_DIM
    cols = wq.shape[-1]
    kv_cols = wkv.shape[-1]
    kv_half = KV_HEADS * HEAD_DIM
    scale = HEAD_DIM**-0.5
    me = lax.axis_index("tensor")
    one_way_barrier(me, line, -1)
    kv_loads, q_loads, o_loads = weight_loads(packed, wq, wo, wkv, wsem)
    for load in o_loads + q_loads + kv_loads:
        load.start()

    def move(o):
        return pltpu.make_async_remote_copy(
            src_ref=partial_ref.at[o],
            dst_ref=from_right.at[o],
            send_sem=send.at[o],
            recv_sem=recv.at[o],
            device_id={"tensor": me - 1},
            device_id_type=MESH,
        )

    def through_norm(values, gain, grad_out):
        inverse = lax.rsqrt(jnp.mean(values * values, axis=-1, keepdims=True) + EPSILON)
        weighted = gain * grad_out
        return inverse * weighted - inverse * inverse * inverse * values * jnp.mean(
            weighted * values, axis=-1, keepdims=True
        )

    middle_grad = dy_ref[...] + through_norm(mid_ref[...], gain_ref[1:2, :], dn2_ref[...])
    dx_ref[...] = middle_grad
    branch_grad = middle_grad.astype(BF)
    low, rank = rank_ref[0], rank_ref[1]
    rank_grad = dot_t(branch_grad, res_ref[...]).astype(BF)
    gres_ref[...] = t_dot(rank, branch_grad)
    gatt_ref[...] = t_dot(rank_grad, attended_ref[...])
    for load in o_loads:
        load.wait()
    for t in range(line):
        span = slice(t * cols, (t + 1) * cols)
        do_ref[:, span] = (dot(branch_grad, flat(wo, t)) + dot(rank_grad, att_ref[:, span])).astype(BF)
    for h in range(heads):
        span = slice(h * HEAD_DIM, (h + 1) * HEAD_DIM)
        both = do_ref[:, span].astype(F32) * attended_ref[:, span].astype(F32)
        delta[h] = jnp.sum(both.T, axis=0, keepdims=True)
    dq_acc[...] = jnp.zeros_like(dq_acc)

    def block(o):
        allowed = allowed_keys(info_ref, o, rows, rows)
        dkv_acc[...] = jnp.zeros_like(dkv_acc)

        def one(h, carry):
            kv_head = h // group
            k = kv_ref[o, :, head_cols(kv_head)]
            v = kv_ref[o, :, head_cols(KV_HEADS + kv_head)]
            q = q_ref[:, head_cols(h)]
            do = do_ref[:, head_cols(h)]
            scores = dot_t(k, q) * scale - log_ref[h]
            soft = jnp.exp(jnp.where(allowed, scores, MASKED_SCORE))
            grad = (soft * (dot_t(v, do) - delta[h])).astype(BF)
            dq_acc[h] += t_dot(k, grad)
            dkv_acc[:, head_cols(kv_head)] += dot(grad, q) * scale
            dkv_acc[:, head_cols(KV_HEADS + kv_head)] += dot(soft.astype(BF), do)
            return carry

        lax.fori_loop(0, heads, one, 0)
        partial_ref[o] = dkv_acc[...].astype(BF)

    for s in range(2 * line - 1):
        if s < line:

            @pl.when(me >= s)
            def _():
                block(s)

        for h in range(line - 1):
            o = s - h
            if 0 <= o < line - 1 - h:

                @pl.when(me == line - 1 - h)
                def _():
                    if h > 0:
                        move(o).wait_recv()
                        partial_ref[o] = (partial_ref[o].astype(F32) + from_right[o].astype(F32)).astype(BF)
                    move(o).start()

    cos, sin = cos_ref[...], -sin_ref[...]
    for h in range(heads):
        dq_ref[:, h * HEAD_DIM : (h + 1) * HEAD_DIM] = rotated(dq_acc[h].T * scale, cos, sin).astype(BF)
    dq = dq_ref[...]
    gq_ref[...] = t_dot(low, dq)
    low_grad = dot_t(dq, bq_ref[...])
    for load in q_loads:
        load.wait()
    normed_grad = dot_t(dq[:, :cols], flat(wq, 0))
    for t in range(1, line):
        normed_grad = normed_grad + dot_t(dq[:, t * cols : (t + 1) * cols], flat(wq, t))
    dkv_acc[...] = partial_ref[me].astype(F32)

    @pl.when(me < line - 1)
    def _():
        move(me).wait_recv()
        dkv_acc[...] += from_right[me].astype(F32)

    for h in range(KV_HEADS):
        span = slice(h * HEAD_DIM, (h + 1) * HEAD_DIM)
        dkv_acc[:, span] = rotated(dkv_acc[:, span], cos, sin)
    dkv = dkv_acc[...].astype(BF)
    gkv_ref[...] = t_dot(low, dkv)
    low_grad = (low_grad + dot_t(dkv, bkv_ref[...])).astype(BF)
    glow_ref[...] = t_dot(low_grad, normed_ref[...])
    for load in kv_loads:
        load.wait()
    for t in range(line):
        normed_grad = normed_grad + dot_t(dkv[:, t * kv_cols : (t + 1) * kv_cols], flat(wkv, t))
    normed_grad = normed_grad + dot_t(low_grad, low_ref[...])
    dx_ref[...] += through_norm(x_ref[...], gain_ref[0:1, :], normed_grad)
    for o in range(line - 1):

        @pl.when(me > o)
        def _():
            move(o).wait_send()


def attend_backward(x, middle, dy, dn2, w, ad, kept, info, tables):
    line = lax.axis_size("tensor")
    rows, width = x.shape
    heads = width // HEAD_DIM
    kv_width = 2 * KV_HEADS * HEAD_DIM
    groups, low_rows = w["packed"].shape[0], w["packed"].shape[2]
    return pl.pallas_call(
        partial(attend_back_kernel, line, heads // KV_HEADS),
        in_specs=[pl.BlockSpec(memory_space=pltpu.SMEM)] + [vspec()] * 18 + [hspec()],
        out_specs=[vspec()] * 6,
        out_shape=[
            jax.ShapeDtypeStruct((rows, width), F32),
            jax.ShapeDtypeStruct((3 * RANK, width), F32),
            jax.ShapeDtypeStruct((3 * RANK, width), F32),
            jax.ShapeDtypeStruct((3 * RANK, width), F32),
            jax.ShapeDtypeStruct((3 * RANK, width), F32),
            jax.ShapeDtypeStruct((3 * RANK, kv_width), F32),
        ],
        scratch_shapes=[
            pltpu.VMEM((line, groups, low_rows, width // line), BF),
            pltpu.VMEM((line, groups, low_rows, width // line), BF),
            pltpu.VMEM((line, groups, low_rows, kv_width // line), BF),
            pltpu.VMEM((rows, width), BF),
            pltpu.VMEM((heads, HEAD_DIM, rows), F32),
            pltpu.VMEM((rows, width), BF),
            pltpu.VMEM((rows, kv_width), F32),
            pltpu.VMEM((line, rows, kv_width), BF),
            pltpu.VMEM((line, rows, kv_width), BF),
            pltpu.VMEM((heads, 1, rows), F32),
            pltpu.SemaphoreType.DMA((3, line)),
            pltpu.SemaphoreType.DMA((line,)),
            pltpu.SemaphoreType.DMA((line,)),
        ],
        compiler_params=pltpu.CompilerParams(
            collective_id=3, has_side_effects=True, vmem_limit_bytes=VMEM_LIMIT
        ),
        cost_estimate=pl.CostEstimate(
            flops=4 * rows * width * width * 2, bytes_accessed=5 * width * width, transcendentals=0
        ),
    )(
        info, x, middle, dy, dn2, w["gain"], ad["low"], ad["q"], ad["kv"], ad["attend"], ad["res_one"],
        tables[0], tables[1], *kept, w["packed"],
    )


def swap(pair):
    return lax.all_to_all(pair, "section", split_axis=0, concat_axis=0, tiled=True)


def at_rows(a, first, rows):
    return jnp.pad(a, [(first, rows - first - a.shape[0]), (0, 0)])


def local(
    inputs,
    lengths,
    adapter_ids,
    cotangent,
    norm_gain,
    query_weight,
    query_bias,
    keyvalue_weight,
    keyvalue_bias,
    output_weight,
    expand_weight,
    shrink_weight,
    adapter_input,
    adapter_query,
    adapter_keyvalue,
    adapter_expand,
    adapter_attend,
    adapter_shrink,
    adapter_residual,
):
    layers = lax.axis_size("section")
    tensor = lax.axis_size("tensor")
    core = lax.axis_index("section")
    place = lax.axis_index("tensor")
    rows, width = inputs.shape[1:]
    tokens = layers * rows * tensor * lax.axis_size("dp")
    kv_half = KV_HEADS * HEAD_DIM
    hidden = expand_weight.shape[3]
    padding = -hidden % (2 * LANES)
    r = RANK

    def padded(m):
        return jnp.pad(m, [(0, 0)] * (m.ndim - 1) + [(0, padding)])

    kv = jnp.concatenate([keyvalue_weight[0, 0], keyvalue_weight[0, 1]], axis=1)
    kv_cols = kv.shape[1] // tensor
    kv = lax.dynamic_slice_in_dim(kv, place * kv_cols, kv_cols, 1)
    attn = jnp.concatenate([query_weight[0], output_weight[0].T, kv], axis=1)
    q_cols = query_weight.shape[2]
    part = attn.shape[0] // layers
    attn = swap(attn.reshape(layers, part, attn.shape[1]))
    mlp = padded(jnp.concatenate([expand_weight[0], shrink_weight[0].T[None]], axis=0))
    mlp = swap(jnp.swapaxes(mlp.reshape(3, layers, part, mlp.shape[2]), 0, 1))
    every = ("dp", "section")
    small = jnp.concatenate([norm_gain[0, 0], norm_gain[0, 1], keyvalue_bias[0].reshape(-1)], axis=0)
    small = swap(jnp.broadcast_to(small[None], (layers,) + small.shape)).astype(F32)

    def pick(stack):
        chosen = jnp.stack(
            [lax.dynamic_index_in_dim(stack[0], adapter_ids[i], 0, keepdims=False) for i in range(layers)]
        )
        return swap(chosen)

    heads_part = jnp.concatenate(
        [adapter_query[0], jnp.swapaxes(adapter_attend[0], 1, 2)]
        + [jnp.pad(query_bias[0][None, None], [(0, adapter_query.shape[1] - 1), (0, r - 1), (0, 0)], mode="edge")],
        axis=1,
    )
    heads_part = pick(heads_part[None])
    first_attn, line_attn, heads_part = gather_first(attn, heads_part.reshape(-1, q_cols))
    heads_part = jnp.moveaxis(heads_part.reshape(tensor, layers, 3 * r, q_cols), 0, 2)
    heads_part = heads_part.reshape(layers, 3 * r, width)

    def weights(layer):
        packed = first_attn if layer == 0 else lax.all_gather(line_attn, every, axis=0)
        return dict(
            gain=small[layer, : 2 * width].reshape(2, width),
            packed=packed,
            mlp=lax.all_gather(mlp[layer], every, axis=0),
            kv_bias=small[layer, 2 * width :][None],
        )

    low_high, keyvalue, expand, shrink, residual = (
        pick(stack) for stack in (adapter_input, adapter_keyvalue, adapter_expand, adapter_shrink, adapter_residual)
    )
    def adapters(layer):
        return dict(
            low=low_high[layer, :, : 3 * r],
            high=low_high[layer, :, 3 * r :],
            q=at_rows(heads_part[layer, :r], 0, 3 * r),
            attend=at_rows(heads_part[layer, r : 2 * r], 0, 3 * r),
            q_bias=heads_part[layer, 2 * r : 2 * r + 1].astype(F32),
            kv=jnp.concatenate(
                [at_rows(keyvalue[layer, 0], r, 3 * r), at_rows(keyvalue[layer, 1], 2 * r, 3 * r)], axis=1
            ),
            expand=jnp.stack([at_rows(padded(expand[layer, i]), i * r, 2 * r) for i in range(2)]),
            shrink=padded(shrink[layer].T),
            res_one=at_rows(residual[layer, 0], 0, 3 * r),
            res_two=residual[layer, 1],
        )

    x = lax.dynamic_index_in_dim(inputs, core, 0, keepdims=False).astype(F32)
    cot = lax.dynamic_index_in_dim(cotangent, core, 0, keepdims=False).astype(F32)
    length = lax.dynamic_index_in_dim(lengths, core, 0, keepdims=False)
    own_id = lax.dynamic_index_in_dim(adapter_ids, core, 0, keepdims=False)
    first_slot = place * rows
    info = jnp.stack([first_slot, length]).astype(jnp.int32)
    tables = rotary_tables(first_slot, rows)
    slot_ids = first_slot + jnp.arange(rows, dtype=jnp.int32)

    w = [weights(layer) for layer in range(layers)]
    ad = [adapters(layer) for layer in range(layers)]
    outs, kept = [], []
    for layer in range(layers):
        middle, normed_two, attn_kept = attend_forward(x, w[layer], ad[layer], info, tables)
        shrunk, mlp_kept = mlp_forward(normed_two, w[layer], ad[layer])
        outs.append((middle + shrunk).astype(BF))
        kept.append((x, middle, attn_kept, mlp_kept))
        x = outs[-1].astype(F32)
    count = adapter_input.shape[1]
    pad_one = jnp.zeros((r, width - 2 * kv_half), F32)
    chosen_row = at_rows(
        jnp.pad((jnp.arange(count, dtype=jnp.int32) == own_id).astype(BF)[None], [(0, 0), (0, width - count)]), 0, 8
    )
    grad = cot * (slot_ids < length).astype(F32)[:, None]
    grads, gathered = [None] * layers, [None] * layers
    for layer in reversed(range(layers)):
        x, middle, attn_kept, mlp_kept = kept[layer]
        if layer < layers - 1:
            grad, whole_here = lax.optimization_barrier((grad, whole_here))
        dn2, g_high, g_expand, g_shrink, g_res_two = mlp_backward(grad.astype(BF), w[layer], ad[layer], mlp_kept)
        grad, g_low, g_res_one, g_q, g_attend, g_kv = attend_backward(
            x, middle, grad, dn2, w[layer], ad[layer], attn_kept, info, tables
        )
        grads[layer] = grad
        g_kv = jnp.concatenate([g_kv[r : 2 * r, :kv_half], g_kv[2 * r :, kv_half:], pad_one], axis=1)
        whole_here = jnp.concatenate(
            [g_low, g_high, g_res_one[:r], g_res_two, g_kv, g_q[:r], g_attend[:r]], axis=0
        ).astype(BF)
        if layer < layers - 1:
            whole_here, gathered[layer + 1] = lax.optimization_barrier((whole_here, gathered[layer + 1]))
        whole = lax.psum(whole_here, "tensor")
        mine = lax.dynamic_slice_in_dim(whole[8 * r :], place * q_cols, q_cols, 1)
        parts = jnp.concatenate([g_expand, g_shrink], axis=0).astype(BF)
        block = jnp.concatenate(
            [whole[: 8 * r], mine.reshape(-1, width), parts.reshape(-1, width), chosen_row], axis=0
        )
        gathered[layer] = lax.all_gather(block, ("section", "dp"), axis=0)
    layer_output = swap(jnp.stack(outs))
    input_grad = swap(jnp.stack(grads))

    block = jnp.where(core == 0, gathered[0], gathered[1])
    pick_matrix = block[:, -8, :count]
    total = jnp.einsum("sa,srw->arw", pick_matrix, block[:, :-8], preferred_element_type=F32)
    total = total * (1.0 / math.sqrt(tokens))
    q_rows = 2 * r * q_cols // width
    heads_sum = total[:, 8 * r : 8 * r + q_rows].reshape(count, 2 * r, q_cols)
    ff_sum = total[:, 8 * r + q_rows :].reshape(count, 3 * r, hidden + padding)[..., :hidden]
    kv_sum = total[:, 7 * r : 8 * r]
    return (
        layer_output[None],
        input_grad[None],
        jnp.swapaxes(total[:, : 5 * r], 1, 2)[None],
        heads_sum[:, :r][None],
        jnp.stack([kv_sum[..., :kv_half], kv_sum[..., kv_half : 2 * kv_half]], axis=1)[None],
        jnp.stack([ff_sum[:, :r], ff_sum[:, r : 2 * r]], axis=1)[None],
        jnp.swapaxes(heads_sum[:, r:], 1, 2)[None],
        jnp.swapaxes(ff_sum[:, 2 * r :], 1, 2)[None],
        jnp.stack([total[:, 5 * r : 6 * r], total[:, 6 * r : 7 * r]], axis=1)[None],
    )


def solution(mesh):
    placed = (
        P("dp", "tensor", None),
        P("dp"),
        P("dp"),
        P("dp", "tensor", None),
        P("section", None, None),
        P("section", "dp", "tensor"),
        P("section", "tensor"),
        P("section", None, "dp", None),
        P("section", None, None),
        P("section", "tensor", "dp"),
        P("section", None, "dp", "tensor"),
        P("section", "tensor", "dp"),
        P("section", None, None, None),
        P("section", None, None, "tensor"),
        P("section", None, None, None, None),
        P("section", None, None, None, "tensor"),
        P("section", None, "tensor", None),
        P("section", None, "tensor", None),
        P("section", None, None, None, None),
    )
    return jax.shard_map(
        local,
        mesh=mesh,
        in_specs=placed,
        out_specs=(
            P("section", "dp", "tensor", None),
            P("section", "dp", "tensor", None),
            P("section", None, None, None),
            P("section", None, None, "tensor"),
            P("section", None, None, None, None),
            P("section", None, None, None, "tensor"),
            P("section", None, "tensor", None),
            P("section", None, "tensor", None),
            P("section", None, None, None, None),
        ),
        check_vma=False,
    )
```

time: 1280 us -> 955 us (0.75)
  waiting for transfers between devices: 408 us -> 115 us
  Pallas kernels: 475 us -> 645 us
  blocking collectives: 112 us -> 26.3 us
  matrix products: 58.5 us -> 1.53 us
  local copies, waits for them, and re-layouts: 125 us -> 72.2 us
    all_gather x12 -> x5, waiting for transfers between devices: 333 us -> 36 us  [the longest x2 26.5 us: local(): gathered[layer] = lax.all_gather(block, ('section', 'dp'), axis=0)]
    pallas_call x4 -> x5, Pallas kernels: 61.1 us -> 211 us  [the longest x1 91.6 us: gather_first(): pl.pallas_call(partial(gather_kernel, line, peers), in_specs=[hspec()] *...]
    all_gather x5 -> x0, blocking collectives: 62.4 us -> none  [the longest x1 22.1 us: local(): lax.all_gather(query_bias[0], ('section', 'tensor'), axis=0, tiled=True)]
    dot_general x51 -> x1, matrix products: 58.5 us -> 1.53 us  [local(): jnp.einsum('sa,srw->arw', pick_matrix, block[:, :-8], preferred_element_t...]
    psum x1 -> x2, waiting for transfers between devices: 33.4 us -> 77.6 us  [local(): whole = lax.psum(whole_here, 'tensor')]
    slice x32 -> x17, local copies, waits for them, and re-layouts: 51.7 us -> 11.4 us  [the longest x3 3.92 us: local(): total[:, 8 * r + q_rows:].reshape(count, 3 * r, hidden + padding)]
    reduce_scatter x2 -> x0, waiting for transfers between devices: 38.2 us -> none  [fold(): lax.psum_scatter(partial_rows.astype(BF), 'tensor', scatter_dimension=0,...]
    pallas_call x2, Pallas kernels: 210 us -> 236 us  [mlp_forward(): pl.pallas_call(partial(mlp_kernel, line, CHUNKS, ff_tile(hidden)), in_spe...]
  transfers between devices with their start and end apart: 22 -> 14, of which waited for: 13 -> 5; matrix products, arithmetic and copies ran while one was open for 12% -> 5% of each run, Pallas kernels for 2% -> 42%
where the time goes in v3:
time: 955 us; the launch traced here: 945 us
  Pallas kernels  645 us (68%)
  waiting for transfers between devices  115 us (12%)
  local copies, waits for them, and re-layouts  72.2 us (8%)
  other arithmetic  41.6 us (4%)
  blocking collectives  26.3 us (3%)
  starting transfers between devices  23.9 us (3%)
  between operations  19.4 us (2%)
    pallas_call x2, Pallas kernels, mlp_forward(): pl.pallas_call(partial(mlp_kernel, line, CHUNKS, ff_tile(hidden)), in_spe...  236 us
    pallas_call x2, Pallas kernels, mlp_backward(): pl.pallas_call(partial(mlp_back_kernel, line, CHUNKS, ff_tile(hidden)), i...  198 us
    pallas_call x1, Pallas kernels, gather_first(): pl.pallas_call(partial(gather_kernel, line, peers), in_specs=[hspec()] *...  91.6 us
    pallas_call x2, Pallas kernels, attend_backward(): pl.pallas_call(partial(attend_back_kernel, line, heads // KV_HEADS), in_s...  81.6 us
    psum x2, waiting for transfers between devices, local(): whole = lax.psum(whole_here, 'tensor')  77.6 us
    pallas_call x2, Pallas kernels, attend_forward(): pl.pallas_call(partial(attend_kernel, line, heads // KV_HEADS), in_specs=...  37.4 us
    unnamed x96, local copies, waits for them, and re-layouts  33.5 us
    all_gather x2, waiting for transfers between devices, local(): gathered[layer] = lax.all_gather(block, ('section', 'dp'), axis=0)  26.5 us
  transfers between devices with their start and end apart: 14, of which 5 were waited for; matrix products, arithmetic and copies ran while one was open for 5% of the time, Pallas kernels for 42%

profile of v3, /device:TPU:0, one launch (start us, length us, event | category | flops | bytes accessed | tf_op | source)
XLA Modules:
  0.0 944.8 jit_solution(9249858130981330939)
XLA Ops:
  7.2 4.3 copy.81
  11.5 3.8 copy.82
  18.1 8.0 all_to_all.56
  39.6 5.0 all_to_all.57.attn
  44.6 91.6 %shard_map.253 = (bf16[8,4,192,896]{3,2,1,0:T(8,128)(2,1)}, bf16[4,192,896]{2,1,0:T(8,128)(2,1)}, bf16[4,96,384]{2,1,0:T(8,128)(2,1)}) custom-call(bf16[2,192,896]{2,1,0:T(8,128)(2,1)} %all_to_all.57.attn, bf16[96,384]{1,0:T(8,128)(2,1)} %bitcast.227), custom_call_target="tpu_custom_call" | custom-call | tf_op jit(solution)/shard_map/pallas_call | solution.py:625
  145.8 3.5 all-to-all-start.3
  179.4 3.5 all-to-all-start.7
  190.6 19.4 %shard_map.254 = (f32[256,1536]{1,0:T(8,128)}, bf16[256,1536]{1,0:T(8,128)(2,1)}, bf16[256,1536]{1,0:T(8,128)(2,1)}, bf16[2,256,48]{2,1,0:T(8,128)(2,1)}, bf16[2...) custom-call(s32[2]{0:T(128)} %pad_add_fusion.info_ref, ...), custom_call_target="tpu_custom_call" | custom-call | flops 4831838208 | bytes 11796480 | tf_op jit(solution)/shard_map/pallas_call | solution.py:814
  212.4 127.2 %shard_map.255 = (f32[4,64,1536]{2,1,0:T(8,128)}, bf16[4,4,64,1536]{3,2,1,0:T(8,128)(2,1)}, bf16[4,256,2304]{2,1,0:T(8,128)(2,1)}, bf16[4,256,2304]{2,1,0:T(8,128)(2,1)}) custom-call(bf16[4,64,1536]{2,1,0:T(8,128)(2,1)} %bitcast.238, bf16[8,3,192,2304]{3,2,1,0:T(8,128)(2,1)} %all-gather.9.cloned.1.call-done.packed, bf16[1536,32]{1,0:T(8,128)(2,1)} %bitcast.222, ...), custom_call_target="tpu_custom_call" | custom-call | flops 21743271936 | bytes 30670848 | tf_op jit(solution)/shard_map/pallas_call | solution.py:297
  342.9 18.0 %shard_map.256 = (f32[256,1536]{1,0:T(8,128)}, bf16[256,1536]{1,0:T(8,128)(2,1)}, bf16[256,1536]{1,0:T(8,128)(2,1)}, bf16[2,256,48]{2,1,0:T(8,128)(2,1)}, bf16[2...) custom-call(s32[2]{0:T(128)} %pad_add_fusion.info_ref, ...), custom_call_target="tpu_custom_call" | custom-call | flops 4831838208 | bytes 11796480 | tf_op jit(solution)/shard_map/pallas_call | solution.py:814
  360.9 9.5 %all-gather.11.cloned.1.call-done.packed = bf16[8,3,192,2304]{3,2,1,0:T(8,128)(2,1)} async-done(((bf16[1,3,192,2304]{3,2,1,0:T(8,128)(2,1)}), bf16[8,3,192,2304]{3,2,1,0:T(8,128)(2,1)}) %all-gather.11.cloned.1.call-update) | async-done | bytes 21233680 | tf_op jit(solution)/shard_map/all_gather | solution.py:1107
  370.4 109.1 %shard_map.257 = (f32[4,64,1536]{2,1,0:T(8,128)}, bf16[4,4,64,1536]{3,2,1,0:T(8,128)(2,1)}, bf16[4,256,2304]{2,1,0:T(8,128)(2,1)}, bf16[4,256,2304]{2,1,0:T(8,128)(2,1)}) custom-call(bf16[4,64,1536]{2,1,0:T(8,128)(2,1)} %bitcast.239, bf16[8,3,192,2304]{3,2,1,0:T(8,128)(2,1)} %all-gather.11.cloned.1.call-done.packed, bf16[1536,32]{1,0:T(8,128)(2,1)} %bitcast.224, ...), custom_call_target="tpu_custom_call" | custom-call | flops 21743271936 | bytes 30670848 | tf_op jit(solution)/shard_map/pallas_call | solution.py:297
  479.5 97.9 %shard_map.258 = (f32[4,64,1536]{2,1,0:T(8,128)}, f32[32,1536]{1,0:T(8,128)}, f32[2,32,2304]{2,1,0:T(8,128)}, f32[16,2304]{1,0:T(8,128)}, f32[16,1536]{1,0:T(8,128)}) custom-call(bf16[4,64,1536]{2,1,0:T(8,128)(2,1)} %multiply_convert_fusion.ds_ref, bf16[8,3,192,2304]{3,2,1,0:T(8,128)(2,1)} %all-gather.11.cloned.1.call-done.packed, ...), custom_call_target="tpu_custom_call" | custom-call | flops 21743271936 | bytes 30670848 | tf_op jit(solution)/shard_map/pallas_call | solution.py:439
  577.5 38.6 %shard_map.259 = (f32[256,1536]{1,0:T(8,128)}, f32[48,1536]{1,0:T(8,128)}, f32[48,1536]{1,0:T(8,128)}, f32[48,1536]{1,0:T(8,128)}, f32[48,1536]{1,0:T(8,128)}, /*index=5*/f32[48,512]{1,0:T(8,128)}) custom-call(s32[2]{0:T(128)} %pad_add_fusion.info_ref, f32[256,1536]{1,0:T(8,128)} %get-tuple-element.153.x_ref, f32[256,1536]{1,0:T(8,128)} %get-tuple-element.67.mid_ref, ...), custom_call_target="tpu_custom_call" | custom-call | flops 4831838208 | bytes 11796480 | tf_op jit(solution)/shard_map/pallas_call | solution.py:991
  621.9 41.1 %all-reduce.26.cloned.1.call-done = bf16[160,1536]{1,0:T(8,128)(2,1)} async-done(((bf16[160,1536]{1,0:T(8,128)(2,1)}), bf16[160,1536]{1,0:T(8,128)(2,1)}) %all-reduce.26.cloned.1.call-update) | async-done | bytes 491536 | tf_op jit(solution)/shard_map/psum | solution.py:1170
  666.9 99.8 %shard_map.260 = (f32[4,64,1536]{2,1,0:T(8,128)}, f32[32,1536]{1,0:T(8,128)}, f32[2,32,2304]{2,1,0:T(8,128)}, f32[16,2304]{1,0:T(8,128)}, f32[16,1536]{1,0:T(8,128)}) custom-call(bf16[4,64,1536]{2,1,0:T(8,128)(2,1)} %bitcast.221, bf16[8,3,192,2304]{3,2,1,0:T(8,128)(2,1)} %all-gather.9.cloned.1.call-done.packed, bf16[4,256,1536]{2,1,0:T(8,128)(2,1)} %bitcast.236, ...), custom_call_target="tpu_custom_call" | custom-call | flops 21743271936 | bytes 30670848 | tf_op jit(solution)/shard_map/pallas_call | solution.py:439
  767.8 43.0 %shard_map.261 = (f32[256,1536]{1,0:T(8,128)}, f32[48,1536]{1,0:T(8,128)}, f32[48,1536]{1,0:T(8,128)}, f32[48,1536]{1,0:T(8,128)}, f32[48,1536]{1,0:T(8,128)}, /*index=5*/f32[48,512]{1,0:T(8,128)}) custom-call(s32[2]{0:T(128)} %pad_add_fusion.info_ref, f32[256,1536]{1,0:T(8,128)} %bitcast_convert_fusion.x_ref, f32[256,1536]{1,0:T(8,128)} %get-tuple-element.63.mid_ref, ...), custom_call_target="tpu_custom_call" | custom-call | flops 4831838208 | bytes 11796480 | tf_op jit(solution)/shard_map/pallas_call | solution.py:991
  817.3 36.5 %all-reduce.28.cloned.1.call-done = bf16[160,1536]{1,0:T(8,128)(2,1)} async-done(((bf16[160,1536]{1,0:T(8,128)(2,1)}), bf16[160,1536]{1,0:T(8,128)(2,1)}) %all-reduce.28.cloned.1.call-update) | async-done | bytes 491536 | tf_op jit(solution)/shard_map/psum | solution.py:1170
  857.8 7.5 all_to_all.58
  866.7 5.8 all_to_all.59
  872.5 26.4 %all-gather.17.cloned.1.call-done = bf16[1728,1536]{1,0:T(8,128)(2,1)} async-done(((bf16[216,1536]{1,0:T(8,128)(2,1)}), bf16[1728,1536]{1,0:T(8,128)(2,1)}) %all-gather.17.cloned.1.call-update) | async-done | bytes 5308432 | tf_op jit(solution)/shard_map/all_gather | solution.py:1176
  898.9 7.0 copy_select_fusion
  914.8 3.9 copy.91
  925.7 4.2 copy.93
  (253 shorter events, 110.8 us)
Async XLA Ops:
  7.2 205.2 %all-gather.9.cloned.1.call-start = ((), (), s32[]{:S(2)}) async-start(), calls=%async_computation.11 | async-start | bytes 23887872 | tf_op jit(solution)/shard_map/all_gather | solution.py:1107
  34.8 4.7 all-to-all-start.2
  38.2 304.8 %all-gather.13.cloned.1.call-start = ((), (), s32[]{:S(2)}) async-start(), calls=%async_computation.15 | async-start | bytes 12386304 | tf_op jit(solution)/shard_map/all_gather | solution.py:1103
  136.2 234.2 %all-gather.11.cloned.1.call-start = ((), (), s32[]{:S(2)}) async-start(), calls=%async_computation.12 | async-start | bytes 23887872 | tf_op jit(solution)/shard_map/all_gather | solution.py:1107
  138.6 7.1 all-to-all-start.5
  144.9 11.9 %copy-start.38 = (s32[2]{0:T(128)S(1)}, s32[2]{0:T(128)}, u32[]{:S(2)}) copy-start(s32[2]{0:T(128)} %param.20) | copy-start | bytes 28
  145.8 6.8 all-to-all-start.3
  152.6 6.4 all-to-all-start
  159.0 6.5 all-to-all-start.8
  165.5 13.9 %all-to-all-start.4 = ((bf16[2,2,16,256]{3,2,1,0:T(8,128)(2,1)}), bf16[2,2,16,256]{3,2,1,0:T(8,128)(2,1)S(1)}, u32[]{:S(2)}, u32[]{:S(2)}) async-start(bf16[2,2,16,256]{3,2,1,0:T(8,128)(2,1)} %pad_maximum_fusion.18), calls=%async_computation.4 | async-start | bytes 65536 | tf_op jit(solution)/shard_map/all_to_all | solution.py:1031
  173.8 12.4 %copy-start.20 = (bf16[2,256,1536]{2,1,0:T(8,128)(2,1)S(1)}, bf16[2,256,1536]{2,1,0:T(8,128)(2,1)}, u32[]{:S(2)}) copy-start(bf16[2,256,1536]{2,1,0:T(8,128)(2,1)} %param.19) | copy-start | bytes 4718596
  179.4 8.3 all-to-all-start.7
  182.9 480.1 %all-reduce.26.cloned.1.call-start = ((), (), s32[]{:S(2)}) async-start(), calls=%async_computation.13 | async-start | bytes 983040 | tf_op jit(solution)/shard_map/psum | solution.py:1170
  212.4 127.2 %copy-start.6 = (f32[256,1536]{1,0:T(8,128)S(1)}, f32[256,1536]{1,0:T(8,128)}, u32[]{:S(2)}) copy-start(f32[256,1536]{1,0:T(8,128)} %get-tuple-element.63.mid_ref) | copy-start | bytes 4718596
  577.4 40.6 %copy-start.27 = (f32[32,1536]{1,0:T(8,128)S(1)}, f32[32,1536]{1,0:T(8,128)}, u32[]{:S(2)}) copy-start(f32[32,1536]{1,0:T(8,128)} %get-tuple-element.82) | copy-start | bytes 589828
  577.5 41.5 %copy-start.33 = (f32[16,1536]{1,0:T(8,128)S(1)}, f32[16,1536]{1,0:T(8,128)}, u32[]{:S(2)}) copy-start(f32[16,1536]{1,0:T(8,128)} %get-tuple-element.84) | copy-start | bytes 294916
  621.6 193.9 %all-gather.15.cloned.1.call-start = ((), (), s32[]{:S(2)}) async-start(), calls=%async_computation.16 | async-start | bytes 5971968 | tf_op jit(solution)/shard_map/all_gather | solution.py:1176
  621.7 44.2 %copy-start.2 = (f32[256,1536]{1,0:T(8,128)S(1)}, f32[256,1536]{1,0:T(8,128)}, u32[]{:S(2)}) copy-start(f32[256,1536]{1,0:T(8,128)} %get-tuple-element.88.dy_ref) | copy-start | bytes 4718596
  665.8 187.9 %all-reduce.28.cloned.1.call-start = ((), (), s32[]{:S(2)}) async-start(), calls=%async_computation.14 | async-start | bytes 983040 | tf_op jit(solution)/shard_map/psum | solution.py:1170
  767.8 45.0 %copy-start.26 = (f32[32,1536]{1,0:T(8,128)S(1)}, f32[32,1536]{1,0:T(8,128)}, u32[]{:S(2)}) copy-start(f32[32,1536]{1,0:T(8,128)} %get-tuple-element.101) | copy-start | bytes 589828
  767.8 45.9 %copy-start.32 = (f32[16,1536]{1,0:T(8,128)S(1)}, f32[16,1536]{1,0:T(8,128)}, u32[]{:S(2)}) copy-start(f32[16,1536]{1,0:T(8,128)} %get-tuple-element.103) | copy-start | bytes 294916
  816.3 82.6 %all-gather.17.cloned.1.call-start = ((), (), s32[]{:S(2)}) async-start(), calls=%async_computation.17 | async-start | bytes 5971968 | tf_op jit(solution)/shard_map/all_gather | solution.py:1176
  816.4 41.2 %copy-start.3 = (f32[256,1536]{1,0:T(8,128)S(1)}, f32[256,1536]{1,0:T(8,128)}, u32[]{:S(2)}) copy-start(f32[256,1536]{1,0:T(8,128)} %get-tuple-element.88.dy_ref) | copy-start | bytes 4718596
  816.4 41.2 %copy-start.13 = (f32[256,1536]{1,0:T(8,128)S(1)}, f32[256,1536]{1,0:T(8,128)}, u32[]{:S(2)}) copy-start(f32[256,1536]{1,0:T(8,128)} %get-tuple-element.99) | copy-start | bytes 4718596
  (31 other events, 135.1 us)
Sparse Core Ops, SparseCore 0:
  29.0 162.7 all-gather.8
  193.7 65.4 all-gather.12
  261.7 108.7 all-gather.10
  621.7 41.2 all-reduce.25
  666.0 41.1 all-gather.14
  816.4 37.2 all-reduce.27
  857.7 41.1 all-gather.16

commit v4 on v3

--- a/solution.py
+++ b/solution.py
@@ -43,6 +43,67 @@
     return jnp.concatenate([cos, cos], axis=1), jnp.concatenate([-sin, sin], axis=1)
 
 
+B_INPUT, B_RES_ONE, B_RES_TWO, B_KV, B_MISC, B_FF, B_FF_TAIL, B_HEADS, B_ROWS = 0, 5, 6, 7, 8, 9, 12, 15, 18
+
+
+def rows_of(first, count=1):
+    return slice(first * RANK, (first + count) * RANK)
+
+
+def pick_kernel(
+    ids_ref, input_ref, res_ref, kv_ref, expand_ref, shrink_ref, query_ref, attend_ref, gain_ref, kvb_ref, qb_ref,
+    out_ref, heads_ref,
+):
+    width = out_ref.shape[2]
+    out_ref[0] = jnp.zeros(out_ref.shape[1:], BF)
+    out_ref[0, rows_of(B_INPUT, 5)] = input_ref[0]
+    out_ref[0, rows_of(B_RES_ONE, 2)] = res_ref[0]
+    kv_half = kv_ref.shape[2]
+    for i in range(2):
+        out_ref[0, rows_of(B_KV), i * kv_half : (i + 1) * kv_half] = kv_ref[0, rows_of(i)]
+    misc = rows_of(B_MISC).start
+    out_ref[0, misc : misc + 2] = gain_ref[...]
+    out_ref[0, misc + 2 : misc + 3, : 2 * kv_half] = kvb_ref[...]
+    tail = expand_ref.shape[2] - width
+    for i in range(3):
+        part = expand_ref[0, rows_of(i)] if i < 2 else shrink_ref[0]
+        out_ref[0, rows_of(B_FF + i)] = part[:, :width]
+        out_ref[0, rows_of(B_FF_TAIL + i), :tail] = part[:, width:]
+    heads_ref[0] = jnp.zeros(heads_ref.shape[1:], BF)
+    heads_ref[0, rows_of(0)] = query_ref[0]
+    heads_ref[0, rows_of(1)] = attend_ref[0]
+    heads_ref[0, 2 * RANK : 2 * RANK + 1] = qb_ref[...]
+
+
+def pick_adapters(ids, stacks, shared):
+    count = ids.shape[0]
+    width = stacks[0].shape[2]
+    q_cols = stacks[5].shape[2]
+    shapes = [(B_ROWS * RANK, width), (3 * RANK, q_cols)]
+    return pl.pallas_call(
+        pick_kernel,
+        grid_spec=pltpu.PrefetchScalarGridSpec(
+            num_scalar_prefetch=1,
+            grid=(count,),
+            in_specs=[pl.BlockSpec((1,) + a.shape[1:], lambda i, ids: (ids[i], 0, 0)) for a in stacks]
+            + [pl.BlockSpec(a.shape, lambda i, ids: (0, 0)) for a in shared],
+            out_specs=[pl.BlockSpec((1,) + a, lambda i, ids: (i, 0, 0)) for a in shapes],
+        ),
+        out_shape=[jax.ShapeDtypeStruct((count,) + a, BF) for a in shapes],
+    )(ids, *stacks, *shared)
+
+
+def spread_factors(bundle_ref, expand_ref, ash_ref):
+    width = bundle_ref.shape[1]
+    tail = ash_ref.shape[1] - width
+    expand_ref[...] = jnp.zeros_like(expand_ref)
+    for i in range(2):
+        expand_ref[i, rows_of(i), :width] = bundle_ref[rows_of(B_FF + i)]
+        expand_ref[i, rows_of(i), width:] = bundle_ref[rows_of(B_FF_TAIL + i), :tail]
+    ash_ref[:, :width] = bundle_ref[rows_of(B_FF + 2)]
+    ash_ref[:, width:] = bundle_ref[rows_of(B_FF_TAIL + 2), :tail]
+
+
 def vspec():
     return pl.BlockSpec(memory_space=pltpu.VMEM)
 
@@ -132,7 +193,7 @@
 
             @pl.when(jnp.logical_and(within(c, chunks), me == h))
             def _():
-                for j in range(h + 1, line):
+                for j in range(line - 1, h, -1):
                     if h > 0:
                         rs(c, j, 1).wait_recv()
                         partial_ref[c, j] = (
@@ -203,22 +264,47 @@
     return [pltpu.VMEM(slots, BF)] * 4 + [pltpu.SemaphoreType.DMA((chunks, line))] * 7
 
 
+def ff_loads(packed, refs, wsem):
+    halves, parts, _, rows, cols = packed.shape
+    return [
+        pltpu.make_async_copy(
+            packed.at[h, p, i],
+            ref.at[pl.ds(h * rows, rows), pl.ds(p * cols, cols)],
+            wsem.at[i, h, p],
+        )
+        for i, ref in enumerate(refs)
+        for h in range(halves)
+        for p in range(parts)
+    ]
+
+
+def clear_tail(packed, refs):
+    hidden = packed.shape[0] * packed.shape[3]
+    for ref in refs:
+        if ref.shape[0] > hidden:
+            ref[hidden:] = jnp.zeros((ref.shape[0] - hidden, ref.shape[1]), BF)
+
+
 def mlp_kernel(
     line, chunks, tile,
-    n2_ref, packed, high_ref, expand_ref, ash_ref, res_ref,
+    n2_ref, packed, bundle_ref,
     out_ref, n2_out, gate_out, up_out,
     gathered, partial_ref, from_left, from_right, s0, s1, s2, s3, s4, s5, s6,
-    wg, wu, ws, gate_st, up_st, acc, wsem, osem, nsem,
+    wg, wu, ws, gate_st, up_st, acc, expand_ref, ash_ref, wsem, osem, nsem,
 ):
     rows, width = n2_ref.shape[1:]
     every = line * rows
-    tiles = wg.shape[2] // tile
+    tiles = wg.shape[0] // tile
+    high = bundle_ref[rows_of(B_INPUT + 3, 2)]
+    res = bundle_ref[rows_of(B_RES_TWO)]
     me = lax.axis_index("tensor")
-    loads = [pltpu.make_async_copy(packed.at[:, i], ref, wsem.at[i]) for i, ref in enumerate((wg, wu, ws))]
+    loads = ff_loads(packed, (wg, wu, ws), wsem)
 
     def begin():
         for load in loads:
             load.start()
+        clear_tail(packed, (wg, wu, ws))
+        spread_factors(bundle_ref, expand_ref, ash_ref)
         for c in range(chunks):
             gathered[c, me] = n2_ref[c]
 
@@ -246,16 +332,16 @@
 
         keep(c).start()
         x = gathered[c].reshape(every, width)
-        er = dot(x, high_ref[...]).astype(BF)
+        er = dot_t(x, high).astype(BF)
 
         def one(f, rank):
             cols = pl.ds(pl.multiple_of(f * tile, tile), tile)
-            gate = dot(x, wg[:, :, cols].reshape(width, tile)) + dot(er, expand_ref[0, :, cols])
-            up = dot(x, wu[:, :, cols].reshape(width, tile)) + dot(er, expand_ref[1, :, cols])
+            gate = dot_t(x, wg[cols]) + dot(er, expand_ref[0, :, cols])
+            up = dot_t(x, wu[cols]) + dot(er, expand_ref[1, :, cols])
             gate_st[slot, :, cols] = gate.astype(BF)
             up_st[slot, :, cols] = up.astype(BF)
             act = (gate * (1.0 / (1.0 + jnp.exp(-gate))) * up).astype(BF)
-            now = dot_t(act, ws[:, :, cols].reshape(width, tile))
+            now = dot(act, ws[cols])
 
             @pl.when(f == 0)
             def _():
@@ -268,7 +354,7 @@
             return rank + dot_t(act, ash_ref[:, cols])
 
         rank = lax.fori_loop(0, tiles, one, jnp.zeros((every, ash_ref.shape[0]), F32))
-        total = acc[...] + dot(rank.astype(BF), res_ref[...])
+        total = acc[...] + dot(rank.astype(BF), res)
         partial_ref[c] = total.astype(BF).reshape(line, rows, width)
         for save in saves(c, slot):
             save.start()
@@ -288,15 +374,16 @@
     return hidden // 3 if hidden % (3 * LANES) == 0 else LANES
 
 
-def mlp_forward(n2, w, ad):
+def mlp_forward(n2, w):
     line = lax.axis_size("tensor")
     rows, width = n2.shape
-    groups, _, _, hidden = w["mlp"].shape
+    halves, groups, _, low_rows, _ = w["mlp"].shape
+    hidden = halves * low_rows + -(halves * low_rows) % (2 * LANES)
     part = rows // CHUNKS
     every = line * part
     out, n2_all, gate, up = pl.pallas_call(
         partial(mlp_kernel, line, CHUNKS, ff_tile(hidden)),
-        in_specs=[vspec(), hspec()] + [vspec()] * 4,
+        in_specs=[vspec(), hspec(), vspec()],
         out_specs=[vspec()] + [hspec()] * 3,
         out_shape=[
             jax.ShapeDtypeStruct((CHUNKS, part, width), F32),
@@ -305,11 +392,13 @@
             jax.ShapeDtypeStruct((CHUNKS, every, hidden), BF),
         ],
         scratch_shapes=exchange_scratch(line, CHUNKS, part, width)
-        + [pltpu.VMEM((groups, width // groups, hidden), BF)] * 3
+        + [pltpu.VMEM((hidden, width), BF)] * 3
         + [pltpu.VMEM((2, every, hidden), BF)] * 2
         + [
             pltpu.VMEM((every, width), F32),
-            pltpu.SemaphoreType.DMA((3,)),
+            pltpu.VMEM((2, 2 * RANK, hidden), BF),
+            pltpu.VMEM((RANK, hidden), BF),
+            pltpu.SemaphoreType.DMA((3, halves, groups)),
             pltpu.SemaphoreType.DMA((2, 2)),
             pltpu.SemaphoreType.DMA((CHUNKS,)),
         ],
@@ -322,24 +411,25 @@
             transcendentals=line * rows * hidden,
         ),
     )(
-        n2.reshape(CHUNKS, part, width), w["mlp"],
-        ad["high"], ad["expand"], ad["shrink"], ad["res_two"],
+        n2.reshape(CHUNKS, part, width), w["mlp"], w["bundle"],
     )
     return out.reshape(rows, width), (n2_all.reshape(CHUNKS, every, width), gate, up)
 
 
 def mlp_back_kernel(
     line, chunks, tile,
-    ds_ref, packed, n2_hbm, gate_in, up_in, high_ref, expand_ref, ash_ref, res_ref,
-    out_ref, ghigh_ref, gexp_ref, gsh_ref, gres_ref,
+    ds_ref, packed, n2_hbm, gate_in, up_in, bundle_ref,
+    out_ref, whole_ref, parts_ref,
     gathered, partial_ref, from_left, from_right, s0, s1, s2, s3, s4, s5, s6,
-    wg, wu, ws, gate_st, up_st, n2_st, acc, wsem, isem,
+    wg, wu, ws, gate_st, up_st, n2_st, acc, ghigh_ref, gexp_ref, gsh_ref, gres_ref, expand_ref, ash_ref, wsem, isem,
 ):
     rows, width = ds_ref.shape[1:]
     every = line * rows
-    tiles = wg.shape[2] // tile
+    tiles = wg.shape[0] // tile
+    high = bundle_ref[rows_of(B_INPUT + 3, 2)]
+    res = bundle_ref[rows_of(B_RES_TWO)]
     me = lax.axis_index("tensor")
-    loads = [pltpu.make_async_copy(packed.at[:, i], ref, wsem.at[i]) for i, ref in enumerate((wg, wu, ws))]
+    loads = ff_loads(packed, (wg, wu, ws), wsem)
 
     def fetch(c):
         slot = c % 2
@@ -352,6 +442,8 @@
     def begin():
         for load in loads:
             load.start()
+        clear_tail(packed, (wg, wu, ws))
+        spread_factors(bundle_ref, expand_ref, ash_ref)
         for one in fetch(0):
             one.start()
         for c in range(chunks):
@@ -377,13 +469,13 @@
 
         ds = gathered[c].reshape(every, width)
         n2 = n2_st[slot]
-        er = dot(n2, high_ref[...]).astype(BF)
-        rank_in = dot_t(ds, res_ref[...]).astype(BF)
+        er = dot_t(n2, high).astype(BF)
+        rank_in = dot_t(ds, res).astype(BF)
 
         def one(f, carry):
             rank_out, srank = carry
             cols = pl.ds(pl.multiple_of(f * tile, tile), tile)
-            act_grad = dot(ds, ws[:, :, cols].reshape(width, tile)) + dot(rank_in, ash_ref[:, cols])
+            act_grad = dot_t(ds, ws[cols]) + dot(rank_in, ash_ref[:, cols])
             gate = gate_st[slot, :, cols].astype(F32)
             up = up_st[slot, :, cols].astype(F32)
             sig = 1.0 / (1.0 + jnp.exp(-gate))
@@ -391,7 +483,7 @@
             act = (silu * up).astype(BF)
             gate_grad = (act_grad * up * (sig + silu * (1.0 - sig))).astype(BF)
             up_grad = (act_grad * silu).astype(BF)
-            now = dot_t(gate_grad, wg[:, :, cols].reshape(width, tile)) + dot_t(up_grad, wu[:, :, cols].reshape(width, tile))
+            now = dot(gate_grad, wg[cols]) + dot(up_grad, wu[cols])
 
             @pl.when(f == 0)
             def _():
@@ -418,7 +510,7 @@
             ),
         )
         rank_out = rank_out.astype(BF)
-        total = acc[...] + dot_t(rank_out, high_ref[...])
+        total = acc[...] + dot(rank_out, high)
         partial_ref[c] = total.astype(BF).reshape(line, rows, width)
         ghigh_ref[...] += t_dot(rank_out, n2)
         gres_ref[...] += t_dot(srank.astype(BF), ds)
@@ -427,33 +519,46 @@
         line, chunks, gathered, partial_ref, from_left, from_right, out_ref,
         (s0, s1, s2, s3, s4, s5, s6), begin, work,
     )
-
-
-def mlp_backward(ds, w, ad, saved):
+    whole_ref[: 2 * RANK] = ghigh_ref[...].astype(BF)
+    whole_ref[2 * RANK :] = gres_ref[...].astype(BF)
+    extra = gsh_ref.shape[1] - width
+    parts_ref[3 * RANK :, extra:] = jnp.zeros((3 * RANK, width - extra), BF)
+    for i, part in enumerate((gexp_ref[0, :RANK], gexp_ref[1, RANK:], gsh_ref[...])):
+        part = part.astype(BF)
+        parts_ref[i * RANK : (i + 1) * RANK] = part[:, :width]
+        parts_ref[(3 + i) * RANK : (4 + i) * RANK, :extra] = part[:, width:]
+
+
+def mlp_backward(ds, w, saved):
     n2_all, gate, up = saved
     line = lax.axis_size("tensor")
     rows, width = ds.shape
-    groups, _, _, hidden = w["mlp"].shape
+    halves, groups, _, low_rows, _ = w["mlp"].shape
+    hidden = halves * low_rows + -(halves * low_rows) % (2 * LANES)
     part = rows // CHUNKS
     every = line * part
-    out, g_high, g_expand, g_shrink, g_res = pl.pallas_call(
+    out, whole, parts = pl.pallas_call(
         partial(mlp_back_kernel, line, CHUNKS, ff_tile(hidden)),
-        in_specs=[vspec()] + [hspec()] * 4 + [vspec()] * 4,
-        out_specs=[vspec()] * 5,
+        in_specs=[vspec()] + [hspec()] * 4 + [vspec()],
+        out_specs=[vspec()] * 3,
         out_shape=[
             jax.ShapeDtypeStruct((CHUNKS, part, width), F32),
-            jax.ShapeDtypeStruct((2 * RANK, width), F32),
-            jax.ShapeDtypeStruct((2, 2 * RANK, hidden), F32),
-            jax.ShapeDtypeStruct((RANK, hidden), F32),
-            jax.ShapeDtypeStruct((RANK, width), F32),
+            jax.ShapeDtypeStruct((3 * RANK, width), BF),
+            jax.ShapeDtypeStruct((6 * RANK, width), BF),
         ],
         scratch_shapes=exchange_scratch(line, CHUNKS, part, width)
-        + [pltpu.VMEM((groups, width // groups, hidden), BF)] * 3
+        + [pltpu.VMEM((hidden, width), BF)] * 3
         + [pltpu.VMEM((2, every, hidden), BF)] * 2
         + [
             pltpu.VMEM((2, every, width), BF),
             pltpu.VMEM((every, width), F32),
-            pltpu.SemaphoreType.DMA((3,)),
+            pltpu.VMEM((2 * RANK, width), F32),
+            pltpu.VMEM((2, 2 * RANK, hidden), F32),
+            pltpu.VMEM((RANK, hidden), F32),
+            pltpu.VMEM((RANK, width), F32),
+            pltpu.VMEM((2, 2 * RANK, hidden), BF),
+            pltpu.VMEM((RANK, hidden), BF),
+            pltpu.SemaphoreType.DMA((3, halves, groups)),
             pltpu.SemaphoreType.DMA((3, 2)),
         ],
         compiler_params=pltpu.CompilerParams(
@@ -465,18 +570,16 @@
             transcendentals=line * rows * hidden,
         ),
     )(
-        ds.reshape(CHUNKS, part, width), w["mlp"], n2_all, gate, up,
-        ad["high"], ad["expand"], ad["shrink"], ad["res_two"],
+        ds.reshape(CHUNKS, part, width), w["mlp"], n2_all, gate, up, w["bundle"],
     )
-    g_expand = jnp.concatenate([g_expand[0, :RANK], g_expand[1, RANK:]], axis=0)
-    return out.reshape(rows, width), g_high, g_expand, g_shrink, g_res
+    return out.reshape(rows, width), whole, parts
 
 
 def gather_kernel(
     line, peers,
-    attn, extra,
-    first_out, second_out, extra_out,
-    own_sem, z_recv, z_right, z_left, dp_recv, dp_send, core_recv, core_send,
+    attn, bundles, heads,
+    first_out, second_out, bundle_out,
+    own_sem, z_recv, z_right, z_left, dp_recv, dp_send, core_recv, core_send, side_recv, side_send, side_own,
 ):
     me, spot, core = lax.axis_index("tensor"), lax.axis_index("dp"), lax.axis_index("section")
     other = 1 - core
@@ -500,13 +603,36 @@
     pl.semaphore_wait(barrier, jnp.where(has_left, 1, 0) + jnp.where(has_right, 1, 0) + peers)
 
     mine = spot * 2 + core
+    plain, part = bundles.shape[1] - heads.shape[1], heads.shape[2]
+
+    def head_place(layer, o):
+        return bundle_out.at[layer, pl.ds(plain, heads.shape[1]), pl.ds(o * part, part)]
 
     def places(o):
-        return first_out.at[mine, o], second_out.at[o], extra_out.at[o]
-
-    sources = (attn.at[0], attn.at[1], extra)
+        return first_out.at[mine, o], second_out.at[o], head_place(core, o), head_place(other, o)
+
+    sides = [
+        pltpu.make_async_remote_copy(
+            src_ref=src,
+            dst_ref=dst,
+            send_sem=side_send.at[i],
+            recv_sem=side_recv.at[i],
+            device_id={"section": other},
+            device_id_type=MESH,
+        )
+        for i, (src, dst) in enumerate(
+            (
+                (bundles.at[other, pl.ds(0, plain)], bundle_out.at[core, pl.ds(0, plain)]),
+                (heads.at[other], head_place(core, me)),
+            )
+        )
+    ]
+    side_keep = pltpu.make_async_copy(
+        bundles.at[core, pl.ds(0, plain)], bundle_out.at[core, pl.ds(0, plain)], side_own
+    )
+    sources = (attn.at[0], attn.at[1], heads.at[core], head_place(other, me))
     keeps = [
-        pltpu.make_async_copy(src, dst, own_sem.at[i]) for i, (src, dst) in enumerate(zip(sources, places(me)))
+        pltpu.make_async_copy(src, dst, own_sem.at[i]) for i, (src, dst) in enumerate(zip(sources[:3], places(me)))
     ]
 
     def remote(src, dst, send, recv, **where):
@@ -539,7 +665,11 @@
             to_peer(k, o, own).start()
         to_core(spot, o, own).start()
 
-    for i in range(3):
+    for side in sides:
+        side.start()
+    for i in range(4):
+        if i == 3:
+            sides[1].wait_recv()
 
         @pl.when(has_right)
         def _():
@@ -553,8 +683,9 @@
             spread_first(me, True)
     for keep in keeps:
         keep.start()
+    side_keep.start()
     for d in range(1, line):
-        for i in range(3):
+        for i in range(4):
 
             @pl.when(me >= d)
             def _():
@@ -601,7 +732,7 @@
                 core_recv.at[p, o],
                 section=other,
             ).wait_recv()
-        for i in range(3):
+        for i in range(4):
 
             @pl.when(jnp.logical_and(has_right, me >= o))
             def _():
@@ -616,27 +747,32 @@
     lax.fori_loop(0, line, finish, 0)
     for keep in keeps:
         keep.wait()
-
-
-def gather_first(attn, extra):
+    side_keep.wait()
+    sides[0].wait_recv()
+    for side in sides:
+        side.wait_send()
+
+
+def gather_first(attn, bundles, heads):
     line, peers = lax.axis_size("tensor"), lax.axis_size("dp")
     cores, part, cols = attn.shape
     dma = pltpu.SemaphoreType.DMA
     return pl.pallas_call(
         partial(gather_kernel, line, peers),
-        in_specs=[hspec()] * 2,
+        in_specs=[hspec()] * 3,
         out_specs=[hspec()] * 3,
         out_shape=[
             jax.ShapeDtypeStruct((peers * cores, line, part, cols), BF),
             jax.ShapeDtypeStruct((line, part, cols), BF),
-            jax.ShapeDtypeStruct((line,) + extra.shape, BF),
+            jax.ShapeDtypeStruct(bundles.shape, BF),
         ],
-        scratch_shapes=[dma((3,)), dma((3, line)), dma((3, line)), dma((3, line))]
-        + [dma((peers, line))] * 4,
+        scratch_shapes=[dma((3,)), dma((4, line)), dma((4, line)), dma((4, line))]
+        + [dma((peers, line))] * 4
+        + [dma((2,)), dma((2,)), dma],
         compiler_params=pltpu.CompilerParams(
             collective_id=4, has_side_effects=True, vmem_limit_bytes=VMEM_LIMIT
         ),
-    )(attn, extra)
+    )(attn, bundles, heads)
 
 
 def rotated(x, cos, sin):
@@ -684,6 +820,16 @@
         pl.semaphore_wait(barrier, 1)
 
 
+def spread_qkv(bundle_ref, bq_ref, bkv_ref):
+    kv_half = bkv_ref.shape[1] // 2
+    bq_ref[...] = jnp.zeros_like(bq_ref)
+    bkv_ref[...] = jnp.zeros_like(bkv_ref)
+    bq_ref[rows_of(0)] = bundle_ref[rows_of(B_HEADS)]
+    for i in range(2):
+        span = slice(i * kv_half, (i + 1) * kv_half)
+        bkv_ref[rows_of(1 + i), span] = bundle_ref[rows_of(B_KV), span]
+
+
 def kv_exchange(me, line, kvbuf, recv, send):
     def move(o):
         return pltpu.make_async_remote_copy(
@@ -700,9 +846,9 @@
 
 def attend_kernel(
     line, group,
-    info_ref, x_ref, gain_ref, qb_ref, kvb_ref, low_ref, bq_ref, bkv_ref, att_ref, res_ref, cos_ref, sin_ref, packed,
-    mid_ref, n2_ref, normed_ref, rank_ref, q_ref, kv_out, attended_ref, log_ref,
-    wq, wo, wkv, kvbuf, acc, peak, total, wsem, recv, send, ksem,
+    info_ref, x_ref, bundle_ref, cos_ref, sin_ref, packed,
+    mid_ref, n2_ref, normed_ref, lowr_ref, rank_ref, q_ref, kv_out, attended_ref, log_ref,
+    wq, wo, wkv, kvbuf, acc, peak, total, bq_ref, bkv_ref, wsem, recv, send, ksem,
 ):
     rows, width = x_ref.shape
     heads = width // HEAD_DIM
@@ -715,16 +861,20 @@
     for load in kv_loads + q_loads + o_loads:
         load.start()
     move = kv_exchange(me, line, kvbuf, recv, send)
-    x = x_ref[...]
+    spread_qkv(bundle_ref, bq_ref, bkv_ref)
+    misc = bundle_ref[rows_of(B_MISC)].astype(F32)
+    q_bias = bundle_ref[rows_of(B_HEADS + 2)].astype(F32)[:1]
+    low_in = bundle_ref[rows_of(B_INPUT, 3)]
+    x = x_ref[...].astype(F32)
     inverse = lax.rsqrt(jnp.mean(x * x, axis=-1, keepdims=True) + EPSILON)
-    normed_ref[...] = (x * inverse * gain_ref[0:1, :]).astype(BF)
-    low = dot(normed_ref[...], low_ref[...]).astype(BF)
+    normed_ref[...] = (x * inverse * misc[0:1]).astype(BF)
+    low = dot_t(normed_ref[...], low_in).astype(BF)
     cos, sin = cos_ref[...], sin_ref[...]
     for load in kv_loads:
         load.wait()
     for t in range(line):
         span = slice(t * kv_cols, (t + 1) * kv_cols)
-        kv = dot(normed_ref[...], flat(wkv, t)) + kvb_ref[:, span] + dot(low, bkv_ref[:, span])
+        kv = dot(normed_ref[...], flat(wkv, t)) + misc[2:3, span] + dot(low, bkv_ref[:, span])
         for h in range(kv_cols // HEAD_DIM):
             at = t * kv_cols + h * HEAD_DIM
             one = kv[:, h * HEAD_DIM : (h + 1) * HEAD_DIM]
@@ -740,7 +890,7 @@
         load.wait()
     for t in range(line):
         span = slice(t * cols, (t + 1) * cols)
-        q = dot(normed_ref[...], flat(wq, t)) + qb_ref[:, span] + dot(low, bq_ref[:, span])
+        q = dot(normed_ref[...], flat(wq, t)) + q_bias[:, span] + dot(low, bq_ref[:, span])
         for h in range(cols // HEAD_DIM):
             at = t * cols + h * HEAD_DIM
             q_ref[:, at : at + HEAD_DIM] = rotated(
@@ -786,17 +936,17 @@
     for h in range(heads):
         attended_ref[:, h * HEAD_DIM : (h + 1) * HEAD_DIM] = (acc[h] * (1.0 / total[h])).T.astype(BF)
         log_ref[h] = peak[h] + jnp.log(total[h])
-    rank = dot_t(attended_ref[...], att_ref[...]).astype(BF)
-    rank_ref[0] = low
-    rank_ref[1] = rank
-    middle = x_ref[...] + dot(rank, res_ref[...])
+    rank = dot_t(attended_ref[...], bundle_ref[rows_of(B_HEADS + 1)]).astype(BF)
+    lowr_ref[...] = low
+    rank_ref[...] = rank
+    middle = x_ref[...].astype(F32) + dot(rank, bundle_ref[rows_of(B_RES_ONE)])
     for load in o_loads:
         load.wait()
     for t in range(line):
         middle = middle + dot_t(attended_ref[:, t * cols : (t + 1) * cols], flat(wo, t))
     mid_ref[...] = middle
     inverse = lax.rsqrt(jnp.mean(middle * middle, axis=-1, keepdims=True) + EPSILON)
-    n2_ref[...] = (middle * inverse * gain_ref[1:2, :]).astype(BF)
+    n2_ref[...] = (middle * inverse * misc[1:2]).astype(BF)
     keep.wait()
     for o in range(line):
 
@@ -805,7 +955,7 @@
             move(o).wait_send()
 
 
-def attend_forward(x, w, ad, info, tables):
+def attend_forward(x, w, info, tables):
     line = lax.axis_size("tensor")
     rows, width = x.shape
     heads = width // HEAD_DIM
@@ -813,13 +963,14 @@
     groups, low_rows = w["packed"].shape[0], w["packed"].shape[2]
     outs = pl.pallas_call(
         partial(attend_kernel, line, heads // KV_HEADS),
-        in_specs=[pl.BlockSpec(memory_space=pltpu.SMEM)] + [vspec()] * 11 + [hspec()],
-        out_specs=[vspec()] * 5 + [hspec()] + [vspec()] * 2,
+        in_specs=[pl.BlockSpec(memory_space=pltpu.SMEM)] + [vspec()] * 4 + [hspec()],
+        out_specs=[vspec()] * 6 + [hspec()] + [vspec()] * 2,
         out_shape=[
             jax.ShapeDtypeStruct((rows, width), F32),
             jax.ShapeDtypeStruct((rows, width), BF),
             jax.ShapeDtypeStruct((rows, width), BF),
-            jax.ShapeDtypeStruct((2, rows, 3 * RANK), BF),
+            jax.ShapeDtypeStruct((rows, 3 * RANK), BF),
+            jax.ShapeDtypeStruct((rows, RANK), BF),
             jax.ShapeDtypeStruct((rows, width), BF),
             jax.ShapeDtypeStruct((line, rows, kv_width), BF),
             jax.ShapeDtypeStruct((rows, width), BF),
@@ -833,6 +984,8 @@
             pltpu.VMEM((heads, HEAD_DIM, rows), F32),
             pltpu.VMEM((heads, 1, rows), F32),
             pltpu.VMEM((heads, 1, rows), F32),
+            pltpu.VMEM((3 * RANK, width), BF),
+            pltpu.VMEM((3 * RANK, kv_width), BF),
             pltpu.SemaphoreType.DMA((3, line)),
             pltpu.SemaphoreType.DMA((line,)),
             pltpu.SemaphoreType.DMA((line,)),
@@ -845,18 +998,17 @@
             flops=4 * rows * width * width * 2, bytes_accessed=5 * width * width, transcendentals=0
         ),
     )(
-        info, x, w["gain"], ad["q_bias"], w["kv_bias"], ad["low"], ad["q"], ad["kv"], ad["attend"],
-        ad["res_one"], tables[0], tables[1], w["packed"],
+        info, x, w["bundle"], tables[0], tables[1], w["packed"],
     )
     return outs[0], outs[1], outs[2:]
 
 
 def attend_back_kernel(
     line, group,
-    info_ref, x_ref, mid_ref, dy_ref, dn2_ref, gain_ref, low_ref, bq_ref, bkv_ref, att_ref, res_ref, cos_ref, sin_ref,
-    normed_ref, rank_ref, q_ref, kv_ref, attended_ref, log_ref, packed,
-    dx_ref, glow_ref, gres_ref, gq_ref, gatt_ref, gkv_ref,
-    wq, wo, wkv, do_ref, dq_acc, dq_ref, dkv_acc, partial_ref, from_right, delta, wsem, recv, send,
+    info_ref, x_ref, mid_ref, dy_ref, dn2_ref, bundle_ref, cos_ref, sin_ref,
+    normed_ref, lowr_ref, rank_ref, q_ref, kv_ref, attended_ref, log_ref, packed,
+    dx_ref, dx_low_ref, grads_ref,
+    wq, wo, wkv, do_ref, dq_acc, dq_ref, dkv_acc, partial_ref, from_right, delta, bq_ref, bkv_ref, wsem, recv, send,
 ):
     rows, width = x_ref.shape
     heads = width // HEAD_DIM
@@ -887,18 +1039,21 @@
             weighted * values, axis=-1, keepdims=True
         )
 
-    middle_grad = dy_ref[...] + through_norm(mid_ref[...], gain_ref[1:2, :], dn2_ref[...])
+    spread_qkv(bundle_ref, bq_ref, bkv_ref)
+    misc = bundle_ref[rows_of(B_MISC)].astype(F32)
+    att = bundle_ref[rows_of(B_HEADS + 1)]
+    middle_grad = dy_ref[...].astype(F32) + through_norm(mid_ref[...], misc[1:2], dn2_ref[...])
     dx_ref[...] = middle_grad
     branch_grad = middle_grad.astype(BF)
-    low, rank = rank_ref[0], rank_ref[1]
-    rank_grad = dot_t(branch_grad, res_ref[...]).astype(BF)
-    gres_ref[...] = t_dot(rank, branch_grad)
-    gatt_ref[...] = t_dot(rank_grad, attended_ref[...])
+    low, rank = lowr_ref[...], rank_ref[...]
+    rank_grad = dot_t(branch_grad, bundle_ref[rows_of(B_RES_ONE)]).astype(BF)
+    grads_ref[3 * RANK : 4 * RANK] = t_dot(rank, branch_grad).astype(BF)
+    grads_ref[6 * RANK :] = t_dot(rank_grad, attended_ref[...]).astype(BF)
     for load in o_loads:
         load.wait()
     for t in range(line):
         span = slice(t * cols, (t + 1) * cols)
-        do_ref[:, span] = (dot(branch_grad, flat(wo, t)) + dot(rank_grad, att_ref[:, span])).astype(BF)
+        do_ref[:, span] = (dot(branch_grad, flat(wo, t)) + dot(rank_grad, att[:, span])).astype(BF)
     for h in range(heads):
         span = slice(h * HEAD_DIM, (h + 1) * HEAD_DIM)
         both = do_ref[:, span].astype(F32) * attended_ref[:, span].astype(F32)
@@ -948,7 +1103,7 @@
     for h in range(heads):
         dq_ref[:, h * HEAD_DIM : (h + 1) * HEAD_DIM] = rotated(dq_acc[h].T * scale, cos, sin).astype(BF)
     dq = dq_ref[...]
-    gq_ref[...] = t_dot(low, dq)
+    grads_ref[5 * RANK : 6 * RANK] = t_dot(low, dq)[:RANK].astype(BF)
     low_grad = dot_t(dq, bq_ref[...])
     for load in q_loads:
         load.wait()
@@ -966,15 +1121,20 @@
         span = slice(h * HEAD_DIM, (h + 1) * HEAD_DIM)
         dkv_acc[:, span] = rotated(dkv_acc[:, span], cos, sin)
     dkv = dkv_acc[...].astype(BF)
-    gkv_ref[...] = t_dot(low, dkv)
+    kv_grad = t_dot(low, dkv).astype(BF)
+    grads_ref[4 * RANK : 5 * RANK, :kv_half] = kv_grad[RANK : 2 * RANK, :kv_half]
+    grads_ref[4 * RANK : 5 * RANK, kv_half : 2 * kv_half] = kv_grad[2 * RANK :, kv_half:]
+    grads_ref[4 * RANK : 5 * RANK, 2 * kv_half :] = jnp.zeros((RANK, width - 2 * kv_half), BF)
     low_grad = (low_grad + dot_t(dkv, bkv_ref[...])).astype(BF)
-    glow_ref[...] = t_dot(low_grad, normed_ref[...])
+    grads_ref[: 3 * RANK] = t_dot(low_grad, normed_ref[...]).astype(BF)
     for load in kv_loads:
         load.wait()
     for t in range(line):
         normed_grad = normed_grad + dot_t(dkv[:, t * kv_cols : (t + 1) * kv_cols], flat(wkv, t))
-    normed_grad = normed_grad + dot_t(low_grad, low_ref[...])
-    dx_ref[...] += through_norm(x_ref[...], gain_ref[0:1, :], normed_grad)
+    normed_grad = normed_grad + dot(low_grad, bundle_ref[rows_of(B_INPUT, 3)])
+    dx = dx_ref[...] + through_norm(x_ref[...].astype(F32), misc[0:1], normed_grad)
+    dx_ref[...] = dx
+    dx_low_ref[...] = dx.astype(BF)
     for o in range(line - 1):
 
         @pl.when(me > o)
@@ -982,7 +1142,7 @@
             move(o).wait_send()
 
 
-def attend_backward(x, middle, dy, dn2, w, ad, kept, info, tables):
+def attend_backward(x, middle, dy, dn2, w, kept, info, tables):
     line = lax.axis_size("tensor")
     rows, width = x.shape
     heads = width // HEAD_DIM
@@ -990,15 +1150,12 @@
     groups, low_rows = w["packed"].shape[0], w["packed"].shape[2]
     return pl.pallas_call(
         partial(attend_back_kernel, line, heads // KV_HEADS),
-        in_specs=[pl.BlockSpec(memory_space=pltpu.SMEM)] + [vspec()] * 18 + [hspec()],
-        out_specs=[vspec()] * 6,
+        in_specs=[pl.BlockSpec(memory_space=pltpu.SMEM)] + [vspec()] * 14 + [hspec()],
+        out_specs=[vspec()] * 3,
         out_shape=[
             jax.ShapeDtypeStruct((rows, width), F32),
-            jax.ShapeDtypeStruct((3 * RANK, width), F32),
-            jax.ShapeDtypeStruct((3 * RANK, width), F32),
-            jax.ShapeDtypeStruct((3 * RANK, width), F32),
-            jax.ShapeDtypeStruct((3 * RANK, width), F32),
-            jax.ShapeDtypeStruct((3 * RANK, kv_width), F32),
+            jax.ShapeDtypeStruct((rows, width), BF),
+            jax.ShapeDtypeStruct((7 * RANK, width), BF),
         ],
         scratch_shapes=[
             pltpu.VMEM((line, groups, low_rows, width // line), BF),
@@ -1011,28 +1168,96 @@
             pltpu.VMEM((line, rows, kv_width), BF),
             pltpu.VMEM((line, rows, kv_width), BF),
             pltpu.VMEM((heads, 1, rows), F32),
+            pltpu.VMEM((3 * RANK, width), BF),
+            pltpu.VMEM((3 * RANK, kv_width), BF),
             pltpu.SemaphoreType.DMA((3, line)),
             pltpu.SemaphoreType.DMA((line,)),
             pltpu.SemaphoreType.DMA((line,)),
         ],
         compiler_params=pltpu.CompilerParams(
-            collective_id=3, has_side_effects=True, vmem_limit_bytes=VMEM_LIMIT
+            collective_id=3 if dy.dtype == F32 else 5, has_side_effects=True, vmem_limit_bytes=VMEM_LIMIT
         ),
         cost_estimate=pl.CostEstimate(
             flops=4 * rows * width * width * 2, bytes_accessed=5 * width * width, transcendentals=0
         ),
     )(
-        info, x, middle, dy, dn2, w["gain"], ad["low"], ad["q"], ad["kv"], ad["attend"], ad["res_one"],
-        tables[0], tables[1], *kept, w["packed"],
+        info, x, middle, dy, dn2, w["bundle"], tables[0], tables[1], *kept, w["packed"],
     )
+
+
+def total_kernel(
+    scale, hidden, q_cols,
+    first, second,
+    input_ref, query_ref, kv_ref, expand_ref, attend_ref, shrink_ref, res_ref,
+    block, sem,
+):
+    r = RANK
+    a = pl.program_id(0)
+    core = lax.axis_index("section")
+    width = block.shape[2]
+    extra = hidden - width
+    pad = extra + -hidden % (2 * LANES)
+
+    @pl.when(jnp.logical_and(a == 0, core == 0))
+    def _():
+        load = pltpu.make_async_copy(first, block, sem)
+        load.start()
+        load.wait()
+
+    @pl.when(jnp.logical_and(a == 0, core != 0))
+    def _():
+        load = pltpu.make_async_copy(second, block, sem)
+        load.start()
+        load.wait()
+
+    lane = lax.broadcasted_iota(jnp.int32, (1, LANES), 1)
+    weights = []
+    for i in range(block.shape[0]):
+        names = block[i, 13 * r : 14 * r, pad : pad + LANES][:1].astype(F32)
+        weights.append(jnp.sum(jnp.where(lane == a, names, 0.0), axis=1, keepdims=True) * scale)
+
+    def summed(row, rows, col, cols):
+        result = weights[0] * block[0, row : row + rows, col : col + cols].astype(F32)
+        for i in range(1, block.shape[0]):
+            result = result + weights[i] * block[i, row : row + rows, col : col + cols].astype(F32)
+        return result
+
+    step = 4 * LANES
+    for col in range(0, width, step):
+        input_ref[0, :, col : col + step] = summed(0, 5 * r, col, step)
+    res_ref[0, 0] = summed(5 * r, r, 0, width)
+    res_ref[0, 1] = summed(6 * r, r, 0, width)
+    kv = summed(7 * r, r, 0, 2 * kv_ref.shape[3])
+    kv_ref[0, 0] = kv[:, : kv_ref.shape[3]]
+    kv_ref[0, 1] = kv[:, kv_ref.shape[3] :]
+    for i in range(2):
+        expand_ref[0, i, :, :width] = summed((8 + i) * r, r, 0, width)
+        expand_ref[0, i, :, width:] = summed((11 + i) * r, r, 0, pad)[:, :extra]
+    shrink_ref[0, :, :width] = summed(10 * r, r, 0, width)
+    shrink_ref[0, :, width:] = summed(13 * r, r, 0, pad)[:, :extra]
+    query_ref[0] = summed(11 * r, r, pad, q_cols)
+    attend_ref[0] = summed(12 * r, r, pad, q_cols)
+
+
+def total_by_adapter(first, second, count, scale, hidden, q_cols, kv_half):
+    width = first.shape[2]
+    r = RANK
+    shapes = [
+        (5 * r, width), (r, q_cols), (2, r, kv_half), (2, r, hidden), (r, q_cols), (r, hidden), (2, r, width),
+    ]
+    return pl.pallas_call(
+        partial(total_kernel, scale, hidden, q_cols),
+        grid=(count,),
+        in_specs=[hspec()] * 2,
+        out_specs=[pl.BlockSpec((1,) + s, lambda a, n=len(s): (a,) + (0,) * n) for s in shapes],
+        out_shape=[jax.ShapeDtypeStruct((count,) + s, F32) for s in shapes],
+        scratch_shapes=[pltpu.VMEM(first.shape, BF), pltpu.SemaphoreType.DMA],
+        compiler_params=pltpu.CompilerParams(vmem_limit_bytes=VMEM_LIMIT),
+    )(first, second)
 
 
 def swap(pair):
     return lax.all_to_all(pair, "section", split_axis=0, concat_axis=0, tiled=True)
-
-
-def at_rows(a, first, rows):
-    return jnp.pad(a, [(first, rows - first - a.shape[0]), (0, 0)])
 
 
 def local(
@@ -1064,71 +1289,47 @@
     tokens = layers * rows * tensor * lax.axis_size("dp")
     kv_half = KV_HEADS * HEAD_DIM
     hidden = expand_weight.shape[3]
-    padding = -hidden % (2 * LANES)
     r = RANK
 
-    def padded(m):
-        return jnp.pad(m, [(0, 0)] * (m.ndim - 1) + [(0, padding)])
-
+    def turned(stack):
+        return jnp.swapaxes(stack[0], 1, 2)
+
+    def lined(stack):
+        return stack[0].reshape(stack.shape[1], -1, stack.shape[-1])
+
+    bundles, heads = pick_adapters(
+        adapter_ids,
+        (
+            turned(adapter_input), lined(adapter_residual), lined(adapter_keyvalue), lined(adapter_expand),
+            turned(adapter_shrink), adapter_query[0], turned(adapter_attend),
+        ),
+        (norm_gain[0], keyvalue_bias.reshape(1, -1), query_bias),
+    )
+
+    ff = jnp.concatenate(
+        [m.reshape(layers, 1, hidden // layers, m.shape[1]) for m in (*turned(expand_weight), shrink_weight[0])],
+        axis=1,
+    )
+    ff = swap(ff)
     kv = jnp.concatenate([keyvalue_weight[0, 0], keyvalue_weight[0, 1]], axis=1)
     kv_cols = kv.shape[1] // tensor
     kv = lax.dynamic_slice_in_dim(kv, place * kv_cols, kv_cols, 1)
     attn = jnp.concatenate([query_weight[0], output_weight[0].T, kv], axis=1)
     q_cols = query_weight.shape[2]
-    part = attn.shape[0] // layers
-    attn = swap(attn.reshape(layers, part, attn.shape[1]))
-    mlp = padded(jnp.concatenate([expand_weight[0], shrink_weight[0].T[None]], axis=0))
-    mlp = swap(jnp.swapaxes(mlp.reshape(3, layers, part, mlp.shape[2]), 0, 1))
-    every = ("dp", "section")
-    small = jnp.concatenate([norm_gain[0, 0], norm_gain[0, 1], keyvalue_bias[0].reshape(-1)], axis=0)
-    small = swap(jnp.broadcast_to(small[None], (layers,) + small.shape)).astype(F32)
-
-    def pick(stack):
-        chosen = jnp.stack(
-            [lax.dynamic_index_in_dim(stack[0], adapter_ids[i], 0, keepdims=False) for i in range(layers)]
-        )
-        return swap(chosen)
-
-    heads_part = jnp.concatenate(
-        [adapter_query[0], jnp.swapaxes(adapter_attend[0], 1, 2)]
-        + [jnp.pad(query_bias[0][None, None], [(0, adapter_query.shape[1] - 1), (0, r - 1), (0, 0)], mode="edge")],
-        axis=1,
-    )
-    heads_part = pick(heads_part[None])
-    first_attn, line_attn, heads_part = gather_first(attn, heads_part.reshape(-1, q_cols))
-    heads_part = jnp.moveaxis(heads_part.reshape(tensor, layers, 3 * r, q_cols), 0, 2)
-    heads_part = heads_part.reshape(layers, 3 * r, width)
+    attn = swap(attn.reshape(layers, attn.shape[0] // layers, attn.shape[1]))
+    first_attn, line_attn, bundle = gather_first(attn, bundles, heads)
 
     def weights(layer):
-        packed = first_attn if layer == 0 else lax.all_gather(line_attn, every, axis=0)
-        return dict(
-            gain=small[layer, : 2 * width].reshape(2, width),
-            packed=packed,
-            mlp=lax.all_gather(mlp[layer], every, axis=0),
-            kv_bias=small[layer, 2 * width :][None],
-        )
-
-    low_high, keyvalue, expand, shrink, residual = (
-        pick(stack) for stack in (adapter_input, adapter_keyvalue, adapter_expand, adapter_shrink, adapter_residual)
-    )
-    def adapters(layer):
-        return dict(
-            low=low_high[layer, :, : 3 * r],
-            high=low_high[layer, :, 3 * r :],
-            q=at_rows(heads_part[layer, :r], 0, 3 * r),
-            attend=at_rows(heads_part[layer, r : 2 * r], 0, 3 * r),
-            q_bias=heads_part[layer, 2 * r : 2 * r + 1].astype(F32),
-            kv=jnp.concatenate(
-                [at_rows(keyvalue[layer, 0], r, 3 * r), at_rows(keyvalue[layer, 1], 2 * r, 3 * r)], axis=1
-            ),
-            expand=jnp.stack([at_rows(padded(expand[layer, i]), i * r, 2 * r) for i in range(2)]),
-            shrink=padded(shrink[layer].T),
-            res_one=at_rows(residual[layer, 0], 0, 3 * r),
-            res_two=residual[layer, 1],
-        )
-
-    x = lax.dynamic_index_in_dim(inputs, core, 0, keepdims=False).astype(F32)
-    cot = lax.dynamic_index_in_dim(cotangent, core, 0, keepdims=False).astype(F32)
+        packed = first_attn if layer == 0 else lax.all_gather(line_attn, ("dp", "section"), axis=0)
+        mlp = lax.all_gather(ff[layer], ("section", "dp"), axis=0)
+        mlp = mlp.reshape(layers, -1, *mlp.shape[1:])
+        if mlp.shape[4] % LANES:
+            mlp = jnp.moveaxis(mlp, 1, 3)
+            mlp = mlp.reshape(layers, 1, *mlp.shape[1:3], width)
+        return dict(packed=packed, mlp=mlp, bundle=bundle[layer])
+
+    x = lax.dynamic_index_in_dim(inputs, core, 0, keepdims=False)
+    cot = lax.dynamic_index_in_dim(cotangent, core, 0, keepdims=False)
     length = lax.dynamic_index_in_dim(lengths, core, 0, keepdims=False)
     own_id = lax.dynamic_index_in_dim(adapter_ids, core, 0, keepdims=False)
     first_slot = place * rows
@@ -1137,65 +1338,54 @@
     slot_ids = first_slot + jnp.arange(rows, dtype=jnp.int32)
 
     w = [weights(layer) for layer in range(layers)]
-    ad = [adapters(layer) for layer in range(layers)]
     outs, kept = [], []
     for layer in range(layers):
-        middle, normed_two, attn_kept = attend_forward(x, w[layer], ad[layer], info, tables)
-        shrunk, mlp_kept = mlp_forward(normed_two, w[layer], ad[layer])
+        middle, normed_two, attn_kept = attend_forward(x, w[layer], info, tables)
+        shrunk, mlp_kept = mlp_forward(normed_two, w[layer])
         outs.append((middle + shrunk).astype(BF))
         kept.append((x, middle, attn_kept, mlp_kept))
-        x = outs[-1].astype(F32)
+        x = outs[-1]
     count = adapter_input.shape[1]
-    pad_one = jnp.zeros((r, width - 2 * kv_half), F32)
-    chosen_row = at_rows(
-        jnp.pad((jnp.arange(count, dtype=jnp.int32) == own_id).astype(BF)[None], [(0, 0), (0, width - count)]), 0, 8
-    )
-    grad = cot * (slot_ids < length).astype(F32)[:, None]
+    extra = hidden + -hidden % (2 * LANES) - width
+    names = (jnp.arange(LANES, dtype=jnp.int32) == own_id).astype(BF)[None]
+
+    def gather_block(attn_part, whole, parts):
+        mine = lax.dynamic_slice_in_dim(attn_part[5 * r :], place * q_cols, q_cols, 1)
+        parts = lax.dynamic_update_slice(parts, mine, (3 * r, extra))
+        parts = lax.dynamic_update_slice(parts, names, (5 * r, extra))
+        block = jnp.concatenate(
+            [attn_part[: 3 * r], whole[: 2 * r], attn_part[3 * r : 4 * r], whole[2 * r :], attn_part[4 * r : 5 * r]]
+            + [parts],
+            axis=0,
+        )
+        return lax.all_gather(block, ("section", "dp"), axis=0)
+
+    grad = low_grad = jnp.where((slot_ids < length)[:, None], cot, jnp.zeros_like(cot))
     grads, gathered = [None] * layers, [None] * layers
     for layer in reversed(range(layers)):
         x, middle, attn_kept, mlp_kept = kept[layer]
         if layer < layers - 1:
-            grad, whole_here = lax.optimization_barrier((grad, whole_here))
-        dn2, g_high, g_expand, g_shrink, g_res_two = mlp_backward(grad.astype(BF), w[layer], ad[layer], mlp_kept)
-        grad, g_low, g_res_one, g_q, g_attend, g_kv = attend_backward(
-            x, middle, grad, dn2, w[layer], ad[layer], attn_kept, info, tables
-        )
+            low_grad, here = lax.optimization_barrier((low_grad, here))
+        dn2, whole, parts = mlp_backward(low_grad, w[layer], mlp_kept)
+        if layer < layers - 1:
+            total, dn2 = lax.optimization_barrier((total, dn2))
+            gathered[layer + 1] = gather_block(*total, last_parts)
+        grad, low_grad, attn_part = attend_backward(x, middle, grad, dn2, w[layer], attn_kept, info, tables)
         grads[layer] = grad
-        g_kv = jnp.concatenate([g_kv[r : 2 * r, :kv_half], g_kv[2 * r :, kv_half:], pad_one], axis=1)
-        whole_here = jnp.concatenate(
-            [g_low, g_high, g_res_one[:r], g_res_two, g_kv, g_q[:r], g_attend[:r]], axis=0
-        ).astype(BF)
+        here = (attn_part, whole)
         if layer < layers - 1:
-            whole_here, gathered[layer + 1] = lax.optimization_barrier((whole_here, gathered[layer + 1]))
-        whole = lax.psum(whole_here, "tensor")
-        mine = lax.dynamic_slice_in_dim(whole[8 * r :], place * q_cols, q_cols, 1)
-        parts = jnp.concatenate([g_expand, g_shrink], axis=0).astype(BF)
-        block = jnp.concatenate(
-            [whole[: 8 * r], mine.reshape(-1, width), parts.reshape(-1, width), chosen_row], axis=0
-        )
-        gathered[layer] = lax.all_gather(block, ("section", "dp"), axis=0)
+            here, gathered[layer + 1] = lax.optimization_barrier((here, gathered[layer + 1]))
+        total = lax.psum(here, "tensor")
+        last_parts = parts
+    gathered[0] = gather_block(*total, parts)
     layer_output = swap(jnp.stack(outs))
     input_grad = swap(jnp.stack(grads))
-
-    block = jnp.where(core == 0, gathered[0], gathered[1])
-    pick_matrix = block[:, -8, :count]
-    total = jnp.einsum("sa,srw->arw", pick_matrix, block[:, :-8], preferred_element_type=F32)
-    total = total * (1.0 / math.sqrt(tokens))
-    q_rows = 2 * r * q_cols // width
-    heads_sum = total[:, 8 * r : 8 * r + q_rows].reshape(count, 2 * r, q_cols)
-    ff_sum = total[:, 8 * r + q_rows :].reshape(count, 3 * r, hidden + padding)[..., :hidden]
-    kv_sum = total[:, 7 * r : 8 * r]
-    return (
-        layer_output[None],
-        input_grad[None],
-        jnp.swapaxes(total[:, : 5 * r], 1, 2)[None],
-        heads_sum[:, :r][None],
-        jnp.stack([kv_sum[..., :kv_half], kv_sum[..., kv_half : 2 * kv_half]], axis=1)[None],
-        jnp.stack([ff_sum[:, :r], ff_sum[:, r : 2 * r]], axis=1)[None],
-        jnp.swapaxes(heads_sum[:, r:], 1, 2)[None],
-        jnp.swapaxes(ff_sum[:, 2 * r :], 1, 2)[None],
-        jnp.stack([total[:, 5 * r : 6 * r], total[:, 6 * r : 7 * r]], axis=1)[None],
+    totals = total_by_adapter(
+        gathered[0], gathered[1], count, 1.0 / math.sqrt(tokens), hidden, q_cols, kv_half
     )
+    turned = (0, 4, 5)
+    totals = [jnp.swapaxes(total, 1, 2) if i in turned else total for i, total in enumerate(totals)]
+    return (layer_output[None], input_grad[None]) + tuple(total[None] for total in totals)
 
 
 def solution(mesh):

time: 955 us -> 882 us (0.924)
  waiting for transfers between devices: 115 us -> 157 us
  local copies, waits for them, and re-layouts: 72.2 us -> 31.9 us
  other arithmetic: 41.6 us -> 11.7 us
  starting transfers between devices: 23.9 us -> 3.8 us
  Pallas kernels: 645 us -> 634 us
    all_gather x5, waiting for transfers between devices: 36 us -> 116 us  [the longest x2 83.6 us: weights(): mlp = lax.all_gather(ff[layer], ('section', 'dp'), axis=0)]
    psum x2, waiting for transfers between devices: 77.6 us -> 40.3 us  [local(): total = lax.psum(here, 'tensor')]
    pallas_call x2, Pallas kernels: 236 us -> 203 us  [mlp_forward(): pl.pallas_call(partial(mlp_kernel, line, CHUNKS, ff_tile(hidden)), in_spe...]
    all_to_all x7 -> x1, starting transfers between devices: 23.6 us -> 3.52 us  [swap(): lax.all_to_all(pair, 'section', split_axis=0, concat_axis=0, tiled=True)]
    pallas_call x2, Pallas kernels: 198 us -> 213 us  [mlp_backward(): pl.pallas_call(partial(mlp_back_kernel, line, CHUNKS, ff_tile(hidden)), i...]
    pallas_call x0 -> x2, Pallas kernels: none -> 14.6 us  [the longest x1 11.4 us: total_by_adapter(): pl.pallas_call(partial(total_kernel, scale, hidden, q_cols), grid=(count,...]
    unnamed x96 -> x57, local copies, waits for them, and re-layouts: 33.5 us -> 20 us
    all_to_all x4 -> x3, blocking collectives: 26.3 us -> 20.4 us  [swap(): lax.all_to_all(pair, 'section', split_axis=0, concat_axis=0, tiled=True)]
  transfers between devices with their start and end apart: 14 -> 8, of which waited for: 5 -> 5; matrix products, arithmetic and copies ran while one was open for 5% -> 2% of each run, Pallas kernels for 42% -> 44%
where the time goes in v4:
time: 882 us; the launch traced here: 874 us
  Pallas kernels  634 us (72%)
  waiting for transfers between devices  157 us (18%)
  local copies, waits for them, and re-layouts  31.9 us (4%)
  blocking collectives  20.4 us (2%)
  between operations  14.8 us (2%)
  other arithmetic  11.7 us (1%)
    pallas_call x2, Pallas kernels, mlp_backward(): pl.pallas_call(partial(mlp_back_kernel, line, CHUNKS, ff_tile(hidden)), i...  213 us
    pallas_call x2, Pallas kernels, mlp_forward(): pl.pallas_call(partial(mlp_kernel, line, CHUNKS, ff_tile(hidden)), in_spe...  203 us
    pallas_call x1, Pallas kernels, gather_first(): pl.pallas_call(partial(gather_kernel, line, peers), in_specs=[hspec()] *...  95.2 us
    all_gather x2, waiting for transfers between devices, weights(): mlp = lax.all_gather(ff[layer], ('section', 'dp'), axis=0)  83.6 us
    pallas_call x2, Pallas kernels, attend_backward(): pl.pallas_call(partial(attend_back_kernel, line, heads // KV_HEADS), in_s...  72.4 us
    psum x2, waiting for transfers between devices, local(): total = lax.psum(here, 'tensor')  40.3 us
    pallas_call x2, Pallas kernels, attend_forward(): pl.pallas_call(partial(attend_kernel, line, heads // KV_HEADS), in_specs=...  36.7 us
    all_gather x2, waiting for transfers between devices, gather_block(): return lax.all_gather(block, ('section', 'dp'), axis=0)  32.7 us
  transfers between devices with their start and end apart: 8, of which 5 were waited for; matrix products, arithmetic and copies ran while one was open for 2% of the time, Pallas kernels for 44%

profile of v4, /device:TPU:0, one launch (start us, length us, event | category | flops | bytes accessed | tf_op | source)
XLA Modules:
  0.0 874.5 jit_solution(14320307003459117070)
XLA Ops:
  7.2 2.5 fusion.7
  10.9 7.9 all_to_all.20
  18.7 2.8 fusion.6
  23.8 3.5 all-to-all-start
  28.0 3.2 shard_map.250
  32.0 95.2 %shard_map.251 = (bf16[8,4,192,896]{3,2,1,0:T(8,128)(2,1)}, bf16[4,192,896]{2,1,0:T(8,128)(2,1)}, bf16[2,288,1536]{2,1,0:T(8,128)(2,1)}) custom-call(bf16[2,192,896]{2,1,0:T(8,128)(2,1)} %copy-done.7, bf16[2,288,1536]{2,1,0:T(8,128)(2,1)} %get-tuple-element.65.bundles, bf16[2,48,384]{2,1,0:T(8,128)(2,1)} %get-tuple-element.66.heads), custom_call_target="tpu_custom_call" | custom-call | tf_op jit(solution)/shard_map/pallas_call | solution.py:760
  136.1 19.1 %shard_map.252 = (f32[256,1536]{1,0:T(8,128)}, bf16[256,1536]{1,0:T(8,128)(2,1)}, bf16[256,1536]{1,0:T(8,128)(2,1)}, bf16[256,48]{1,0:T(8,128)(2,1)}, bf16[256,1...) custom-call(s32[2]{0:T(128)} %pad_add_fusion.info_ref, ...), custom_call_target="tpu_custom_call" | custom-call | flops 4831838208 | bytes 11796480 | tf_op jit(solution)/shard_map/pallas_call | solution.py:964
  157.3 29.0 %all-gather.9.cloned.1.call-done = bf16[8,3,1120,384]{3,2,1,0:T(8,128)(2,1)} async-done(((bf16[1,3,1120,384]{3,2,1,0:T(8,128)(2,1)}), bf16[8,3,1120,384]{3,2,1,0:T(8,128)(2,1)}) %all-gather.9.cloned.1.call-update) | async-done | bytes 20643856 | tf_op jit(solution)/shard_map/all_gather | solution.py:1324
  186.3 101.6 %shard_map.253 = (f32[4,64,1536]{2,1,0:T(8,128)}, bf16[4,4,64,1536]{3,2,1,0:T(8,128)(2,1)}, bf16[4,256,2304]{2,1,0:T(8,128)(2,1)}, bf16[4,256,2304]{2,1,0:T(8,128)(2,1)}) custom-call(bf16[4,64,1536]{2,1,0:T(8,128)(2,1)} %bitcast.128, bf16[2,4,3,1120,384]{4,3,2,1,0:T(8,128)(2,1)} %bitcast.114, bf16[288,1536]{1,0:T(8,128)(2,1)} %get-tuple-element.132.bundle_ref), custom_call_target="tpu_custom_call" | custom-call | flops 21743271936 | bytes 30670848 | tf_op jit(solution)/shard_map/pallas_call | solution.py:384
  287.9 2.5 fusion.1.x_ref
  290.4 17.6 %shard_map.254 = (f32[256,1536]{1,0:T(8,128)}, bf16[256,1536]{1,0:T(8,128)(2,1)}, bf16[256,1536]{1,0:T(8,128)(2,1)}, bf16[256,48]{1,0:T(8,128)(2,1)}, bf16[256,1...) custom-call(s32[2]{0:T(128)} %pad_add_fusion.info_ref, ...), custom_call_target="tpu_custom_call" | custom-call | flops 4831838208 | bytes 11796480 | tf_op jit(solution)/shard_map/pallas_call | solution.py:964
  308.0 54.5 %all-gather.11.cloned.1.call-done = bf16[8,3,1120,384]{3,2,1,0:T(8,128)(2,1)} async-done(((bf16[1,3,1120,384]{3,2,1,0:T(8,128)(2,1)}), bf16[8,3,1120,384]{3,2,1,0:T(8,128)(2,1)}) %all-gather.11.cloned.1.call-update) | async-done | bytes 20643856 | tf_op jit(solution)/shard_map/all_gather | solution.py:1324
  362.5 101.4 %shard_map.255 = (f32[4,64,1536]{2,1,0:T(8,128)}, bf16[4,4,64,1536]{3,2,1,0:T(8,128)(2,1)}, bf16[4,256,2304]{2,1,0:T(8,128)(2,1)}, bf16[4,256,2304]{2,1,0:T(8,128)(2,1)}) custom-call(bf16[4,64,1536]{2,1,0:T(8,128)(2,1)} %bitcast.129, bf16[2,4,3,1120,384]{4,3,2,1,0:T(8,128)(2,1)} %bitcast.116, bf16[288,1536]{1,0:T(8,128)(2,1)} %get-tuple-element.131.bundle_ref), custom_call_target="tpu_custom_call" | custom-call | flops 21743271936 | bytes 30670848 | tf_op jit(solution)/shard_map/pallas_call | solution.py:384
  463.9 97.7 %shard_map.256 = (f32[4,64,1536]{2,1,0:T(8,128)}, bf16[48,1536]{1,0:T(8,128)(2,1)}, bf16[96,1536]{1,0:T(8,128)(2,1)}) custom-call(bf16[4,64,1536]{2,1,0:T(8,128)(2,1)} %broadcast_select_fusion.ds_ref, bf16[2,4,3,1120,384]{4,3,2,1,0:T(8,128)(2,1)} %bitcast.117, bf16[4,256,1536]{2,1,0:T(8,128)(2,1)} %bitcast.127, ...), custom_call_target="tpu_custom_call" | custom-call | flops 21743271936 | bytes 30670848 | tf_op jit(solution)/shard_map/pallas_call | solution.py:540
  561.5 36.5 %shard_map.257 = (f32[256,1536]{1,0:T(8,128)}, bf16[256,1536]{1,0:T(8,128)(2,1)}, bf16[112,1536]{1,0:T(8,128)(2,1)}) custom-call(s32[2]{0:T(128)} %pad_add_fusion.info_ref, bf16[256,1536]{1,0:T(8,128)(2,1)} %fusion.1.x_ref, f32[256,1536]{1,0:T(8,128)} %get-tuple-element.73.mid_ref, bf16[256,1536]{1,0:T(8,128)(2,1)} %get-tuple-element.125.dy_ref, ...), custom_call_target="tpu_custom_call" | custom-call | flops 4831838208 | bytes 11796480 | tf_op jit(solution)/shard_map/pallas_call | solution.py:1151
  598.2 115.0 %shard_map.258 = (f32[4,64,1536]{2,1,0:T(8,128)}, bf16[48,1536]{1,0:T(8,128)(2,1)}, bf16[96,1536]{1,0:T(8,128)(2,1)}) custom-call(bf16[4,64,1536]{2,1,0:T(8,128)(2,1)} %bitcast.122, bf16[2,4,3,1120,384]{4,3,2,1,0:T(8,128)(2,1)} %bitcast.115, bf16[4,256,1536]{2,1,0:T(8,128)(2,1)} %bitcast.126, bf16[4,256,2304]{2,1,0:T(8,128)(2,1)} %get-tuple-element.93.gate_in, ...), custom_call_target="tpu_custom_call" | custom-call | flops 21743271936 | bytes 30670848 | tf_op jit(solution)/shard_map/pallas_call | solution.py:540
  719.5 35.9 %shard_map.259 = (f32[256,1536]{1,0:T(8,128)}, bf16[256,1536]{1,0:T(8,128)(2,1)}, bf16[112,1536]{1,0:T(8,128)(2,1)}) custom-call(s32[2]{0:T(128)} %pad_add_fusion.info_ref, bf16[256,1536]{1,0:T(8,128)(2,1)} %dynamic-slice_bitcast_fusion.x_ref, f32[256,1536]{1,0:T(8,128)} %get-tuple-element.69.mid_ref, f32[256,1536]{1,0:T(8,128)} %get-tuple-element.87.dy_ref, ...), custom_call_target="tpu_custom_call" | custom-call | flops 4831838208 | bytes 11796480 | tf_op jit(solution)/shard_map/pallas_call | solution.py:1151
  755.4 4.6 all-gather.15.cloned.1.call-done
  760.1 40.3 %all-reduce.5.cloned.1.call-done = (bf16[112,1536]{1,0:T(8,128)(2,1)}, bf16[48,1536]{1,0:T(8,128)(2,1)}) async-done(((bf16[112,1536]{1,0:T(8,128)(2,1)}, bf16[48,1536]{1,0:T(8,128)(2,1)}), (bf16[112,1536]{1,0:T(8,128)(2,1)}, bf16[48,1536]{1,0:T(8,128)(2,1)})) %all-reduce.5.cloned.1.call-update) | async-done | bytes 491536 | tf_op jit(solution)/shard_map/psum | solution.py:1378
  811.0 5.3 all_to_all.21
  816.5 7.3 all_to_all.22
  823.8 28.1 %all-gather.17.cloned.1.call-done = bf16[1792,1536]{1,0:T(8,128)(2,1)} async-done(((bf16[224,1536]{1,0:T(8,128)(2,1)}), bf16[1792,1536]{1,0:T(8,128)(2,1)}) %all-gather.17.cloned.1.call-update) | async-done | bytes 5505040 | tf_op jit(solution)/shard_map/all_gather | solution.py:1361
  851.9 11.4 %shard_map.260 = (f32[8,80,1536]{2,1,0:T(8,128)}, f32[8,16,384]{2,1,0:T(8,128)}, f32[8,2,16,256]{3,2,1,0:T(8,128)}, f32[8,2,16,2240]{3,2,1,0:T(8,128)}, f32[8,16...) custom-call(bf16[8,224,1536]{2,1,0:T(8,128)(2,1)} %bitcast.92, bf16[8,224,1536]{2,1,0:T(8,128)(2,1)} %bitcast.91), custom_call_target="tpu_custom_call" | custom-call | tf_op jit(solution)/shard_map/pallas_call | solution.py:1248
  865.7 1.7 copy.55
  (103 shorter events, 35.2 us)
Async XLA Ops:
  7.2 126.7 %copy-start = (bf16[2,256,1536]{2,1,0:T(8,128)(2,1)S(1)}, bf16[2,256,1536]{2,1,0:T(8,128)(2,1)}, u32[]{:S(2)}) copy-start(bf16[2,256,1536]{2,1,0:T(8,128)(2,1)} %param.19) | copy-start | bytes 4718596
  7.2 179.1 %all-gather.9.cloned.1.call-start = ((), (), s32[]{:S(2)}) async-start(), calls=%async_computation.4 | async-start | bytes 23224320 | tf_op jit(solution)/shard_map/all_gather | solution.py:1324
  7.2 2.6 copy-start.9
  21.6 1.3 copy-start.18
  22.8 4.6 copy-start.19
  23.8 7.3 all-to-all-start
  27.3 263.1 %all-gather.13.cloned.1.call-start = ((), (), s32[]{:S(2)}) async-start(), calls=%async_computation.6 | async-start | bytes 12386304 | tf_op jit(solution)/shard_map/all_gather | solution.py:1323
  127.2 1.4 copy-start.21
  127.2 235.3 %all-gather.11.cloned.1.call-start = ((), (), s32[]{:S(2)}) async-start(), calls=%async_computation.5 | async-start | bytes 23224320 | tf_op jit(solution)/shard_map/all_gather | solution.py:1324
  128.0 6.8 copy-start.8
  128.0 585.2 %all-reduce.7.cloned.1.call-start = ((), (), s32[]{:S(2)}) async-start(), calls=%async_computation.10 | async-start | bytes 983040 | tf_op jit(solution)/shard_map/psum | solution.py:1378
  136.1 19.1 %copy-start.14 = (bf16[2,256,1536]{2,1,0:T(8,128)(2,1)S(1)}, bf16[2,256,1536]{2,1,0:T(8,128)(2,1)}, u32[]{:S(2)}) copy-start(bf16[2,256,1536]{2,1,0:T(8,128)(2,1)} %param.22) | copy-start | bytes 4718596
  186.3 101.6 %copy-start.6 = (f32[256,1536]{1,0:T(8,128)S(1)}, f32[256,1536]{1,0:T(8,128)}, u32[]{:S(2)}) copy-start(f32[256,1536]{1,0:T(8,128)} %get-tuple-element.69.mid_ref) | copy-start | bytes 4718596
  598.1 161.9 %all-gather.15.cloned.1.call-start = ((), (), s32[]{:S(2)}) async-start(), calls=%async_computation.7 | async-start | bytes 6193152 | tf_op jit(solution)/shard_map/all_gather | solution.py:1361
  598.2 120.2 %copy-start.17 = (bf16[96,1536]{1,0:T(8,128)(2,1)S(1)}, bf16[96,1536]{1,0:T(8,128)(2,1)}, u32[]{:S(2)}) copy-start(bf16[96,1536]{1,0:T(8,128)(2,1)} %get-tuple-element.109) | copy-start | bytes 884740
  719.5 81.0 %all-reduce.5.cloned.1.call-start = ((), (), s32[]{:S(2)}) async-start(), calls=%async_computation.9 | async-start | bytes 983040 | tf_op jit(solution)/shard_map/psum | solution.py:1378
  719.5 83.4 %copy-start.16 = (bf16[96,1536]{1,0:T(8,128)(2,1)S(1)}, bf16[96,1536]{1,0:T(8,128)(2,1)}, u32[]{:S(2)}) copy-start(bf16[96,1536]{1,0:T(8,128)(2,1)} %get-tuple-element.112) | copy-start | bytes 884740
  719.5 90.1 %copy-start.10 = (f32[4,64,1536]{2,1,0:T(8,128)S(1)}, f32[4,64,1536]{2,1,0:T(8,128)}, u32[]{:S(2)}) copy-start(f32[4,64,1536]{2,1,0:T(8,128)} %get-tuple-element.75) | copy-start | bytes 4718596
  755.4 54.2 %copy-start.4 = (f32[256,1536]{1,0:T(8,128)S(1)}, f32[256,1536]{1,0:T(8,128)}, u32[]{:S(2)}) copy-start(f32[256,1536]{1,0:T(8,128)} %get-tuple-element.73.mid_ref) | copy-start | bytes 4718596
  760.0 91.8 %all-gather.17.cloned.1.call-start = ((), (), s32[]{:S(2)}) async-start(), calls=%async_computation.8 | async-start | bytes 6193152 | tf_op jit(solution)/shard_map/all_gather | solution.py:1361
  811.0 5.3 copy-start.5
  811.0 5.3 copy-start.11
  863.3 2.5 copy-start.2
  863.3 4.1 copy-start.1
  (6 other events, 5.8 us)
Sparse Core Ops, SparseCore 0:
  21.7 164.5 all-gather.8
  188.2 65.4 all-gather.12
  256.2 106.2 all-gather.10
  598.2 45.1 all-reduce.6
  719.6 40.3 all-gather.14
  762.4 37.9 all-reduce.4
  809.8 42.0 all-gather.16

commit v5 on v4

--- a/solution.py
+++ b/solution.py
@@ -759,7 +759,7 @@
     dma = pltpu.SemaphoreType.DMA
     return pl.pallas_call(
         partial(gather_kernel, line, peers),
-        in_specs=[hspec()] * 3,
+        in_specs=[vspec()] * 3,
         out_specs=[hspec()] * 3,
         out_shape=[
             jax.ShapeDtypeStruct((peers * cores, line, part, cols), BF),
@@ -1185,6 +1185,247 @@
     )
 
 
+def reduce_kernel(
+    line, peers, extra,
+    attn_ref, whole_ref, parts_ref, names_ref, y_first, y_second, g_first, g_second,
+    out, y_out, g_out,
+    mine, z_in, quarter, z_recv, z_send, dp_recv, dp_send, own_sem, t_recv, t_right, t_left,
+    side_recv, side_send, side_own,
+):
+    r = RANK
+    me, spot, core = lax.axis_index("tensor"), lax.axis_index("dp"), lax.axis_index("section")
+    width = mine.shape[1]
+    cols = width // line
+    seqs = out.shape[0]
+    seq = spot * 2 + core
+    has_left, has_right = me > 0, me < line - 1
+    barrier = pltpu.get_barrier_semaphore()
+
+    def greet(**where):
+        pl.semaphore_signal(barrier, inc=1, device_id=where, device_id_type=MESH)
+
+    for k in range(1, line):
+        greet(tensor=lax.rem(me + k, line))
+
+    greet(section=1 - core)
+
+    @pl.when(core == 0)
+    def _():
+        for k in range(1, peers):
+            for c in range(2):
+                greet(section=c, dp=lax.rem(spot + k, peers))
+
+    pl.semaphore_wait(barrier, line - 1 + peers)
+
+    def remote(src, dst, send, recv, **where):
+        return pltpu.make_async_remote_copy(
+            src_ref=src, dst_ref=dst, send_sem=send, recv_sem=recv, device_id=where, device_id_type=MESH
+        )
+
+    def lanes(t):
+        return pl.ds(pl.multiple_of(t * cols, LANES), cols)
+
+    def pieces(s):
+        return (
+            (parts_ref.at[pl.ds(0, 3 * r)], out.at[s, pl.ds(8 * r, 3 * r)]),
+            (parts_ref.at[pl.ds(3 * r, 3 * r), pl.ds(0, extra)], out.at[s, pl.ds(11 * r, 3 * r), pl.ds(0, extra)]),
+            (names_ref, out.at[s, pl.ds(13 * r, r), pl.ds(extra, LANES)]),
+            (quarter.at[pl.ds(0, 8 * r)], out.at[s, pl.ds(0, 8 * r), lanes(me)]),
+            (quarter.at[pl.ds(8 * r, 2 * r)], out.at[s, pl.ds(11 * r, 2 * r), pl.ds(extra, cols)]),
+        )
+
+    def to_peer(k, i):
+        src, dst = pieces(seq)[i]
+        return remote(src, dst, dp_send.at[k, i], dp_recv.at[seq, i], section=0, dp=lax.rem(spot + k, peers))
+
+    def stay(i):
+        src, dst = pieces(seq)[i]
+        return pltpu.make_async_copy(src, dst, own_sem.at[i])
+
+    def send_pieces(which):
+        for i in which:
+            for k in range(1, peers):
+                to_peer(k, i).start()
+
+            @pl.when(core != 0)
+            def _():
+                to_peer(0, i).start()
+
+            @pl.when(core == 0)
+            def _():
+                stay(i).start()
+
+    def across(k):
+        to = lax.rem(me + k, line)
+        return remote(mine.at[:, lanes(to)], z_in.at[me], z_send.at[k], z_recv.at[me], tensor=to)
+
+    def incoming(k):
+        o = lax.rem(me + k, line)
+        return remote(mine.at[:, lanes(me)], z_in.at[o], z_send.at[k], z_recv.at[o], tensor=o)
+
+    def side(i, src, dst):
+        return remote(src, dst.at[core], side_send.at[i], side_recv.at[i], section=1 - core)
+
+    def side_keep(i, src, dst):
+        return pltpu.make_async_copy(src, dst.at[core], side_own.at[i])
+
+    pairs = ((y_first, y_second, y_out), (g_first, g_second, g_out))
+
+    for first, rows, ref, start in (
+        (0, 3, attn_ref, 0), (3, 2, whole_ref, 0), (5, 1, attn_ref, 3), (6, 1, whole_ref, 2), (7, 3, attn_ref, 4),
+    ):
+        mine[rows_of(first, rows)] = ref[rows_of(start, rows)]
+    for k in range(1, line):
+        across(k).start()
+    send_pieces((0, 1, 2))
+    for c in range(2):
+
+        @pl.when(core == c)
+        def _():
+            for i, (first, second, dst) in enumerate(pairs):
+                side(i, first if c == 1 else second, dst).start()
+                side_keep(i, second if c == 1 else first, dst).start()
+
+    total = mine[:, lanes(me)].astype(F32)
+    for k in range(1, line):
+        incoming(k).wait_recv()
+        total = total + z_in[lax.rem(me + k, line)].astype(F32)
+    quarter[...] = total.astype(BF)
+    send_pieces((3, 4))
+
+    def arrived(s, i):
+        src, dst = pieces(s)[i]
+        return remote(src, dst, dp_send.at[0, i], dp_recv.at[s, i], section=0)
+
+    def along(s, o, side):
+        place = out.at[s, pl.ds(0, 8 * r), lanes(o)]
+        return remote(
+            place, place, (t_right if side > 0 else t_left).at[s, o], t_recv.at[s, o], tensor=me + side
+        )
+
+    @pl.when(core == 0)
+    def _():
+        def own_rows(n, carry):
+            s = lax.rem(seq + n, seqs)
+
+            @pl.when(n == 0)
+            def _():
+                stay(3).wait()
+
+            @pl.when(n > 0)
+            def _():
+                arrived(s, 3).wait_recv()
+
+            @pl.when(has_right)
+            def _():
+                along(s, me, 1).start()
+
+            @pl.when(has_left)
+            def _():
+                along(s, me, -1).start()
+
+            return carry
+
+        lax.fori_loop(0, seqs, own_rows, 0)
+        for d in range(1, line):
+
+            def others(n, carry):
+                s = lax.rem(seq + n, seqs)
+
+                @pl.when(me >= d)
+                def _():
+                    along(s, me - d, 1).wait_recv()
+
+                    @pl.when(has_right)
+                    def _():
+                        along(s, me - d, 1).start()
+
+                @pl.when(me + d < line)
+                def _():
+                    along(s, me + d, -1).wait_recv()
+
+                    @pl.when(has_left)
+                    def _():
+                        along(s, me + d, -1).start()
+
+                return carry
+
+            lax.fori_loop(0, seqs, others, 0)
+
+        def finish(n, carry):
+            s = lax.rem(seq + n, seqs)
+
+            @pl.when(n > 0)
+            def _():
+                for i in (0, 1, 2, 4):
+                    arrived(s, i).wait_recv()
+
+            for o in range(line):
+
+                @pl.when(jnp.logical_and(has_right, me >= o))
+                def _():
+                    along(s, o, 1).wait_send()
+
+                @pl.when(jnp.logical_and(has_left, me <= o))
+                def _():
+                    along(s, o, -1).wait_send()
+
+            return carry
+
+        lax.fori_loop(0, seqs, finish, 0)
+        for i in (0, 1, 2, 4):
+            stay(i).wait()
+
+    for k in range(1, line):
+        across(k).wait_send()
+    for i in range(5):
+        for k in range(1, peers):
+            to_peer(k, i).wait_send()
+
+        @pl.when(core != 0)
+        def _():
+            to_peer(0, i).wait_send()
+    for i, (first, _, dst) in enumerate(pairs):
+        side(i, first, dst).wait()
+        side_keep(i, first, dst).wait()
+
+
+def reduce_first(attn_part, whole, parts, names, extra, outs, grads):
+    line, peers = lax.axis_size("tensor"), lax.axis_size("dp")
+    width = parts.shape[1]
+    seqs = 2 * peers
+    dma = pltpu.SemaphoreType.DMA
+    return pl.pallas_call(
+        partial(reduce_kernel, line, peers, extra),
+        in_specs=[vspec()] * 8,
+        out_specs=[hspec()] * 3,
+        out_shape=[
+            jax.ShapeDtypeStruct((seqs, 14 * RANK, width), BF),
+            jax.ShapeDtypeStruct((2,) + outs[0].shape, outs[0].dtype),
+            jax.ShapeDtypeStruct((2,) + grads[0].shape, grads[0].dtype),
+        ],
+        scratch_shapes=[
+            pltpu.VMEM((10 * RANK, width), BF),
+            pltpu.VMEM((line, 10 * RANK, width // line), BF),
+            pltpu.VMEM((10 * RANK, width // line), BF),
+            dma((line,)),
+            dma((line,)),
+            dma((seqs, 5)),
+            dma((peers, 5)),
+            dma((5,)),
+            dma((seqs, line)),
+            dma((seqs, line)),
+            dma((seqs, line)),
+            dma((2,)),
+            dma((2,)),
+            dma((2,)),
+        ],
+        compiler_params=pltpu.CompilerParams(
+            collective_id=6, has_side_effects=True, vmem_limit_bytes=VMEM_LIMIT
+        ),
+    )(attn_part, whole, parts, names, *outs, *grads)
+
+
 def total_kernel(
     scale, hidden, q_cols,
     first, second,
@@ -1373,13 +1614,12 @@
         grad, low_grad, attn_part = attend_backward(x, middle, grad, dn2, w[layer], attn_kept, info, tables)
         grads[layer] = grad
         here = (attn_part, whole)
-        if layer < layers - 1:
-            here, gathered[layer + 1] = lax.optimization_barrier((here, gathered[layer + 1]))
-        total = lax.psum(here, "tensor")
-        last_parts = parts
-    gathered[0] = gather_block(*total, parts)
-    layer_output = swap(jnp.stack(outs))
-    input_grad = swap(jnp.stack(grads))
+        if layer > 0:
+            total = lax.psum(here, "tensor")
+            last_parts = parts
+    gathered[0], layer_output, input_grad = reduce_first(
+        *here, parts, jnp.pad(names, [(0, r - 1), (0, 0)]), extra, outs, grads
+    )
     totals = total_by_adapter(
         gathered[0], gathered[1], count, 1.0 / math.sqrt(tokens), hidden, q_cols, kv_half
     )

time: 882 us -> 839 us (0.951)
  waiting for transfers between devices: 157 us -> 81.9 us
  Pallas kernels: 634 us -> 686 us
  blocking collectives: 20.4 us -> 7.87 us
    pallas_call x1 -> x2, Pallas kernels: 95.2 us -> 147 us  [the longest x1 96.2 us: gather_first(): pl.pallas_call(partial(gather_kernel, line, peers), in_specs=[vspec()] *...]
    psum x2 -> x1, waiting for transfers between devices: 40.3 us -> 0.02 us  [local(): total = lax.psum(here, 'tensor')]
    all_gather x2 -> x1, waiting for transfers between devices: 32.7 us -> 0.02 us  [gather_block(): return lax.all_gather(block, ('section', 'dp'), axis=0)]
    all_to_all x3 -> x1, blocking collectives: 20.4 us -> 7.87 us  [swap(): lax.all_to_all(pair, 'section', split_axis=0, concat_axis=0, tiled=True)]
    unnamed x57 -> x44, local copies, waits for them, and re-layouts: 20 us -> 14.1 us
  transfers between devices with their start and end apart: 8 -> 6, of which waited for: 5 -> 2; matrix products, arithmetic and copies ran while one was open for 2% -> 2% of each run, Pallas kernels for 44% -> 53%
where the time goes in v5:
time: 839 us; the launch traced here: 832 us
  Pallas kernels  686 us (82%)
  waiting for transfers between devices  81.9 us (10%)
  local copies, waits for them, and re-layouts  25.5 us (3%)
  between operations  14.4 us (2%)
  other arithmetic  12.2 us (1%)
    pallas_call x2, Pallas kernels, mlp_backward(): pl.pallas_call(partial(mlp_back_kernel, line, CHUNKS, ff_tile(hidden)), i...  213 us
    pallas_call x2, Pallas kernels, mlp_forward(): pl.pallas_call(partial(mlp_kernel, line, CHUNKS, ff_tile(hidden)), in_spe...  202 us
    pallas_call x1, Pallas kernels, gather_first(): pl.pallas_call(partial(gather_kernel, line, peers), in_specs=[vspec()] *...  96.2 us
    all_gather x2, waiting for transfers between devices, weights(): mlp = lax.all_gather(ff[layer], ('section', 'dp'), axis=0)  81.1 us
    pallas_call x2, Pallas kernels, attend_backward(): pl.pallas_call(partial(attend_back_kernel, line, heads // KV_HEADS), in_s...  72.9 us
    pallas_call x1, Pallas kernels, reduce_first(): pl.pallas_call(partial(reduce_kernel, line, peers, extra), in_specs=[vspe...  50.5 us
    pallas_call x2, Pallas kernels, attend_forward(): pl.pallas_call(partial(attend_kernel, line, heads // KV_HEADS), in_specs=...  37.1 us
  transfers between devices with their start and end apart: 6, of which 2 were waited for; matrix products, arithmetic and copies ran while one was open for 2% of the time, Pallas kernels for 53%

profile of v5, /device:TPU:0, one launch (start us, length us, event | category | flops | bytes accessed | tf_op | source)
XLA Modules:
  0.0 831.7 jit_solution(6204645415328076530)
XLA Ops:
  7.2 2.5 fusion.7
  10.9 7.9 all_to_all.10
  18.7 2.8 fusion.6
  23.8 3.5 all-to-all-start
  28.0 3.2 shard_map.250
  32.0 96.2 %shard_map.251 = (bf16[8,4,192,896]{3,2,1,0:T(8,128)(2,1)}, bf16[4,192,896]{2,1,0:T(8,128)(2,1)}, bf16[2,288,1536]{2,1,0:T(8,128)(2,1)}) custom-call(bf16[2,192,896]{2,1,0:T(8,128)(2,1)} %copy-done.5, bf16[2,288,1536]{2,1,0:T(8,128)(2,1)} %get-tuple-element.65.bundles, bf16[2,48,384]{2,1,0:T(8,128)(2,1)} %get-tuple-element.66.heads), custom_call_target="tpu_custom_call" | custom-call | tf_op jit(solution)/shard_map/pallas_call | solution.py:760
  137.1 19.5 %shard_map.252 = (f32[256,1536]{1,0:T(8,128)}, bf16[256,1536]{1,0:T(8,128)(2,1)}, bf16[256,1536]{1,0:T(8,128)(2,1)}, bf16[256,48]{1,0:T(8,128)(2,1)}, bf16[256,1...) custom-call(s32[2]{0:T(128)} %pad_add_fusion.info_ref, ...), custom_call_target="tpu_custom_call" | custom-call | flops 4831838208 | bytes 11796480 | tf_op jit(solution)/shard_map/pallas_call | solution.py:964
  158.7 25.7 %all-gather.7.cloned.1.call-done = bf16[8,3,1120,384]{3,2,1,0:T(8,128)(2,1)} async-done(((bf16[1,3,1120,384]{3,2,1,0:T(8,128)(2,1)}), bf16[8,3,1120,384]{3,2,1,0:T(8,128)(2,1)}) %all-gather.7.cloned.1.call-update) | async-done | bytes 20643856 | tf_op jit(solution)/shard_map/all_gather | solution.py:1565
  184.4 100.6 %shard_map.253 = (f32[4,64,1536]{2,1,0:T(8,128)}, bf16[4,4,64,1536]{3,2,1,0:T(8,128)(2,1)}, bf16[4,256,2304]{2,1,0:T(8,128)(2,1)}, bf16[4,256,2304]{2,1,0:T(8,128)(2,1)}) custom-call(bf16[4,64,1536]{2,1,0:T(8,128)(2,1)} %bitcast.118, bf16[2,4,3,1120,384]{4,3,2,1,0:T(8,128)(2,1)} %bitcast.104, bf16[288,1536]{1,0:T(8,128)(2,1)} %get-tuple-element.130.bundle_ref), custom_call_target="tpu_custom_call" | custom-call | flops 21743271936 | bytes 30670848 | tf_op jit(solution)/shard_map/pallas_call | solution.py:384
  285.0 2.5 fusion.1.x_ref.y_first
  287.5 17.6 %shard_map.254 = (f32[256,1536]{1,0:T(8,128)}, bf16[256,1536]{1,0:T(8,128)(2,1)}, bf16[256,1536]{1,0:T(8,128)(2,1)}, bf16[256,48]{1,0:T(8,128)(2,1)}, bf16[256,1...) custom-call(s32[2]{0:T(128)} %pad_add_fusion.info_ref, ...), custom_call_target="tpu_custom_call" | custom-call | flops 4831838208 | bytes 11796480 | tf_op jit(solution)/shard_map/pallas_call | solution.py:964
  305.1 55.4 %all-gather.9.cloned.1.call-done = bf16[8,3,1120,384]{3,2,1,0:T(8,128)(2,1)} async-done(((bf16[1,3,1120,384]{3,2,1,0:T(8,128)(2,1)}), bf16[8,3,1120,384]{3,2,1,0:T(8,128)(2,1)}) %all-gather.9.cloned.1.call-update) | async-done | bytes 20643856 | tf_op jit(solution)/shard_map/all_gather | solution.py:1565
  360.5 101.3 %shard_map.255 = (f32[4,64,1536]{2,1,0:T(8,128)}, bf16[4,4,64,1536]{3,2,1,0:T(8,128)(2,1)}, bf16[4,256,2304]{2,1,0:T(8,128)(2,1)}, bf16[4,256,2304]{2,1,0:T(8,128)(2,1)}) custom-call(bf16[4,64,1536]{2,1,0:T(8,128)(2,1)} %bitcast.119, bf16[2,4,3,1120,384]{4,3,2,1,0:T(8,128)(2,1)} %bitcast.106, bf16[288,1536]{1,0:T(8,128)(2,1)} %get-tuple-element.129.bundle_ref), custom_call_target="tpu_custom_call" | custom-call | flops 21743271936 | bytes 30670848 | tf_op jit(solution)/shard_map/pallas_call | solution.py:384
  461.8 97.8 %shard_map.256 = (f32[4,64,1536]{2,1,0:T(8,128)}, bf16[48,1536]{1,0:T(8,128)(2,1)}, bf16[96,1536]{1,0:T(8,128)(2,1)}) custom-call(bf16[4,64,1536]{2,1,0:T(8,128)(2,1)} %broadcast_select_fusion.ds_ref, bf16[2,4,3,1120,384]{4,3,2,1,0:T(8,128)(2,1)} %bitcast.107, bf16[4,256,1536]{2,1,0:T(8,128)(2,1)} %bitcast.117, ...), custom_call_target="tpu_custom_call" | custom-call | flops 21743271936 | bytes 30670848 | tf_op jit(solution)/shard_map/pallas_call | solution.py:540
  559.6 36.5 %shard_map.257 = (f32[256,1536]{1,0:T(8,128)}, bf16[256,1536]{1,0:T(8,128)(2,1)}, bf16[112,1536]{1,0:T(8,128)(2,1)}) custom-call(s32[2]{0:T(128)} %pad_add_fusion.info_ref, bf16[256,1536]{1,0:T(8,128)(2,1)} %fusion.1.x_ref.y_first, f32[256,1536]{1,0:T(8,128)} %get-tuple-element.73.mid_ref, bf16[256,1536]{1,0:T(8,128)(2,1)} %get-tuple-element.123.dy_ref, ...), custom_call_target="tpu_custom_call" | custom-call | flops 4831838208 | bytes 11796480 | tf_op jit(solution)/shard_map/pallas_call | solution.py:1151
  596.2 115.0 %shard_map.258 = (f32[4,64,1536]{2,1,0:T(8,128)}, bf16[48,1536]{1,0:T(8,128)(2,1)}, bf16[96,1536]{1,0:T(8,128)(2,1)}) custom-call(bf16[4,64,1536]{2,1,0:T(8,128)(2,1)} %bitcast.112, bf16[2,4,3,1120,384]{4,3,2,1,0:T(8,128)(2,1)} %bitcast.105, bf16[4,256,1536]{2,1,0:T(8,128)(2,1)} %bitcast.116, bf16[4,256,2304]{2,1,0:T(8,128)(2,1)} %get-tuple-element.92.gate_in, ...), custom_call_target="tpu_custom_call" | custom-call | flops 21743271936 | bytes 30670848 | tf_op jit(solution)/shard_map/pallas_call | solution.py:540
  711.3 1.7 slice_dynamic-update-slice_fusion
  713.9 1.5 slice_dynamic-update-slice_fusion.1
  715.4 1.4 slice_dynamic-update-slice_fusion.4
  716.9 1.4 slice_dynamic-update-slice_fusion.3
  722.4 36.3 %shard_map.259 = (f32[256,1536]{1,0:T(8,128)}, bf16[256,1536]{1,0:T(8,128)(2,1)}, bf16[112,1536]{1,0:T(8,128)(2,1)}) custom-call(s32[2]{0:T(128)} %pad_add_fusion.info_ref, bf16[256,1536]{1,0:T(8,128)(2,1)} %dynamic-slice_bitcast_fusion.x_ref, f32[256,1536]{1,0:T(8,128)} %get-tuple-element.69.mid_ref, f32[256,1536]{1,0:T(8,128)} %get-tuple-element.86.dy_ref.g_second, ...), custom_call_target="tpu_custom_call" | custom-call | flops 4831838208 | bytes 11796480 | tf_op jit(solution)/shard_map/pallas_call | solution.py:1151
  758.7 50.5 %shard_map.260 = (bf16[8,224,1536]{2,1,0:T(8,128)(2,1)}, bf16[2,256,1536]{2,1,0:T(8,128)(2,1)}, f32[2,256,1536]{2,1,0:T(8,128)}) custom-call(bf16[112,1536]{1,0:T(8,128)(2,1)} %get-tuple-element.103.attn_ref, bf16[48,1536]{1,0:T(8,128)(2,1)} %get-tuple-element.104.whole_ref, bf16[96,1536]{1,0:T(8,128)(2,1)} %get-tuple-element.105.parts_ref, ...), custom_call_target="tpu_custom_call" | custom-call | tf_op jit(solution)/shard_map/pallas_call | solution.py:1398
  809.3 11.5 %shard_map.261 = (f32[8,80,1536]{2,1,0:T(8,128)}, f32[8,16,384]{2,1,0:T(8,128)}, f32[8,2,16,256]{3,2,1,0:T(8,128)}, f32[8,2,16,2240]{3,2,1,0:T(8,128)}, f32[8,16...) custom-call(bf16[8,224,1536]{2,1,0:T(8,128)(2,1)} %get-tuple-element.110.first, ...), custom_call_target="tpu_custom_call" | custom-call | tf_op jit(solution)/shard_map/pallas_call | solution.py:1489
  823.3 1.7 copy.46
  (78 shorter events, 23.2 us)
Async XLA Ops:
  7.2 127.7 %copy-start = (bf16[2,256,1536]{2,1,0:T(8,128)(2,1)S(1)}, bf16[2,256,1536]{2,1,0:T(8,128)(2,1)}, u32[]{:S(2)}) copy-start(bf16[2,256,1536]{2,1,0:T(8,128)(2,1)} %param.19) | copy-start | bytes 4718596
  7.2 177.2 %all-gather.7.cloned.1.call-start = ((), (), s32[]{:S(2)}) async-start(), calls=%async_computation.2 | async-start | bytes 23224320 | tf_op jit(solution)/shard_map/all_gather | solution.py:1565
  7.2 2.6 copy-start.7
  21.6 1.0 copy-start.12
  21.6 1.2 copy-start.10
  21.6 1.3 copy-start.14
  22.8 4.6 copy-start.15
  23.8 7.3 all-to-all-start
  27.3 260.2 %all-gather.11.cloned.1.call-start = ((), (), s32[]{:S(2)}) async-start(), calls=%async_computation.4 | async-start | bytes 12386304 | tf_op jit(solution)/shard_map/all_gather | solution.py:1564
  31.1 0.8 copy-start.5
  128.2 0.8 copy-start.16
  128.2 1.4 copy-start.17
  128.2 232.3 %all-gather.9.cloned.1.call-start = ((), (), s32[]{:S(2)}) async-start(), calls=%async_computation.3 | async-start | bytes 23224320 | tf_op jit(solution)/shard_map/all_gather | solution.py:1565
  129.0 6.8 copy-start.6
  129.0 582.3 %all-reduce.4.cloned.1.call-start = ((), (), s32[]{:S(2)}) async-start(), calls=%async_computation.6 | async-start | bytes 983040 | tf_op jit(solution)/shard_map/psum | solution.py:1618
  137.1 19.5 %copy-start.11 = (bf16[2,256,1536]{2,1,0:T(8,128)(2,1)S(1)}, bf16[2,256,1536]{2,1,0:T(8,128)(2,1)}, u32[]{:S(2)}) copy-start(bf16[2,256,1536]{2,1,0:T(8,128)(2,1)} %param.22) | copy-start | bytes 4718596
  184.4 100.6 %copy-start.2 = (f32[256,1536]{1,0:T(8,128)S(1)}, f32[256,1536]{1,0:T(8,128)}, u32[]{:S(2)}) copy-start(f32[256,1536]{1,0:T(8,128)} %get-tuple-element.69.mid_ref) | copy-start | bytes 4718596
  596.1 213.2 %all-gather.13.cloned.1.call-start = ((), (), s32[]{:S(2)}) async-start(), calls=%async_computation.5 | async-start | bytes 6193152 | tf_op jit(solution)/shard_map/all_gather | solution.py:1602
  596.2 123.5 %copy-start.13 = (bf16[96,1536]{1,0:T(8,128)(2,1)S(1)}, bf16[96,1536]{1,0:T(8,128)(2,1)}, u32[]{:S(2)}) copy-start(bf16[96,1536]{1,0:T(8,128)(2,1)} %get-tuple-element.113) | copy-start | bytes 884740
  596.2 125.1 %copy-start.9 = (f32[4,64,1536]{2,1,0:T(8,128)S(1)}, f32[4,64,1536]{2,1,0:T(8,128)}, u32[]{:S(2)}) copy-start(f32[4,64,1536]{2,1,0:T(8,128)} %get-tuple-element.106) | copy-start | bytes 4718596
  711.3 10.0 %copy-start.3 = (f32[256,1536]{1,0:T(8,128)S(1)}, f32[256,1536]{1,0:T(8,128)}, u32[]{:S(2)}) copy-start(f32[256,1536]{1,0:T(8,128)} %get-tuple-element.73.mid_ref) | copy-start | bytes 4718596
  809.3 11.6 %copy-start.8 = (bf16[2,256,1536]{2,1,0:T(8,128)(2,1)S(1)}, bf16[2,256,1536]{2,1,0:T(8,128)(2,1)}, u32[]{:S(2)}) copy-start(bf16[2,256,1536]{2,1,0:T(8,128)(2,1)} %get-tuple-element.108) | copy-start | bytes 4718596
  820.8 2.5 copy-start.4
  820.9 4.1 copy-start.1
Sparse Core Ops, SparseCore 0:
  21.7 162.6 all-gather.6
  186.3 65.4 all-gather.10
  254.3 106.2 all-gather.8
  596.3 45.1 all-reduce.3
  720.8 40.3 all-gather.12

commit v6 on v5

--- a/solution.py
+++ b/solution.py
@@ -371,7 +371,7 @@
 
 
 def ff_tile(hidden):
-    return hidden // 3 if hidden % (3 * LANES) == 0 else LANES
+    return hidden
 
 
 def mlp_forward(n2, w):
@@ -418,7 +418,7 @@
 
 def mlp_back_kernel(
     line, chunks, tile,
-    ds_ref, packed, n2_hbm, gate_in, up_in, bundle_ref,
+    ds_ref, packed, n2_hbm, gate_in, up_in, bundle_ref, names_ref,
     out_ref, whole_ref, parts_ref,
     gathered, partial_ref, from_left, from_right, s0, s1, s2, s3, s4, s5, s6,
     wg, wu, ws, gate_st, up_st, n2_st, acc, ghigh_ref, gexp_ref, gsh_ref, gres_ref, expand_ref, ash_ref, wsem, isem,
@@ -527,9 +527,10 @@
         part = part.astype(BF)
         parts_ref[i * RANK : (i + 1) * RANK] = part[:, :width]
         parts_ref[(3 + i) * RANK : (4 + i) * RANK, :extra] = part[:, width:]
-
-
-def mlp_backward(ds, w, saved):
+    parts_ref[rows_of(5), extra : extra + LANES] = names_ref[...]
+
+
+def mlp_backward(ds, w, saved, names):
     n2_all, gate, up = saved
     line = lax.axis_size("tensor")
     rows, width = ds.shape
@@ -539,7 +540,7 @@
     every = line * part
     out, whole, parts = pl.pallas_call(
         partial(mlp_back_kernel, line, CHUNKS, ff_tile(hidden)),
-        in_specs=[vspec()] + [hspec()] * 4 + [vspec()],
+        in_specs=[vspec()] + [hspec()] * 4 + [vspec()] * 2,
         out_specs=[vspec()] * 3,
         out_shape=[
             jax.ShapeDtypeStruct((CHUNKS, part, width), F32),
@@ -570,7 +571,7 @@
             transcendentals=line * rows * hidden,
         ),
     )(
-        ds.reshape(CHUNKS, part, width), w["mlp"], n2_all, gate, up, w["bundle"],
+        ds.reshape(CHUNKS, part, width), w["mlp"], n2_all, gate, up, w["bundle"], names,
     )
     return out.reshape(rows, width), whole, parts
 
@@ -598,8 +599,19 @@
         greet(tensor=me + 1)
 
     greet(section=other)
+    square = peers == 4
+
+    def partner(k):
+        if square:
+            return (None, spot + 1 - 2 * lax.rem(spot, 2), lax.rem(spot + 2, 4), 3 - spot)[k]
+        return lax.rem(spot + k, peers)
+
+    def origin(k):
+        return partner(k) if square else lax.rem(spot + peers - k, peers)
+
+    direct = (1, 2) if square else tuple(range(1, peers))
     for k in range(1, peers):
-        greet(dp=lax.rem(spot + k, peers))
+        greet(dp=partner(k))
     pl.semaphore_wait(barrier, jnp.where(has_left, 1, 0) + jnp.where(has_right, 1, 0) + peers)
 
     mine = spot * 2 + core
@@ -650,20 +662,30 @@
             tensor=me + side,
         )
 
-    def to_peer(k, o, own):
-        dst = first_out.at[mine, o]
+    outs = (first_out,)
+
+    def to_peer(lay, k, o, own):
+        dst = outs[lay].at[mine, o]
         return remote(
-            attn.at[0] if own else dst, dst, dp_send.at[k, o], dp_recv.at[spot, o], dp=lax.rem(spot + k, peers)
-        )
-
-    def to_core(p, o, own):
-        dst = first_out.at[p * 2 + core, o]
-        return remote(attn.at[0] if own else dst, dst, core_send.at[p, o], core_recv.at[p, o], section=other)
-
-    def spread_first(o, own):
-        for k in range(1, peers):
-            to_peer(k, o, own).start()
-        to_core(spot, o, own).start()
+            attn.at[lay] if own else dst, dst, dp_send.at[lay, k, o], dp_recv.at[lay, spot, o], dp=partner(k)
+        )
+
+    def from_peer(lay, k, o):
+        p = origin(k)
+        slot = outs[lay].at[p * 2 + core, o]
+        to = partner(3 - k) if square and k < 3 else p
+        return remote(slot, slot, dp_send.at[lay, peers - 1, o], dp_recv.at[lay, p, o], dp=to)
+
+    def to_core(lay, p, o, own):
+        dst = outs[lay].at[p * 2 + core, o]
+        return remote(
+            attn.at[lay] if own else dst, dst, core_send.at[lay, p, o], core_recv.at[lay, p, o], section=other
+        )
+
+    def spread(lay, o, own):
+        for k in direct:
+            to_peer(lay, k, o, own).start()
+        to_core(lay, spot, o, own).start()
 
     for side in sides:
         side.start()
@@ -680,7 +702,7 @@
             along(i, me, -1, True).start()
 
         if i == 0:
-            spread_first(me, True)
+            spread(i, me, True)
     for keep in keeps:
         keep.start()
     side_keep.start()
@@ -696,7 +718,7 @@
                     along(i, me - d, 1, False).start()
 
                 if i == 0:
-                    spread_first(me - d, False)
+                    spread(i, me - d, False)
 
             @pl.when(me + d < line)
             def _():
@@ -707,31 +729,46 @@
                     along(i, me + d, -1, False).start()
 
                 if i == 0:
-                    spread_first(me + d, False)
-
-    def pass_on(o, carry):
-        for k in range(1, peers):
-            p = lax.rem(spot + peers - k, peers)
-            remote(
-                first_out.at[p * 2 + core, o], first_out.at[p * 2 + core, o], dp_send.at[k, o], dp_recv.at[p, o], dp=p
-            ).wait_recv()
-            to_core(p, o, False).start()
+                    spread(i, me + d, False)
+
+    half = line // 2
+
+    def pass_on(n, carry):
+        o = lax.rem(me + n, line)
+        for lay in range(1):
+            for k in direct:
+                from_peer(lay, k, o).wait_recv()
+                if square:
+
+                    @pl.when(o < half if k == 1 else o >= half)
+                    def _():
+                        from_peer(lay, k, o).start()
+
+                to_core(lay, origin(k), o, False).start()
         return carry
 
     lax.fori_loop(0, line, pass_on, 0)
 
+    def pass_last(n, carry):
+        o = lax.rem(me + n, line)
+        for lay in range(1):
+            from_peer(lay, 3, o).wait_recv()
+            to_core(lay, origin(3), o, False).start()
+        return carry
+
+    if square:
+        lax.fori_loop(0, line, pass_last, 0)
+
     def finish(o, carry):
-        for k in range(1, peers):
-            to_peer(k, o, False).wait_send()
-        for p in range(peers):
-            to_core(p, o, False).wait_send()
-            remote(
-                first_out.at[p * 2 + other, o],
-                first_out.at[p * 2 + other, o],
-                core_send.at[p, o],
-                core_recv.at[p, o],
-                section=other,
-            ).wait_recv()
+        for lay in range(1):
+            for k in direct:
+                to_peer(lay, k, o, False).wait_send()
+            if square:
+                from_peer(lay, 1, o).wait_send()
+            for p in range(peers):
+                to_core(lay, p, o, False).wait_send()
+                slot = outs[lay].at[p * 2 + other, o]
+                remote(slot, slot, core_send.at[lay, p, o], core_recv.at[lay, p, o], section=other).wait_recv()
         for i in range(4):
 
             @pl.when(jnp.logical_and(has_right, me >= o))
@@ -767,7 +804,7 @@
             jax.ShapeDtypeStruct(bundles.shape, BF),
         ],
         scratch_shapes=[dma((3,)), dma((4, line)), dma((4, line)), dma((4, line))]
-        + [dma((peers, line))] * 4
+        + [dma((1, peers, line))] * 4
         + [dma((2,)), dma((2,)), dma],
         compiler_params=pltpu.CompilerParams(
             collective_id=4, has_side_effects=True, vmem_limit_bytes=VMEM_LIMIT
@@ -1187,7 +1224,7 @@
 
 def reduce_kernel(
     line, peers, extra,
-    attn_ref, whole_ref, parts_ref, names_ref, y_first, y_second, g_first, g_second,
+    attn_ref, whole_ref, parts_ref, y_first, y_second, g_first, g_second,
     out, y_out, g_out,
     mine, z_in, quarter, z_recv, z_send, dp_recv, dp_send, own_sem, t_recv, t_right, t_left,
     side_recv, side_send, side_own,
@@ -1229,7 +1266,10 @@
         return (
             (parts_ref.at[pl.ds(0, 3 * r)], out.at[s, pl.ds(8 * r, 3 * r)]),
             (parts_ref.at[pl.ds(3 * r, 3 * r), pl.ds(0, extra)], out.at[s, pl.ds(11 * r, 3 * r), pl.ds(0, extra)]),
-            (names_ref, out.at[s, pl.ds(13 * r, r), pl.ds(extra, LANES)]),
+            (
+                parts_ref.at[pl.ds(5 * r, r), pl.ds(extra, LANES)],
+                out.at[s, pl.ds(13 * r, r), pl.ds(extra, LANES)],
+            ),
             (quarter.at[pl.ds(0, 8 * r)], out.at[s, pl.ds(0, 8 * r), lanes(me)]),
             (quarter.at[pl.ds(8 * r, 2 * r)], out.at[s, pl.ds(11 * r, 2 * r), pl.ds(extra, cols)]),
         )
@@ -1390,14 +1430,14 @@
         side_keep(i, first, dst).wait()
 
 
-def reduce_first(attn_part, whole, parts, names, extra, outs, grads):
+def reduce_first(attn_part, whole, parts, extra, outs, grads):
     line, peers = lax.axis_size("tensor"), lax.axis_size("dp")
     width = parts.shape[1]
     seqs = 2 * peers
     dma = pltpu.SemaphoreType.DMA
     return pl.pallas_call(
         partial(reduce_kernel, line, peers, extra),
-        in_specs=[vspec()] * 8,
+        in_specs=[vspec()] * 7,
         out_specs=[hspec()] * 3,
         out_shape=[
             jax.ShapeDtypeStruct((seqs, 14 * RANK, width), BF),
@@ -1423,14 +1463,14 @@
         compiler_params=pltpu.CompilerParams(
             collective_id=6, has_side_effects=True, vmem_limit_bytes=VMEM_LIMIT
         ),
-    )(attn_part, whole, parts, names, *outs, *grads)
+    )(attn_part, whole, parts, *outs, *grads)
 
 
 def total_kernel(
     scale, hidden, q_cols,
-    first, second,
+    first, attn_in, whole_in, parts_in,
     input_ref, query_ref, kv_ref, expand_ref, attend_ref, shrink_ref, res_ref,
-    block, sem,
+    block, ids, sem,
 ):
     r = RANK
     a = pl.program_id(0)
@@ -1441,46 +1481,63 @@
 
     @pl.when(jnp.logical_and(a == 0, core == 0))
     def _():
-        load = pltpu.make_async_copy(first, block, sem)
+        load = pltpu.make_async_copy(first, block, sem.at[0])
         load.start()
         load.wait()
 
     @pl.when(jnp.logical_and(a == 0, core != 0))
     def _():
-        load = pltpu.make_async_copy(second, block, sem)
-        load.start()
-        load.wait()
-
-    lane = lax.broadcasted_iota(jnp.int32, (1, LANES), 1)
-    weights = []
+        def load(src, start, first, count, at):
+            return pltpu.make_async_copy(src.at[:, rows_of(start, count)], block.at[:, rows_of(first, count)], sem.at[at])
+
+        loads = [
+            load(attn_in, 0, 0, 3, 1), load(whole_in, 0, 3, 2, 2), load(attn_in, 3, 5, 1, 3),
+            load(whole_in, 2, 6, 1, 4), load(attn_in, 4, 7, 1, 5), load(parts_in, 0, 8, 6, 6),
+        ]
+        for one in loads:
+            one.start()
+        for one in loads:
+            one.wait()
+        mine = pl.ds(pl.multiple_of(lax.axis_index("tensor") * q_cols, LANES), q_cols)
+        last = pltpu.make_async_copy(
+            attn_in.at[:, rows_of(5, 2), mine], block.at[:, rows_of(11, 2), pl.ds(pad, q_cols)], sem.at[7]
+        )
+        last.start()
+        last.wait()
+
+    @pl.when(a == 0)
+    def _():
+        lane = lax.broadcasted_iota(jnp.int32, (1, LANES), 1).astype(F32)
+        for i in range(block.shape[0]):
+            names = block[i, 13 * r : 14 * r, pad : pad + LANES][:1].astype(F32)
+            ids[i] = jnp.sum(lane * names).astype(jnp.int32)
+
+    for ref in (input_ref, query_ref, kv_ref, expand_ref, attend_ref, shrink_ref, res_ref):
+        ref[...] = jnp.zeros_like(ref)
+
     for i in range(block.shape[0]):
-        names = block[i, 13 * r : 14 * r, pad : pad + LANES][:1].astype(F32)
-        weights.append(jnp.sum(jnp.where(lane == a, names, 0.0), axis=1, keepdims=True) * scale)
-
-    def summed(row, rows, col, cols):
-        result = weights[0] * block[0, row : row + rows, col : col + cols].astype(F32)
-        for i in range(1, block.shape[0]):
-            result = result + weights[i] * block[i, row : row + rows, col : col + cols].astype(F32)
-        return result
-
-    step = 4 * LANES
-    for col in range(0, width, step):
-        input_ref[0, :, col : col + step] = summed(0, 5 * r, col, step)
-    res_ref[0, 0] = summed(5 * r, r, 0, width)
-    res_ref[0, 1] = summed(6 * r, r, 0, width)
-    kv = summed(7 * r, r, 0, 2 * kv_ref.shape[3])
-    kv_ref[0, 0] = kv[:, : kv_ref.shape[3]]
-    kv_ref[0, 1] = kv[:, kv_ref.shape[3] :]
-    for i in range(2):
-        expand_ref[0, i, :, :width] = summed((8 + i) * r, r, 0, width)
-        expand_ref[0, i, :, width:] = summed((11 + i) * r, r, 0, pad)[:, :extra]
-    shrink_ref[0, :, :width] = summed(10 * r, r, 0, width)
-    shrink_ref[0, :, width:] = summed(13 * r, r, 0, pad)[:, :extra]
-    query_ref[0] = summed(11 * r, r, pad, q_cols)
-    attend_ref[0] = summed(12 * r, r, pad, q_cols)
-
-
-def total_by_adapter(first, second, count, scale, hidden, q_cols, kv_half):
+
+        @pl.when(ids[i] == a)
+        def _():
+            def part(row, rows, col, cols):
+                return block[i, row : row + rows, col : col + cols].astype(F32) * scale
+
+            input_ref[0] += part(0, 5 * r, 0, width)
+            res_ref[0, 0] += part(5 * r, r, 0, width)
+            res_ref[0, 1] += part(6 * r, r, 0, width)
+            kv = part(7 * r, r, 0, 2 * kv_ref.shape[3])
+            kv_ref[0, 0] += kv[:, : kv_ref.shape[3]]
+            kv_ref[0, 1] += kv[:, kv_ref.shape[3] :]
+            for j in range(2):
+                expand_ref[0, j, :, :width] += part((8 + j) * r, r, 0, width)
+                expand_ref[0, j, :, width:] += part((11 + j) * r, r, 0, pad)[:, :extra]
+            shrink_ref[0, :, :width] += part(10 * r, r, 0, width)
+            shrink_ref[0, :, width:] += part(13 * r, r, 0, pad)[:, :extra]
+            query_ref[0] += part(11 * r, r, pad, q_cols)
+            attend_ref[0] += part(12 * r, r, pad, q_cols)
+
+
+def total_by_adapter(first, attn_in, whole_in, parts_in, count, scale, hidden, q_cols, kv_half):
     width = first.shape[2]
     r = RANK
     shapes = [
@@ -1489,12 +1546,16 @@
     return pl.pallas_call(
         partial(total_kernel, scale, hidden, q_cols),
         grid=(count,),
-        in_specs=[hspec()] * 2,
+        in_specs=[hspec()] * 4,
         out_specs=[pl.BlockSpec((1,) + s, lambda a, n=len(s): (a,) + (0,) * n) for s in shapes],
         out_shape=[jax.ShapeDtypeStruct((count,) + s, F32) for s in shapes],
-        scratch_shapes=[pltpu.VMEM(first.shape, BF), pltpu.SemaphoreType.DMA],
+        scratch_shapes=[
+            pltpu.VMEM(first.shape, BF),
+            pltpu.SMEM((first.shape[0],), jnp.int32),
+            pltpu.SemaphoreType.DMA((8,)),
+        ],
         compiler_params=pltpu.CompilerParams(vmem_limit_bytes=VMEM_LIMIT),
-    )(first, second)
+    )(first, attn_in, whole_in, parts_in)
 
 
 def swap(pair):
@@ -1588,18 +1649,10 @@
         x = outs[-1]
     count = adapter_input.shape[1]
     extra = hidden + -hidden % (2 * LANES) - width
-    names = (jnp.arange(LANES, dtype=jnp.int32) == own_id).astype(BF)[None]
-
-    def gather_block(attn_part, whole, parts):
-        mine = lax.dynamic_slice_in_dim(attn_part[5 * r :], place * q_cols, q_cols, 1)
-        parts = lax.dynamic_update_slice(parts, mine, (3 * r, extra))
-        parts = lax.dynamic_update_slice(parts, names, (5 * r, extra))
-        block = jnp.concatenate(
-            [attn_part[: 3 * r], whole[: 2 * r], attn_part[3 * r : 4 * r], whole[2 * r :], attn_part[4 * r : 5 * r]]
-            + [parts],
-            axis=0,
-        )
-        return lax.all_gather(block, ("section", "dp"), axis=0)
+    names = jnp.broadcast_to((jnp.arange(LANES, dtype=jnp.int32) == own_id).astype(BF)[None], (r, LANES))
+
+    def gather_all(*arrays):
+        return [lax.all_gather(a, ("section", "dp"), axis=0) for a in arrays]
 
     grad = low_grad = jnp.where((slot_ids < length)[:, None], cot, jnp.zeros_like(cot))
     grads, gathered = [None] * layers, [None] * layers
@@ -1607,21 +1660,19 @@
         x, middle, attn_kept, mlp_kept = kept[layer]
         if layer < layers - 1:
             low_grad, here = lax.optimization_barrier((low_grad, here))
-        dn2, whole, parts = mlp_backward(low_grad, w[layer], mlp_kept)
+        dn2, whole, parts = mlp_backward(low_grad, w[layer], mlp_kept, names)
         if layer < layers - 1:
             total, dn2 = lax.optimization_barrier((total, dn2))
-            gathered[layer + 1] = gather_block(*total, last_parts)
+            gathered[layer + 1] = gather_all(*total, last_parts)
         grad, low_grad, attn_part = attend_backward(x, middle, grad, dn2, w[layer], attn_kept, info, tables)
         grads[layer] = grad
         here = (attn_part, whole)
         if layer > 0:
             total = lax.psum(here, "tensor")
             last_parts = parts
-    gathered[0], layer_output, input_grad = reduce_first(
-        *here, parts, jnp.pad(names, [(0, r - 1), (0, 0)]), extra, outs, grads
-    )
+    gathered[0], layer_output, input_grad = reduce_first(*here, parts, extra, outs, grads)
     totals = total_by_adapter(
-        gathered[0], gathered[1], count, 1.0 / math.sqrt(tokens), hidden, q_cols, kv_half
+        gathered[0], *gathered[1], count, 1.0 / math.sqrt(tokens), hidden, q_cols, kv_half
     )
     turned = (0, 4, 5)
     totals = [jnp.swapaxes(total, 1, 2) if i in turned else total for i, total in enumerate(totals)]

time: 839 us -> 810 us (0.965)
  waiting for transfers between devices: 81.9 us -> 70.1 us
  local copies, waits for them, and re-layouts: 25.5 us -> 16.2 us
  Pallas kernels: 686 us -> 677 us
    all_gather x2, waiting for transfers between devices: 81.1 us -> 65.1 us  [weights(): mlp = lax.all_gather(ff[layer], ('section', 'dp'), axis=0)]
  transfers between devices with their start and end apart: 6 -> 8, of which waited for: 2 -> 3; matrix products, arithmetic and copies ran while one was open for 2% -> 2% of each run, Pallas kernels for 53% -> 55%
where the time goes in v6:
time: 810 us; the launch traced here: 802 us
  Pallas kernels  677 us (84%)
  waiting for transfers between devices  70.1 us (9%)
  local copies, waits for them, and re-layouts  16.2 us (2%)
  between operations  14.9 us (2%)
  other arithmetic  12.2 us (2%)
    pallas_call x2, Pallas kernels, mlp_forward(): pl.pallas_call(partial(mlp_kernel, line, CHUNKS, ff_tile(hidden)), in_spe...  205 us
    pallas_call x2, Pallas kernels, mlp_backward(): pl.pallas_call(partial(mlp_back_kernel, line, CHUNKS, ff_tile(hidden)), i...  205 us
    pallas_call x1, Pallas kernels, gather_first(): pl.pallas_call(partial(gather_kernel, line, peers), in_specs=[vspec()] *...  91.5 us
    pallas_call x2, Pallas kernels, attend_backward(): pl.pallas_call(partial(attend_back_kernel, line, heads // KV_HEADS), in_s...  72.7 us
    all_gather x2, waiting for transfers between devices, weights(): mlp = lax.all_gather(ff[layer], ('section', 'dp'), axis=0)  65.1 us
    pallas_call x1, Pallas kernels, reduce_first(): pl.pallas_call(partial(reduce_kernel, line, peers, extra), in_specs=[vspe...  55 us
    pallas_call x2, Pallas kernels, attend_forward(): pl.pallas_call(partial(attend_kernel, line, heads // KV_HEADS), in_specs=...  36.1 us
  transfers between devices with their start and end apart: 8, of which 3 were waited for; matrix products, arithmetic and copies ran while one was open for 2% of the time, Pallas kernels for 55%

profile of v6, /device:TPU:0, one launch (start us, length us, event | category | flops | bytes accessed | tf_op | source)
XLA Modules:
  0.0 802.1 jit_solution(5594640381345484620)
XLA Ops:
  7.2 2.5 fusion.7
  10.9 7.9 all_to_all.10
  18.7 2.8 fusion.6
  23.8 3.5 all-to-all-start
  28.0 3.2 shard_map.250
  32.0 91.5 %shard_map.251 = (bf16[8,4,192,896]{3,2,1,0:T(8,128)(2,1)}, bf16[4,192,896]{2,1,0:T(8,128)(2,1)}, bf16[2,288,1536]{2,1,0:T(8,128)(2,1)}) custom-call(bf16[2,192,896]{2,1,0:T(8,128)(2,1)} %copy-done.5, bf16[2,288,1536]{2,1,0:T(8,128)(2,1)} %get-tuple-element.65.bundles, bf16[2,48,384]{2,1,0:T(8,128)(2,1)} %get-tuple-element.66.heads), custom_call_target="tpu_custom_call" | custom-call | tf_op jit(solution)/shard_map/pallas_call | solution.py:797
  126.9 1.2 pad_add_fusion.info_ref
  131.1 1.3 slice_bitcast_fusion
  132.4 18.3 %shard_map.252 = (f32[256,1536]{1,0:T(8,128)}, bf16[256,1536]{1,0:T(8,128)(2,1)}, bf16[256,1536]{1,0:T(8,128)(2,1)}, bf16[256,48]{1,0:T(8,128)(2,1)}, bf16[256,1...) custom-call(s32[2]{0:T(128)} %pad_add_fusion.info_ref, ...), custom_call_target="tpu_custom_call" | custom-call | flops 4831838208 | bytes 11796480 | tf_op jit(solution)/shard_map/pallas_call | solution.py:1001
  152.8 14.5 %all-gather.11.cloned.1.call-done = bf16[8,3,1120,384]{3,2,1,0:T(8,128)(2,1)} async-done(((bf16[1,3,1120,384]{3,2,1,0:T(8,128)(2,1)}), bf16[8,3,1120,384]{3,2,1,0:T(8,128)(2,1)}) %all-gather.11.cloned.1.call-update) | async-done | bytes 20643856 | tf_op jit(solution)/shard_map/all_gather | solution.py:1626
  167.3 106.3 %shard_map.253 = (f32[4,64,1536]{2,1,0:T(8,128)}, bf16[4,4,64,1536]{3,2,1,0:T(8,128)(2,1)}, bf16[4,256,2304]{2,1,0:T(8,128)(2,1)}, bf16[4,256,2304]{2,1,0:T(8,128)(2,1)}) custom-call(bf16[4,64,1536]{2,1,0:T(8,128)(2,1)} %bitcast.122, bf16[2,4,3,1120,384]{4,3,2,1,0:T(8,128)(2,1)} %bitcast.108, bf16[288,1536]{1,0:T(8,128)(2,1)} %get-tuple-element.130.bundle_ref), custom_call_target="tpu_custom_call" | custom-call | flops 21743271936 | bytes 30670848 | tf_op jit(solution)/shard_map/pallas_call | solution.py:384
  273.6 2.5 fusion.1.x_ref.y_first
  276.1 17.8 %shard_map.254 = (f32[256,1536]{1,0:T(8,128)}, bf16[256,1536]{1,0:T(8,128)(2,1)}, bf16[256,1536]{1,0:T(8,128)(2,1)}, bf16[256,48]{1,0:T(8,128)(2,1)}, bf16[256,1...) custom-call(s32[2]{0:T(128)} %pad_add_fusion.info_ref, ...), custom_call_target="tpu_custom_call" | custom-call | flops 4831838208 | bytes 11796480 | tf_op jit(solution)/shard_map/pallas_call | solution.py:1001
  293.9 50.7 %all-gather.13.cloned.1.call-done = bf16[8,3,1120,384]{3,2,1,0:T(8,128)(2,1)} async-done(((bf16[1,3,1120,384]{3,2,1,0:T(8,128)(2,1)}), bf16[8,3,1120,384]{3,2,1,0:T(8,128)(2,1)}) %all-gather.13.cloned.1.call-update) | async-done | bytes 20643856 | tf_op jit(solution)/shard_map/all_gather | solution.py:1626
  344.5 99.0 %shard_map.255 = (f32[4,64,1536]{2,1,0:T(8,128)}, bf16[4,4,64,1536]{3,2,1,0:T(8,128)(2,1)}, bf16[4,256,2304]{2,1,0:T(8,128)(2,1)}, bf16[4,256,2304]{2,1,0:T(8,128)(2,1)}) custom-call(bf16[4,64,1536]{2,1,0:T(8,128)(2,1)} %bitcast.123, bf16[2,4,3,1120,384]{4,3,2,1,0:T(8,128)(2,1)} %bitcast.110, bf16[288,1536]{1,0:T(8,128)(2,1)} %get-tuple-element.129.bundle_ref), custom_call_target="tpu_custom_call" | custom-call | flops 21743271936 | bytes 30670848 | tf_op jit(solution)/shard_map/pallas_call | solution.py:384
  444.2 94.0 %shard_map.256 = (f32[4,64,1536]{2,1,0:T(8,128)}, bf16[48,1536]{1,0:T(8,128)(2,1)}, bf16[96,1536]{1,0:T(8,128)(2,1)}) custom-call(bf16[4,64,1536]{2,1,0:T(8,128)(2,1)} %broadcast_select_fusion.ds_ref, bf16[2,4,3,1120,384]{4,3,2,1,0:T(8,128)(2,1)} %bitcast.111, bf16[4,256,1536]{2,1,0:T(8,128)(2,1)} %bitcast.121, ...), custom_call_target="tpu_custom_call" | custom-call | flops 21743271936 | bytes 30670848 | tf_op jit(solution)/shard_map/pallas_call | solution.py:541
  538.2 35.7 %shard_map.257 = (f32[256,1536]{1,0:T(8,128)}, bf16[256,1536]{1,0:T(8,128)(2,1)}, bf16[112,1536]{1,0:T(8,128)(2,1)}) custom-call(s32[2]{0:T(128)} %pad_add_fusion.info_ref, bf16[256,1536]{1,0:T(8,128)(2,1)} %fusion.1.x_ref.y_first, f32[256,1536]{1,0:T(8,128)} %get-tuple-element.73.mid_ref, bf16[256,1536]{1,0:T(8,128)(2,1)} %get-tuple-element.123.dy_ref, ...), custom_call_target="tpu_custom_call" | custom-call | flops 4831838208 | bytes 11796480 | tf_op jit(solution)/shard_map/pallas_call | solution.py:1188
  574.0 110.5 %shard_map.258 = (f32[4,64,1536]{2,1,0:T(8,128)}, bf16[48,1536]{1,0:T(8,128)(2,1)}, bf16[96,1536]{1,0:T(8,128)(2,1)}) custom-call(bf16[4,64,1536]{2,1,0:T(8,128)(2,1)} %bitcast.116, bf16[2,4,3,1120,384]{4,3,2,1,0:T(8,128)(2,1)} %bitcast.109, bf16[4,256,1536]{2,1,0:T(8,128)(2,1)} %bitcast.120, bf16[4,256,2304]{2,1,0:T(8,128)(2,1)} %get-tuple-element.92.gate_in, ...), custom_call_target="tpu_custom_call" | custom-call | flops 21743271936 | bytes 30670848 | tf_op jit(solution)/shard_map/pallas_call | solution.py:541
  687.0 37.0 %shard_map.259 = (f32[256,1536]{1,0:T(8,128)}, bf16[256,1536]{1,0:T(8,128)(2,1)}, bf16[112,1536]{1,0:T(8,128)(2,1)}) custom-call(s32[2]{0:T(128)} %pad_add_fusion.info_ref, bf16[256,1536]{1,0:T(8,128)(2,1)} %dynamic-slice_bitcast_fusion.x_ref, f32[256,1536]{1,0:T(8,128)} %get-tuple-element.69.mid_ref, f32[256,1536]{1,0:T(8,128)} %get-tuple-element.86.dy_ref.g_second, ...), custom_call_target="tpu_custom_call" | custom-call | flops 4831838208 | bytes 11796480 | tf_op jit(solution)/shard_map/pallas_call | solution.py:1188
  724.0 55.0 %shard_map.260 = (bf16[8,224,1536]{2,1,0:T(8,128)(2,1)}, bf16[2,256,1536]{2,1,0:T(8,128)(2,1)}, f32[2,256,1536]{2,1,0:T(8,128)}) custom-call(bf16[112,1536]{1,0:T(8,128)(2,1)} %get-tuple-element.103.attn_ref, bf16[48,1536]{1,0:T(8,128)(2,1)} %get-tuple-element.104.whole_ref, bf16[96,1536]{1,0:T(8,128)(2,1)} %get-tuple-element.105.parts_ref, ...), custom_call_target="tpu_custom_call" | custom-call | tf_op jit(solution)/shard_map/pallas_call | solution.py:1438
  779.1 3.0 all-gather.17.cloned.1.call-done
  782.0 8.7 %shard_map.261 = (f32[8,80,1536]{2,1,0:T(8,128)}, f32[8,16,384]{2,1,0:T(8,128)}, f32[8,2,16,256]{3,2,1,0:T(8,128)}, f32[8,2,16,2240]{3,2,1,0:T(8,128)}, f32[8,16...) custom-call(bf16[8,224,1536]{2,1,0:T(8,128)(2,1)} %get-tuple-element.110.first, ...), custom_call_target="tpu_custom_call" | custom-call | tf_op jit(solution)/shard_map/pallas_call | solution.py:1546
  791.9 1.3 copy-done.4
  793.2 1.7 copy.39
  (73 shorter events, 17.5 us)
Async XLA Ops:
  7.2 123.0 %copy-start = (bf16[2,256,1536]{2,1,0:T(8,128)(2,1)S(1)}, bf16[2,256,1536]{2,1,0:T(8,128)(2,1)}, u32[]{:S(2)}) copy-start(bf16[2,256,1536]{2,1,0:T(8,128)(2,1)} %param.19) | copy-start | bytes 4718596
  7.2 160.1 %all-gather.11.cloned.1.call-start = ((), (), s32[]{:S(2)}) async-start(), calls=%async_computation.2 | async-start | bytes 23224320 | tf_op jit(solution)/shard_map/all_gather | solution.py:1626
  7.2 2.6 copy-start.7
  21.6 1.0 copy-start.12
  21.6 1.2 copy-start.10
  21.6 1.3 copy-start.13
  22.8 4.6 copy-start.14
  23.8 7.3 all-to-all-start
  27.3 248.7 %all-gather.15.cloned.1.call-start = ((), (), s32[]{:S(2)}) async-start(), calls=%async_computation.4 | async-start | bytes 12386304 | tf_op jit(solution)/shard_map/all_gather | solution.py:1625
  123.5 0.9 copy-start.15
  123.5 1.4 copy-start.16
  123.6 221.0 %all-gather.13.cloned.1.call-start = ((), (), s32[]{:S(2)}) async-start(), calls=%async_computation.3 | async-start | bytes 23224320 | tf_op jit(solution)/shard_map/all_gather | solution.py:1626
  124.3 6.8 copy-start.6
  124.3 560.2 %all-reduce.3.cloned.1.call-start = ((), (), s32[]{:S(2)}) async-start(), calls=%async_computation.8 | async-start | bytes 983040 | tf_op jit(solution)/shard_map/psum | solution.py:1671
  132.4 18.3 %copy-start.11 = (bf16[2,256,1536]{2,1,0:T(8,128)(2,1)S(1)}, bf16[2,256,1536]{2,1,0:T(8,128)(2,1)}, u32[]{:S(2)}) copy-start(bf16[2,256,1536]{2,1,0:T(8,128)(2,1)} %param.22) | copy-start | bytes 4718596
  167.3 106.3 %copy-start.2 = (f32[256,1536]{1,0:T(8,128)S(1)}, f32[256,1536]{1,0:T(8,128)}, u32[]{:S(2)}) copy-start(f32[256,1536]{1,0:T(8,128)} %get-tuple-element.69.mid_ref) | copy-start | bytes 4718596
  573.9 205.1 %all-gather.19.cloned.1.call-start = ((), (), s32[]{:S(2)}) async-start(), calls=%async_computation.6 | async-start | bytes 1327104 | tf_op jit(solution)/shard_map/all_gather | solution.py:1655
  574.0 111.9 %copy-start.3 = (f32[256,1536]{1,0:T(8,128)S(1)}, f32[256,1536]{1,0:T(8,128)}, u32[]{:S(2)}) copy-start(f32[256,1536]{1,0:T(8,128)} %get-tuple-element.73.mid_ref) | copy-start | bytes 4718596
  574.0 111.9 %copy-start.9 = (f32[4,64,1536]{2,1,0:T(8,128)S(1)}, f32[4,64,1536]{2,1,0:T(8,128)}, u32[]{:S(2)}) copy-start(f32[4,64,1536]{2,1,0:T(8,128)} %get-tuple-element.106) | copy-start | bytes 4718596
  684.6 94.5 %all-gather.21.cloned.1.call-start = ((), (), s32[]{:S(2)}) async-start(), calls=%async_computation.7 | async-start | bytes 2654208 | tf_op jit(solution)/shard_map/all_gather | solution.py:1655
  685.2 96.9 %all-gather.17.cloned.1.call-start = ((), (), s32[]{:S(2)}) async-start(), calls=%async_computation.5 | async-start | bytes 3096576 | tf_op jit(solution)/shard_map/all_gather | solution.py:1655
  782.0 8.7 %copy-start.8 = (bf16[2,256,1536]{2,1,0:T(8,128)(2,1)S(1)}, bf16[2,256,1536]{2,1,0:T(8,128)(2,1)}, u32[]{:S(2)}) copy-start(bf16[2,256,1536]{2,1,0:T(8,128)(2,1)} %get-tuple-element.108) | copy-start | bytes 4718596
  790.7 2.5 copy-start.4
  790.7 4.1 copy-start.1
  (1 other events, 0.8 us)
Sparse Core Ops, SparseCore 0:
  21.7 145.4 all-gather.10
  169.1 66.6 all-gather.14
  238.3 106.2 all-gather.12
  574.1 45.9 all-reduce.2
  684.7 23.2 all-gather.18
  709.9 40.3 all-gather.20
  752.3 29.6 all-gather.16

commit v7 on v6

--- a/solution.py
+++ b/solution.py
@@ -953,7 +953,7 @@
             peak[h] = top
             return carry
 
-        lax.fori_loop(0, heads, one, 0)
+        lax.fori_loop(0, heads, one, 0, unroll=12)
 
     for d in range(line):
 
@@ -1115,7 +1115,7 @@
             dkv_acc[:, head_cols(KV_HEADS + kv_head)] += dot(soft.astype(BF), do)
             return carry
 
-        lax.fori_loop(0, heads, one, 0)
+        lax.fori_loop(0, heads, one, 0, unroll=12)
         partial_ref[o] = dkv_acc[...].astype(BF)
 
     for s in range(2 * line - 1):

time: 810 us -> 802 us (level)
  Pallas kernels: 677 us -> 658 us
  waiting for transfers between devices: 70.1 us -> 79.2 us
    pallas_call x2, Pallas kernels: 205 us -> 195 us  [mlp_backward(): pl.pallas_call(partial(mlp_back_kernel, line, CHUNKS, ff_tile(hidden)), i...]
  transfers between devices with their start and end apart: 8 -> 8, of which waited for: 3 -> 3; matrix products, arithmetic and copies ran while one was open for 2% -> 2% of each run, Pallas kernels for 55% -> 53%
where the time goes in v7:
time: 802 us; the launch traced here: 792 us
  Pallas kernels  658 us (82%)
  waiting for transfers between devices  79.2 us (10%)
  local copies, waits for them, and re-layouts  16.2 us (2%)
  between operations  14.7 us (2%)
  other arithmetic  12.2 us (2%)
    pallas_call x2, Pallas kernels, mlp_forward(): pl.pallas_call(partial(mlp_kernel, line, CHUNKS, ff_tile(hidden)), in_spe...  202 us
    pallas_call x2, Pallas kernels, mlp_backward(): pl.pallas_call(partial(mlp_back_kernel, line, CHUNKS, ff_tile(hidden)), i...  195 us
    pallas_call x1, Pallas kernels, gather_first(): pl.pallas_call(partial(gather_kernel, line, peers), in_specs=[vspec()] *...  91.5 us
    pallas_call x2, Pallas kernels, attend_backward(): pl.pallas_call(partial(attend_back_kernel, line, heads // KV_HEADS), in_s...  72.6 us
    all_gather x2, waiting for transfers between devices, weights(): mlp = lax.all_gather(ff[layer], ('section', 'dp'), axis=0)  71.9 us
    pallas_call x1, Pallas kernels, reduce_first(): pl.pallas_call(partial(reduce_kernel, line, peers, extra), in_specs=[vspe...  52.8 us
    pallas_call x2, Pallas kernels, attend_forward(): pl.pallas_call(partial(attend_kernel, line, heads // KV_HEADS), in_specs=...  32.5 us
  transfers between devices with their start and end apart: 8, of which 3 were waited for; matrix products, arithmetic and copies ran while one was open for 2% of the time, Pallas kernels for 53%

profile of v7, /device:TPU:0, one launch (start us, length us, event | category | flops | bytes accessed | tf_op | source)
XLA Modules:
  0.0 792.3 jit_solution(1954168043049522372)
XLA Ops:
  7.2 2.5 fusion.7
  10.9 7.9 all_to_all.10
  18.7 2.8 fusion.6
  23.8 3.5 all-to-all-start
  28.0 3.2 shard_map.250
  32.0 91.5 %shard_map.251 = (bf16[8,4,192,896]{3,2,1,0:T(8,128)(2,1)}, bf16[4,192,896]{2,1,0:T(8,128)(2,1)}, bf16[2,288,1536]{2,1,0:T(8,128)(2,1)}) custom-call(bf16[2,192,896]{2,1,0:T(8,128)(2,1)} %copy-done.5, bf16[2,288,1536]{2,1,0:T(8,128)(2,1)} %get-tuple-element.65.bundles, bf16[2,48,384]{2,1,0:T(8,128)(2,1)} %get-tuple-element.66.heads), custom_call_target="tpu_custom_call" | custom-call | tf_op jit(solution)/shard_map/pallas_call | solution.py:797
  126.9 1.2 pad_add_fusion.info_ref
  131.1 1.3 slice_bitcast_fusion
  132.4 16.6 %shard_map.252 = (f32[256,1536]{1,0:T(8,128)}, bf16[256,1536]{1,0:T(8,128)(2,1)}, bf16[256,1536]{1,0:T(8,128)(2,1)}, bf16[256,48]{1,0:T(8,128)(2,1)}, bf16[256,1...) custom-call(s32[2]{0:T(128)} %pad_add_fusion.info_ref, ...), custom_call_target="tpu_custom_call" | custom-call | flops 4831838208 | bytes 11796480 | tf_op jit(solution)/shard_map/pallas_call | solution.py:1001
  151.1 16.1 %all-gather.11.cloned.1.call-done = bf16[8,3,1120,384]{3,2,1,0:T(8,128)(2,1)} async-done(((bf16[1,3,1120,384]{3,2,1,0:T(8,128)(2,1)}), bf16[8,3,1120,384]{3,2,1,0:T(8,128)(2,1)}) %all-gather.11.cloned.1.call-update) | async-done | bytes 20643856 | tf_op jit(solution)/shard_map/all_gather | solution.py:1626
  167.3 103.1 %shard_map.253 = (f32[4,64,1536]{2,1,0:T(8,128)}, bf16[4,4,64,1536]{3,2,1,0:T(8,128)(2,1)}, bf16[4,256,2304]{2,1,0:T(8,128)(2,1)}, bf16[4,256,2304]{2,1,0:T(8,128)(2,1)}) custom-call(bf16[4,64,1536]{2,1,0:T(8,128)(2,1)} %bitcast.122, bf16[2,4,3,1120,384]{4,3,2,1,0:T(8,128)(2,1)} %bitcast.108, bf16[288,1536]{1,0:T(8,128)(2,1)} %get-tuple-element.130.bundle_ref), custom_call_target="tpu_custom_call" | custom-call | flops 21743271936 | bytes 30670848 | tf_op jit(solution)/shard_map/pallas_call | solution.py:384
  270.3 2.5 fusion.1.x_ref.y_first
  272.8 15.9 %shard_map.254 = (f32[256,1536]{1,0:T(8,128)}, bf16[256,1536]{1,0:T(8,128)(2,1)}, bf16[256,1536]{1,0:T(8,128)(2,1)}, bf16[256,48]{1,0:T(8,128)(2,1)}, bf16[256,1...) custom-call(s32[2]{0:T(128)} %pad_add_fusion.info_ref, ...), custom_call_target="tpu_custom_call" | custom-call | flops 4831838208 | bytes 11796480 | tf_op jit(solution)/shard_map/pallas_call | solution.py:1001
  288.7 55.8 %all-gather.13.cloned.1.call-done = bf16[8,3,1120,384]{3,2,1,0:T(8,128)(2,1)} async-done(((bf16[1,3,1120,384]{3,2,1,0:T(8,128)(2,1)}), bf16[8,3,1120,384]{3,2,1,0:T(8,128)(2,1)}) %all-gather.13.cloned.1.call-update) | async-done | bytes 20643856 | tf_op jit(solution)/shard_map/all_gather | solution.py:1626
  344.5 99.0 %shard_map.255 = (f32[4,64,1536]{2,1,0:T(8,128)}, bf16[4,4,64,1536]{3,2,1,0:T(8,128)(2,1)}, bf16[4,256,2304]{2,1,0:T(8,128)(2,1)}, bf16[4,256,2304]{2,1,0:T(8,128)(2,1)}) custom-call(bf16[4,64,1536]{2,1,0:T(8,128)(2,1)} %bitcast.123, bf16[2,4,3,1120,384]{4,3,2,1,0:T(8,128)(2,1)} %bitcast.110, bf16[288,1536]{1,0:T(8,128)(2,1)} %get-tuple-element.129.bundle_ref), custom_call_target="tpu_custom_call" | custom-call | flops 21743271936 | bytes 30670848 | tf_op jit(solution)/shard_map/pallas_call | solution.py:384
  444.1 94.1 %shard_map.256 = (f32[4,64,1536]{2,1,0:T(8,128)}, bf16[48,1536]{1,0:T(8,128)(2,1)}, bf16[96,1536]{1,0:T(8,128)(2,1)}) custom-call(bf16[4,64,1536]{2,1,0:T(8,128)(2,1)} %broadcast_select_fusion.ds_ref, bf16[2,4,3,1120,384]{4,3,2,1,0:T(8,128)(2,1)} %bitcast.111, bf16[4,256,1536]{2,1,0:T(8,128)(2,1)} %bitcast.121, ...), custom_call_target="tpu_custom_call" | custom-call | flops 21743271936 | bytes 30670848 | tf_op jit(solution)/shard_map/pallas_call | solution.py:541
  538.2 37.3 %shard_map.257 = (f32[256,1536]{1,0:T(8,128)}, bf16[256,1536]{1,0:T(8,128)(2,1)}, bf16[112,1536]{1,0:T(8,128)(2,1)}) custom-call(s32[2]{0:T(128)} %pad_add_fusion.info_ref, bf16[256,1536]{1,0:T(8,128)(2,1)} %fusion.1.x_ref.y_first, f32[256,1536]{1,0:T(8,128)} %get-tuple-element.73.mid_ref, bf16[256,1536]{1,0:T(8,128)(2,1)} %get-tuple-element.123.dy_ref, ...), custom_call_target="tpu_custom_call" | custom-call | flops 4831838208 | bytes 11796480 | tf_op jit(solution)/shard_map/pallas_call | solution.py:1188
  575.7 101.2 %shard_map.258 = (f32[4,64,1536]{2,1,0:T(8,128)}, bf16[48,1536]{1,0:T(8,128)(2,1)}, bf16[96,1536]{1,0:T(8,128)(2,1)}) custom-call(bf16[4,64,1536]{2,1,0:T(8,128)(2,1)} %bitcast.116, bf16[2,4,3,1120,384]{4,3,2,1,0:T(8,128)(2,1)} %bitcast.109, bf16[4,256,1536]{2,1,0:T(8,128)(2,1)} %bitcast.120, bf16[4,256,2304]{2,1,0:T(8,128)(2,1)} %get-tuple-element.92.gate_in, ...), custom_call_target="tpu_custom_call" | custom-call | flops 21743271936 | bytes 30670848 | tf_op jit(solution)/shard_map/pallas_call | solution.py:541
  679.4 35.2 %shard_map.259 = (f32[256,1536]{1,0:T(8,128)}, bf16[256,1536]{1,0:T(8,128)(2,1)}, bf16[112,1536]{1,0:T(8,128)(2,1)}) custom-call(s32[2]{0:T(128)} %pad_add_fusion.info_ref, bf16[256,1536]{1,0:T(8,128)(2,1)} %dynamic-slice_bitcast_fusion.x_ref, f32[256,1536]{1,0:T(8,128)} %get-tuple-element.69.mid_ref, f32[256,1536]{1,0:T(8,128)} %get-tuple-element.86.dy_ref.g_second, ...), custom_call_target="tpu_custom_call" | custom-call | flops 4831838208 | bytes 11796480 | tf_op jit(solution)/shard_map/pallas_call | solution.py:1188
  714.7 52.8 %shard_map.260 = (bf16[8,224,1536]{2,1,0:T(8,128)(2,1)}, bf16[2,256,1536]{2,1,0:T(8,128)(2,1)}, f32[2,256,1536]{2,1,0:T(8,128)}) custom-call(bf16[112,1536]{1,0:T(8,128)(2,1)} %get-tuple-element.103.attn_ref, bf16[48,1536]{1,0:T(8,128)(2,1)} %get-tuple-element.104.whole_ref, bf16[96,1536]{1,0:T(8,128)(2,1)} %get-tuple-element.105.parts_ref, ...), custom_call_target="tpu_custom_call" | custom-call | tf_op jit(solution)/shard_map/pallas_call | solution.py:1438
  767.6 5.2 all-gather.17.cloned.1.call-done
  772.8 8.3 %shard_map.261 = (f32[8,80,1536]{2,1,0:T(8,128)}, f32[8,16,384]{2,1,0:T(8,128)}, f32[8,2,16,256]{3,2,1,0:T(8,128)}, f32[8,2,16,2240]{3,2,1,0:T(8,128)}, f32[8,16...) custom-call(bf16[8,224,1536]{2,1,0:T(8,128)(2,1)} %get-tuple-element.110.first, ...), custom_call_target="tpu_custom_call" | custom-call | tf_op jit(solution)/shard_map/pallas_call | solution.py:1546
  782.3 1.3 copy-done.4
  783.6 1.7 copy.39
  (73 shorter events, 17.5 us)
Async XLA Ops:
  7.2 123.0 %copy-start = (bf16[2,256,1536]{2,1,0:T(8,128)(2,1)S(1)}, bf16[2,256,1536]{2,1,0:T(8,128)(2,1)}, u32[]{:S(2)}) copy-start(bf16[2,256,1536]{2,1,0:T(8,128)(2,1)} %param.19) | copy-start | bytes 4718596
  7.2 160.1 %all-gather.11.cloned.1.call-start = ((), (), s32[]{:S(2)}) async-start(), calls=%async_computation.2 | async-start | bytes 23224320 | tf_op jit(solution)/shard_map/all_gather | solution.py:1626
  7.2 2.6 copy-start.7
  21.6 1.0 copy-start.12
  21.6 1.2 copy-start.10
  21.6 1.3 copy-start.13
  22.8 4.6 copy-start.14
  23.8 7.3 all-to-all-start
  27.3 245.5 %all-gather.15.cloned.1.call-start = ((), (), s32[]{:S(2)}) async-start(), calls=%async_computation.4 | async-start | bytes 12386304 | tf_op jit(solution)/shard_map/all_gather | solution.py:1625
  123.5 0.9 copy-start.15
  123.5 1.4 copy-start.16
  123.6 221.0 %all-gather.13.cloned.1.call-start = ((), (), s32[]{:S(2)}) async-start(), calls=%async_computation.3 | async-start | bytes 23224320 | tf_op jit(solution)/shard_map/all_gather | solution.py:1626
  124.3 6.8 copy-start.6
  124.3 552.6 %all-reduce.3.cloned.1.call-start = ((), (), s32[]{:S(2)}) async-start(), calls=%async_computation.8 | async-start | bytes 983040 | tf_op jit(solution)/shard_map/psum | solution.py:1671
  132.4 16.6 %copy-start.11 = (bf16[2,256,1536]{2,1,0:T(8,128)(2,1)S(1)}, bf16[2,256,1536]{2,1,0:T(8,128)(2,1)}, u32[]{:S(2)}) copy-start(bf16[2,256,1536]{2,1,0:T(8,128)(2,1)} %param.22) | copy-start | bytes 4718596
  167.3 103.1 %copy-start.2 = (f32[256,1536]{1,0:T(8,128)S(1)}, f32[256,1536]{1,0:T(8,128)}, u32[]{:S(2)}) copy-start(f32[256,1536]{1,0:T(8,128)} %get-tuple-element.69.mid_ref) | copy-start | bytes 4718596
  575.6 191.9 %all-gather.19.cloned.1.call-start = ((), (), s32[]{:S(2)}) async-start(), calls=%async_computation.6 | async-start | bytes 1327104 | tf_op jit(solution)/shard_map/all_gather | solution.py:1655
  575.6 102.7 %copy-start.3 = (f32[256,1536]{1,0:T(8,128)S(1)}, f32[256,1536]{1,0:T(8,128)}, u32[]{:S(2)}) copy-start(f32[256,1536]{1,0:T(8,128)} %get-tuple-element.73.mid_ref) | copy-start | bytes 4718596
  575.6 102.7 %copy-start.9 = (f32[4,64,1536]{2,1,0:T(8,128)S(1)}, f32[4,64,1536]{2,1,0:T(8,128)}, u32[]{:S(2)}) copy-start(f32[4,64,1536]{2,1,0:T(8,128)} %get-tuple-element.106) | copy-start | bytes 4718596
  677.0 90.6 %all-gather.21.cloned.1.call-start = ((), (), s32[]{:S(2)}) async-start(), calls=%async_computation.7 | async-start | bytes 2654208 | tf_op jit(solution)/shard_map/all_gather | solution.py:1655
  677.5 95.3 %all-gather.17.cloned.1.call-start = ((), (), s32[]{:S(2)}) async-start(), calls=%async_computation.5 | async-start | bytes 3096576 | tf_op jit(solution)/shard_map/all_gather | solution.py:1655
  772.8 8.3 %copy-start.8 = (bf16[2,256,1536]{2,1,0:T(8,128)(2,1)S(1)}, bf16[2,256,1536]{2,1,0:T(8,128)(2,1)}, u32[]{:S(2)}) copy-start(bf16[2,256,1536]{2,1,0:T(8,128)(2,1)} %get-tuple-element.108) | copy-start | bytes 4718596
  781.1 2.5 copy-start.4
  781.1 4.1 copy-start.1
  (1 other events, 0.8 us)
Sparse Core Ops, SparseCore 0:
  21.7 145.4 all-gather.10
  169.1 66.6 all-gather.14
  238.3 106.1 all-gather.12
  575.7 40.0 all-reduce.2
  677.1 24.5 all-gather.18
  703.6 39.5 all-gather.20
  745.2 27.5 all-gather.16

commit v8 on v7

--- a/solution.py
+++ b/solution.py
@@ -14,7 +14,7 @@
 EPSILON = 1e-06
 ROPE_BASE = 1000000.0
 MASKED_SCORE = -1e30
-CHUNKS = 4
+CHUNKS = 8
 LANES = 128
 VMEM_LIMIT = 60 * 2**20
 MESH = pl.DeviceIdType.MESH

time: 802 us -> 789 us (0.984)
  Pallas kernels: 658 us -> 646 us
where the time goes in v8:
time: 789 us; the launch traced here: 780 us
  Pallas kernels  646 us (82%)
  waiting for transfers between devices  78.9 us (10%)
  local copies, waits for them, and re-layouts  16.2 us (2%)
  between operations  14.9 us (2%)
  other arithmetic  12.2 us (2%)
    pallas_call x2, Pallas kernels, mlp_forward(): pl.pallas_call(partial(mlp_kernel, line, CHUNKS, ff_tile(hidden)), in_spe...  200 us
    pallas_call x2, Pallas kernels, mlp_backward(): pl.pallas_call(partial(mlp_back_kernel, line, CHUNKS, ff_tile(hidden)), i...  188 us
    pallas_call x1, Pallas kernels, gather_first(): pl.pallas_call(partial(gather_kernel, line, peers), in_specs=[vspec()] *...  91.5 us
    all_gather x2, waiting for transfers between devices, weights(): mlp = lax.all_gather(ff[layer], ('section', 'dp'), axis=0)  72 us
    pallas_call x2, Pallas kernels, attend_backward(): pl.pallas_call(partial(attend_back_kernel, line, heads // KV_HEADS), in_s...  68.7 us
    pallas_call x1, Pallas kernels, reduce_first(): pl.pallas_call(partial(reduce_kernel, line, peers, extra), in_specs=[vspe...  52.8 us
    pallas_call x2, Pallas kernels, attend_forward(): pl.pallas_call(partial(attend_kernel, line, heads // KV_HEADS), in_specs=...  33.3 us
  transfers between devices with their start and end apart: 8, of which 3 were waited for; matrix products, arithmetic and copies ran while one was open for 2% of the time, Pallas kernels for 53%

profile of v8, /device:TPU:0, one launch (start us, length us, event | category | flops | bytes accessed | tf_op | source)
XLA Modules:
  0.0 779.6 jit_solution(8814748549425691166)
XLA Ops:
  7.2 2.5 fusion.7
  10.9 7.9 %all_to_all.10 = bf16[2,3,1120,384]{3,2,1,0:T(8,128)(2,1)S(1)} all-to-all(bf16[2,3,1120,384]{3,2,1,0:T(8,128)(2,1)S(1)} %pad_maximum_fusion), channel_id=1, replica_groups=mesh['section'=2,'dp'=4,'tensor'=4] {'section'}, dimensions={0} | all-to-all | bytes 10321920 | tf_op jit(solution)/shard_map/all_to_all | solution.py:1562
  18.7 2.8 fusion.6
  23.8 3.5 all-to-all-start
  28.0 3.2 shard_map.250
  32.0 91.5 %shard_map.251 = (bf16[8,4,192,896]{3,2,1,0:T(8,128)(2,1)}, bf16[4,192,896]{2,1,0:T(8,128)(2,1)}, bf16[2,288,1536]{2,1,0:T(8,128)(2,1)}) custom-call(bf16[2,192,896]{2,1,0:T(8,128)(2,1)} %copy-done.5, bf16[2,288,1536]{2,1,0:T(8,128)(2,1)} %get-tuple-element.65.bundles, bf16[2,48,384]{2,1,0:T(8,128)(2,1)} %get-tuple-element.66.heads), custom_call_target="tpu_custom_call" | custom-call | tf_op jit(solution)/shard_map/pallas_call | solution.py:797
  125.6 1.2 pad_add_fusion.info_ref
  131.1 1.3 slice_bitcast_fusion
  132.4 16.6 %shard_map.252 = (f32[256,1536]{1,0:T(8,128)}, bf16[256,1536]{1,0:T(8,128)(2,1)}, bf16[256,1536]{1,0:T(8,128)(2,1)}, bf16[256,48]{1,0:T(8,128)(2,1)}, bf16[256,1...) custom-call(s32[2]{0:T(128)} %pad_add_fusion.info_ref, ...), custom_call_target="tpu_custom_call" | custom-call | flops 4831838208 | bytes 11796480 | tf_op jit(solution)/shard_map/pallas_call | solution.py:1001
  151.1 16.2 %all-gather.11.cloned.1.call-done = bf16[8,3,1120,384]{3,2,1,0:T(8,128)(2,1)} async-done(((bf16[1,3,1120,384]{3,2,1,0:T(8,128)(2,1)}), bf16[8,3,1120,384]{3,2,1,0:T(8,128)(2,1)}) %all-gather.11.cloned.1.call-update) | async-done | bytes 20643856 | tf_op jit(solution)/shard_map/all_gather | solution.py:1626
  167.3 102.3 %shard_map.253 = (f32[8,32,1536]{2,1,0:T(8,128)}, bf16[8,4,32,1536]{3,2,1,0:T(8,128)(2,1)}, bf16[8,128,2304]{2,1,0:T(8,128)(2,1)}, bf16[8,128,2304]{2,1,0:T(8,128)(2,1)}) custom-call(bf16[8,32,1536]{2,1,0:T(8,128)(2,1)} %bitcast.122, bf16[2,4,3,1120,384]{4,3,2,1,0:T(8,128)(2,1)} %bitcast.108, bf16[288,1536]{1,0:T(8,128)(2,1)} %get-tuple-element.130.bundle_ref), custom_call_target="tpu_custom_call" | custom-call | flops 21743271936 | bytes 30670848 | tf_op jit(solution)/shard_map/pallas_call | solution.py:384
  269.6 2.5 fusion.1.x_ref.y_first
  272.0 16.7 %shard_map.254 = (f32[256,1536]{1,0:T(8,128)}, bf16[256,1536]{1,0:T(8,128)(2,1)}, bf16[256,1536]{1,0:T(8,128)(2,1)}, bf16[256,48]{1,0:T(8,128)(2,1)}, bf16[256,1...) custom-call(s32[2]{0:T(128)} %pad_add_fusion.info_ref, ...), custom_call_target="tpu_custom_call" | custom-call | flops 4831838208 | bytes 11796480 | tf_op jit(solution)/shard_map/pallas_call | solution.py:1001
  288.7 55.8 %all-gather.13.cloned.1.call-done = bf16[8,3,1120,384]{3,2,1,0:T(8,128)(2,1)} async-done(((bf16[1,3,1120,384]{3,2,1,0:T(8,128)(2,1)}), bf16[8,3,1120,384]{3,2,1,0:T(8,128)(2,1)}) %all-gather.13.cloned.1.call-update) | async-done | bytes 20643856 | tf_op jit(solution)/shard_map/all_gather | solution.py:1626
  344.5 97.9 %shard_map.255 = (f32[8,32,1536]{2,1,0:T(8,128)}, bf16[8,4,32,1536]{3,2,1,0:T(8,128)(2,1)}, bf16[8,128,2304]{2,1,0:T(8,128)(2,1)}, bf16[8,128,2304]{2,1,0:T(8,128)(2,1)}) custom-call(bf16[8,32,1536]{2,1,0:T(8,128)(2,1)} %bitcast.123, bf16[2,4,3,1120,384]{4,3,2,1,0:T(8,128)(2,1)} %bitcast.110, bf16[288,1536]{1,0:T(8,128)(2,1)} %get-tuple-element.129.bundle_ref), custom_call_target="tpu_custom_call" | custom-call | flops 21743271936 | bytes 30670848 | tf_op jit(solution)/shard_map/pallas_call | solution.py:384
  443.0 89.4 %shard_map.256 = (f32[8,32,1536]{2,1,0:T(8,128)}, bf16[48,1536]{1,0:T(8,128)(2,1)}, bf16[96,1536]{1,0:T(8,128)(2,1)}) custom-call(bf16[8,32,1536]{2,1,0:T(8,128)(2,1)} %broadcast_select_fusion.ds_ref, bf16[2,4,3,1120,384]{4,3,2,1,0:T(8,128)(2,1)} %bitcast.111, bf16[8,128,1536]{2,1,0:T(8,128)(2,1)} %bitcast.121, ...), custom_call_target="tpu_custom_call" | custom-call | flops 21743271936 | bytes 30670848 | tf_op jit(solution)/shard_map/pallas_call | solution.py:541
  532.4 34.4 %shard_map.257 = (f32[256,1536]{1,0:T(8,128)}, bf16[256,1536]{1,0:T(8,128)(2,1)}, bf16[112,1536]{1,0:T(8,128)(2,1)}) custom-call(s32[2]{0:T(128)} %pad_add_fusion.info_ref, bf16[256,1536]{1,0:T(8,128)(2,1)} %fusion.1.x_ref.y_first, f32[256,1536]{1,0:T(8,128)} %get-tuple-element.73.mid_ref, bf16[256,1536]{1,0:T(8,128)(2,1)} %get-tuple-element.123.dy_ref, ...), custom_call_target="tpu_custom_call" | custom-call | flops 4831838208 | bytes 11796480 | tf_op jit(solution)/shard_map/pallas_call | solution.py:1188
  566.9 98.3 %shard_map.258 = (f32[8,32,1536]{2,1,0:T(8,128)}, bf16[48,1536]{1,0:T(8,128)(2,1)}, bf16[96,1536]{1,0:T(8,128)(2,1)}) custom-call(bf16[8,32,1536]{2,1,0:T(8,128)(2,1)} %bitcast.116, bf16[2,4,3,1120,384]{4,3,2,1,0:T(8,128)(2,1)} %bitcast.109, bf16[8,128,1536]{2,1,0:T(8,128)(2,1)} %bitcast.120, bf16[8,128,2304]{2,1,0:T(8,128)(2,1)} %get-tuple-element.92.gate_in, ...), custom_call_target="tpu_custom_call" | custom-call | flops 21743271936 | bytes 30670848 | tf_op jit(solution)/shard_map/pallas_call | solution.py:541
  667.7 34.2 %shard_map.259 = (f32[256,1536]{1,0:T(8,128)}, bf16[256,1536]{1,0:T(8,128)(2,1)}, bf16[112,1536]{1,0:T(8,128)(2,1)}) custom-call(s32[2]{0:T(128)} %pad_add_fusion.info_ref, bf16[256,1536]{1,0:T(8,128)(2,1)} %dynamic-slice_bitcast_fusion.x_ref, f32[256,1536]{1,0:T(8,128)} %get-tuple-element.69.mid_ref, f32[256,1536]{1,0:T(8,128)} %get-tuple-element.86.dy_ref.g_second, ...), custom_call_target="tpu_custom_call" | custom-call | flops 4831838208 | bytes 11796480 | tf_op jit(solution)/shard_map/pallas_call | solution.py:1188
  701.9 52.8 %shard_map.260 = (bf16[8,224,1536]{2,1,0:T(8,128)(2,1)}, bf16[2,256,1536]{2,1,0:T(8,128)(2,1)}, f32[2,256,1536]{2,1,0:T(8,128)}) custom-call(bf16[112,1536]{1,0:T(8,128)(2,1)} %get-tuple-element.103.attn_ref, bf16[48,1536]{1,0:T(8,128)(2,1)} %get-tuple-element.104.whole_ref, bf16[96,1536]{1,0:T(8,128)(2,1)} %get-tuple-element.105.parts_ref, ...), custom_call_target="tpu_custom_call" | custom-call | tf_op jit(solution)/shard_map/pallas_call | solution.py:1438
  754.8 4.9 all-gather.17.cloned.1.call-done
  759.7 8.4 %shard_map.261 = (f32[8,80,1536]{2,1,0:T(8,128)}, f32[8,16,384]{2,1,0:T(8,128)}, f32[8,2,16,256]{3,2,1,0:T(8,128)}, f32[8,2,16,2240]{3,2,1,0:T(8,128)}, f32[8,16...) custom-call(bf16[8,224,1536]{2,1,0:T(8,128)(2,1)} %get-tuple-element.110.first, ...), custom_call_target="tpu_custom_call" | custom-call | tf_op jit(solution)/shard_map/pallas_call | solution.py:1546
  769.3 1.3 copy-done.4
  770.6 1.7 copy.39
  (73 shorter events, 17.5 us)
Async XLA Ops:
  7.2 123.0 %copy-start = (bf16[2,256,1536]{2,1,0:T(8,128)(2,1)S(1)}, bf16[2,256,1536]{2,1,0:T(8,128)(2,1)}, u32[]{:S(2)}) copy-start(bf16[2,256,1536]{2,1,0:T(8,128)(2,1)} %param.19) | copy-start | bytes 4718596
  7.2 160.1 %all-gather.11.cloned.1.call-start = ((), (), s32[]{:S(2)}) async-start(), calls=%async_computation.2 | async-start | bytes 23224320 | tf_op jit(solution)/shard_map/all_gather | solution.py:1626
  7.2 2.6 copy-start.7
  21.6 1.0 copy-start.12
  21.6 1.2 copy-start.10
  21.6 1.3 copy-start.13
  22.8 4.6 copy-start.14
  23.8 7.3 all-to-all-start
  27.3 244.7 %all-gather.15.cloned.1.call-start = ((), (), s32[]{:S(2)}) async-start(), calls=%async_computation.4 | async-start | bytes 12386304 | tf_op jit(solution)/shard_map/all_gather | solution.py:1625
  123.5 0.9 copy-start.15
  123.5 1.4 copy-start.16
  123.6 221.0 %all-gather.13.cloned.1.call-start = ((), (), s32[]{:S(2)}) async-start(), calls=%async_computation.3 | async-start | bytes 23224320 | tf_op jit(solution)/shard_map/all_gather | solution.py:1626
  124.3 6.8 copy-start.6
  124.3 540.9 %all-reduce.3.cloned.1.call-start = ((), (), s32[]{:S(2)}) async-start(), calls=%async_computation.8 | async-start | bytes 983040 | tf_op jit(solution)/shard_map/psum | solution.py:1671
  132.4 16.6 %copy-start.11 = (bf16[2,256,1536]{2,1,0:T(8,128)(2,1)S(1)}, bf16[2,256,1536]{2,1,0:T(8,128)(2,1)}, u32[]{:S(2)}) copy-start(bf16[2,256,1536]{2,1,0:T(8,128)(2,1)} %param.22) | copy-start | bytes 4718596
  167.3 102.3 %copy-start.2 = (f32[256,1536]{1,0:T(8,128)S(1)}, f32[256,1536]{1,0:T(8,128)}, u32[]{:S(2)}) copy-start(f32[256,1536]{1,0:T(8,128)} %get-tuple-element.69.mid_ref) | copy-start | bytes 4718596
  566.9 187.9 %all-gather.19.cloned.1.call-start = ((), (), s32[]{:S(2)}) async-start(), calls=%async_computation.6 | async-start | bytes 1327104 | tf_op jit(solution)/shard_map/all_gather | solution.py:1655
  566.9 99.7 %copy-start.3 = (f32[256,1536]{1,0:T(8,128)S(1)}, f32[256,1536]{1,0:T(8,128)}, u32[]{:S(2)}) copy-start(f32[256,1536]{1,0:T(8,128)} %get-tuple-element.73.mid_ref) | copy-start | bytes 4718596
  566.9 99.7 %copy-start.9 = (f32[8,32,1536]{2,1,0:T(8,128)S(1)}, f32[8,32,1536]{2,1,0:T(8,128)}, u32[]{:S(2)}) copy-start(f32[8,32,1536]{2,1,0:T(8,128)} %get-tuple-element.106) | copy-start | bytes 4718596
  665.2 89.6 %all-gather.21.cloned.1.call-start = ((), (), s32[]{:S(2)}) async-start(), calls=%async_computation.7 | async-start | bytes 2654208 | tf_op jit(solution)/shard_map/all_gather | solution.py:1655
  665.8 93.9 %all-gather.17.cloned.1.call-start = ((), (), s32[]{:S(2)}) async-start(), calls=%async_computation.5 | async-start | bytes 3096576 | tf_op jit(solution)/shard_map/all_gather | solution.py:1655
  759.7 8.4 %copy-start.8 = (bf16[2,256,1536]{2,1,0:T(8,128)(2,1)S(1)}, bf16[2,256,1536]{2,1,0:T(8,128)(2,1)}, u32[]{:S(2)}) copy-start(bf16[2,256,1536]{2,1,0:T(8,128)(2,1)} %get-tuple-element.108) | copy-start | bytes 4718596
  768.2 2.5 copy-start.4
  768.2 4.1 copy-start.1
  (1 other events, 0.8 us)
Sparse Core Ops, SparseCore 0:
  21.7 145.4 all-gather.10
  169.1 66.6 all-gather.14
  238.3 106.2 all-gather.12
  567.0 42.5 all-reduce.2
  665.4 23.4 all-gather.18
  690.7 39.4 all-gather.20
  732.2 27.4 all-gather.16

commit v9 on v8

--- a/solution.py
+++ b/solution.py
@@ -574,6 +574,65 @@
         ds.reshape(CHUNKS, part, width), w["mlp"], n2_all, gate, up, w["bundle"], names,
     )
     return out.reshape(rows, width), whole, parts
+
+
+def halves_kernel(expand, shrink, first, second, stage, in_sem, keep_sem, send_sem, recv_sem):
+    core = lax.axis_index("section")
+    half = first.shape[1]
+    barrier = pltpu.get_barrier_semaphore()
+    pl.semaphore_signal(barrier, inc=1, device_id={"section": 1 - core}, device_id_type=MESH)
+    for c in range(2):
+
+        @pl.when(core == c)
+        def _():
+            own = (expand.at[:, pl.ds(c * half, half)], shrink.at[pl.ds(c * half, half)])
+            for i, dst in enumerate((stage.at[pl.ds(0, 2)], stage.at[2])):
+                pltpu.make_async_copy(own[i], dst, in_sem.at[i]).start()
+
+    pl.semaphore_wait(barrier, 1)
+    for c, out in enumerate((first, second)):
+
+        @pl.when(core == c)
+        def _():
+            away = (expand.at[:, pl.ds((1 - c) * half, half)], shrink.at[pl.ds((1 - c) * half, half)])
+            places = (out.at[pl.ds(0, 2)], out.at[2])
+            sends = [
+                pltpu.make_async_remote_copy(
+                    src_ref=away[i],
+                    dst_ref=places[i],
+                    send_sem=send_sem.at[i],
+                    recv_sem=recv_sem.at[i],
+                    device_id={"section": 1 - c},
+                    device_id_type=MESH,
+                )
+                for i in range(2)
+            ]
+            for send in sends:
+                send.start()
+            own = (expand.at[:, pl.ds(c * half, half)], shrink.at[pl.ds(c * half, half)])
+            for i, dst in enumerate((stage.at[pl.ds(0, 2)], stage.at[2])):
+                pltpu.make_async_copy(own[i], dst, in_sem.at[i]).wait()
+            keep = pltpu.make_async_copy(stage, out, keep_sem)
+            keep.start()
+            keep.wait()
+            for send in sends:
+                send.wait()
+
+
+def weight_halves(expand, shrink):
+    _, hidden, cols = expand.shape
+    shape = (3, hidden // 2, cols)
+    dma = pltpu.SemaphoreType.DMA
+    return pl.pallas_call(
+        halves_kernel,
+        in_specs=[hspec()] * 2,
+        out_specs=[hspec()] * 2,
+        out_shape=[jax.ShapeDtypeStruct(shape, BF)] * 2,
+        scratch_shapes=[pltpu.VMEM(shape, BF), dma((2,)), dma, dma((2,)), dma((2,))],
+        compiler_params=pltpu.CompilerParams(
+            collective_id=7, has_side_effects=True, vmem_limit_bytes=VMEM_LIMIT
+        ),
+    )(expand, shrink)
 
 
 def gather_kernel(
@@ -1608,11 +1667,7 @@
         (norm_gain[0], keyvalue_bias.reshape(1, -1), query_bias),
     )
 
-    ff = jnp.concatenate(
-        [m.reshape(layers, 1, hidden // layers, m.shape[1]) for m in (*turned(expand_weight), shrink_weight[0])],
-        axis=1,
-    )
-    ff = swap(ff)
+    ff = weight_halves(turned(expand_weight), shrink_weight[0])
     kv = jnp.concatenate([keyvalue_weight[0, 0], keyvalue_weight[0, 1]], axis=1)
     kv_cols = kv.shape[1] // tensor
     kv = lax.dynamic_slice_in_dim(kv, place * kv_cols, kv_cols, 1)

time: 789 us -> 781 us (0.990)
  transfers between devices with their start and end apart: 8 -> 8, of which waited for: 3 -> 3; matrix products, arithmetic and copies ran while one was open for 2% -> 2% of each run, Pallas kernels for 53% -> 54%
where the time goes in v9:
time: 781 us; the launch traced here: 771 us
  Pallas kernels  650 us (83%)
  waiting for transfers between devices  79 us (10%)
  between operations  14.9 us (2%)
  local copies, waits for them, and re-layouts  11.6 us (1%)
  other arithmetic  11.2 us (1%)
    pallas_call x2, Pallas kernels, mlp_forward(): pl.pallas_call(partial(mlp_kernel, line, CHUNKS, ff_tile(hidden)), in_spe...  200 us
    pallas_call x2, Pallas kernels, mlp_backward(): pl.pallas_call(partial(mlp_back_kernel, line, CHUNKS, ff_tile(hidden)), i...  188 us
    pallas_call x1, Pallas kernels, gather_first(): pl.pallas_call(partial(gather_kernel, line, peers), in_specs=[vspec()] *...  91.5 us
    all_gather x2, waiting for transfers between devices, weights(): mlp = lax.all_gather(ff[layer], ('section', 'dp'), axis=0)  72 us
    pallas_call x2, Pallas kernels, attend_backward(): pl.pallas_call(partial(attend_back_kernel, line, heads // KV_HEADS), in_s...  68.8 us
    pallas_call x1, Pallas kernels, reduce_first(): pl.pallas_call(partial(reduce_kernel, line, peers, extra), in_specs=[vspe...  52.8 us
    pallas_call x2, Pallas kernels, attend_forward(): pl.pallas_call(partial(attend_kernel, line, heads // KV_HEADS), in_specs=...  32.9 us
  transfers between devices with their start and end apart: 8, of which 3 were waited for; matrix products, arithmetic and copies ran while one was open for 2% of the time, Pallas kernels for 54%

profile of v9, /device:TPU:0, one launch (start us, length us, event | category | flops | bytes accessed | tf_op | source)
XLA Modules:
  0.0 771.0 jit_solution(16286546264321617022)
XLA Ops:
  7.2 5.4 shard_map.253
  14.8 3.5 all-to-all-start
  19.0 3.2 shard_map.250
  23.0 91.5 %shard_map.251 = (bf16[8,4,192,896]{3,2,1,0:T(8,128)(2,1)}, bf16[4,192,896]{2,1,0:T(8,128)(2,1)}, bf16[2,288,1536]{2,1,0:T(8,128)(2,1)}) custom-call(bf16[2,192,896]{2,1,0:T(8,128)(2,1)} %copy-done.5, bf16[2,288,1536]{2,1,0:T(8,128)(2,1)} %get-tuple-element.67.bundles, bf16[2,48,384]{2,1,0:T(8,128)(2,1)} %get-tuple-element.68.heads), custom_call_target="tpu_custom_call" | custom-call | tf_op jit(solution)/shard_map/pallas_call | solution.py:856
  116.6 1.3 pad_add_fusion.info_ref
  122.2 1.3 slice_bitcast_fusion
  123.5 16.5 %shard_map.252 = (f32[256,1536]{1,0:T(8,128)}, bf16[256,1536]{1,0:T(8,128)(2,1)}, bf16[256,1536]{1,0:T(8,128)(2,1)}, bf16[256,48]{1,0:T(8,128)(2,1)}, bf16[256,1...) custom-call(s32[2]{0:T(128)} %pad_add_fusion.info_ref, ...), custom_call_target="tpu_custom_call" | custom-call | flops 4831838208 | bytes 11796480 | tf_op jit(solution)/shard_map/pallas_call | solution.py:1060
  142.1 16.2 %all-gather.13.cloned.1.call-done = bf16[24,1120,384]{2,1,0:T(8,128)(2,1)} async-done(((bf16[3,1120,384]{2,1,0:T(8,128)(2,1)}), bf16[24,1120,384]{2,1,0:T(8,128)(2,1)}) %all-gather.13.cloned.1.call-update) | async-done | bytes 20643856 | tf_op jit(solution)/shard_map/all_gather | solution.py:1681
  158.2 102.1 %shard_map.254 = (f32[8,32,1536]{2,1,0:T(8,128)}, bf16[8,4,32,1536]{3,2,1,0:T(8,128)(2,1)}, bf16[8,128,2304]{2,1,0:T(8,128)(2,1)}, bf16[8,128,2304]{2,1,0:T(8,128)(2,1)}) custom-call(bf16[8,32,1536]{2,1,0:T(8,128)(2,1)} %bitcast.118, bf16[2,4,3,1120,384]{4,3,2,1,0:T(8,128)(2,1)} %bitcast.104, bf16[288,1536]{1,0:T(8,128)(2,1)} %get-tuple-element.130.bundle_ref), custom_call_target="tpu_custom_call" | custom-call | flops 21743271936 | bytes 30670848 | tf_op jit(solution)/shard_map/pallas_call | solution.py:384
  260.3 2.5 fusion.1.x_ref.y_first
  262.8 16.4 %shard_map.255 = (f32[256,1536]{1,0:T(8,128)}, bf16[256,1536]{1,0:T(8,128)(2,1)}, bf16[256,1536]{1,0:T(8,128)(2,1)}, bf16[256,48]{1,0:T(8,128)(2,1)}, bf16[256,1...) custom-call(s32[2]{0:T(128)} %pad_add_fusion.info_ref, ...), custom_call_target="tpu_custom_call" | custom-call | flops 4831838208 | bytes 11796480 | tf_op jit(solution)/shard_map/pallas_call | solution.py:1060
  279.2 55.8 %all-gather.17.cloned.1.call-done = bf16[24,1120,384]{2,1,0:T(8,128)(2,1)} async-done(((bf16[3,1120,384]{2,1,0:T(8,128)(2,1)}), bf16[24,1120,384]{2,1,0:T(8,128)(2,1)}) %all-gather.17.cloned.1.call-update) | async-done | bytes 20643856 | tf_op jit(solution)/shard_map/all_gather | solution.py:1681
  335.0 97.9 %shard_map.256 = (f32[8,32,1536]{2,1,0:T(8,128)}, bf16[8,4,32,1536]{3,2,1,0:T(8,128)(2,1)}, bf16[8,128,2304]{2,1,0:T(8,128)(2,1)}, bf16[8,128,2304]{2,1,0:T(8,128)(2,1)}) custom-call(bf16[8,32,1536]{2,1,0:T(8,128)(2,1)} %bitcast.119, bf16[2,4,3,1120,384]{4,3,2,1,0:T(8,128)(2,1)} %bitcast.106, bf16[288,1536]{1,0:T(8,128)(2,1)} %get-tuple-element.129.bundle_ref), custom_call_target="tpu_custom_call" | custom-call | flops 21743271936 | bytes 30670848 | tf_op jit(solution)/shard_map/pallas_call | solution.py:384
  433.5 89.3 %shard_map.257 = (f32[8,32,1536]{2,1,0:T(8,128)}, bf16[48,1536]{1,0:T(8,128)(2,1)}, bf16[96,1536]{1,0:T(8,128)(2,1)}) custom-call(bf16[8,32,1536]{2,1,0:T(8,128)(2,1)} %broadcast_select_fusion.ds_ref, bf16[2,4,3,1120,384]{4,3,2,1,0:T(8,128)(2,1)} %bitcast.107, bf16[8,128,1536]{2,1,0:T(8,128)(2,1)} %bitcast.117, ...), custom_call_target="tpu_custom_call" | custom-call | flops 21743271936 | bytes 30670848 | tf_op jit(solution)/shard_map/pallas_call | solution.py:541
  522.8 34.5 %shard_map.258 = (f32[256,1536]{1,0:T(8,128)}, bf16[256,1536]{1,0:T(8,128)(2,1)}, bf16[112,1536]{1,0:T(8,128)(2,1)}) custom-call(s32[2]{0:T(128)} %pad_add_fusion.info_ref, bf16[256,1536]{1,0:T(8,128)(2,1)} %fusion.1.x_ref.y_first, f32[256,1536]{1,0:T(8,128)} %get-tuple-element.76.mid_ref, bf16[256,1536]{1,0:T(8,128)(2,1)} %get-tuple-element.127.dy_ref, ...), custom_call_target="tpu_custom_call" | custom-call | flops 4831838208 | bytes 11796480 | tf_op jit(solution)/shard_map/pallas_call | solution.py:1247
  557.5 98.3 %shard_map.259 = (f32[8,32,1536]{2,1,0:T(8,128)}, bf16[48,1536]{1,0:T(8,128)(2,1)}, bf16[96,1536]{1,0:T(8,128)(2,1)}) custom-call(bf16[8,32,1536]{2,1,0:T(8,128)(2,1)} %bitcast.112, bf16[2,4,3,1120,384]{4,3,2,1,0:T(8,128)(2,1)} %bitcast.105, bf16[8,128,1536]{2,1,0:T(8,128)(2,1)} %bitcast.116, bf16[8,128,2304]{2,1,0:T(8,128)(2,1)} %get-tuple-element.96.gate_in, ...), custom_call_target="tpu_custom_call" | custom-call | flops 21743271936 | bytes 30670848 | tf_op jit(solution)/shard_map/pallas_call | solution.py:541
  657.1 1.1 fusion.y_second
  658.2 34.2 %shard_map.260 = (f32[256,1536]{1,0:T(8,128)}, bf16[256,1536]{1,0:T(8,128)(2,1)}, bf16[112,1536]{1,0:T(8,128)(2,1)}) custom-call(s32[2]{0:T(128)} %pad_add_fusion.info_ref, bf16[256,1536]{1,0:T(8,128)(2,1)} %dynamic-slice_bitcast_fusion.x_ref, f32[256,1536]{1,0:T(8,128)} %get-tuple-element.71.mid_ref, f32[256,1536]{1,0:T(8,128)} %get-tuple-element.90.dy_ref.g_second, ...), custom_call_target="tpu_custom_call" | custom-call | flops 4831838208 | bytes 11796480 | tf_op jit(solution)/shard_map/pallas_call | solution.py:1247
  692.5 52.8 %shard_map.261 = (bf16[8,224,1536]{2,1,0:T(8,128)(2,1)}, bf16[2,256,1536]{2,1,0:T(8,128)(2,1)}, f32[2,256,1536]{2,1,0:T(8,128)}) custom-call(bf16[112,1536]{1,0:T(8,128)(2,1)} %get-tuple-element.107.attn_ref, bf16[48,1536]{1,0:T(8,128)(2,1)} %get-tuple-element.108.whole_ref, bf16[96,1536]{1,0:T(8,128)(2,1)} %get-tuple-element.109.parts_ref, ...), custom_call_target="tpu_custom_call" | custom-call | tf_op jit(solution)/shard_map/pallas_call | solution.py:1497
  745.4 4.9 all-gather.19.cloned.1.call-done
  750.3 8.4 %shard_map.262 = (f32[8,80,1536]{2,1,0:T(8,128)}, f32[8,16,384]{2,1,0:T(8,128)}, f32[8,2,16,256]{3,2,1,0:T(8,128)}, f32[8,2,16,2240]{3,2,1,0:T(8,128)}, f32[8,16...) custom-call(bf16[8,224,1536]{2,1,0:T(8,128)(2,1)} %get-tuple-element.114.first, ...), custom_call_target="tpu_custom_call" | custom-call | tf_op jit(solution)/shard_map/pallas_call | solution.py:1605
  758.7 1.1 copy.35
  759.9 1.3 copy-done.4
  761.2 1.7 copy.36
  (68 shorter events, 14.9 us)
Async XLA Ops:
  7.2 114.0 %copy-start = (bf16[2,256,1536]{2,1,0:T(8,128)(2,1)S(1)}, bf16[2,256,1536]{2,1,0:T(8,128)(2,1)}, u32[]{:S(2)}) copy-start(bf16[2,256,1536]{2,1,0:T(8,128)(2,1)} %param.19) | copy-start | bytes 4718596
  7.2 151.1 %all-gather.13.cloned.1.call-start = ((), (), s32[]{:S(2)}) async-start(), calls=%async_computation.1 | async-start | bytes 23224320 | tf_op jit(solution)/shard_map/all_gather | solution.py:1681
  12.6 1.0 copy-start.11
  12.6 1.2 copy-start.9
  12.7 1.3 copy-start.12
  13.8 4.6 copy-start.13
  14.8 7.3 all-to-all-start
  18.4 244.4 %all-gather.15.cloned.1.call-start = ((), (), s32[]{:S(2)}) async-start(), calls=%async_computation.2 | async-start | bytes 12386304 | tf_op jit(solution)/shard_map/all_gather | solution.py:1680
  22.2 0.8 copy-start.5
  114.5 0.8 copy-start.14
  114.5 1.4 copy-start.15
  114.6 220.4 %all-gather.17.cloned.1.call-start = ((), (), s32[]{:S(2)}) async-start(), calls=%async_computation.3 | async-start | bytes 23224320 | tf_op jit(solution)/shard_map/all_gather | solution.py:1681
  115.3 6.9 copy-start.6
  115.3 540.4 %all-reduce.3.cloned.1.call-start = ((), (), s32[]{:S(2)}) async-start(), calls=%async_computation.7 | async-start | bytes 983040 | tf_op jit(solution)/shard_map/psum | solution.py:1726
  123.5 16.6 %copy-start.10 = (bf16[2,256,1536]{2,1,0:T(8,128)(2,1)S(1)}, bf16[2,256,1536]{2,1,0:T(8,128)(2,1)}, u32[]{:S(2)}) copy-start(bf16[2,256,1536]{2,1,0:T(8,128)(2,1)} %param.22) | copy-start | bytes 4718596
  158.2 102.1 %copy-start.2 = (f32[256,1536]{1,0:T(8,128)S(1)}, f32[256,1536]{1,0:T(8,128)}, u32[]{:S(2)}) copy-start(f32[256,1536]{1,0:T(8,128)} %get-tuple-element.71.mid_ref) | copy-start | bytes 4718596
  557.4 187.9 %all-gather.21.cloned.1.call-start = ((), (), s32[]{:S(2)}) async-start(), calls=%async_computation.5 | async-start | bytes 1327104 | tf_op jit(solution)/shard_map/all_gather | solution.py:1710
  557.4 99.7 %copy-start.3 = (f32[256,1536]{1,0:T(8,128)S(1)}, f32[256,1536]{1,0:T(8,128)}, u32[]{:S(2)}) copy-start(f32[256,1536]{1,0:T(8,128)} %get-tuple-element.76.mid_ref) | copy-start | bytes 4718596
  557.4 99.7 %copy-start.8 = (f32[8,32,1536]{2,1,0:T(8,128)S(1)}, f32[8,32,1536]{2,1,0:T(8,128)}, u32[]{:S(2)}) copy-start(f32[8,32,1536]{2,1,0:T(8,128)} %get-tuple-element.110) | copy-start | bytes 4718596
  655.8 89.6 %all-gather.23.cloned.1.call-start = ((), (), s32[]{:S(2)}) async-start(), calls=%async_computation.6 | async-start | bytes 2654208 | tf_op jit(solution)/shard_map/all_gather | solution.py:1710
  656.4 93.9 %all-gather.19.cloned.1.call-start = ((), (), s32[]{:S(2)}) async-start(), calls=%async_computation.4 | async-start | bytes 3096576 | tf_op jit(solution)/shard_map/all_gather | solution.py:1710
  750.3 8.4 %copy-start.7 = (bf16[2,256,1536]{2,1,0:T(8,128)(2,1)S(1)}, bf16[2,256,1536]{2,1,0:T(8,128)(2,1)}, u32[]{:S(2)}) copy-start(bf16[2,256,1536]{2,1,0:T(8,128)(2,1)} %get-tuple-element.112) | copy-start | bytes 4718596
  758.7 2.5 copy-start.4
  761.2 2.5 copy-start.1
Sparse Core Ops, SparseCore 0:
  12.8 145.4 all-gather.12
  160.1 66.6 all-gather.14
  228.7 106.2 all-gather.16
  557.5 43.3 all-reduce.2
  655.9 23.4 all-gather.20
  681.2 39.4 all-gather.22
  722.7 27.5 all-gather.18

commit v10 on v9

--- a/solution.py
+++ b/solution.py
@@ -1714,17 +1714,17 @@
     for layer in reversed(range(layers)):
         x, middle, attn_kept, mlp_kept = kept[layer]
         if layer < layers - 1:
-            low_grad, here = lax.optimization_barrier((low_grad, here))
+            low_grad, here, last_parts = lax.optimization_barrier((low_grad, here, last_parts))
         dn2, whole, parts = mlp_backward(low_grad, w[layer], mlp_kept, names)
         if layer < layers - 1:
             total, dn2 = lax.optimization_barrier((total, dn2))
-            gathered[layer + 1] = gather_all(*total, last_parts)
+            gathered[layer + 1] = gather_all(*total) + last_parts
         grad, low_grad, attn_part = attend_backward(x, middle, grad, dn2, w[layer], attn_kept, info, tables)
         grads[layer] = grad
         here = (attn_part, whole)
         if layer > 0:
             total = lax.psum(here, "tensor")
-            last_parts = parts
+            last_parts = gather_all(parts)
     gathered[0], layer_output, input_grad = reduce_first(*here, parts, extra, outs, grads)
     totals = total_by_adapter(
         gathered[0], *gathered[1], count, 1.0 / math.sqrt(tokens), hidden, q_cols, kv_half

time: 781 us -> 779 us (level)
  transfers between devices with their start and end apart: 8 -> 8, of which waited for: 3 -> 2; matrix products, arithmetic and copies ran while one was open for 2% -> 2% of each run, Pallas kernels for 54% -> 59%
where the time goes in v10:
time: 779 us; the launch traced here: 770 us
  Pallas kernels  655 us (84%)
  waiting for transfers between devices  73.5 us (9%)
  between operations  15 us (2%)
  local copies, waits for them, and re-layouts  11.6 us (1%)
  other arithmetic  11.2 us (1%)
    pallas_call x2, Pallas kernels, mlp_forward(): pl.pallas_call(partial(mlp_kernel, line, CHUNKS, ff_tile(hidden)), in_spe...  200 us
    pallas_call x2, Pallas kernels, mlp_backward(): pl.pallas_call(partial(mlp_back_kernel, line, CHUNKS, ff_tile(hidden)), i...  191 us
    pallas_call x1, Pallas kernels, gather_first(): pl.pallas_call(partial(gather_kernel, line, peers), in_specs=[vspec()] *...  91.5 us
    all_gather x2, waiting for transfers between devices, weights(): mlp = lax.all_gather(ff[layer], ('section', 'dp'), axis=0)  72 us
    pallas_call x2, Pallas kernels, attend_backward(): pl.pallas_call(partial(attend_back_kernel, line, heads // KV_HEADS), in_s...  67.7 us
    pallas_call x1, Pallas kernels, reduce_first(): pl.pallas_call(partial(reduce_kernel, line, peers, extra), in_specs=[vspe...  54.6 us
    pallas_call x2, Pallas kernels, attend_forward(): pl.pallas_call(partial(attend_kernel, line, heads // KV_HEADS), in_specs=...  32.9 us
  transfers between devices with their start and end apart: 8, of which 2 were waited for; matrix products, arithmetic and copies ran while one was open for 2% of the time, Pallas kernels for 59%

profile of v10, /device:TPU:0, one launch (start us, length us, event | category | flops | bytes accessed | tf_op | source)
XLA Modules:
  0.0 770.4 jit_solution(8163446217410392093)
XLA Ops:
  7.2 5.4 shard_map.253
  14.8 3.5 all-to-all-start
  19.0 3.2 shard_map.250
  23.0 91.5 %shard_map.251 = (bf16[8,4,192,896]{3,2,1,0:T(8,128)(2,1)}, bf16[4,192,896]{2,1,0:T(8,128)(2,1)}, bf16[2,288,1536]{2,1,0:T(8,128)(2,1)}) custom-call(bf16[2,192,896]{2,1,0:T(8,128)(2,1)} %copy-done.5, bf16[2,288,1536]{2,1,0:T(8,128)(2,1)} %get-tuple-element.68.bundles, bf16[2,48,384]{2,1,0:T(8,128)(2,1)} %get-tuple-element.69.heads), custom_call_target="tpu_custom_call" | custom-call | tf_op jit(solution)/shard_map/pallas_call | solution.py:856
  116.6 1.3 pad_add_fusion.info_ref
  122.2 1.3 slice_bitcast_fusion
  123.5 16.5 %shard_map.252 = (f32[256,1536]{1,0:T(8,128)}, bf16[256,1536]{1,0:T(8,128)(2,1)}, bf16[256,1536]{1,0:T(8,128)(2,1)}, bf16[256,48]{1,0:T(8,128)(2,1)}, bf16[256,1...) custom-call(s32[2]{0:T(128)} %pad_add_fusion.info_ref, ...), custom_call_target="tpu_custom_call" | custom-call | flops 4831838208 | bytes 11796480 | tf_op jit(solution)/shard_map/pallas_call | solution.py:1060
  140.0 1.0 bitcast_select_fusion
  142.1 16.2 %all-gather.13.cloned.1.call-done = bf16[24,1120,384]{2,1,0:T(8,128)(2,1)} async-done(((bf16[3,1120,384]{2,1,0:T(8,128)(2,1)}), bf16[24,1120,384]{2,1,0:T(8,128)(2,1)}) %all-gather.13.cloned.1.call-update) | async-done | bytes 20643856 | tf_op jit(solution)/shard_map/all_gather | solution.py:1681
  158.2 102.1 %shard_map.254 = (f32[8,32,1536]{2,1,0:T(8,128)}, bf16[8,4,32,1536]{3,2,1,0:T(8,128)(2,1)}, bf16[8,128,2304]{2,1,0:T(8,128)(2,1)}, bf16[8,128,2304]{2,1,0:T(8,128)(2,1)}) custom-call(bf16[8,32,1536]{2,1,0:T(8,128)(2,1)} %bitcast.118, bf16[2,4,3,1120,384]{4,3,2,1,0:T(8,128)(2,1)} %bitcast.104, bf16[288,1536]{1,0:T(8,128)(2,1)} %get-tuple-element.132.bundle_ref), custom_call_target="tpu_custom_call" | custom-call | flops 21743271936 | bytes 30670848 | tf_op jit(solution)/shard_map/pallas_call | solution.py:384
  260.3 2.5 fusion.1.x_ref.y_first
  262.8 16.4 %shard_map.255 = (f32[256,1536]{1,0:T(8,128)}, bf16[256,1536]{1,0:T(8,128)(2,1)}, bf16[256,1536]{1,0:T(8,128)(2,1)}, bf16[256,48]{1,0:T(8,128)(2,1)}, bf16[256,1...) custom-call(s32[2]{0:T(128)} %pad_add_fusion.info_ref, ...), custom_call_target="tpu_custom_call" | custom-call | flops 4831838208 | bytes 11796480 | tf_op jit(solution)/shard_map/pallas_call | solution.py:1060
  279.2 55.8 %all-gather.17.cloned.1.call-done = bf16[24,1120,384]{2,1,0:T(8,128)(2,1)} async-done(((bf16[3,1120,384]{2,1,0:T(8,128)(2,1)}), bf16[24,1120,384]{2,1,0:T(8,128)(2,1)}) %all-gather.17.cloned.1.call-update) | async-done | bytes 20643856 | tf_op jit(solution)/shard_map/all_gather | solution.py:1681
  335.0 97.9 %shard_map.256 = (f32[8,32,1536]{2,1,0:T(8,128)}, bf16[8,4,32,1536]{3,2,1,0:T(8,128)(2,1)}, bf16[8,128,2304]{2,1,0:T(8,128)(2,1)}, bf16[8,128,2304]{2,1,0:T(8,128)(2,1)}) custom-call(bf16[8,32,1536]{2,1,0:T(8,128)(2,1)} %bitcast.119, bf16[2,4,3,1120,384]{4,3,2,1,0:T(8,128)(2,1)} %bitcast.106, bf16[288,1536]{1,0:T(8,128)(2,1)} %get-tuple-element.131.bundle_ref), custom_call_target="tpu_custom_call" | custom-call | flops 21743271936 | bytes 30670848 | tf_op jit(solution)/shard_map/pallas_call | solution.py:384
  433.5 89.3 %shard_map.257 = (f32[8,32,1536]{2,1,0:T(8,128)}, bf16[48,1536]{1,0:T(8,128)(2,1)}, bf16[96,1536]{1,0:T(8,128)(2,1)}) custom-call(bf16[8,32,1536]{2,1,0:T(8,128)(2,1)} %broadcast_select_fusion.ds_ref, bf16[2,4,3,1120,384]{4,3,2,1,0:T(8,128)(2,1)} %bitcast.107, bf16[8,128,1536]{2,1,0:T(8,128)(2,1)} %bitcast.117, ...), custom_call_target="tpu_custom_call" | custom-call | flops 21743271936 | bytes 30670848 | tf_op jit(solution)/shard_map/pallas_call | solution.py:541
  522.9 31.6 %shard_map.258 = (f32[256,1536]{1,0:T(8,128)}, bf16[256,1536]{1,0:T(8,128)(2,1)}, bf16[112,1536]{1,0:T(8,128)(2,1)}) custom-call(s32[2]{0:T(128)} %pad_add_fusion.info_ref, bf16[256,1536]{1,0:T(8,128)(2,1)} %fusion.1.x_ref.y_first, f32[256,1536]{1,0:T(8,128)} %get-tuple-element.77.mid_ref, bf16[256,1536]{1,0:T(8,128)(2,1)} %get-tuple-element.129.dy_ref, ...), custom_call_target="tpu_custom_call" | custom-call | flops 4831838208 | bytes 11796480 | tf_op jit(solution)/shard_map/pallas_call | solution.py:1247
  554.6 102.2 %shard_map.259 = (f32[8,32,1536]{2,1,0:T(8,128)}, bf16[48,1536]{1,0:T(8,128)(2,1)}, bf16[96,1536]{1,0:T(8,128)(2,1)}) custom-call(bf16[8,32,1536]{2,1,0:T(8,128)(2,1)} %bitcast.112, bf16[2,4,3,1120,384]{4,3,2,1,0:T(8,128)(2,1)} %bitcast.105, bf16[8,128,1536]{2,1,0:T(8,128)(2,1)} %bitcast.116, bf16[8,128,2304]{2,1,0:T(8,128)(2,1)} %get-tuple-element.98.gate_in, ...), custom_call_target="tpu_custom_call" | custom-call | flops 21743271936 | bytes 30670848 | tf_op jit(solution)/shard_map/pallas_call | solution.py:541
  657.6 1.1 fusion.y_second
  658.7 36.1 %shard_map.260 = (f32[256,1536]{1,0:T(8,128)}, bf16[256,1536]{1,0:T(8,128)(2,1)}, bf16[112,1536]{1,0:T(8,128)(2,1)}) custom-call(s32[2]{0:T(128)} %pad_add_fusion.info_ref, bf16[256,1536]{1,0:T(8,128)(2,1)} %dynamic-slice_bitcast_fusion.x_ref, f32[256,1536]{1,0:T(8,128)} %get-tuple-element.72.mid_ref, f32[256,1536]{1,0:T(8,128)} %get-tuple-element.91.dy_ref.g_second, ...), custom_call_target="tpu_custom_call" | custom-call | flops 4831838208 | bytes 11796480 | tf_op jit(solution)/shard_map/pallas_call | solution.py:1247
  694.8 54.6 %shard_map.261 = (bf16[8,224,1536]{2,1,0:T(8,128)(2,1)}, bf16[2,256,1536]{2,1,0:T(8,128)(2,1)}, f32[2,256,1536]{2,1,0:T(8,128)}) custom-call(bf16[112,1536]{1,0:T(8,128)(2,1)} %get-tuple-element.109.attn_ref, bf16[48,1536]{1,0:T(8,128)(2,1)} %get-tuple-element.110.whole_ref, bf16[96,1536]{1,0:T(8,128)(2,1)} %get-tuple-element.111.parts_ref, ...), custom_call_target="tpu_custom_call" | custom-call | tf_op jit(solution)/shard_map/pallas_call | solution.py:1497
  749.5 8.6 %shard_map.262 = (f32[8,80,1536]{2,1,0:T(8,128)}, f32[8,16,384]{2,1,0:T(8,128)}, f32[8,2,16,256]{3,2,1,0:T(8,128)}, f32[8,2,16,2240]{3,2,1,0:T(8,128)}, f32[8,16...) custom-call(bf16[8,224,1536]{2,1,0:T(8,128)(2,1)} %get-tuple-element.116.first, ...), custom_call_target="tpu_custom_call" | custom-call | tf_op jit(solution)/shard_map/pallas_call | solution.py:1605
  758.1 1.1 copy.35
  759.3 1.3 copy-done.4
  760.6 1.7 copy.36
  (68 shorter events, 13.4 us)
Async XLA Ops:
  7.2 114.0 %copy-start = (bf16[2,256,1536]{2,1,0:T(8,128)(2,1)S(1)}, bf16[2,256,1536]{2,1,0:T(8,128)(2,1)}, u32[]{:S(2)}) copy-start(bf16[2,256,1536]{2,1,0:T(8,128)(2,1)} %param.19) | copy-start | bytes 4718596
  7.2 151.1 %all-gather.13.cloned.1.call-start = ((), (), s32[]{:S(2)}) async-start(), calls=%async_computation.1 | async-start | bytes 23224320 | tf_op jit(solution)/shard_map/all_gather | solution.py:1681
  12.6 1.0 copy-start.11
  12.6 1.2 copy-start.9
  12.7 1.3 copy-start.12
  13.8 4.6 copy-start.13
  14.8 7.3 all-to-all-start
  18.4 244.4 %all-gather.15.cloned.1.call-start = ((), (), s32[]{:S(2)}) async-start(), calls=%async_computation.2 | async-start | bytes 12386304 | tf_op jit(solution)/shard_map/all_gather | solution.py:1680
  22.2 0.8 copy-start.5
  114.5 0.8 copy-start.14
  114.5 1.4 copy-start.15
  114.6 220.4 %all-gather.17.cloned.1.call-start = ((), (), s32[]{:S(2)}) async-start(), calls=%async_computation.3 | async-start | bytes 23224320 | tf_op jit(solution)/shard_map/all_gather | solution.py:1681
  115.3 6.9 copy-start.6
  115.3 439.2 %all-gather.19.cloned.1.call-start = ((), (), s32[]{:S(2)}) async-start(), calls=%async_computation.4 | async-start | bytes 2654208 | tf_op jit(solution)/shard_map/all_gather | solution.py:1710
  123.5 16.6 %copy-start.10 = (bf16[2,256,1536]{2,1,0:T(8,128)(2,1)S(1)}, bf16[2,256,1536]{2,1,0:T(8,128)(2,1)}, u32[]{:S(2)}) copy-start(bf16[2,256,1536]{2,1,0:T(8,128)(2,1)} %param.22) | copy-start | bytes 4718596
  158.2 102.1 %copy-start.2 = (f32[256,1536]{1,0:T(8,128)S(1)}, f32[256,1536]{1,0:T(8,128)}, u32[]{:S(2)}) copy-start(f32[256,1536]{1,0:T(8,128)} %get-tuple-element.72.mid_ref) | copy-start | bytes 4718596
  522.8 133.9 %all-reduce.3.cloned.1.call-start = ((), (), s32[]{:S(2)}) async-start(), calls=%async_computation.7 | async-start | bytes 983040 | tf_op jit(solution)/shard_map/psum | solution.py:1726
  554.5 194.9 %all-gather.23.cloned.1.call-start = ((), (), s32[]{:S(2)}) async-start(), calls=%async_computation.6 | async-start | bytes 1327104 | tf_op jit(solution)/shard_map/all_gather | solution.py:1710
  554.6 103.0 %copy-start.3 = (f32[256,1536]{1,0:T(8,128)S(1)}, f32[256,1536]{1,0:T(8,128)}, u32[]{:S(2)}) copy-start(f32[256,1536]{1,0:T(8,128)} %get-tuple-element.77.mid_ref) | copy-start | bytes 4718596
  554.6 103.0 %copy-start.8 = (f32[8,32,1536]{2,1,0:T(8,128)S(1)}, f32[8,32,1536]{2,1,0:T(8,128)}, u32[]{:S(2)}) copy-start(f32[8,32,1536]{2,1,0:T(8,128)} %get-tuple-element.112) | copy-start | bytes 4718596
  656.8 92.7 %all-gather.21.cloned.1.call-start = ((), (), s32[]{:S(2)}) async-start(), calls=%async_computation.5 | async-start | bytes 3096576 | tf_op jit(solution)/shard_map/all_gather | solution.py:1710
  749.5 8.6 %copy-start.7 = (bf16[2,256,1536]{2,1,0:T(8,128)(2,1)S(1)}, bf16[2,256,1536]{2,1,0:T(8,128)(2,1)}, u32[]{:S(2)}) copy-start(bf16[2,256,1536]{2,1,0:T(8,128)(2,1)} %get-tuple-element.114) | copy-start | bytes 4718596
  758.1 2.5 copy-start.4
  760.6 2.5 copy-start.1
Sparse Core Ops, SparseCore 0:
  12.8 145.4 all-gather.12
  160.1 66.6 all-gather.14
  228.7 106.1 all-gather.16
  523.0 26.2 all-gather.18
  554.6 40.7 all-reduce.2
  656.9 23.5 all-gather.22
  682.6 43.1 all-gather.20

commit v11 on v10

--- a/solution.py
+++ b/solution.py
@@ -14,6 +14,7 @@
 EPSILON = 1e-06
 ROPE_BASE = 1000000.0
 MASKED_SCORE = -1e30
+LOG2_E = math.log2(math.e)
 CHUNKS = 8
 LANES = 128
 VMEM_LIMIT = 60 * 2**20
@@ -1003,10 +1004,10 @@
             kv_head = h // group
             k = kvbuf[o, :, head_cols(kv_head)]
             v = kvbuf[o, :, head_cols(KV_HEADS + kv_head)]
-            scores = jnp.where(allowed, dot_t(k, q_ref[:, head_cols(h)]) * scale, MASKED_SCORE)
+            scores = jnp.where(allowed, dot_t(k, q_ref[:, head_cols(h)]) * (scale * LOG2_E), MASKED_SCORE)
             top = jnp.maximum(peak[h], jnp.max(scores, axis=0, keepdims=True))
-            soft = jnp.exp(scores - top)
-            shift = jnp.exp(peak[h] - top)
+            soft = jnp.exp2(scores - top)
+            shift = jnp.exp2(peak[h] - top)
             total[h] = total[h] * shift + jnp.sum(soft, axis=0, keepdims=True)
             acc[h] = acc[h] * shift + t_dot(v, soft.astype(BF))
             peak[h] = top
@@ -1031,7 +1032,7 @@
     keep.start()
     for h in range(heads):
         attended_ref[:, h * HEAD_DIM : (h + 1) * HEAD_DIM] = (acc[h] * (1.0 / total[h])).T.astype(BF)
-        log_ref[h] = peak[h] + jnp.log(total[h])
+        log_ref[h] = peak[h] + jnp.log(total[h]) * LOG2_E
     rank = dot_t(attended_ref[...], bundle_ref[rows_of(B_HEADS + 1)]).astype(BF)
     lowr_ref[...] = low
     rank_ref[...] = rank
@@ -1166,8 +1167,8 @@
             v = kv_ref[o, :, head_cols(KV_HEADS + kv_head)]
             q = q_ref[:, head_cols(h)]
             do = do_ref[:, head_cols(h)]
-            scores = dot_t(k, q) * scale - log_ref[h]
-            soft = jnp.exp(jnp.where(allowed, scores, MASKED_SCORE))
+            scores = dot_t(k, q) * (scale * LOG2_E) - log_ref[h]
+            soft = jnp.exp2(jnp.where(allowed, scores, MASKED_SCORE))
             grad = (soft * (dot_t(v, do) - delta[h])).astype(BF)
             dq_acc[h] += t_dot(k, grad)
             dkv_acc[:, head_cols(kv_head)] += dot(grad, q) * scale

time: 779 us -> 778 us (level)
  no operation moved by 1% of the time
where the time goes in v11:
time: 778 us; the launch traced here: 771 us
  Pallas kernels  656 us (84%)
  waiting for transfers between devices  73.4 us (9%)
  between operations  14.7 us (2%)
  local copies, waits for them, and re-layouts  11.6 us (1%)
  other arithmetic  11.2 us (1%)
    pallas_call x2, Pallas kernels, mlp_forward(): pl.pallas_call(partial(mlp_kernel, line, CHUNKS, ff_tile(hidden)), in_spe...  200 us
    pallas_call x2, Pallas kernels, mlp_backward(): pl.pallas_call(partial(mlp_back_kernel, line, CHUNKS, ff_tile(hidden)), i...  191 us
    pallas_call x1, Pallas kernels, gather_first(): pl.pallas_call(partial(gather_kernel, line, peers), in_specs=[vspec()] *...  91.5 us
    all_gather x2, waiting for transfers between devices, weights(): mlp = lax.all_gather(ff[layer], ('section', 'dp'), axis=0)  71.9 us
    pallas_call x2, Pallas kernels, attend_backward(): pl.pallas_call(partial(attend_back_kernel, line, heads // KV_HEADS), in_s...  68.3 us
    pallas_call x1, Pallas kernels, reduce_first(): pl.pallas_call(partial(reduce_kernel, line, peers, extra), in_specs=[vspe...  54.6 us
    pallas_call x2, Pallas kernels, attend_forward(): pl.pallas_call(partial(attend_kernel, line, heads // KV_HEADS), in_specs=...  33.3 us
  transfers between devices with their start and end apart: 8, of which 2 were waited for; matrix products, arithmetic and copies ran while one was open for 2% of the time, Pallas kernels for 59%

profile of v11, /device:TPU:0, one launch (start us, length us, event | category | flops | bytes accessed | tf_op | source)
XLA Modules:
  0.0 770.7 jit_solution(18081202967740817401)
XLA Ops:
  7.2 5.4 shard_map.253
  14.8 3.5 all-to-all-start
  19.0 3.2 shard_map.250
  23.0 91.5 %shard_map.251 = (bf16[8,4,192,896]{3,2,1,0:T(8,128)(2,1)}, bf16[4,192,896]{2,1,0:T(8,128)(2,1)}, bf16[2,288,1536]{2,1,0:T(8,128)(2,1)}) custom-call(bf16[2,192,896]{2,1,0:T(8,128)(2,1)} %copy-done.5, bf16[2,288,1536]{2,1,0:T(8,128)(2,1)} %get-tuple-element.68.bundles, bf16[2,48,384]{2,1,0:T(8,128)(2,1)} %get-tuple-element.69.heads), custom_call_target="tpu_custom_call" | custom-call | tf_op jit(solution)/shard_map/pallas_call | solution.py:857
  116.6 1.3 pad_add_fusion.info_ref
  122.2 1.3 slice_bitcast_fusion
  123.5 16.7 %shard_map.252 = (f32[256,1536]{1,0:T(8,128)}, bf16[256,1536]{1,0:T(8,128)(2,1)}, bf16[256,1536]{1,0:T(8,128)(2,1)}, bf16[256,48]{1,0:T(8,128)(2,1)}, bf16[256,1...) custom-call(s32[2]{0:T(128)} %pad_add_fusion.info_ref, ...), custom_call_target="tpu_custom_call" | custom-call | flops 4831838208 | bytes 11796480 | tf_op jit(solution)/shard_map/pallas_call | solution.py:1061
  140.1 1.0 bitcast_select_fusion
  142.2 16.1 %all-gather.13.cloned.1.call-done = bf16[24,1120,384]{2,1,0:T(8,128)(2,1)} async-done(((bf16[3,1120,384]{2,1,0:T(8,128)(2,1)}), bf16[24,1120,384]{2,1,0:T(8,128)(2,1)}) %all-gather.13.cloned.1.call-update) | async-done | bytes 20643856 | tf_op jit(solution)/shard_map/all_gather | solution.py:1682
  158.2 101.9 %shard_map.254 = (f32[8,32,1536]{2,1,0:T(8,128)}, bf16[8,4,32,1536]{3,2,1,0:T(8,128)(2,1)}, bf16[8,128,2304]{2,1,0:T(8,128)(2,1)}, bf16[8,128,2304]{2,1,0:T(8,128)(2,1)}) custom-call(bf16[8,32,1536]{2,1,0:T(8,128)(2,1)} %bitcast.118, bf16[2,4,3,1120,384]{4,3,2,1,0:T(8,128)(2,1)} %bitcast.104, bf16[288,1536]{1,0:T(8,128)(2,1)} %get-tuple-element.132.bundle_ref), custom_call_target="tpu_custom_call" | custom-call | flops 21743271936 | bytes 30670848 | tf_op jit(solution)/shard_map/pallas_call | solution.py:385
  260.1 2.5 fusion.1.x_ref.y_first
  262.6 16.7 %shard_map.255 = (f32[256,1536]{1,0:T(8,128)}, bf16[256,1536]{1,0:T(8,128)(2,1)}, bf16[256,1536]{1,0:T(8,128)(2,1)}, bf16[256,48]{1,0:T(8,128)(2,1)}, bf16[256,1...) custom-call(s32[2]{0:T(128)} %pad_add_fusion.info_ref, ...), custom_call_target="tpu_custom_call" | custom-call | flops 4831838208 | bytes 11796480 | tf_op jit(solution)/shard_map/pallas_call | solution.py:1061
  279.3 55.8 %all-gather.17.cloned.1.call-done = bf16[24,1120,384]{2,1,0:T(8,128)(2,1)} async-done(((bf16[3,1120,384]{2,1,0:T(8,128)(2,1)}), bf16[24,1120,384]{2,1,0:T(8,128)(2,1)}) %all-gather.17.cloned.1.call-update) | async-done | bytes 20643856 | tf_op jit(solution)/shard_map/all_gather | solution.py:1682
  335.1 97.9 %shard_map.256 = (f32[8,32,1536]{2,1,0:T(8,128)}, bf16[8,4,32,1536]{3,2,1,0:T(8,128)(2,1)}, bf16[8,128,2304]{2,1,0:T(8,128)(2,1)}, bf16[8,128,2304]{2,1,0:T(8,128)(2,1)}) custom-call(bf16[8,32,1536]{2,1,0:T(8,128)(2,1)} %bitcast.119, bf16[2,4,3,1120,384]{4,3,2,1,0:T(8,128)(2,1)} %bitcast.106, bf16[288,1536]{1,0:T(8,128)(2,1)} %get-tuple-element.131.bundle_ref), custom_call_target="tpu_custom_call" | custom-call | flops 21743271936 | bytes 30670848 | tf_op jit(solution)/shard_map/pallas_call | solution.py:385
  433.5 89.3 %shard_map.257 = (f32[8,32,1536]{2,1,0:T(8,128)}, bf16[48,1536]{1,0:T(8,128)(2,1)}, bf16[96,1536]{1,0:T(8,128)(2,1)}) custom-call(bf16[8,32,1536]{2,1,0:T(8,128)(2,1)} %broadcast_select_fusion.ds_ref, bf16[2,4,3,1120,384]{4,3,2,1,0:T(8,128)(2,1)} %bitcast.107, bf16[8,128,1536]{2,1,0:T(8,128)(2,1)} %bitcast.117, ...), custom_call_target="tpu_custom_call" | custom-call | flops 21743271936 | bytes 30670848 | tf_op jit(solution)/shard_map/pallas_call | solution.py:542
  523.0 31.7 %shard_map.258 = (f32[256,1536]{1,0:T(8,128)}, bf16[256,1536]{1,0:T(8,128)(2,1)}, bf16[112,1536]{1,0:T(8,128)(2,1)}) custom-call(s32[2]{0:T(128)} %pad_add_fusion.info_ref, bf16[256,1536]{1,0:T(8,128)(2,1)} %fusion.1.x_ref.y_first, f32[256,1536]{1,0:T(8,128)} %get-tuple-element.77.mid_ref, bf16[256,1536]{1,0:T(8,128)(2,1)} %get-tuple-element.129.dy_ref, ...), custom_call_target="tpu_custom_call" | custom-call | flops 4831838208 | bytes 11796480 | tf_op jit(solution)/shard_map/pallas_call | solution.py:1248
  554.8 101.9 %shard_map.259 = (f32[8,32,1536]{2,1,0:T(8,128)}, bf16[48,1536]{1,0:T(8,128)(2,1)}, bf16[96,1536]{1,0:T(8,128)(2,1)}) custom-call(bf16[8,32,1536]{2,1,0:T(8,128)(2,1)} %bitcast.112, bf16[2,4,3,1120,384]{4,3,2,1,0:T(8,128)(2,1)} %bitcast.105, bf16[8,128,1536]{2,1,0:T(8,128)(2,1)} %bitcast.116, bf16[8,128,2304]{2,1,0:T(8,128)(2,1)} %get-tuple-element.98.gate_in, ...), custom_call_target="tpu_custom_call" | custom-call | flops 21743271936 | bytes 30670848 | tf_op jit(solution)/shard_map/pallas_call | solution.py:542
  657.6 1.1 fusion.y_second
  658.7 36.5 %shard_map.260 = (f32[256,1536]{1,0:T(8,128)}, bf16[256,1536]{1,0:T(8,128)(2,1)}, bf16[112,1536]{1,0:T(8,128)(2,1)}) custom-call(s32[2]{0:T(128)} %pad_add_fusion.info_ref, bf16[256,1536]{1,0:T(8,128)(2,1)} %dynamic-slice_bitcast_fusion.x_ref, f32[256,1536]{1,0:T(8,128)} %get-tuple-element.72.mid_ref, f32[256,1536]{1,0:T(8,128)} %get-tuple-element.91.dy_ref.g_second, ...), custom_call_target="tpu_custom_call" | custom-call | flops 4831838208 | bytes 11796480 | tf_op jit(solution)/shard_map/pallas_call | solution.py:1248
  695.2 54.6 %shard_map.261 = (bf16[8,224,1536]{2,1,0:T(8,128)(2,1)}, bf16[2,256,1536]{2,1,0:T(8,128)(2,1)}, f32[2,256,1536]{2,1,0:T(8,128)}) custom-call(bf16[112,1536]{1,0:T(8,128)(2,1)} %get-tuple-element.109.attn_ref, bf16[48,1536]{1,0:T(8,128)(2,1)} %get-tuple-element.110.whole_ref, bf16[96,1536]{1,0:T(8,128)(2,1)} %get-tuple-element.111.parts_ref, ...), custom_call_target="tpu_custom_call" | custom-call | tf_op jit(solution)/shard_map/pallas_call | solution.py:1498
  750.0 8.7 %shard_map.262 = (f32[8,80,1536]{2,1,0:T(8,128)}, f32[8,16,384]{2,1,0:T(8,128)}, f32[8,2,16,256]{3,2,1,0:T(8,128)}, f32[8,2,16,2240]{3,2,1,0:T(8,128)}, f32[8,16...) custom-call(bf16[8,224,1536]{2,1,0:T(8,128)(2,1)} %get-tuple-element.116.first, ...), custom_call_target="tpu_custom_call" | custom-call | tf_op jit(solution)/shard_map/pallas_call | solution.py:1606
  758.6 1.1 copy.35
  759.8 1.3 copy-done.4
  761.1 1.7 copy.36
  (68 shorter events, 13.4 us)
Async XLA Ops:
  7.2 114.0 %copy-start = (bf16[2,256,1536]{2,1,0:T(8,128)(2,1)S(1)}, bf16[2,256,1536]{2,1,0:T(8,128)(2,1)}, u32[]{:S(2)}) copy-start(bf16[2,256,1536]{2,1,0:T(8,128)(2,1)} %param.19) | copy-start | bytes 4718596
  7.2 151.1 %all-gather.13.cloned.1.call-start = ((), (), s32[]{:S(2)}) async-start(), calls=%async_computation.1 | async-start | bytes 23224320 | tf_op jit(solution)/shard_map/all_gather | solution.py:1682
  12.6 1.0 copy-start.11
  12.6 1.2 copy-start.9
  12.7 1.3 copy-start.12
  13.8 4.6 copy-start.13
  14.8 7.3 all-to-all-start
  18.4 244.2 %all-gather.15.cloned.1.call-start = ((), (), s32[]{:S(2)}) async-start(), calls=%async_computation.2 | async-start | bytes 12386304 | tf_op jit(solution)/shard_map/all_gather | solution.py:1681
  22.2 0.8 copy-start.5
  114.5 0.8 copy-start.14
  114.5 1.4 copy-start.15
  114.6 220.5 %all-gather.17.cloned.1.call-start = ((), (), s32[]{:S(2)}) async-start(), calls=%async_computation.3 | async-start | bytes 23224320 | tf_op jit(solution)/shard_map/all_gather | solution.py:1682
  115.3 6.9 copy-start.6
  115.3 439.4 %all-gather.19.cloned.1.call-start = ((), (), s32[]{:S(2)}) async-start(), calls=%async_computation.4 | async-start | bytes 2654208 | tf_op jit(solution)/shard_map/all_gather | solution.py:1711
  123.5 16.7 %copy-start.10 = (bf16[2,256,1536]{2,1,0:T(8,128)(2,1)S(1)}, bf16[2,256,1536]{2,1,0:T(8,128)(2,1)}, u32[]{:S(2)}) copy-start(bf16[2,256,1536]{2,1,0:T(8,128)(2,1)} %param.22) | copy-start | bytes 4718596
  158.2 101.9 %copy-start.2 = (f32[256,1536]{1,0:T(8,128)S(1)}, f32[256,1536]{1,0:T(8,128)}, u32[]{:S(2)}) copy-start(f32[256,1536]{1,0:T(8,128)} %get-tuple-element.72.mid_ref) | copy-start | bytes 4718596
  522.9 133.9 %all-reduce.3.cloned.1.call-start = ((), (), s32[]{:S(2)}) async-start(), calls=%async_computation.7 | async-start | bytes 983040 | tf_op jit(solution)/shard_map/psum | solution.py:1727
  554.8 195.1 %all-gather.23.cloned.1.call-start = ((), (), s32[]{:S(2)}) async-start(), calls=%async_computation.6 | async-start | bytes 1327104 | tf_op jit(solution)/shard_map/all_gather | solution.py:1711
  554.8 102.8 %copy-start.3 = (f32[256,1536]{1,0:T(8,128)S(1)}, f32[256,1536]{1,0:T(8,128)}, u32[]{:S(2)}) copy-start(f32[256,1536]{1,0:T(8,128)} %get-tuple-element.77.mid_ref) | copy-start | bytes 4718596
  554.8 102.8 %copy-start.8 = (f32[8,32,1536]{2,1,0:T(8,128)S(1)}, f32[8,32,1536]{2,1,0:T(8,128)}, u32[]{:S(2)}) copy-start(f32[8,32,1536]{2,1,0:T(8,128)} %get-tuple-element.112) | copy-start | bytes 4718596
  656.8 93.1 %all-gather.21.cloned.1.call-start = ((), (), s32[]{:S(2)}) async-start(), calls=%async_computation.5 | async-start | bytes 3096576 | tf_op jit(solution)/shard_map/all_gather | solution.py:1711
  749.9 8.7 %copy-start.7 = (bf16[2,256,1536]{2,1,0:T(8,128)(2,1)S(1)}, bf16[2,256,1536]{2,1,0:T(8,128)(2,1)}, u32[]{:S(2)}) copy-start(bf16[2,256,1536]{2,1,0:T(8,128)(2,1)} %get-tuple-element.114) | copy-start | bytes 4718596
  758.6 2.5 copy-start.4
  761.1 2.5 copy-start.1
Sparse Core Ops, SparseCore 0:
  12.8 145.4 all-gather.12
  160.1 66.7 all-gather.14
  228.8 106.2 all-gather.16
  523.0 26.2 all-gather.18
  554.9 41.0 all-reduce.2
  657.0 23.0 all-gather.22
  682.1 42.7 all-gather.20
